TPU v7x, 32 devices: a whole 2x2x4 slice. The times are simulated.
32 devices in a mesh: row: 8 (over z, x), col: 4 (over y, core).
Axes of the slice: x: 2, y: 2, z: 4, core: 2. Of those that a mesh axis runs over, the one named last changes fastest.
Arguments:
- a_blocks: bfloat16 [192, 32, 4096], P('row', 'col'), may hold values from -0.125 to 0.125
- a_cols: int32 [192, 32], P('row'), may hold values from 0 to 191, as said below
- counts: int32 [192], P('row'), may hold values from 8 to 32
- p_blocks: bfloat16 [192, 4, 4096], P('row'), may hold values from -0.8984375 to 0.8984375
- p_cols: int32 [192, 4], replicated, may hold values from 0 to 63, as said below
Outputs:
- coarse: bfloat16 [64, 56, 4096], P('row')
Inputs may be any that keep to these rules, and one draw needn't show every extreme that they name: `a_cols`: slot 0 of block row i names i itself; every slot's column lies within 24 of its row. `p_cols`: the four columns of fine block row i are distinct before clipping to the grid and lie within 8 of (i // 24) * 8 + ((i % 24) * 8) // 24.
All inputs are finite; a program needn't handle non-finite values.
Results may differ from a plain program's by a relative error of at most 0.015.
Values may be sent and summed in bfloat16 or wider, within the bound.
No kernel may reach another device: no remote copies, remote signals or barrier semaphores. Data moves between devices by JAX's collectives and lax.ppermute only.
A program may use at most 192 MiB of HBM per device.

v0:
```python
import jax
import jax.numpy as jnp
from jax import lax
from jax.sharding import PartitionSpec as P

BS = 64
CB = 8


def with_halo(cells, sides, width):
    for axis, dim in sides:
        count = lax.axis_size(axis)
        ends = count - 1
        head = lax.slice_in_dim(cells, 0, width, axis=dim)
        tail = lax.slice_in_dim(cells, cells.shape[dim] - width, cells.shape[dim], axis=dim)
        cells = jnp.concatenate(
            [
                lax.ppermute(tail, axis, [(i, (i + 1) % count) for i in range(ends)]),
                cells,
                lax.ppermute(head, axis, [((i + 1) % count, i) for i in range(ends)]),
            ],
            axis=dim,
        )
    return cells


def blocks(flat):
    return flat.reshape(flat.shape[:-1] + (BS, BS))


def combine_rims(extended, coarse_rows):
    lower = extended[:coarse_rows]
    middle = extended[2 * coarse_rows : 3 * coarse_rows]
    upper = extended[4 * coarse_rows :]
    total = jnp.pad(lower, ((0, 0), (0, 2 * coarse_rows), (0, 0)))
    total = total + jnp.pad(middle, ((0, 0), (coarse_rows, coarse_rows), (0, 0)))
    total = total + jnp.pad(upper, ((0, 0), (2 * coarse_rows, 0), (0, 0)))
    return total


def body(a_blocks, a_cols, counts, p_blocks, p_cols):
    slab_rows = p_blocks.shape[0]
    ncol = lax.axis_size("col")
    share = slab_rows // ncol
    row_index = lax.axis_index("row")
    col_index = lax.axis_index("col")
    span = 5 * CB
    p_near = blocks(with_halo(p_blocks, (("row", 0),), slab_rows))
    padded_ids = jnp.pad(p_cols, ((slab_rows, slab_rows), (0, 0)), constant_values=-1000000)
    near_ids = lax.dynamic_slice_in_dim(padded_ids, row_index * slab_rows, 3 * slab_rows, 0)
    first = col_index * share
    gathered = blocks(lax.all_to_all(a_blocks, "col", split_axis=0, concat_axis=1, tiled=True))
    cols = lax.dynamic_slice_in_dim(a_cols, first, share, 0)
    live_count = lax.dynamic_slice_in_dim(counts, first, share, 0)
    live = jnp.arange(cols.shape[1], dtype=jnp.int32)[None, :] < live_count[:, None]
    local = cols - (row_index - 1) * slab_rows
    picked = p_near[local]
    prods = jnp.einsum("nkab,nktbc->nktac", gathered, picked, preferred_element_type=jnp.float32)
    window = near_ids[local] - (row_index - 2) * CB
    onehot = (
        (window[..., None] == jnp.arange(span, dtype=jnp.int32)) & live[:, :, None, None]
    ).astype(jnp.float32)
    product_ap = jnp.einsum("nktw,nktac->nwac", onehot, prods).astype(jnp.bfloat16)
    own = blocks(lax.dynamic_slice_in_dim(p_blocks, first, share, 0))
    own_ids = (
        lax.dynamic_slice_in_dim(p_cols, row_index * slab_rows + first, share, 0)
        - (row_index - 1) * CB
    )
    onehot_rows = (own_ids[..., None] == jnp.arange(3 * CB, dtype=jnp.int32)).astype(jnp.float32)
    second = jnp.einsum("nsba,nwbc->nswac", own, product_ap, preferred_element_type=jnp.float32)
    partial_rows = jnp.einsum("nsi,nswac->iwac", onehot_rows, second)
    partial_flat = partial_rows.reshape(3 * CB, span, BS * BS)
    extended = with_halo(partial_flat, (("row", 0),), CB)
    total = combine_rims(extended, CB)
    summed = lax.psum(total, "col")
    return summed.astype(jnp.bfloat16)


def solution(mesh):
    return jax.shard_map(
        body,
        mesh=mesh,
        in_specs=(P("row", "col", None), P("row", None), P("row"), P("row", None, None), P()),
        out_specs=P("row", None, None),
        check_vma=False,
    )
```

profile of v0, /device:TPU:9, one launch (start us, length us, event | category | flops | bytes accessed | tf_op | source)
XLA Modules:
  0.0 560.6 jit_solution(12921285199912833216)
XLA Ops:
  0.0 3.0 collective-permute-start.1
  3.0 2.3 collective-permute-start
  5.3 5.5 all-to-all-start
  10.8 1.0 constant_dynamic-slice_fusion
  11.8 0.7 dynamic_slice.18
  12.6 0.7 compare_select_fusion
  13.3 0.1 reshape.44
  13.4 0.8 copy.7
  14.2 0.4 reshape.68
  14.6 0.7 gather_fusion
  15.3 0.8 dynamic-slice_subtract_fusion
  16.0 0.1 iota_compare_fusion.2
  16.1 1.2 fusion.11
  17.3 20.1 %collective-permute-done.1 = bf16[24,4,4096]{2,1,0:T(4,128)(2,1)S(1)} collective-permute-done((bf16[24,4,4096]{2,1,0:T(4,128)(2,1)}, bf16[24,4,4096]{2,1,0:T(4,128)(2,1)S(1)}, u32[]{:S(2)}, u32[]{:S(2)}) %collective-permute-start.1) | collective-permute-done | bytes 786464 | tf_op jit(solution)/shard_map/ppermute | solution.py:20
  37.4 1.1 collective-permute-done
  38.4 2.7 pad_maximum_fusion
  41.1 1.3 copy.8
  42.4 6.2 %reshape.39 = bf16[72,4,64,64]{3,2,0,1:T(8,128)(2,1)} reshape(bf16[72,4,4096]{2,0,1:T(8,128)(2,1)S(1)} %copy.8) | data formatting | bytes 4718592 | tf_op jit(solution)/shard_map/reshape | solution.py:28
  48.6 10.6 %gather_fusion.1 = bf16[192,4,64,64]{3,2,1,0:T(8,128)(2,1)} fusion(bf16[72,4,64,64]{3,2,0,1:T(8,128)(2,1)} %reshape.39, s32[1024]{0:T(1024)S(1)} %pad_clamp_fusion), kind=kCustom, calls=%fused_computation.1 | custom fusion | bytes 12583680 | tf_op jit(solution)/shard_map/gather | solution.py:57
  59.1 0.0 all-to-all-done
  59.1 2.7 copy.29
  61.8 4.3 reshape.64
  66.1 9.1 %convolution_bitcast_fusion = bf16[6,32,4,64,64]{3,4,2,1,0:T(8,128)(2,1)} fusion(bf16[6,32,4,64,64]{4,3,2,1,0:T(8,128)(2,1)} %bitcast.51, bf16[6,32,64,64,1]{3,2,1,0,4:T(8,128)(2,1)S(1)} %reshape.64), kind=kOutput, calls=%fused_computation.5 | convolution fusion | flops 402653184 | bytes 14155776 | tf_op jit(solution)/shard_map/nkab,nktbc->nktac/dot_general | solution.py:58
  75.3 0.0 copy-start
  75.3 17.7 %copy.15 = bf16[6,32,4,64,64]{4,1,2,3,0:T(8,128)(2,1)} copy(bf16[6,32,4,64,64]{3,4,2,1,0:T(8,128)(2,1)} %convolution_bitcast_fusion) | data formatting | bytes 12582912 | tf_op jit(solution)/shard_map/nkab,nktbc->nktac/transpose | solution.py:58
  92.9 0.0 copy-done
  92.9 6.4 %fusion.12 = bf16[6,40,64,64,1]{3,1,4,2,0:T(8,128)(2,1)S(1)} fusion(bf16[6,32,4,64,64]{4,1,2,3,0:T(8,128)(2,1)} %copy.15, pred[6,32,4,40,1]{3,2,1,0,4:T(4,128)(4,1)S(1)} %copy-done), kind=kOutput, calls=%fused_computation.17 | convolution fusion | flops 251658240 | bytes 8288256 | tf_op jit(solution)/shard_map/nktw,nktac->nwac/dot_general | solution.py:63
  99.3 7.9 %fusion.6 = bf16[6,40,64,4,64]{4,2,3,1,0:T(8,128)(2,1)} fusion(bf16[6,40,64,64,1]{3,1,4,2,0:T(8,128)(2,1)S(1)} %fusion.12, bf16[6,4,64,64,1]{3,2,1,0,4:T(8,128)(2,1)S(1)} %reshape.68), kind=kOutput, calls=%fused_computation.9 | convolution fusion | flops 503316480 | bytes 10027008 | tf_op jit(solution)/shard_map/nsba,nwbc->nswac/dot_general | solution.py:70
  107.3 28.3 %copy.19 = bf16[6,40,64,4,64]{2,0,3,4,1:T(8,128)(2,1)} copy(bf16[6,40,64,4,64]{4,2,3,1,0:T(8,128)(2,1)} %fusion.6) | data formatting | bytes 15728640 | tf_op jit(solution)/shard_map/nsba,nwbc->nswac/dot_general | solution.py:70
  135.6 20.8 %fusion.2 = f32[24,40,64,64]{3,0,2,1:T(8,128)} fusion(bf16[6,40,64,4,64]{2,0,3,4,1:T(8,128)(2,1)} %copy.19, s32[6,4]{0,1:T(4,128)S(1)} %dynamic-slice_subtract_fusion), kind=kOutput, calls=%fused_computation.4 | convolution fusion | flops 188744256 | bytes 23593056 | tf_op jit(solution)/shard_map/nsi,nswac->iwac/dot_general | solution.py:71
  156.4 18.7 %fusion.17 = (f32[8,40,64,64]{3,0,2,1:T(8,128)S(1)}, f32[8,40,64,64]{3,0,2,1:T(8,128)}, f32[8,40,64,64]{3,0,2,1:T(8,128)}) fusion(f32[24,40,64,64]{3,0,2,1:T(8,128)} %fusion.2), kind=kLoop, calls=%fused_computation.29 | loop fusion | bytes 31457280 | tf_op jit(solution)/shard_map/slice | solution.py:15
  175.1 5.9 %copy.10 = f32[8,40,64,64]{3,2,1,0:T(8,128)} copy(f32[8,40,64,64]{3,0,2,1:T(8,128)S(1)} %get-tuple-element.5) | data formatting | bytes 10485760 | tf_op jit(solution)/shard_map/slice | solution.py:15
  181.0 9.7 %slice.19 = f32[8,40,4096]{2,1,0:T(8,128)} reshape(f32[8,40,64,64]{3,2,1,0:T(8,128)} %copy.10) | data formatting | bytes 10485760 | tf_op jit(solution)/shard_map/slice | solution.py:15
  190.7 4.0 collective-permute-start.2
  194.7 10.0 %copy.12 = f32[8,40,64,64]{3,2,1,0:T(8,128)} copy(f32[8,40,64,64]{3,0,2,1:T(8,128)} %get-tuple-element.6) | data formatting | bytes 10485760 | tf_op jit(solution)/shard_map/slice | solution.py:14
  204.7 9.7 %slice.23 = f32[8,40,4096]{2,1,0:T(8,128)} reshape(f32[8,40,64,64]{3,2,1,0:T(8,128)} %copy.12) | data formatting | bytes 10485760 | tf_op jit(solution)/shard_map/slice | solution.py:14
  214.4 2.2 collective-permute-start.3
  216.6 10.0 %copy.11 = f32[8,40,64,64]{3,2,1,0:T(8,128)} copy(f32[8,40,64,64]{3,0,2,1:T(8,128)} %get-tuple-element.7) | data formatting | bytes 10485760 | tf_op jit(solution)/shard_map/slice | solution.py:33
  226.5 9.7 %slice.21 = f32[8,40,4096]{2,1,0:T(8,128)} reshape(f32[8,40,64,64]{3,2,1,0:T(8,128)} %copy.11) | data formatting | bytes 10485760 | tf_op jit(solution)/shard_map/slice | solution.py:33
  236.3 183.0 %collective-permute-done.2 = f32[8,40,4096]{2,1,0:T(8,128)} collective-permute-done((f32[8,40,4096]{2,1,0:T(8,128)}, f32[8,40,4096]{2,1,0:T(8,128)}, u32[]{:S(2)}, u32[]{:S(2)}) %collective-permute-start.2) | collective-permute-done | bytes 5242912 | tf_op jit(solution)/shard_map/ppermute | solution.py:18
  419.2 1.9 collective-permute-done.3
  421.1 9.3 %pad_add_fusion = f32[8,56,4096]{2,1,0:T(8,128)} fusion(f32[8,40,4096]{2,1,0:T(8,128)} %collective-permute-done.3, f32[8,40,4096]{2,1,0:T(8,128)} %slice.21, f32[8,40,4096]{2,1,0:T(8,128)} %collective-permute-done.2), kind=kLoop, calls=%fused_computation.7 | loop fusion | flops 3670016 | bytes 23068672 | tf_op jit(solution)/shard_map/add | solution.py:37
  430.4 130.3 %all-reduce.5 = bf16[8,56,4096]{2,1,0:T(8,128)(2,1)} all-reduce(f32[8,56,4096]{2,1,0:T(8,128)} %pad_add_fusion), channel_id=1, replica_groups=mesh['row'=8,'col'=4] {'col'}, use_global_device_ids=true, to_apply=%region_0.1 | all-reduce | flops 1835008 | bytes 11010048 | tf_op jit(solution)/shard_map/psum | solution.py:75
  (3 shorter events, 0.0 us)
Async XLA Ops:
  0.0 37.4 %collective-permute-start.1 = (bf16[24,4,4096]{2,1,0:T(4,128)(2,1)}, bf16[24,4,4096]{2,1,0:T(4,128)(2,1)S(1)}, u32[]{:S(2)}, u32[]{:S(2)}) collective-permute-start(bf16[24,4,4096]{2,1,0:T(4,128)(2,1)} %param.8), channel_id=1, source_target_pairs={{4,0},{8,4},{12,8},{16,12},{20,16},{24,20},{28,24},{5,1},{9,5},{13... | collective-permute-start | bytes 2359304 | tf_op jit(solution)/shard_map/ppermute | solution.py:20
  3.0 35.4 %collective-permute-start = (bf16[24,4,4096]{2,1,0:T(4,128)(2,1)}, bf16[24,4,4096]{2,1,0:T(4,128)(2,1)S(1)}, u32[]{:S(2)}, u32[]{:S(2)}) collective-permute-start(bf16[24,4,4096]{2,1,0:T(4,128)(2,1)} %param.8), channel_id=1, source_target_pairs={{0,4},{4,8},{8,12},{12,16},{16,20},{20,24},{24,28},{1,5},{5,9},{9,... | collective-permute-start | bytes 2359304 | tf_op jit(solution)/shard_map/ppermute | solution.py:18
  5.3 53.8 %all-to-all-start = ((bf16[24,8,4096]{2,1,0:T(8,128)(2,1)}), bf16[24,8,4096]{2,1,0:T(8,128)(2,1)}, u32[]{:S(2)}, u32[]{:S(2)}) async-start(bf16[24,8,4096]{2,1,0:T(8,128)(2,1)} %param.5), calls=%async_computation | async-start | bytes 3145728 | tf_op jit(solution)/shard_map/all_to_all | solution.py:52
  75.3 17.7 %copy-start = (pred[6,32,4,40,1]{3,2,1,0,4:T(4,128)(4,1)S(1)}, pred[6,32,4,40,1]{3,2,1,0,4:T(4,128)(4,1)}, u32[]{:S(2)}) copy-start(pred[6,32,4,40,1]{3,2,1,0,4:T(4,128)(4,1)} %fusion.11) | copy-start | bytes 92164
  190.7 228.6 %collective-permute-start.2 = (f32[8,40,4096]{2,1,0:T(8,128)}, f32[8,40,4096]{2,1,0:T(8,128)}, u32[]{:S(2)}, u32[]{:S(2)}) collective-permute-start(f32[8,40,4096]{2,1,0:T(8,128)} %slice.19), channel_id=1, source_target_pairs={{0,4},{4,8},{8,12},{12,16},{16,20},{20,24},{24,28},{1,5},{5,9},{9,... | collective-permute-start | bytes 15728648 | tf_op jit(solution)/shard_map/ppermute | solution.py:18
  214.4 206.7 %collective-permute-start.3 = (f32[8,40,4096]{2,1,0:T(8,128)}, f32[8,40,4096]{2,1,0:T(8,128)}, u32[]{:S(2)}, u32[]{:S(2)}) collective-permute-start(f32[8,40,4096]{2,1,0:T(8,128)} %slice.23), channel_id=1, source_target_pairs={{4,0},{8,4},{12,8},{16,12},{20,16},{24,20},{28,24},{5,1},{9,5},{13... | collective-permute-start | bytes 15728648 | tf_op jit(solution)/shard_map/ppermute | solution.py:20
where the time goes:
time: 563 us; the launch traced here: 561 us
  waiting for transfers between devices  206 us (37%)
  local copies, waits for them, and re-layouts  148 us (26%)
  blocking collectives  130 us (23%)
  matrix products  44.2 us (8%)
  starting transfers between devices  17 us (3%)
  other arithmetic  14.7 us (3%)
    ppermute x2, waiting for transfers between devices, with_halo(): lax.ppermute(tail, axis, [(i, (i + 1) % count) for i in range(ends)])  184 us
    psum x1, blocking collectives, body(): summed = lax.psum(total, 'col')  130 us
    slice x3, local copies, waits for them, and re-layouts, with_halo(): lax.slice_in_dim(cells, cells.shape[dim] - width, cells.shape[dim], axis=...  34.3 us
    dot_general x1, local copies, waits for them, and re-layouts, body(): jnp.einsum('nsba,nwbc->nswac', own, product_ap, preferred_element_type=jn...  28.3 us
    ppermute x2, waiting for transfers between devices, with_halo(): lax.ppermute(head, axis, [((i + 1) % count, i) for i in range(ends)])  21.9 us
    dot_general x1, matrix products, body(): partial_rows = jnp.einsum('nsi,nswac->iwac', onehot_rows, second)  20.8 us
    slice x2, local copies, waits for them, and re-layouts, combine_rims(): middle = extended[2 * coarse_rows:3 * coarse_rows]  19.7 us
    slice x2, local copies, waits for them, and re-layouts, with_halo(): head = lax.slice_in_dim(cells, 0, width, axis=dim)  19.7 us
  transfers between devices with their start and end apart: 5, of which 4 were waited for; matrix products, arithmetic and copies ran while one was open for 12% of the time, Pallas kernels for 0%

commit v1 on v0

v1 whole, which is shorter than its diff:
```python
import functools

import jax
import jax.numpy as jnp
from jax import lax
from jax.experimental import pallas as pl
from jax.experimental.pallas import tpu as pltpu
from jax.sharding import PartitionSpec as P

BS = 64
CB = 8
GROUPS = 5
LANES = 128
BF = jnp.bfloat16
F32 = jnp.float32
MIB = 1 << 20

VM = pl.BlockSpec(memory_space=pltpu.VMEM)
SM = pl.BlockSpec(memory_space=pltpu.SMEM)


def params(mib):
    return pltpu.CompilerParams(vmem_limit_bytes=mib * MIB)


def low_lanes(rows):
    return lax.broadcasted_iota(jnp.int32, (rows, LANES), 1) < BS


def dot(a, b):
    return lax.dot_general(a, b, (((1,), (0,)), ((), ())), preferred_element_type=F32)


def relayout_kernel(x_ref, o_ref, scr):
    rows, nb, _ = x_ref.shape
    low = low_lanes(32)
    for r in range(rows):
        for q in range(32):
            scr[r, pl.ds(q * 8, nb), :] = x_ref[r, :, q * LANES : (q + 1) * LANES].astype(F32)
        for k in range(0, nb, 2):
            x0 = scr[r, pl.ds(k, 32, stride=8), :]
            x1 = scr[r, pl.ds(k + 1, 32, stride=8), :]
            o_ref[r, 0:32, k * BS : (k + 2) * BS] = jnp.where(low, x0, pltpu.roll(x1, BS, 1)).astype(BF)
            o_ref[r, 32:64, k * BS : (k + 2) * BS] = jnp.where(low, pltpu.roll(x0, BS, 1), x1).astype(BF)


def relayout(x, first, rows):
    nb = x.shape[1]
    step = 4
    return pl.pallas_call(
        relayout_kernel,
        grid=(rows // step,),
        out_shape=jax.ShapeDtypeStruct((rows, BS, nb * BS), BF),
        in_specs=[pl.BlockSpec((step, nb, BS * BS), lambda i: (i + first // step, 0, 0))],
        out_specs=pl.BlockSpec((step, BS, nb * BS), lambda i: (i, 0, 0)),
        scratch_shapes=[pltpu.VMEM((step, 256, LANES), F32)],
        compiler_params=params(16),
        name="relayout",
    )(x)


def left_kernel(rb, chunks, pct_ref, pl_ref, o_ref):
    slab = lax.axis_index("row")
    ac = BS // chunks
    low = low_lanes(4 * BS)
    o_ref[...] = jnp.zeros_like(o_ref)

    def pair(ip, carry):
        for half in range(2):
            i = ip * 2 + half
            x = pl_ref[i].astype(F32)
            xt = jnp.concatenate([x, x], axis=0).T
            keep = jnp.where(low if half == 0 else jnp.logical_not(low), xt, 0.0)
            for s in range(4):
                w = pct_ref[s, slab * rb + i] - (slab - 1) * CB
                place = jnp.where(w < CB, w, jnp.where(w < 2 * CB, w + CB, w - CB))
                for ch in range(chunks):
                    piece = keep[s * BS + ch * ac : s * BS + (ch + 1) * ac]
                    old = o_ref[ch, ip, place].astype(F32)
                    o_ref[ch, ip, place] = (old + piece).astype(BF)
        return carry

    lax.fori_loop(0, rb // 2, pair, 0)


def left_factor(pct, p_own, chunks):
    rb = p_own.shape[0]
    return pl.pallas_call(
        functools.partial(left_kernel, rb, chunks),
        out_shape=jax.ShapeDtypeStruct((chunks, rb // 2, 3 * CB, BS // chunks, LANES), BF),
        in_specs=[SM, VM],
        out_specs=VM,
        compiler_params=params(24),
        name="left_factor",
    )(pct, p_own)


def right_kernel(rb, ka, nfb, share, tiles, pct_ref, cols_ref, counts_ref, own, pr, ps, nr, ns, o_ref, place_ref):
    slab = lax.axis_index("row")
    col = lax.axis_index("col")
    core = lax.rem(col, 2)
    half = rb // 2
    base = (slab - 1) * rb
    low1 = lax.broadcasted_iota(jnp.int32, (1, LANES), 1) < BS
    low = low_lanes(BS)
    rows = lax.broadcasted_iota(jnp.int32, (BS, BS), 0)
    cols = lax.broadcasted_iota(jnp.int32, (BS, BS), 1)
    order = (rows == 2 * lax.rem(cols, 32) + cols // 32).astype(F32).astype(BF)

    def window(n):
        if n >= GROUPS * share:
            return jnp.int32(-7)
        return CB * (n % GROUPS) + share * col + n // GROUPS

    wants = [jnp.where(low1, window(p), window(tiles + p)) for p in range(tiles)]

    def fill(src, count, near_first, out_first):
        def one(jj, carry):
            fine = base + near_first + jj
            valid = (fine >= 0) & (fine < nfb)
            at = jnp.clip(fine, 0, nfb - 1)
            x = dot(order, src[jj])
            dups = []
            for t in range(0, 4, 2):
                pair = x[:, t * BS : (t + 2) * BS]
                swapped = pltpu.roll(pair, BS, 1)
                dups += [jnp.where(low, pair, swapped), jnp.where(low, swapped, pair)]
            idx = [jnp.where(valid, pct_ref[t, at] - (slab - 2) * CB, -1000000) for t in range(4)]
            for p in range(tiles):
                total = jnp.zeros((BS, LANES), F32)
                for t in range(4):
                    total = total + jnp.where(wants[p] == idx[t], dups[t], 0.0)
                o_ref[out_first + jj, :, p * LANES : (p + 1) * LANES] = total.astype(BF)
            return carry

        lax.fori_loop(0, count, one, 0)

    fill(own, rb, rb, 0)
    fill(pr, half, half * core, rb)
    fill(ps, half, half * (1 - core), rb + half)
    fill(nr, half, 2 * rb + half * core, 2 * rb)
    fill(ns, half, 2 * rb + half * (1 - core), 2 * rb + half)
    o_ref[3 * rb] = jnp.zeros((BS, tiles * LANES), BF)

    def places(i, carry):
        live = counts_ref[i]
        for k in range(ka):
            near = cols_ref[i, k] - base
            side = near // rb
            inside = near - side * rb
            far = lax.div(inside, half)
            off = inside - half * far + half * lax.rem(far + core, 2)
            spot = jnp.where(side == 1, inside, jnp.where(side == 0, rb + off, 2 * rb + off))
            place_ref[i, k] = jnp.where(k < live, spot, 3 * rb)
        return carry

    lax.fori_loop(0, rb, places, 0)


def right_factor(pct, a_cols, counts, pieces, nfb, share, tiles):
    rb, ka = a_cols.shape
    return pl.pallas_call(
        functools.partial(right_kernel, rb, ka, nfb, share, tiles),
        out_shape=(
            jax.ShapeDtypeStruct((3 * rb + 1, BS, tiles * LANES), BF),
            jax.ShapeDtypeStruct((rb, ka), jnp.int32),
        ),
        in_specs=[SM, SM, SM] + [VM] * 5,
        out_specs=(VM, SM),
        compiler_params=params(24),
        name="right_factor",
    )(pct, a_cols, counts, *pieces)


def product_kernel(first, shifts, has_acc, ks, place_ref, right_ref, *refs):
    col = lax.axis_index("col")
    ny = lax.axis_size("col") // 2
    srcs = refs[: len(shifts)]
    acc_ref = refs[len(shifts)] if has_acc else None
    o_ref = refs[-1]
    rows = o_ref.shape[0]
    width = o_ref.shape[2]
    y, core = col // 2, lax.rem(col, 2)
    firsts = []
    for s, flip in shifts:
        c = core if flip == 0 else 1 - core
        firsts.append((lax.rem(y - s + ny, ny) * 2 + c) * ks)

    def one(i, carry):
        spots = [[place_ref[first + i, f + k] for k in range(ks)] for f in firsts]
        for n0 in range(0, width, 256):
            n1 = min(n0 + 256, width)
            acc = acc_ref[i, :, n0:n1] if has_acc else jnp.zeros((BS, n1 - n0), F32)
            for src, spot in zip(srcs, spots):
                for k in range(0, ks, 4):
                    lhs = src[i, :, k * BS : (k + 4) * BS]
                    rhs = jnp.concatenate([right_ref[spot[k + d], :, n0:n1] for d in range(4)], axis=0)
                    acc = acc + dot(lhs, rhs)
            o_ref[i, :, n0:n1] = acc.astype(o_ref.dtype)
        return carry

    lax.fori_loop(0, rows, one, 0)


def product(place, right, srcs, shifts, first, acc, dtype):
    rows, _, wide = srcs[0].shape
    return pl.pallas_call(
        functools.partial(product_kernel, first, shifts, acc is not None, wide // BS),
        out_shape=jax.ShapeDtypeStruct((rows, BS, right.shape[2]), dtype),
        in_specs=[SM, VM] + [VM] * (len(srcs) + (acc is not None)),
        out_specs=VM,
        compiler_params=params(24),
        name="product",
    )(place, right, *srcs, *([] if acc is None else [acc]))


def coarse_kernel(sets, left_ref, *refs):
    aps = refs[:2]
    outs = refs[2 : 2 + len(sets)]
    scr = refs[-1]
    ac = left_ref.shape[3]
    half = aps[0].shape[0]
    tiles = aps[0].shape[2] // LANES
    low = low_lanes(CB)
    for out, part in zip(outs, sets):
        for n0 in range(0, tiles * LANES, 256):
            n1 = min(n0 + 256, tiles * LANES)
            acc = jnp.zeros((CB * ac, n1 - n0), F32)
            for side, ap in enumerate(aps):
                for g in range(0, half // 2, 2):
                    ip = side * (half // 2) + g
                    lhs = jnp.concatenate(
                        [left_ref[0, ip + d, part * CB : (part + 1) * CB].reshape(CB * ac, LANES) for d in range(2)],
                        axis=1,
                    )
                    rhs = ap[2 * g : 2 * g + 4, :, n0:n1].reshape(4 * BS, n1 - n0)
                    acc = acc + dot(lhs, rhs)
            for p in range(n0 // LANES, n1 // LANES):
                scr[p] = acc[:, p * LANES - n0 : (p + 1) * LANES - n0]
        for p in range(tiles):
            for a in range(0, ac, 2):
                x0 = scr[p, pl.ds(a, CB, stride=ac), :]
                x1 = scr[p, pl.ds(a + 1, CB, stride=ac), :]
                at = slice(a * BS, (a + 2) * BS)
                out[p, :, at] = jnp.where(low, x0, pltpu.roll(x1, BS, 1)).astype(out.dtype)
                out[tiles + p, :, at] = jnp.where(low, pltpu.roll(x0, BS, 1), x1).astype(out.dtype)


def coarse_parts(left, aps, chunk, sets, dtype):
    _, pairs, spots, ac, _ = left.shape
    tiles = aps[0].shape[2] // LANES
    shape = jax.ShapeDtypeStruct((2 * tiles, CB, ac * BS), dtype)
    return pl.pallas_call(
        functools.partial(coarse_kernel, sets),
        grid=(1,),
        out_shape=[shape] * len(sets),
        in_specs=[pl.BlockSpec((1, pairs, spots, ac, LANES), lambda i: (chunk, 0, 0, 0, 0))] + [VM] * 2,
        out_specs=[pl.BlockSpec(shape.shape, lambda i: (0, 0, 0))] * len(sets),
        scratch_shapes=[pltpu.VMEM((tiles, CB * ac, LANES), F32)],
        compiler_params=params(32),
        name="coarse",
    )(left, *aps)


def assemble_kernel(order_ref, *refs):
    out = refs[-1]
    srcs = refs[:-1] if len(refs) % 2 else refs[1:-1]
    x = jnp.concatenate([s[...].reshape(-1, s.shape[2]) for s in srcs], axis=0)
    res = dot(order_ref[...], x)
    wide = out.shape[1]
    for i in range(CB):
        out[i] = res[i * wide : (i + 1) * wide].astype(BF)


def assemble(order, srcs, chunk, total, before):
    n, _, lanes = srcs[0].shape
    step = 512
    per = lanes // step
    wide = n * len(srcs)
    specs = [pl.BlockSpec(order.shape, lambda i: (0, 0))]
    args = [order]
    alias = {}
    if before is not None:
        specs.append(pl.BlockSpec(memory_space=pl.ANY))
        args.append(before)
        alias = {1: 0}
    specs += [pl.BlockSpec((n, CB, step), lambda i: (0, 0, i))] * len(srcs)
    return pl.pallas_call(
        assemble_kernel,
        grid=(per,),
        out_shape=jax.ShapeDtypeStruct((CB, wide, total), BF),
        in_specs=specs,
        out_specs=pl.BlockSpec((CB, wide, step), lambda i: (0, 0, chunk * per + i)),
        input_output_aliases=alias,
        compiler_params=params(24),
        name="assemble",
    )(*args, *srcs)


def assembly_order(shifts, ncol, share):
    col = lax.axis_index("col")
    y, core = col // 2, col % 2
    groups = GROUPS + 2
    size = ncol * share * groups * CB
    out_row = lax.broadcasted_iota(jnp.int32, (size, size), 0)
    src_row = lax.broadcasted_iota(jnp.int32, (size, size), 1)
    per = share * groups * CB
    which, rest = src_row // per, src_row % per
    e, g, i = rest // (groups * CB), rest // CB % groups, rest % CB
    src_col = jnp.zeros_like(which)
    for z, (s, flip) in enumerate(shifts):
        c = (y - s) % (ncol // 2) * 2 + (core + flip) % 2
        src_col = jnp.where(which == z, c, src_col)
    return (out_row == i * (groups * CB) + g * CB + share * src_col + e).astype(BF)


def body(a_blocks, a_cols, counts, p_blocks, p_cols):
    rb, ks, _ = a_blocks.shape
    nrow, ncol = lax.axis_size("row"), lax.axis_size("col")
    ny = ncol // 2
    nfb = p_cols.shape[0]
    share = CB // ncol
    tiles = (GROUPS * share + 1) // 2
    half = rb // 2
    chunks = 2
    core = lax.axis_index("col") % 2

    def over_y(x, s):
        return lax.ppermute(x, "col", [(y * 2 + c, (y + s) % ny * 2 + c) for y in range(ny) for c in range(2)])

    def over_core(x):
        return lax.ppermute(x, "col", [(c, c ^ 1) for c in range(ncol)])

    def upward(x):
        return lax.ppermute(x, "row", [(i, i + 1) for i in range(nrow - 1)])

    def downward(x):
        return lax.ppermute(x, "row", [(i + 1, i) for i in range(nrow - 1)])

    shifts = tuple((s, f) for s in range(ny) for f in range(2))
    pct = p_cols.T

    def gather(x):
        got = [x] + [over_y(x, s) for s in range(1, ny)]
        return [z for g in got for z in (g, over_core(g))]

    a_parts = [gather(relayout(a_blocks, h * half, half)) for h in range(2)]
    p_own = relayout(p_blocks, 0, rb)
    mine = lax.dynamic_slice_in_dim(p_own, core * half, half, 0)
    prev, after = upward(mine), downward(mine)
    pieces = [p_own, prev, over_core(prev), after, over_core(after)]
    left = left_factor(pct, p_own, chunks)
    order = assembly_order(shifts, ncol, share)
    right, place = right_factor(pct, a_cols, counts, pieces, nfb, share, tiles)
    aps = []
    for h in range(2):
        near = product(place, right, a_parts[h][:2], shifts[:2], h * half, None, F32)
        aps.append(product(place, right, a_parts[h][2:], shifts[2:], h * half, near, BF))

    def columns(x, g):
        y = x[: GROUPS * share].reshape((share, GROUPS) + x.shape[1:])
        return jnp.pad(y.astype(F32), ((0, 0), (g, 2 - g), (0, 0), (0, 0)))

    rims = [coarse_parts(left, aps, ch, (0, 1), BF) for ch in range(chunks)]
    mids = [coarse_parts(left, aps, ch, (2,), F32)[0] for ch in range(chunks)]
    out = None
    for ch in range(chunks):
        low, high = rims[ch]
        total = columns(upward(high), 0) + columns(mids[ch], 1) + columns(downward(low), 2)
        total = total.astype(BF).reshape((share * (GROUPS + 2),) + total.shape[2:])
        out = assemble(order, gather(total), ch, BS * BS, out)
    return out


def solution(mesh):
    return jax.shard_map(
        body,
        mesh=mesh,
        in_specs=(P("row", "col", None), P("row", None), P("row"), P("row", None, None), P()),
        out_specs=P("row", None, None),
        check_vma=False,
    )
```

time: 563 us -> 152 us (0.27)
  waiting for transfers between devices: 206 us -> 49.7 us
  local copies, waits for them, and re-layouts: 148 us -> 1.45 us
  blocking collectives: 130 us -> 0 us
  Pallas kernels: 0 us -> 67.6 us
  matrix products: 44.2 us -> 0 us
  starting transfers between devices: 17 us -> 31.8 us
  other arithmetic: 14.7 us -> 0.41 us
    ppermute x4 -> x20, waiting for transfers between devices: 206 us -> 49.7 us  [the longest x3 22.3 us: upward(): return lax.ppermute(x, 'row', [(i, i + 1) for i in range(nrow - 1)])]
    psum x1 -> x0, blocking collectives: 130 us -> none  [body(): summed = lax.psum(total, 'col')]
    slice x7 -> x0, local copies, waits for them, and re-layouts: 73.7 us -> none  [the longest x3 34.3 us: with_halo(): lax.slice_in_dim(cells, cells.shape[dim] - width, cells.shape[dim], axis=...]
    pallas_call x0 -> x15, Pallas kernels: none -> 67.6 us  [the longest x1 29.8 us: right_factor(): pl.pallas_call(functools.partial(right_kernel, rb, ka, nfb, share, tiles)...]
    dot_general x4 -> x0, matrix products: 44.2 us -> none  [the longest x1 20.8 us: body(): partial_rows = jnp.einsum('nsi,nswac->iwac', onehot_rows, second)]
    dot_general x1 -> x0, local copies, waits for them, and re-layouts: 28.3 us -> none  [body(): jnp.einsum('nsba,nwbc->nswac', own, product_ap, preferred_element_type=jn...]
    ppermute x4 -> x20, starting transfers between devices: 11.4 us -> 31.8 us  [the longest x3 10.1 us: downward(): return lax.ppermute(x, 'row', [(i + 1, i) for i in range(nrow - 1)])]
    transpose x1 -> x0, local copies, waits for them, and re-layouts: 17.7 us -> none  [body(): jnp.einsum('nkab,nktbc->nktac', gathered, picked, preferred_element_type=...]
  transfers between devices with their start and end apart: 5 -> 20, of which waited for: 4 -> 10; matrix products, arithmetic and copies ran while one was open for 12% -> 0% of each run, Pallas kernels for 0% -> 37%
where the time goes in v1:
time: 152 us; the launch traced here: 151 us
  Pallas kernels  67.6 us (44%)
  waiting for transfers between devices  49.7 us (33%)
  starting transfers between devices  31.8 us (21%)
    pallas_call x1, Pallas kernels, right_factor(): pl.pallas_call(functools.partial(right_kernel, rb, ka, nfb, share, tiles)...  29.8 us
    ppermute x3, waiting for transfers between devices, upward(): return lax.ppermute(x, 'row', [(i, i + 1) for i in range(nrow - 1)])  22.3 us
    pallas_call x4, Pallas kernels, product(): pl.pallas_call(functools.partial(product_kernel, first, shifts, acc is no...  20.8 us
    ppermute x4, waiting for transfers between devices, over_y(): lax.ppermute(x, 'col', [(y * 2 + c, (y + s) % ny * 2 + c) for y in range(...  19 us
    ppermute x3, starting transfers between devices, downward(): return lax.ppermute(x, 'row', [(i + 1, i) for i in range(nrow - 1)])  10.1 us
    ppermute x10, starting transfers between devices, over_core(): return lax.ppermute(x, 'col', [(c, c ^ 1) for c in range(ncol)])  9.09 us
    ppermute x3, starting transfers between devices, upward(): return lax.ppermute(x, 'row', [(i, i + 1) for i in range(nrow - 1)])  8.45 us
    ppermute x3, waiting for transfers between devices, downward(): return lax.ppermute(x, 'row', [(i + 1, i) for i in range(nrow - 1)])  7.14 us
  transfers between devices with their start and end apart: 20, of which 10 were waited for; matrix products, arithmetic and copies ran while one was open for 0% of the time, Pallas kernels for 37%

profile of v1, /device:TPU:9, one launch (start us, length us, event | category | flops | bytes accessed | tf_op | source)
XLA Modules:
  0.0 151.3 jit_solution(7427586108499505135)
XLA Ops:
  0.0 0.0 copy-start
  0.0 1.4 copy-done
  1.4 0.6 relayout.5.refs_0_
  2.0 1.3 collective-permute-start.7
  3.3 0.6 relayout.4.refs_0_
  3.9 0.3 collective-permute-start.4
  4.2 0.0 copy-done.1
  4.2 0.9 relayout.3.pl_ref.own
  5.1 3.1 %collective-permute-start = (bf16[12,64,256]{2,1,0:T(8,128)(2,1)S(1)}, bf16[12,64,256]{2,1,0:T(8,128)(2,1)S(1)}, u32[]{:S(2)}, u32[]{:S(2)}) collective-permute-start(bf16[12,64,256]{2,1,0:T(8,128)(2,1)S(1)} %constant_dynamic-slice_fusion), channel_id=1, source_target_pairs={{0,4},{4,8},{8,12},{12,16},{16,20},{20,24},{24,28},{1,5},{5,9},{9,... | collective-permute-start | bytes 1179656 | tf_op jit(solution)/shard_map/ppermute | solution.py:335
  8.3 3.1 %collective-permute-start.2 = (bf16[12,64,256]{2,1,0:T(8,128)(2,1)S(1)}, bf16[12,64,256]{2,1,0:T(8,128)(2,1)S(1)}, u32[]{:S(2)}, u32[]{:S(2)}) collective-permute-start(bf16[12,64,256]{2,1,0:T(8,128)(2,1)S(1)} %constant_dynamic-slice_fusion), channel_id=1, source_target_pairs={{4,0},{8,4},{12,8},{16,12},{20,16},{24,20},{28,24},{5,1},{9,5},{13... | collective-permute-start | bytes 1179656 | tf_op jit(solution)/shard_map/ppermute | solution.py:338
  11.3 12.5 %collective-permute-done.pr = bf16[12,64,256]{2,1,0:T(8,128)(2,1)S(1)} collective-permute-done((bf16[12,64,256]{2,1,0:T(8,128)(2,1)S(1)}, bf16[12,64,256]{2,1,0:T(8,128)(2,1)S(1)}, u32[]{:S(2)}, u32[]{:S(2)}) %collective-permute-start) | collective-permute-done | bytes 393248 | tf_op jit(solution)/shard_map/ppermute | solution.py:335
  23.8 2.2 %collective-permute-start.1 = (bf16[12,64,256]{2,1,0:T(8,128)(2,1)S(1)}, bf16[12,64,256]{2,1,0:T(8,128)(2,1)S(1)}, u32[]{:S(2)}, u32[]{:S(2)}) collective-permute-start(bf16[12,64,256]{2,1,0:T(8,128)(2,1)S(1)} %collective-permute-done.pr), channel_id=1, source_target_pairs={{0,1},{1,0},{2,3},{3,2},{4,5},{5,4},{6,7},{7,6},{8,9},{9,8},{10,11... | collective-permute-start | bytes 1179656 | tf_op jit(solution)/shard_map/ppermute | solution.py:332
  26.0 0.0 collective-permute-start.9
  26.0 1.5 collective-permute-done.2.nr
  27.5 0.4 collective-permute-start.6
  27.9 0.0 collective-permute-done.7.refs_0_
  27.9 0.1 collective-permute-start.8
  28.0 9.4 %collective-permute-done.4.refs_0_ = bf16[12,64,512]{2,1,0:T(8,128)(2,1)} collective-permute-done((bf16[12,64,512]{2,1,0:T(8,128)(2,1)S(1)}, bf16[12,64,512]{2,1,0:T(8,128)(2,1)}, u32[]{:S(2)}, u32[]{:S(2)}) %collective-permute-start.4) | collective-permute-done | bytes 786464 | tf_op jit(solution)/shard_map/ppermute | solution.py:329
  37.4 1.5 %collective-permute-start.5 = (bf16[12,64,512]{2,1,0:T(8,128)(2,1)}, bf16[12,64,512]{2,1,0:T(8,128)(2,1)S(1)}, u32[]{:S(2)}, u32[]{:S(2)}) collective-permute-start(bf16[12,64,512]{2,1,0:T(8,128)(2,1)} %collective-permute-done.4.refs_0_), channel_id=1, source_target_pairs={{0,1},{1,0},{2,3},{3,2},{4,5},{5,4},{6,7},{7,6},{8,9},{9,8},{10,11... | collective-permute-start | bytes 2359304 | tf_op jit(solution)/shard_map/ppermute | solution.py:332
  39.0 0.0 collective-permute-done.1.ps
  39.0 0.0 collective-permute-start.3
  39.0 0.0 copy-done.2
  39.0 2.9 %left_factor.1.left_ref = bf16[2,12,24,32,128]{4,3,2,1,0:T(8,128)(2,1)S(1)} custom-call(s32[4,192]{1,0:T(4,128)S(1)} %bitcast.17, bf16[24,64,256]{2,1,0:T(8,128)(2,1)S(1)} %relayout.3.pl_ref.own), custom_call_target="tpu_custom_call" | custom-call | tf_op jit(solution)/shard_map/left_factor/pallas_call | solution.py:88
  41.9 0.0 collective-permute-done.3.ns
  41.9 0.0 copy-done.3
  41.9 0.0 copy-done.4
  41.9 29.8 %right_factor.1 = (bf16[73,64,640]{2,1,0:T(8,128)(2,1)S(1)}, s32[24,32]{1,0:T(8,128)S(1)}) custom-call(s32[4,192]{1,0:T(4,128)S(1)} %bitcast.18, s32[24,32]{1,0:T(8,128)S(1)} %copy-done.3, s32[24]{0:T(128)S(1)} %copy-done.4, bf16[24,64,256]{2,1,0:T(8,128)(2,1)S(1)} %relayout.3.pl_ref.own, bf16[12,64,256]{2,1,0:T(8,128)(2,1)S(1)} %collective-permute-done.pr, ...), custom_call_target="tpu_custom_call" | custom-call | tf_op jit(solution)/shard_map/right_factor/pallas_call | solution.py:162
  71.7 0.0 collective-permute-done.9.refs_1_
  71.7 5.0 %product.6.refs_2_ = f32[12,64,640]{2,1,0:T(8,128)S(1)} custom-call(s32[24,32]{1,0:T(8,128)S(1)} %get-tuple-element.11.place_ref, bf16[73,64,640]{2,1,0:T(8,128)(2,1)S(1)} %get-tuple-element.12.right_ref, bf16[12,64,512]{2,1,0:T(8,128)(2,1)S(1)} %relayout.5.refs_0_, bf16[12,64,512]{2,1,0:T(8,128)(2,1)S(1)} %collective-permute-done.9.refs_1_), custom_call_target="tpu_custom_call" | custom-call | tf_op jit(solution)/shard_map/product/pallas_call | solution.py:207
  76.7 0.0 collective-permute-done.6.refs_1_
  76.7 5.0 %product.4.refs_2_ = f32[12,64,640]{2,1,0:T(8,128)S(1)} custom-call(s32[24,32]{1,0:T(8,128)S(1)} %get-tuple-element.11.place_ref, bf16[73,64,640]{2,1,0:T(8,128)(2,1)S(1)} %get-tuple-element.12.right_ref, bf16[12,64,512]{2,1,0:T(8,128)(2,1)S(1)} %relayout.4.refs_0_, bf16[12,64,512]{2,1,0:T(8,128)(2,1)S(1)} %collective-permute-done.6.refs_1_), custom_call_target="tpu_custom_call" | custom-call | tf_op jit(solution)/shard_map/product/pallas_call | solution.py:207
  81.7 0.0 collective-permute-done.8.refs_1_
  81.7 5.4 %product.7.refs_1_ = bf16[12,64,640]{2,1,0:T(8,128)(2,1)S(1)} custom-call(s32[24,32]{1,0:T(8,128)S(1)} %get-tuple-element.11.place_ref, bf16[73,64,640]{2,1,0:T(8,128)(2,1)S(1)} %get-tuple-element.12.right_ref, bf16[12,64,512]{2,1,0:T(8,128)(2,1)} %collective-permute-done.7.refs_0_, bf16[12,64,512]{2,1,0:T(8,128)(2,1)S(1)} %collective-permute-done.8.refs_1_, ...), custom_call_target="tpu_custom_call" | custom-call | tf_op jit(solution)/shard_map/product/pallas_call | solution.py:207
  87.1 0.0 collective-permute-done.5.refs_1_
  87.2 5.4 %product.5.refs_0_ = bf16[12,64,640]{2,1,0:T(8,128)(2,1)S(1)} custom-call(s32[24,32]{1,0:T(8,128)S(1)} %get-tuple-element.11.place_ref, bf16[73,64,640]{2,1,0:T(8,128)(2,1)S(1)} %get-tuple-element.12.right_ref, bf16[12,64,512]{2,1,0:T(8,128)(2,1)} %collective-permute-done.4.refs_0_, bf16[12,64,512]{2,1,0:T(8,128)(2,1)S(1)} %collective-permute-done.5.refs_1_, ...), custom_call_target="tpu_custom_call" | custom-call | tf_op jit(solution)/shard_map/product/pallas_call | solution.py:207
  92.6 2.1 %coarse.6 = (bf16[10,8,2048]{2,1,0:T(8,128)(2,1)S(1)}, bf16[10,8,2048]{2,1,0:T(8,128)(2,1)S(1)}) custom-call(bf16[2,12,24,32,128]{4,3,2,1,0:T(8,128)(2,1)S(1)} %left_factor.1.left_ref, bf16[12,64,640]{2,1,0:T(8,128)(2,1)S(1)} %product.5.refs_0_, bf16[12,64,640]{2,1,0:T(8,128)(2,1)S(1)} %product.7.refs_1_), custom_call_target="tpu_custom_call" | custom-call | tf_op jit(solution)/shard_map/coarse/pallas_call | solution.py:253
  94.7 3.1 %collective-permute-start.15 = (bf16[10,8,2048]{2,1,0:T(8,128)(2,1)S(1)}, bf16[10,8,2048]{2,1,0:T(8,128)(2,1)S(1)}, u32[]{:S(2)}, u32[]{:S(2)}) collective-permute-start(bf16[10,8,2048]{2,1,0:T(8,128)(2,1)S(1)} %get-tuple-element.15), channel_id=1, source_target_pairs={{0,4},{4,8},{8,12},{12,16},{16,20},{20,24},{24,28},{1,5},{5,9},{9,... | collective-permute-start | bytes 983048 | tf_op jit(solution)/shard_map/ppermute | solution.py:335
  97.8 3.1 %collective-permute-start.16 = (bf16[10,8,2048]{2,1,0:T(8,128)(2,1)S(1)}, bf16[10,8,2048]{2,1,0:T(8,128)(2,1)S(1)}, u32[]{:S(2)}, u32[]{:S(2)}) collective-permute-start(bf16[10,8,2048]{2,1,0:T(8,128)(2,1)S(1)} %get-tuple-element.16), channel_id=1, source_target_pairs={{4,0},{8,4},{12,8},{16,12},{20,16},{24,20},{28,24},{5,1},{9,5},{13... | collective-permute-start | bytes 983048 | tf_op jit(solution)/shard_map/ppermute | solution.py:338
  100.9 2.1 %coarse.4 = (bf16[10,8,2048]{2,1,0:T(8,128)(2,1)S(1)}, bf16[10,8,2048]{2,1,0:T(8,128)(2,1)S(1)}) custom-call(bf16[2,12,24,32,128]{4,3,2,1,0:T(8,128)(2,1)S(1)} %left_factor.1.left_ref, bf16[12,64,640]{2,1,0:T(8,128)(2,1)S(1)} %product.5.refs_0_, bf16[12,64,640]{2,1,0:T(8,128)(2,1)S(1)} %product.7.refs_1_), custom_call_target="tpu_custom_call" | custom-call | tf_op jit(solution)/shard_map/coarse/pallas_call | solution.py:253
  103.0 2.2 %collective-permute-start.10 = (bf16[10,8,2048]{2,1,0:T(8,128)(2,1)S(1)}, bf16[10,8,2048]{2,1,0:T(8,128)(2,1)S(1)}, u32[]{:S(2)}, u32[]{:S(2)}) collective-permute-start(bf16[10,8,2048]{2,1,0:T(8,128)(2,1)S(1)} %get-tuple-element.13), channel_id=1, source_target_pairs={{0,4},{4,8},{8,12},{12,16},{16,20},{20,24},{24,28},{1,5},{5,9},{9,... | collective-permute-start | bytes 983048 | tf_op jit(solution)/shard_map/ppermute | solution.py:335
  105.2 4.0 %collective-permute-start.11 = (bf16[10,8,2048]{2,1,0:T(8,128)(2,1)S(1)}, bf16[10,8,2048]{2,1,0:T(8,128)(2,1)S(1)}, u32[]{:S(2)}, u32[]{:S(2)}) collective-permute-start(bf16[10,8,2048]{2,1,0:T(8,128)(2,1)S(1)} %get-tuple-element.14), channel_id=1, source_target_pairs={{4,0},{8,4},{12,8},{16,12},{20,16},{24,20},{28,24},{5,1},{9,5},{13... | collective-permute-start | bytes 983048 | tf_op jit(solution)/shard_map/ppermute | solution.py:338
  109.2 1.1 coarse.7
  110.2 1.1 coarse.5
  111.3 6.9 %collective-permute-done.15 = bf16[10,8,2048]{2,1,0:T(8,128)(2,1)S(1)} collective-permute-done((bf16[10,8,2048]{2,1,0:T(8,128)(2,1)S(1)}, bf16[10,8,2048]{2,1,0:T(8,128)(2,1)S(1)}, u32[]{:S(2)}, u32[]{:S(2)}) %collective-permute-start.15) | collective-permute-done | bytes 327712 | tf_op jit(solution)/shard_map/ppermute | solution.py:335
  118.2 2.9 %collective-permute-done.16 = bf16[10,8,2048]{2,1,0:T(8,128)(2,1)S(1)} collective-permute-done((bf16[10,8,2048]{2,1,0:T(8,128)(2,1)S(1)}, bf16[10,8,2048]{2,1,0:T(8,128)(2,1)S(1)}, u32[]{:S(2)}, u32[]{:S(2)}) %collective-permute-start.16) | collective-permute-done | bytes 327712 | tf_op jit(solution)/shard_map/ppermute | solution.py:338
  121.1 0.1 add_convert_fusion
  121.2 1.3 collective-permute-start.18
  122.5 2.9 %collective-permute-done.10 = bf16[10,8,2048]{2,1,0:T(8,128)(2,1)S(1)} collective-permute-done((bf16[10,8,2048]{2,1,0:T(8,128)(2,1)S(1)}, bf16[10,8,2048]{2,1,0:T(8,128)(2,1)S(1)}, u32[]{:S(2)}, u32[]{:S(2)}) %collective-permute-start.10) | collective-permute-done | bytes 327712 | tf_op jit(solution)/shard_map/ppermute | solution.py:335
  125.4 2.8 %collective-permute-done.11 = bf16[10,8,2048]{2,1,0:T(8,128)(2,1)S(1)} collective-permute-done((bf16[10,8,2048]{2,1,0:T(8,128)(2,1)S(1)}, bf16[10,8,2048]{2,1,0:T(8,128)(2,1)S(1)}, u32[]{:S(2)}, u32[]{:S(2)}) %collective-permute-start.11) | collective-permute-done | bytes 327712 | tf_op jit(solution)/shard_map/ppermute | solution.py:338
  128.2 0.1 add_convert_fusion.1
  128.3 1.3 collective-permute-start.13
  129.6 0.8 collective-permute-start.17
  130.4 0.1 collective-permute-start.12
  130.5 2.2 %collective-permute-done.18.refs_3_ = bf16[14,8,2048]{2,1,0:T(8,128)(2,1)S(1)} collective-permute-done((bf16[14,8,2048]{2,1,0:T(8,128)(2,1)S(1)}, bf16[14,8,2048]{2,1,0:T(8,128)(2,1)S(1)}, u32[]{:S(2)}, u32[]{:S(2)}) %collective-permute-start.18) | collective-permute-done | bytes 458784 | tf_op jit(solution)/shard_map/ppermute | solution.py:329
  132.8 2.5 %collective-permute-start.19 = (bf16[14,8,2048]{2,1,0:T(8,128)(2,1)S(1)}, bf16[14,8,2048]{2,1,0:T(8,128)(2,1)S(1)}, u32[]{:S(2)}, u32[]{:S(2)}) collective-permute-start(bf16[14,8,2048]{2,1,0:T(8,128)(2,1)S(1)} %collective-permute-done.18.refs_3_), channel_id=1, source_target_pairs={{0,1},{1,0},{2,3},{3,2},{4,5},{5,4},{6,7},{7,6},{8,9},{9,8},{10,11... | collective-permute-start | bytes 1376264 | tf_op jit(solution)/shard_map/ppermute | solution.py:332
  135.3 7.3 %collective-permute-done.13.refs_2_ = bf16[14,8,2048]{2,1,0:T(8,128)(2,1)S(1)} collective-permute-done((bf16[14,8,2048]{2,1,0:T(8,128)(2,1)S(1)}, bf16[14,8,2048]{2,1,0:T(8,128)(2,1)S(1)}, u32[]{:S(2)}, u32[]{:S(2)}) %collective-permute-start.13) | collective-permute-done | bytes 458784 | tf_op jit(solution)/shard_map/ppermute | solution.py:329
  142.6 1.4 collective-permute-start.14
  144.1 0.2 fusion.12.order_ref
  144.2 0.0 collective-permute-done.12.refs_1_
  144.3 1.2 collective-permute-done.14.refs_3_
  145.5 2.9 %assemble.2.refs_0_ = bf16[8,56,4096]{2,1,0:T(8,128)(2,1)} custom-call(bf16[448,448]{1,0:T(8,128)(2,1)S(1)} %fusion.12.order_ref, bf16[14,8,2048]{2,1,0:T(8,128)(2,1)S(1)} %bitcast.13, bf16[14,8,2048]{2,1,0:T(8,128)(2,1)S(1)} %collective-permute-done.12.refs_1_, bf16[14,8,2048]{2,1,0:T(8,128)(2,1)S(1)} %collective-permute-done.13.refs_2_, ...), custom_call_target="tpu_custom_call" | custom-call | tf_op jit(solution)/shard_map/assemble/pallas_call | solution.py:288
  148.4 0.0 collective-permute-done.17.refs_2_
  148.4 0.0 collective-permute-done.19.refs_4_
  148.4 2.9 %assemble.3 = bf16[8,56,4096]{2,1,0:T(8,128)(2,1)} custom-call(bf16[448,448]{1,0:T(8,128)(2,1)S(1)} %fusion.12.order_ref, bf16[8,56,4096]{2,1,0:T(8,128)(2,1)} %assemble.2.refs_0_, bf16[14,8,2048]{2,1,0:T(8,128)(2,1)S(1)} %bitcast.16, bf16[14,8,2048]{2,1,0:T(8,128)(2,1)S(1)} %collective-permute-done.17.refs_2_, ...), custom_call_target="tpu_custom_call", output_to_operand_aliasing={{}: (1, {})} | custom-call | tf_op jit(solution)/shard_map/assemble/pallas_call | solution.py:288
  (8 shorter events, 0.1 us)
Async XLA Ops:
  0.0 1.4 copy-start
  1.4 2.8 %copy-start.1 = (bf16[24,4,4096]{2,1,0:T(4,128)(2,1)S(1)}, bf16[24,4,4096]{2,1,0:T(4,128)(2,1)}, u32[]{:S(2)}) copy-start(bf16[24,4,4096]{2,1,0:T(4,128)(2,1)} %x_ref.3) | copy-start | bytes 2359300
  1.4 37.6 %copy-start.2 = (s32[192,4]{0,1:T(4,128)S(1)}, s32[192,4]{0,1:T(4,128)}, u32[]{:S(2)}) copy-start(s32[192,4]{0,1:T(4,128)} %param.9) | copy-start | bytes 9220
  2.0 25.9 %collective-permute-start.7 = (bf16[12,64,512]{2,1,0:T(8,128)(2,1)S(1)}, bf16[12,64,512]{2,1,0:T(8,128)(2,1)}, u32[]{:S(2)}, u32[]{:S(2)}) collective-permute-start(bf16[12,64,512]{2,1,0:T(8,128)(2,1)S(1)} %relayout.5.refs_0_), channel_id=1, source_target_pairs={{0,2},{1,3},{2,0},{3,1},{4,6},{5,7},{6,4},{7,5},{8,10},{9,11},{10,... | collective-permute-start | bytes 2359304 | tf_op jit(solution)/shard_map/ppermute | solution.py:329
  3.9 33.5 %collective-permute-start.4 = (bf16[12,64,512]{2,1,0:T(8,128)(2,1)S(1)}, bf16[12,64,512]{2,1,0:T(8,128)(2,1)}, u32[]{:S(2)}, u32[]{:S(2)}) collective-permute-start(bf16[12,64,512]{2,1,0:T(8,128)(2,1)S(1)} %relayout.4.refs_0_), channel_id=1, source_target_pairs={{0,2},{1,3},{2,0},{3,1},{4,6},{5,7},{6,4},{7,5},{8,10},{9,11},{10,... | collective-permute-start | bytes 2359304 | tf_op jit(solution)/shard_map/ppermute | solution.py:329
  4.2 37.7 %copy-start.3 = (s32[24,32]{1,0:T(8,128)S(1)}, s32[24,32]{1,0:T(8,128)}, u32[]{:S(2)}) copy-start(s32[24,32]{1,0:T(8,128)} %cols_ref.1) | copy-start | bytes 9220
  4.2 37.7 %copy-start.4 = (s32[24]{0:T(128)S(1)}, s32[24]{0:T(128)}, u32[]{:S(2)}) copy-start(s32[24]{0:T(128)} %counts_ref.1) | copy-start | bytes 292
  5.1 18.7 %collective-permute-start = (bf16[12,64,256]{2,1,0:T(8,128)(2,1)S(1)}, bf16[12,64,256]{2,1,0:T(8,128)(2,1)S(1)}, u32[]{:S(2)}, u32[]{:S(2)}) collective-permute-start(bf16[12,64,256]{2,1,0:T(8,128)(2,1)S(1)} %constant_dynamic-slice_fusion), channel_id=1, source_target_pairs={{0,4},{4,8},{8,12},{12,16},{16,20},{20,24},{24,28},{1,5},{5,9},{9,... | collective-permute-start | bytes 1179656 | tf_op jit(solution)/shard_map/ppermute | solution.py:335
  8.3 19.2 %collective-permute-start.2 = (bf16[12,64,256]{2,1,0:T(8,128)(2,1)S(1)}, bf16[12,64,256]{2,1,0:T(8,128)(2,1)S(1)}, u32[]{:S(2)}, u32[]{:S(2)}) collective-permute-start(bf16[12,64,256]{2,1,0:T(8,128)(2,1)S(1)} %constant_dynamic-slice_fusion), channel_id=1, source_target_pairs={{4,0},{8,4},{12,8},{16,12},{20,16},{24,20},{28,24},{5,1},{9,5},{13... | collective-permute-start | bytes 1179656 | tf_op jit(solution)/shard_map/ppermute | solution.py:338
  23.8 15.2 %collective-permute-start.1 = (bf16[12,64,256]{2,1,0:T(8,128)(2,1)S(1)}, bf16[12,64,256]{2,1,0:T(8,128)(2,1)S(1)}, u32[]{:S(2)}, u32[]{:S(2)}) collective-permute-start(bf16[12,64,256]{2,1,0:T(8,128)(2,1)S(1)} %collective-permute-done.pr), channel_id=1, source_target_pairs={{0,1},{1,0},{2,3},{3,2},{4,5},{5,4},{6,7},{7,6},{8,9},{9,8},{10,11... | collective-permute-start | bytes 1179656 | tf_op jit(solution)/shard_map/ppermute | solution.py:332
  26.0 45.7 %collective-permute-start.9 = (bf16[12,64,512]{2,1,0:T(8,128)(2,1)S(1)}, bf16[12,64,512]{2,1,0:T(8,128)(2,1)S(1)}, u32[]{:S(2)}, u32[]{:S(2)}) collective-permute-start(bf16[12,64,512]{2,1,0:T(8,128)(2,1)S(1)} %relayout.5.refs_0_), channel_id=1, source_target_pairs={{0,1},{1,0},{2,3},{3,2},{4,5},{5,4},{6,7},{7,6},{8,9},{9,8},{10,11... | collective-permute-start | bytes 2359304 | tf_op jit(solution)/shard_map/ppermute | solution.py:332
  27.5 49.2 %collective-permute-start.6 = (bf16[12,64,512]{2,1,0:T(8,128)(2,1)S(1)}, bf16[12,64,512]{2,1,0:T(8,128)(2,1)S(1)}, u32[]{:S(2)}, u32[]{:S(2)}) collective-permute-start(bf16[12,64,512]{2,1,0:T(8,128)(2,1)S(1)} %relayout.4.refs_0_), channel_id=1, source_target_pairs={{0,1},{1,0},{2,3},{3,2},{4,5},{5,4},{6,7},{7,6},{8,9},{9,8},{10,11... | collective-permute-start | bytes 2359304 | tf_op jit(solution)/shard_map/ppermute | solution.py:332
  27.9 53.8 %collective-permute-start.8 = (bf16[12,64,512]{2,1,0:T(8,128)(2,1)}, bf16[12,64,512]{2,1,0:T(8,128)(2,1)S(1)}, u32[]{:S(2)}, u32[]{:S(2)}) collective-permute-start(bf16[12,64,512]{2,1,0:T(8,128)(2,1)} %collective-permute-done.7.refs_0_), channel_id=1, source_target_pairs={{0,1},{1,0},{2,3},{3,2},{4,5},{5,4},{6,7},{7,6},{8,9},{9,8},{10,11... | collective-permute-start | bytes 2359304 | tf_op jit(solution)/shard_map/ppermute | solution.py:332
  37.4 49.7 %collective-permute-start.5 = (bf16[12,64,512]{2,1,0:T(8,128)(2,1)}, bf16[12,64,512]{2,1,0:T(8,128)(2,1)S(1)}, u32[]{:S(2)}, u32[]{:S(2)}) collective-permute-start(bf16[12,64,512]{2,1,0:T(8,128)(2,1)} %collective-permute-done.4.refs_0_), channel_id=1, source_target_pairs={{0,1},{1,0},{2,3},{3,2},{4,5},{5,4},{6,7},{7,6},{8,9},{9,8},{10,11... | collective-permute-start | bytes 2359304 | tf_op jit(solution)/shard_map/ppermute | solution.py:332
  39.0 2.9 %collective-permute-start.3 = (bf16[12,64,256]{2,1,0:T(8,128)(2,1)S(1)}, bf16[12,64,256]{2,1,0:T(8,128)(2,1)S(1)}, u32[]{:S(2)}, u32[]{:S(2)}) collective-permute-start(bf16[12,64,256]{2,1,0:T(8,128)(2,1)S(1)} %collective-permute-done.2.nr), channel_id=1, source_target_pairs={{0,1},{1,0},{2,3},{3,2},{4,5},{5,4},{6,7},{7,6},{8,9},{9,8},{10,11... | collective-permute-start | bytes 1179656 | tf_op jit(solution)/shard_map/ppermute | solution.py:332
  94.7 23.6 %collective-permute-start.15 = (bf16[10,8,2048]{2,1,0:T(8,128)(2,1)S(1)}, bf16[10,8,2048]{2,1,0:T(8,128)(2,1)S(1)}, u32[]{:S(2)}, u32[]{:S(2)}) collective-permute-start(bf16[10,8,2048]{2,1,0:T(8,128)(2,1)S(1)} %get-tuple-element.15), channel_id=1, source_target_pairs={{0,4},{4,8},{8,12},{12,16},{16,20},{20,24},{24,28},{1,5},{5,9},{9,... | collective-permute-start | bytes 983048 | tf_op jit(solution)/shard_map/ppermute | solution.py:335
  97.8 23.3 %collective-permute-start.16 = (bf16[10,8,2048]{2,1,0:T(8,128)(2,1)S(1)}, bf16[10,8,2048]{2,1,0:T(8,128)(2,1)S(1)}, u32[]{:S(2)}, u32[]{:S(2)}) collective-permute-start(bf16[10,8,2048]{2,1,0:T(8,128)(2,1)S(1)} %get-tuple-element.16), channel_id=1, source_target_pairs={{4,0},{8,4},{12,8},{16,12},{20,16},{24,20},{28,24},{5,1},{9,5},{13... | collective-permute-start | bytes 983048 | tf_op jit(solution)/shard_map/ppermute | solution.py:338
  103.0 22.4 %collective-permute-start.10 = (bf16[10,8,2048]{2,1,0:T(8,128)(2,1)S(1)}, bf16[10,8,2048]{2,1,0:T(8,128)(2,1)S(1)}, u32[]{:S(2)}, u32[]{:S(2)}) collective-permute-start(bf16[10,8,2048]{2,1,0:T(8,128)(2,1)S(1)} %get-tuple-element.13), channel_id=1, source_target_pairs={{0,4},{4,8},{8,12},{12,16},{16,20},{20,24},{24,28},{1,5},{5,9},{9,... | collective-permute-start | bytes 983048 | tf_op jit(solution)/shard_map/ppermute | solution.py:335
  105.2 23.0 %collective-permute-start.11 = (bf16[10,8,2048]{2,1,0:T(8,128)(2,1)S(1)}, bf16[10,8,2048]{2,1,0:T(8,128)(2,1)S(1)}, u32[]{:S(2)}, u32[]{:S(2)}) collective-permute-start(bf16[10,8,2048]{2,1,0:T(8,128)(2,1)S(1)} %get-tuple-element.14), channel_id=1, source_target_pairs={{4,0},{8,4},{12,8},{16,12},{20,16},{24,20},{28,24},{5,1},{9,5},{13... | collective-permute-start | bytes 983048 | tf_op jit(solution)/shard_map/ppermute | solution.py:338
  121.2 11.6 %collective-permute-start.18 = (bf16[14,8,2048]{2,1,0:T(8,128)(2,1)S(1)}, bf16[14,8,2048]{2,1,0:T(8,128)(2,1)S(1)}, u32[]{:S(2)}, u32[]{:S(2)}) collective-permute-start(bf16[14,8,2048]{2,1,0:T(8,128)(2,1)S(1)} %bitcast.14), channel_id=1, source_target_pairs={{0,2},{1,3},{2,0},{3,1},{4,6},{5,7},{6,4},{7,5},{8,10},{9,11},{10,... | collective-permute-start | bytes 1376264 | tf_op jit(solution)/shard_map/ppermute | solution.py:329
  128.3 14.3 %collective-permute-start.13 = (bf16[14,8,2048]{2,1,0:T(8,128)(2,1)S(1)}, bf16[14,8,2048]{2,1,0:T(8,128)(2,1)S(1)}, u32[]{:S(2)}, u32[]{:S(2)}) collective-permute-start(bf16[14,8,2048]{2,1,0:T(8,128)(2,1)S(1)} %bitcast.11), channel_id=1, source_target_pairs={{0,2},{1,3},{2,0},{3,1},{4,6},{5,7},{6,4},{7,5},{8,10},{9,11},{10,... | collective-permute-start | bytes 1376264 | tf_op jit(solution)/shard_map/ppermute | solution.py:329
  129.6 18.8 %collective-permute-start.17 = (bf16[14,8,2048]{2,1,0:T(8,128)(2,1)S(1)}, bf16[14,8,2048]{2,1,0:T(8,128)(2,1)S(1)}, u32[]{:S(2)}, u32[]{:S(2)}) collective-permute-start(bf16[14,8,2048]{2,1,0:T(8,128)(2,1)S(1)} %bitcast.15), channel_id=1, source_target_pairs={{0,1},{1,0},{2,3},{3,2},{4,5},{5,4},{6,7},{7,6},{8,9},{9,8},{10,11... | collective-permute-start | bytes 1376264 | tf_op jit(solution)/shard_map/ppermute | solution.py:332
  130.4 13.8 %collective-permute-start.12 = (bf16[14,8,2048]{2,1,0:T(8,128)(2,1)S(1)}, bf16[14,8,2048]{2,1,0:T(8,128)(2,1)S(1)}, u32[]{:S(2)}, u32[]{:S(2)}) collective-permute-start(bf16[14,8,2048]{2,1,0:T(8,128)(2,1)S(1)} %bitcast.12), channel_id=1, source_target_pairs={{0,1},{1,0},{2,3},{3,2},{4,5},{5,4},{6,7},{7,6},{8,9},{9,8},{10,11... | collective-permute-start | bytes 1376264 | tf_op jit(solution)/shard_map/ppermute | solution.py:332
  132.8 15.6 %collective-permute-start.19 = (bf16[14,8,2048]{2,1,0:T(8,128)(2,1)S(1)}, bf16[14,8,2048]{2,1,0:T(8,128)(2,1)S(1)}, u32[]{:S(2)}, u32[]{:S(2)}) collective-permute-start(bf16[14,8,2048]{2,1,0:T(8,128)(2,1)S(1)} %collective-permute-done.18.refs_3_), channel_id=1, source_target_pairs={{0,1},{1,0},{2,3},{3,2},{4,5},{5,4},{6,7},{7,6},{8,9},{9,8},{10,11... | collective-permute-start | bytes 1376264 | tf_op jit(solution)/shard_map/ppermute | solution.py:332
  142.6 2.9 %collective-permute-start.14 = (bf16[14,8,2048]{2,1,0:T(8,128)(2,1)S(1)}, bf16[14,8,2048]{2,1,0:T(8,128)(2,1)S(1)}, u32[]{:S(2)}, u32[]{:S(2)}) collective-permute-start(bf16[14,8,2048]{2,1,0:T(8,128)(2,1)S(1)} %collective-permute-done.13.refs_2_), channel_id=1, source_target_pairs={{0,1},{1,0},{2,3},{3,2},{4,5},{5,4},{6,7},{7,6},{8,9},{9,8},{10,11... | collective-permute-start | bytes 1376264 | tf_op jit(solution)/shard_map/ppermute | solution.py:332

commit v2 on v1

v2 whole, which is shorter than its diff:
```python
import functools

import jax
import jax.numpy as jnp
from jax import lax
from jax.experimental import pallas as pl
from jax.experimental.pallas import tpu as pltpu
from jax.sharding import PartitionSpec as P

BS = 64
CB = 8
GROUPS = 5
LANES = 128
BF = jnp.bfloat16
F32 = jnp.float32
MIB = 1 << 20

VM = pl.BlockSpec(memory_space=pltpu.VMEM)
SM = pl.BlockSpec(memory_space=pltpu.SMEM)


def params(mib):
    return pltpu.CompilerParams(vmem_limit_bytes=mib * MIB)


def cost(us):
    return pl.CostEstimate(flops=0, bytes_accessed=int(us * 3.7e6), transcendentals=0)


def low_lanes(rows):
    return lax.broadcasted_iota(jnp.int32, (rows, LANES), 1) < BS


def dot(a, b):
    return lax.dot_general(a, b, (((1,), (0,)), ((), ())), preferred_element_type=F32)


def relayout_kernel(x_ref, o_ref, scr):
    rows, nb, _ = x_ref.shape
    low = low_lanes(32)
    for r in range(rows):
        for q in range(32):
            scr[r, pl.ds(q * 8, nb), :] = x_ref[r, :, q * LANES : (q + 1) * LANES].astype(F32)
        for k in range(0, nb, 2):
            x0 = scr[r, pl.ds(k, 32, stride=8), :]
            x1 = scr[r, pl.ds(k + 1, 32, stride=8), :]
            o_ref[r, 0:32, k * BS : (k + 2) * BS] = jnp.where(low, x0, pltpu.roll(x1, BS, 1)).astype(BF)
            o_ref[r, 32:64, k * BS : (k + 2) * BS] = jnp.where(low, pltpu.roll(x0, BS, 1), x1).astype(BF)


def relayout(x, first, rows):
    nb = x.shape[1]
    step = 4
    return pl.pallas_call(
        relayout_kernel,
        grid=(rows // step,),
        out_shape=jax.ShapeDtypeStruct((rows, BS, nb * BS), BF),
        in_specs=[pl.BlockSpec((step, nb, BS * BS), lambda i: (i + first // step, 0, 0))],
        out_specs=pl.BlockSpec((step, BS, nb * BS), lambda i: (i, 0, 0)),
        scratch_shapes=[pltpu.VMEM((step, 256, LANES), F32)],
        compiler_params=params(16),
        cost_estimate=cost(0.6),
        name="relayout",
    )(x)


def relayout_both_kernel(x_ref, o_ref, nat_ref, scr, mix):
    relayout_kernel(x_ref, o_ref, scr)
    rows, nb, _ = x_ref.shape
    for r in range(rows):
        for k in range(0, nb, 2):
            at = slice(k * BS, (k + 2) * BS)
            mix[r, k // 2, pl.ds(0, 32, stride=2), :] = o_ref[r, 0:32, at].astype(F32)
            mix[r, k // 2, pl.ds(1, 32, stride=2), :] = o_ref[r, 32:64, at].astype(F32)
            nat_ref[r, :, at] = mix[r, k // 2].astype(BF)


def relayout_both(x):
    rows, nb, _ = x.shape
    step = 4
    shape = jax.ShapeDtypeStruct((rows, BS, nb * BS), BF)
    spec = pl.BlockSpec((step, BS, nb * BS), lambda i: (i, 0, 0))
    return pl.pallas_call(
        relayout_both_kernel,
        grid=(rows // step,),
        out_shape=(shape, shape),
        in_specs=[pl.BlockSpec((step, nb, BS * BS), lambda i: (i, 0, 0))],
        out_specs=(spec, spec),
        scratch_shapes=[pltpu.VMEM((step, 256, LANES), F32), pltpu.VMEM((step, nb // 2, BS, LANES), F32)],
        compiler_params=params(16),
        cost_estimate=cost(1.5),
        name="relayout_both",
    )(x)


def left_kernel(rb, pct_ref, pl_ref, o_ref):
    slab = lax.axis_index("row")
    low = low_lanes(4 * BS)
    o_ref[...] = jnp.zeros_like(o_ref)

    def pair(ip, carry):
        for half in range(2):
            i = ip * 2 + half
            x = pl_ref[i].astype(F32)
            xt = jnp.concatenate([x, x], axis=0).T
            keep = jnp.where(low if half == 0 else jnp.logical_not(low), xt, 0.0)
            for s in range(4):
                w = pct_ref[s, slab * rb + i] - (slab - 1) * CB
                o_ref[ip, w] = (o_ref[ip, w].astype(F32) + keep[s * BS : (s + 1) * BS]).astype(BF)
        return carry

    lax.fori_loop(0, rb // 2, pair, 0)


def left_factor(pct, p_own):
    rb = p_own.shape[0]
    return pl.pallas_call(
        functools.partial(left_kernel, rb),
        out_shape=jax.ShapeDtypeStruct((rb // 2, 3 * CB, BS, LANES), BF),
        in_specs=[SM, VM],
        out_specs=VM,
        compiler_params=params(24),
        cost_estimate=cost(2.9),
        name="left_factor",
    )(pct, p_own)


def right_kernel(rb, nfb, share, tiles, pct_ref, own, pr, ps, nr, ns, o_ref):
    slab = lax.axis_index("row")
    col = lax.axis_index("col")
    core = lax.rem(col, 2)
    half = rb // 2
    base = (slab - 1) * rb
    low = low_lanes(BS)

    def fill(src, count, near_first, out_first):
        def one(jj, carry):
            fine = base + near_first + jj
            valid = (fine >= 0) & (fine < nfb)
            at = jnp.clip(fine, 0, nfb - 1)
            spot = out_first + jj
            for p in range(tiles):
                o_ref[spot, p] = jnp.zeros((BS, LANES), BF)
            for t in range(4):
                w = pct_ref[t, at] - (slab - 2) * CB
                e = (w & (CB - 1)) - share * col

                @pl.when(valid & (e >= 0) & (e < share))
                def _():
                    n = e * GROUPS + (w >> 3)
                    upper = n >= tiles
                    tile = jnp.where(upper, n - tiles, n)
                    pair = src[jj, :, t // 2 * LANES : (t // 2 + 1) * LANES].astype(F32)
                    other = pltpu.roll(pair, BS, 1)
                    both = jnp.where(low, pair, other) if t % 2 == 0 else jnp.where(low, other, pair)
                    keep = jnp.where(low == jnp.logical_not(upper), both, 0.0)
                    o_ref[spot, tile] = (o_ref[spot, tile].astype(F32) + keep).astype(BF)

            return carry

        lax.fori_loop(0, count, one, 0)

    fill(own, rb, rb, 0)
    fill(pr, half, half * core, rb)
    fill(ps, half, half * (1 - core), rb + half)
    fill(nr, half, 2 * rb + half * core, 2 * rb)
    fill(ns, half, 2 * rb + half * (1 - core), 2 * rb + half)
    o_ref[3 * rb] = jnp.zeros((tiles, BS, LANES), BF)


def right_factor(pct, pieces, nfb, share, tiles):
    rb = pieces[0].shape[0]
    return pl.pallas_call(
        functools.partial(right_kernel, rb, nfb, share, tiles),
        out_shape=jax.ShapeDtypeStruct((3 * rb + 1, tiles, BS, LANES), BF),
        in_specs=[SM] + [VM] * 5,
        out_specs=VM,
        compiler_params=params(24),
        cost_estimate=cost(4.0),
        name="right_factor",
    )(pct, *pieces)


def slot_places(a_cols, counts):
    rb, ka = a_cols.shape
    half = rb // 2
    core = lax.axis_index("col") % 2
    near = a_cols - (lax.axis_index("row") - 1) * rb
    before, behind = near < rb, near >= 2 * rb
    inside = near - jnp.where(before, 0, jnp.where(behind, 2 * rb, rb))
    far = (inside >= half).astype(jnp.int32)
    off = inside - half * far + half * jnp.where(far == core, 0, 1)
    spot = jnp.where(before, rb + off, jnp.where(behind, 2 * rb + off, inside))
    live = jnp.arange(ka, dtype=jnp.int32)[None, :] < counts[:, None]
    return jnp.where(live, spot, 3 * rb)


def product_kernel(first, shifts, has_acc, ks, place_ref, right_ref, *refs):
    col = lax.axis_index("col")
    ny = lax.axis_size("col") // 2
    srcs = refs[: len(shifts)]
    acc_ref = refs[len(shifts)] if has_acc else None
    o_ref = refs[-1]
    rows = o_ref.shape[0]
    tiles = right_ref.shape[1]
    y, core = col // 2, lax.rem(col, 2)
    firsts = []
    for s, flip in shifts:
        c = core if flip == 0 else 1 - core
        firsts.append((lax.rem(y - s + ny, ny) * 2 + c) * ks)

    def one(i, carry):
        spots = [[place_ref[first + i, f + k] for k in range(ks)] for f in firsts]
        for p0 in range(0, tiles, 2):
            ps = range(p0, min(p0 + 2, tiles))
            at = slice(p0 * LANES, (ps[-1] + 1) * LANES)
            acc = acc_ref[i, :, at] if has_acc else jnp.zeros((BS, len(ps) * LANES), F32)
            for src, spot in zip(srcs, spots):
                for k in range(0, ks, 4):
                    rhs = [jnp.concatenate([right_ref[spot[k + d], p] for d in range(4)], axis=0) for p in ps]
                    acc = acc + dot(src[i, :, k * BS : (k + 4) * BS], jnp.concatenate(rhs, axis=1))
            o_ref[i, :, at] = acc.astype(o_ref.dtype)
        return carry

    lax.fori_loop(0, rows, one, 0, unroll=4)


def product(place, right, srcs, shifts, first, acc, dtype):
    rows, _, wide = srcs[0].shape
    return pl.pallas_call(
        functools.partial(product_kernel, first, shifts, acc is not None, wide // BS),
        out_shape=jax.ShapeDtypeStruct((rows, BS, right.shape[1] * LANES), dtype),
        in_specs=[SM, VM] + [VM] * (len(srcs) + (acc is not None)),
        out_specs=VM,
        compiler_params=params(24),
        cost_estimate=cost(4.0),
        name="product",
    )(place, right, *srcs, *([] if acc is None else [acc]))


def coarse_kernel(sets, a0, a1, left_ref, *refs):
    outs = refs[-1 - len(sets) : -1]
    aps = refs[: -1 - len(sets)]
    scr = refs[-1]
    ac = a1 - a0
    half = aps[0].shape[0]
    tiles = aps[0].shape[2] // LANES
    for out, (i0, i1) in zip(outs, sets):
        rows = i1 - i0
        low = low_lanes(rows)
        for p0 in range(0, tiles, 2):
            p1 = min(p0 + 2, tiles)
            acc = jnp.zeros((rows * ac, (p1 - p0) * LANES), F32)
            for side, ap in enumerate(aps):
                for g in range(0, half // 2, 2):
                    ip = side * (half // 2) + g
                    lhs = [left_ref[ip + d, i0:i1, a0:a1].reshape(rows * ac, LANES) for d in range(2)]
                    rhs = ap[2 * g : 2 * g + 4, :, p0 * LANES : p1 * LANES].reshape(4 * BS, (p1 - p0) * LANES)
                    acc = acc + dot(jnp.concatenate(lhs, axis=1), rhs)
            for p in range(p0, p1):
                scr[p, 0 : rows * ac] = acc[:, (p - p0) * LANES : (p - p0 + 1) * LANES]
        for p in range(tiles):
            for a in range(0, ac, 2):
                x0 = scr[p, pl.ds(a, rows, stride=ac), :]
                x1 = scr[p, pl.ds(a + 1, rows, stride=ac), :]
                at = slice(a * BS, (a + 2) * BS)
                out[p, :, at] = jnp.where(low, x0, pltpu.roll(x1, BS, 1)).astype(out.dtype)
                out[tiles + p, :, at] = jnp.where(low, pltpu.roll(x0, BS, 1), x1).astype(out.dtype)


def coarse_rows(left, aps, sets, a0, a1, dtype, us):
    tiles = aps[0].shape[2] // LANES
    return pl.pallas_call(
        functools.partial(coarse_kernel, sets, a0, a1),
        out_shape=[jax.ShapeDtypeStruct((2 * tiles, i1 - i0, (a1 - a0) * BS), dtype) for i0, i1 in sets],
        in_specs=[VM] * (1 + len(aps)),
        out_specs=[VM] * len(sets),
        scratch_shapes=[pltpu.VMEM((tiles, max(i1 - i0 for i0, i1 in sets) * (a1 - a0), LANES), F32)],
        compiler_params=params(32),
        cost_estimate=cost(us),
        name="coarse",
    )(left, *aps)


def assemble_kernel(order_ref, *refs):
    out = refs[-1]
    srcs = refs[:-1] if len(refs) % 2 else refs[1:-1]
    x = jnp.concatenate([s[...].reshape(-1, s.shape[2]) for s in srcs], axis=0)
    res = dot(order_ref[...], x)
    wide = out.shape[1]
    for i in range(CB):
        out[i] = res[i * wide : (i + 1) * wide].astype(BF)


def assemble(order, srcs, a0, total, before):
    n, _, lanes = srcs[0].shape
    step = 512
    per = lanes // step
    wide = n * len(srcs)
    specs = [pl.BlockSpec(order.shape, lambda i: (0, 0))]
    args = [order]
    alias = {}
    if before is not None:
        specs.append(pl.BlockSpec(memory_space=pl.ANY))
        args.append(before)
        alias = {1: 0}
    specs += [pl.BlockSpec((n, CB, step), lambda i: (0, 0, i))] * len(srcs)
    return pl.pallas_call(
        assemble_kernel,
        grid=(per,),
        out_shape=jax.ShapeDtypeStruct((CB, wide, total), BF),
        in_specs=specs,
        out_specs=pl.BlockSpec((CB, wide, step), lambda i: (0, 0, a0 * BS // step + i)),
        input_output_aliases=alias,
        compiler_params=params(24),
        cost_estimate=cost(2.9),
        name="assemble",
    )(*args, *srcs)


def assembly_order(shifts, ncol, share):
    col = lax.axis_index("col")
    y, core = col // 2, col % 2
    groups = GROUPS + 2
    size = ncol * share * groups * CB
    out_row = lax.broadcasted_iota(jnp.int32, (size, size), 0)
    src_row = lax.broadcasted_iota(jnp.int32, (size, size), 1)
    per = share * groups * CB
    which, rest = src_row // per, src_row % per
    e, g, i = rest // (groups * CB), rest // CB % groups, rest % CB
    src_col = jnp.zeros_like(which)
    for z, (s, flip) in enumerate(shifts):
        c = (y - s) % (ncol // 2) * 2 + (core + flip) % 2
        src_col = jnp.where(which == z, c, src_col)
    return (out_row == i * (groups * CB) + g * CB + share * src_col + e).astype(BF)


def body(a_blocks, a_cols, counts, p_blocks, p_cols):
    rb, ks, _ = a_blocks.shape
    nrow, ncol = lax.axis_size("row"), lax.axis_size("col")
    ny = ncol // 2
    nfb = p_cols.shape[0]
    share = CB // ncol
    tiles = (GROUPS * share + 1) // 2
    half = rb // 2
    chunks = ((0, 32), (32, 64))
    core = lax.axis_index("col") % 2

    def over_y(x, s):
        return lax.ppermute(x, "col", [(y * 2 + c, (y + s) % ny * 2 + c) for y in range(ny) for c in range(2)])

    def over_core(x):
        return lax.ppermute(x, "col", [(c, c ^ 1) for c in range(ncol)])

    def upward(x):
        return lax.ppermute(x, "row", [(i, i + 1) for i in range(nrow - 1)])

    def downward(x):
        return lax.ppermute(x, "row", [(i + 1, i) for i in range(nrow - 1)])

    shifts = tuple((s, f) for s in range(ny) for f in range(2))
    pct = p_cols.T

    def gather(x):
        got = [x] + [over_y(x, s) for s in range(1, ny)]
        return [z for g in got for z in (g, over_core(g))]

    a_parts = [gather(relayout(a_blocks, h * half, half)) for h in range(2)]
    p_mixed, p_own = relayout_both(p_blocks)
    mine = lax.dynamic_slice_in_dim(p_own, core * half, half, 0)
    prev, after = upward(mine), downward(mine)
    left = left_factor(pct, p_mixed)
    order = assembly_order(shifts, ncol, share)
    place = slot_places(a_cols, counts)
    pieces = [p_own, prev, over_core(prev), after, over_core(after)]
    right = right_factor(pct, pieces, nfb, share, tiles)
    aps = []
    for h in range(2):
        near = product(place, right, a_parts[h][:2], shifts[:2], h * half, None, F32)
        aps.append(product(place, right, a_parts[h][2:], shifts[2:], h * half, near, BF))
        if h == 0:
            early = downward(coarse_rows(left, aps, ((0, CB // 2),), 0, BS, BF, 1.0)[0])

    def columns(x, g):
        y = x[: GROUPS * share].reshape((share, GROUPS) + x.shape[1:])
        return jnp.pad(y.astype(F32), ((0, 0), (g, 2 - g), (0, 0), (0, 0)))

    rims = [coarse_rows(left, aps, ((CB // 2, CB), (2 * CB, 3 * CB)), a0, a1, BF, 2.0) for a0, a1 in chunks]
    mids = [coarse_rows(left, aps, ((CB, 2 * CB),), a0, a1, F32, 1.0)[0] for a0, a1 in chunks]
    out = None
    for (a0, a1), (low, high), mid in zip(chunks, rims, mids):
        lower = jnp.concatenate([early[:, :, a0 * BS : a1 * BS], downward(low)], axis=1)
        total = columns(upward(high), 0) + columns(mid, 1) + columns(lower, 2)
        total = total.astype(BF).reshape((share * (GROUPS + 2),) + total.shape[2:])
        out = assemble(order, gather(total), a0, BS * BS, out)
    return out


def solution(mesh):
    return jax.shard_map(
        body,
        mesh=mesh,
        in_specs=(P("row", "col", None), P("row", None), P("row"), P("row", None, None), P()),
        out_specs=P("row", None, None),
        check_vma=False,
    )
```

time: 152 us -> 132 us (0.87)
  the two profiles are of different devices: /device:TPU:9 before, /device:TPU:25 now
where the time goes in v2:
time: 132 us
  starting transfers between devices  48.4 us (37%)
  Pallas kernels  42.9 us (32%)
  waiting for transfers between devices  36.4 us (28%)
  local copies, waits for them, and re-layouts  3.47 us (3%)
    ppermute x4, waiting for transfers between devices, over_y(): lax.ppermute(x, 'col', [(y * 2 + c, (y + s) % ny * 2 + c) for y in range(...  21 us
    pallas_call x4, Pallas kernels, product(): pl.pallas_call(functools.partial(product_kernel, first, shifts, acc is no...  17.6 us
    ppermute x4, starting transfers between devices, over_y(): lax.ppermute(x, 'col', [(y * 2 + c, (y + s) % ny * 2 + c) for y in range(...  15.8 us
    ppermute x4, starting transfers between devices, downward(): return lax.ppermute(x, 'row', [(i + 1, i) for i in range(nrow - 1)])  13.1 us
    ppermute x10, starting transfers between devices, over_core(): return lax.ppermute(x, 'col', [(c, c ^ 1) for c in range(ncol)])  11.9 us
    pallas_call x1, Pallas kernels, right_factor(): pl.pallas_call(functools.partial(right_kernel, rb, nfb, share, tiles), ou...  8.05 us
    ppermute x3, waiting for transfers between devices, upward(): return lax.ppermute(x, 'row', [(i, i + 1) for i in range(nrow - 1)])  7.94 us
    ppermute x3, starting transfers between devices, upward(): return lax.ppermute(x, 'row', [(i, i + 1) for i in range(nrow - 1)])  7.56 us
  transfers between devices with their start and end apart: 21, of which 8 were waited for; matrix products, arithmetic and copies ran while one was open for 1% of the time, Pallas kernels for 30%

profile of v2, /device:TPU:25, one launch (start us, length us, event | category | flops | bytes accessed | tf_op | source)
XLA Modules:
  0.0 132.3 jit_solution(2539183078745204306)
XLA Ops:
  0.0 1.4 %copy-done = bf16[24,8,4096]{2,1,0:T(8,128)(2,1)S(1)} copy-done((bf16[24,8,4096]{2,1,0:T(8,128)(2,1)S(1)}, bf16[24,8,4096]{2,1,0:T(8,128)(2,1)}, u32[]{:S(2)}) %copy-start) | copy-done | bytes 1572888
  1.4 0.6 relayout.2.refs_0_
  2.0 1.3 collective-permute-start.4
  3.3 0.6 relayout.3.refs_0_
  3.9 0.0 copy-start.5
  3.9 0.3 collective-permute-start.7
  4.2 1.1 copy-done.1
  5.4 1.1 relayout_both.1
  6.5 3.1 %collective-permute-start = (bf16[12,64,256]{2,1,0:T(8,128)(2,1)S(1)}, bf16[12,64,256]{2,1,0:T(8,128)(2,1)S(1)}, u32[]{:S(2)}, u32[]{:S(2)}) collective-permute-start(bf16[12,64,256]{2,1,0:T(8,128)(2,1)S(1)} %constant_dynamic-slice_fusion), channel_id=1, source_target_pairs={{0,4},{4,8},{8,12},{12,16},{16,20},{20,24},{24,28},{1,5},{5,9},{9,... | collective-permute-start | bytes 1179656 | tf_op jit(solution)/shard_map/ppermute | solution.py:356
  9.6 3.1 %collective-permute-start.2 = (bf16[12,64,256]{2,1,0:T(8,128)(2,1)S(1)}, bf16[12,64,256]{2,1,0:T(8,128)(2,1)}, u32[]{:S(2)}, u32[]{:S(2)}) collective-permute-start(bf16[12,64,256]{2,1,0:T(8,128)(2,1)S(1)} %constant_dynamic-slice_fusion), channel_id=1, source_target_pairs={{4,0},{8,4},{12,8},{16,12},{20,16},{24,20},{28,24},{5,1},{9,5},{13... | collective-permute-start | bytes 1179656 | tf_op jit(solution)/shard_map/ppermute | solution.py:359
  12.7 6.0 %collective-permute-done.pr = bf16[12,64,256]{2,1,0:T(8,128)(2,1)S(1)} collective-permute-done((bf16[12,64,256]{2,1,0:T(8,128)(2,1)S(1)}, bf16[12,64,256]{2,1,0:T(8,128)(2,1)S(1)}, u32[]{:S(2)}, u32[]{:S(2)}) %collective-permute-start) | collective-permute-done | bytes 393248 | tf_op jit(solution)/shard_map/ppermute | solution.py:356
  18.7 2.2 %collective-permute-start.1 = (bf16[12,64,256]{2,1,0:T(8,128)(2,1)S(1)}, bf16[12,64,256]{2,1,0:T(8,128)(2,1)S(1)}, u32[]{:S(2)}, u32[]{:S(2)}) collective-permute-start(bf16[12,64,256]{2,1,0:T(8,128)(2,1)S(1)} %collective-permute-done.pr), channel_id=1, source_target_pairs={{0,1},{1,0},{2,3},{3,2},{4,5},{5,4},{6,7},{7,6},{8,9},{9,8},{10,11... | collective-permute-start | bytes 1179656 | tf_op jit(solution)/shard_map/ppermute | solution.py:353
  20.9 0.0 collective-permute-start.6
  20.9 0.0 collective-permute-done.4.refs_0_
  20.9 2.4 %collective-permute-start.5 = (bf16[12,64,512]{2,1,0:T(8,128)(2,1)}, bf16[12,64,512]{2,1,0:T(8,128)(2,1)}, u32[]{:S(2)}, u32[]{:S(2)}) collective-permute-start(bf16[12,64,512]{2,1,0:T(8,128)(2,1)} %collective-permute-done.4.refs_0_), channel_id=1, source_target_pairs={{0,1},{1,0},{2,3},{3,2},{4,5},{5,4},{6,7},{7,6},{8,9},{9,8},{10,11... | collective-permute-start | bytes 2359304 | tf_op jit(solution)/shard_map/ppermute | solution.py:353
  23.3 5.5 %collective-permute-done.2.nr = bf16[12,64,256]{2,1,0:T(8,128)(2,1)} collective-permute-done((bf16[12,64,256]{2,1,0:T(8,128)(2,1)S(1)}, bf16[12,64,256]{2,1,0:T(8,128)(2,1)}, u32[]{:S(2)}, u32[]{:S(2)}) %collective-permute-start.2) | collective-permute-done | bytes 393248 | tf_op jit(solution)/shard_map/ppermute | solution.py:359
  28.8 0.5 collective-permute-start.9
  29.3 8.1 %collective-permute-done.7.refs_0_ = bf16[12,64,512]{2,1,0:T(8,128)(2,1)} collective-permute-done((bf16[12,64,512]{2,1,0:T(8,128)(2,1)S(1)}, bf16[12,64,512]{2,1,0:T(8,128)(2,1)}, u32[]{:S(2)}, u32[]{:S(2)}) %collective-permute-start.7) | collective-permute-done | bytes 786464 | tf_op jit(solution)/shard_map/ppermute | solution.py:350
  37.4 1.5 %collective-permute-start.8 = (bf16[12,64,512]{2,1,0:T(8,128)(2,1)}, bf16[12,64,512]{2,1,0:T(8,128)(2,1)}, u32[]{:S(2)}, u32[]{:S(2)}) collective-permute-start(bf16[12,64,512]{2,1,0:T(8,128)(2,1)} %collective-permute-done.7.refs_0_), channel_id=1, source_target_pairs={{0,1},{1,0},{2,3},{3,2},{4,5},{5,4},{6,7},{7,6},{8,9},{9,8},{10,11... | collective-permute-start | bytes 2359304 | tf_op jit(solution)/shard_map/ppermute | solution.py:353
  39.0 0.0 collective-permute-done.1.ps
  39.0 0.7 copy-done.2
  39.7 0.0 collective-permute-start.3
  39.8 2.9 %left_factor.1.left_ref = bf16[12,24,64,128]{3,2,1,0:T(8,128)(2,1)S(1)} custom-call(s32[4,192]{1,0:T(4,128)S(1)} %bitcast.17, bf16[24,64,256]{2,1,0:T(8,128)(2,1)S(1)} %get-tuple-element.11.pl_ref), custom_call_target="tpu_custom_call" | custom-call | bytes 10730000 | tf_op jit(solution)/shard_map/left_factor/pallas_call | solution.py:117
  42.7 0.1 select_select_fusion.1.place_ref
  42.7 0.0 collective-permute-done.3.ns
  42.8 8.1 %right_factor.1.right_ref = bf16[73,5,64,128]{3,2,1,0:T(8,128)(2,1)S(1)} custom-call(s32[4,192]{1,0:T(4,128)S(1)} %bitcast.18, bf16[24,64,256]{2,1,0:T(8,128)(2,1)S(1)} %get-tuple-element.12.own, bf16[12,64,256]{2,1,0:T(8,128)(2,1)S(1)} %collective-permute-done.pr, bf16[12,64,256]{2,1,0:T(8,128)(2,1)S(1)} %copy-done.3, ...), custom_call_target="tpu_custom_call" | custom-call | bytes 14800000 | tf_op jit(solution)/shard_map/right_factor/pallas_call | solution.py:173
  50.8 4.3 %product.4.refs_2_ = f32[12,64,640]{2,1,0:T(8,128)S(1)} custom-call(s32[24,32]{1,0:T(8,128)S(1)} %select_select_fusion.1.place_ref, bf16[73,5,64,128]{3,2,1,0:T(8,128)(2,1)S(1)} %right_factor.1.right_ref, bf16[12,64,512]{2,1,0:T(8,128)(2,1)S(1)} %relayout.2.refs_0_, bf16[12,64,512]{2,1,0:T(8,128)(2,1)} %collective-permute-done.6.refs_1_), custom_call_target="tpu_custom_call" | custom-call | bytes 14800000 | tf_op jit(solution)/shard_map/product/pallas_call | solution.py:230
  55.1 4.5 %product.5.refs_0_ = bf16[12,64,640]{2,1,0:T(8,128)(2,1)S(1)} custom-call(s32[24,32]{1,0:T(8,128)S(1)} %select_select_fusion.1.place_ref, bf16[73,5,64,128]{3,2,1,0:T(8,128)(2,1)S(1)} %right_factor.1.right_ref, bf16[12,64,512]{2,1,0:T(8,128)(2,1)} %collective-permute-done.4.refs_0_, bf16[12,64,512]{2,1,0:T(8,128)(2,1)} %collective-permute-done.5.refs_1_, ...), custom_call_target="tpu_custom_call" | custom-call | bytes 14800000 | tf_op jit(solution)/shard_map/product/pallas_call | solution.py:230
  59.7 0.9 coarse.7
  60.5 3.7 %collective-permute-start.11 = (bf16[10,4,4096]{2,1,0:T(4,128)(2,1)S(1)}, bf16[10,4,4096]{2,1,0:T(4,128)(2,1)S(1)}, u32[]{:S(2)}, u32[]{:S(2)}) collective-permute-start(bf16[10,4,4096]{2,1,0:T(4,128)(2,1)S(1)} %coarse.7), channel_id=1, source_target_pairs={{4,0},{8,4},{12,8},{16,12},{20,16},{24,20},{28,24},{5,1},{9,5},{13... | collective-permute-start | bytes 983048 | tf_op jit(solution)/shard_map/ppermute | solution.py:359
  64.2 0.0 collective-permute-done.9.refs_1_
  64.2 4.3 %product.6.refs_2_ = f32[12,64,640]{2,1,0:T(8,128)S(1)} custom-call(s32[24,32]{1,0:T(8,128)S(1)} %select_select_fusion.1.place_ref, bf16[73,5,64,128]{3,2,1,0:T(8,128)(2,1)S(1)} %right_factor.1.right_ref, bf16[12,64,512]{2,1,0:T(8,128)(2,1)S(1)} %relayout.3.refs_0_, bf16[12,64,512]{2,1,0:T(8,128)(2,1)} %collective-permute-done.9.refs_1_), custom_call_target="tpu_custom_call" | custom-call | bytes 14800000 | tf_op jit(solution)/shard_map/product/pallas_call | solution.py:230
  68.5 0.0 collective-permute-done.8.refs_1_
  68.5 4.5 %product.7.refs_1_ = bf16[12,64,640]{2,1,0:T(8,128)(2,1)S(1)} custom-call(s32[24,32]{1,0:T(8,128)S(1)} %select_select_fusion.1.place_ref, bf16[73,5,64,128]{3,2,1,0:T(8,128)(2,1)S(1)} %right_factor.1.right_ref, bf16[12,64,512]{2,1,0:T(8,128)(2,1)} %collective-permute-done.7.refs_0_, bf16[12,64,512]{2,1,0:T(8,128)(2,1)} %collective-permute-done.8.refs_1_, ...), custom_call_target="tpu_custom_call" | custom-call | bytes 14800000 | tf_op jit(solution)/shard_map/product/pallas_call | solution.py:230
  73.0 1.6 %coarse.8 = (bf16[10,4,2048]{2,1,0:T(4,128)(2,1)S(1)}, bf16[10,8,2048]{2,1,0:T(8,128)(2,1)S(1)}) custom-call(bf16[12,24,64,128]{3,2,1,0:T(8,128)(2,1)S(1)} %left_factor.1.left_ref, bf16[12,64,640]{2,1,0:T(8,128)(2,1)S(1)} %product.5.refs_0_, bf16[12,64,640]{2,1,0:T(8,128)(2,1)S(1)} %product.7.refs_1_), custom_call_target="tpu_custom_call" | custom-call | bytes 7400000 | tf_op jit(solution)/shard_map/coarse/pallas_call | solution.py:273
  74.7 1.1 coarse.9
  75.7 1.6 %coarse.5 = (bf16[10,4,2048]{2,1,0:T(4,128)(2,1)S(1)}, bf16[10,8,2048]{2,1,0:T(8,128)(2,1)S(1)}) custom-call(bf16[12,24,64,128]{3,2,1,0:T(8,128)(2,1)S(1)} %left_factor.1.left_ref, bf16[12,64,640]{2,1,0:T(8,128)(2,1)S(1)} %product.5.refs_0_, bf16[12,64,640]{2,1,0:T(8,128)(2,1)S(1)} %product.7.refs_1_), custom_call_target="tpu_custom_call" | custom-call | bytes 7400000 | tf_op jit(solution)/shard_map/coarse/pallas_call | solution.py:273
  77.4 1.1 coarse.6
  78.5 2.8 %collective-permute-start.17 = (bf16[10,4,2048]{2,1,0:T(4,128)(2,1)S(1)}, bf16[10,4,2048]{2,1,0:T(4,128)(2,1)S(1)}, u32[]{:S(2)}, u32[]{:S(2)}) collective-permute-start(bf16[10,4,2048]{2,1,0:T(4,128)(2,1)S(1)} %get-tuple-element.16), channel_id=1, source_target_pairs={{4,0},{8,4},{12,8},{16,12},{20,16},{24,20},{28,24},{5,1},{9,5},{13... | collective-permute-start | bytes 491528 | tf_op jit(solution)/shard_map/ppermute | solution.py:359
  81.3 2.5 %collective-permute-start.16 = (bf16[10,8,2048]{2,1,0:T(8,128)(2,1)S(1)}, bf16[10,8,2048]{2,1,0:T(8,128)(2,1)S(1)}, u32[]{:S(2)}, u32[]{:S(2)}) collective-permute-start(bf16[10,8,2048]{2,1,0:T(8,128)(2,1)S(1)} %get-tuple-element.15), channel_id=1, source_target_pairs={{0,4},{4,8},{8,12},{12,16},{16,20},{20,24},{24,28},{1,5},{5,9},{9,... | collective-permute-start | bytes 983048 | tf_op jit(solution)/shard_map/ppermute | solution.py:356
  83.8 3.7 %collective-permute-start.12 = (bf16[10,4,2048]{2,1,0:T(4,128)(2,1)S(1)}, bf16[10,4,2048]{2,1,0:T(4,128)(2,1)S(1)}, u32[]{:S(2)}, u32[]{:S(2)}) collective-permute-start(bf16[10,4,2048]{2,1,0:T(4,128)(2,1)S(1)} %get-tuple-element.14), channel_id=1, source_target_pairs={{4,0},{8,4},{12,8},{16,12},{20,16},{24,20},{28,24},{5,1},{9,5},{13... | collective-permute-start | bytes 491528 | tf_op jit(solution)/shard_map/ppermute | solution.py:359
  87.5 1.9 %collective-permute-start.10 = (bf16[10,8,2048]{2,1,0:T(8,128)(2,1)S(1)}, bf16[10,8,2048]{2,1,0:T(8,128)(2,1)S(1)}, u32[]{:S(2)}, u32[]{:S(2)}) collective-permute-start(bf16[10,8,2048]{2,1,0:T(8,128)(2,1)S(1)} %get-tuple-element.13), channel_id=1, source_target_pairs={{0,4},{4,8},{8,12},{12,16},{16,20},{20,24},{24,28},{1,5},{5,9},{9,... | collective-permute-start | bytes 983048 | tf_op jit(solution)/shard_map/ppermute | solution.py:356
  89.4 0.1 fusion.19
  89.5 0.2 pad_maximum_fusion.1
  89.7 1.9 %collective-permute-done.16 = bf16[10,8,2048]{2,1,0:T(8,128)(2,1)S(1)} collective-permute-done((bf16[10,8,2048]{2,1,0:T(8,128)(2,1)S(1)}, bf16[10,8,2048]{2,1,0:T(8,128)(2,1)S(1)}, u32[]{:S(2)}, u32[]{:S(2)}) %collective-permute-start.16) | collective-permute-done | bytes 327712 | tf_op jit(solution)/shard_map/ppermute | solution.py:356
  91.7 0.1 add_convert_fusion
  91.8 12.0 %collective-permute-start.19 = (bf16[14,8,2048]{2,1,0:T(8,128)(2,1)S(1)}, bf16[14,8,2048]{2,1,0:T(8,128)(2,1)S(1)}, u32[]{:S(2)}, u32[]{:S(2)}) collective-permute-start(bf16[14,8,2048]{2,1,0:T(8,128)(2,1)S(1)} %bitcast.14), channel_id=1, source_target_pairs={{0,2},{1,3},{2,0},{3,1},{4,6},{5,7},{6,4},{7,5},{8,10},{9,11},{10,... | collective-permute-start | bytes 1376264 | tf_op jit(solution)/shard_map/ppermute | solution.py:350
  103.8 0.7 collective-permute-done.12
  104.5 0.2 pad_maximum_fusion
  104.7 0.1 add_convert_fusion.1
  104.8 2.2 %collective-permute-start.14 = (bf16[14,8,2048]{2,1,0:T(8,128)(2,1)S(1)}, bf16[14,8,2048]{2,1,0:T(8,128)(2,1)S(1)}, u32[]{:S(2)}, u32[]{:S(2)}) collective-permute-start(bf16[14,8,2048]{2,1,0:T(8,128)(2,1)S(1)} %bitcast.11), channel_id=1, source_target_pairs={{0,2},{1,3},{2,0},{3,1},{4,6},{5,7},{6,4},{7,5},{8,10},{9,11},{10,... | collective-permute-start | bytes 1376264 | tf_op jit(solution)/shard_map/ppermute | solution.py:350
  107.0 0.7 collective-permute-start.18
  107.7 0.1 collective-permute-start.13
  107.8 6.0 %collective-permute-done.19.refs_3_ = bf16[14,8,2048]{2,1,0:T(8,128)(2,1)S(1)} collective-permute-done((bf16[14,8,2048]{2,1,0:T(8,128)(2,1)S(1)}, bf16[14,8,2048]{2,1,0:T(8,128)(2,1)S(1)}, u32[]{:S(2)}, u32[]{:S(2)}) %collective-permute-start.19) | collective-permute-done | bytes 458784 | tf_op jit(solution)/shard_map/ppermute | solution.py:350
  113.8 2.9 %collective-permute-start.20 = (bf16[14,8,2048]{2,1,0:T(8,128)(2,1)S(1)}, bf16[14,8,2048]{2,1,0:T(8,128)(2,1)S(1)}, u32[]{:S(2)}, u32[]{:S(2)}) collective-permute-start(bf16[14,8,2048]{2,1,0:T(8,128)(2,1)S(1)} %collective-permute-done.19.refs_3_), channel_id=1, source_target_pairs={{0,1},{1,0},{2,3},{3,2},{4,5},{5,4},{6,7},{7,6},{8,9},{9,8},{10,11... | collective-permute-start | bytes 1376264 | tf_op jit(solution)/shard_map/ppermute | solution.py:353
  116.7 6.9 %collective-permute-done.14.refs_2_ = bf16[14,8,2048]{2,1,0:T(8,128)(2,1)S(1)} collective-permute-done((bf16[14,8,2048]{2,1,0:T(8,128)(2,1)S(1)}, bf16[14,8,2048]{2,1,0:T(8,128)(2,1)S(1)}, u32[]{:S(2)}, u32[]{:S(2)}) %collective-permute-start.14) | collective-permute-done | bytes 458784 | tf_op jit(solution)/shard_map/ppermute | solution.py:350
  123.6 1.5 %collective-permute-start.15 = (bf16[14,8,2048]{2,1,0:T(8,128)(2,1)S(1)}, bf16[14,8,2048]{2,1,0:T(8,128)(2,1)S(1)}, u32[]{:S(2)}, u32[]{:S(2)}) collective-permute-start(bf16[14,8,2048]{2,1,0:T(8,128)(2,1)S(1)} %collective-permute-done.14.refs_2_), channel_id=1, source_target_pairs={{0,1},{1,0},{2,3},{3,2},{4,5},{5,4},{6,7},{7,6},{8,9},{9,8},{10,11... | collective-permute-start | bytes 1376264 | tf_op jit(solution)/shard_map/ppermute | solution.py:353
  125.1 0.2 fusion.12.order_ref
  125.3 0.0 collective-permute-done.13.refs_1_
  125.3 1.2 collective-permute-done.15.refs_3_
  126.6 2.9 %assemble.2.refs_0_ = bf16[8,56,4096]{2,1,0:T(8,128)(2,1)} custom-call(bf16[448,448]{1,0:T(8,128)(2,1)S(1)} %fusion.12.order_ref, bf16[14,8,2048]{2,1,0:T(8,128)(2,1)S(1)} %bitcast.13, bf16[14,8,2048]{2,1,0:T(8,128)(2,1)S(1)} %collective-permute-done.13.refs_1_, bf16[14,8,2048]{2,1,0:T(8,128)(2,1)S(1)} %collective-permute-done.14.refs_2_, ...), custom_call_target="tpu_custom_call" | custom-call | bytes 10730000 | tf_op jit(solution)/shard_map/assemble/pallas_call | solution.py:308
  129.4 0.0 collective-permute-done.18.refs_2_
  129.4 0.0 collective-permute-done.20.refs_4_
  129.4 2.9 %assemble.3 = bf16[8,56,4096]{2,1,0:T(8,128)(2,1)} custom-call(bf16[448,448]{1,0:T(8,128)(2,1)S(1)} %fusion.12.order_ref, bf16[8,56,4096]{2,1,0:T(8,128)(2,1)} %assemble.2.refs_0_, bf16[14,8,2048]{2,1,0:T(8,128)(2,1)S(1)} %bitcast.16, bf16[14,8,2048]{2,1,0:T(8,128)(2,1)S(1)} %collective-permute-done.18.refs_2_, ...), custom_call_target="tpu_custom_call", output_to_operand_aliasing={{}: (1, {})} | custom-call | bytes 10730000 | tf_op jit(solution)/shard_map/assemble/pallas_call | solution.py:308
  (19 shorter events, 0.1 us)
Async XLA Ops:
  0.0 1.4 %copy-start = (bf16[24,8,4096]{2,1,0:T(8,128)(2,1)S(1)}, bf16[24,8,4096]{2,1,0:T(8,128)(2,1)}, u32[]{:S(2)}) copy-start(bf16[24,8,4096]{2,1,0:T(8,128)(2,1)} %x_ref.5) | copy-start | bytes 4718596
  1.4 38.3 %copy-start.4 = (s32[192,4]{0,1:T(4,128)S(1)}, s32[192,4]{0,1:T(4,128)}, u32[]{:S(2)}) copy-start(s32[192,4]{0,1:T(4,128)} %param.9) | copy-start | bytes 9220
  2.0 18.9 %collective-permute-start.4 = (bf16[12,64,512]{2,1,0:T(8,128)(2,1)S(1)}, bf16[12,64,512]{2,1,0:T(8,128)(2,1)}, u32[]{:S(2)}, u32[]{:S(2)}) collective-permute-start(bf16[12,64,512]{2,1,0:T(8,128)(2,1)S(1)} %relayout.2.refs_0_), channel_id=1, source_target_pairs={{0,2},{1,3},{2,0},{3,1},{4,6},{5,7},{6,4},{7,5},{8,10},{9,11},{10,... | collective-permute-start | bytes 2359304 | tf_op jit(solution)/shard_map/ppermute | solution.py:350
  3.9 38.7 %copy-start.5 = (s32[24,32]{1,0:T(8,128)S(1)}, s32[24,32]{1,0:T(8,128)}, u32[]{:S(2)}) copy-start(s32[24,32]{1,0:T(8,128)} %param.6) | copy-start | bytes 9220
  3.9 33.5 %collective-permute-start.7 = (bf16[12,64,512]{2,1,0:T(8,128)(2,1)S(1)}, bf16[12,64,512]{2,1,0:T(8,128)(2,1)}, u32[]{:S(2)}, u32[]{:S(2)}) collective-permute-start(bf16[12,64,512]{2,1,0:T(8,128)(2,1)S(1)} %relayout.3.refs_0_), channel_id=1, source_target_pairs={{0,2},{1,3},{2,0},{3,1},{4,6},{5,7},{6,4},{7,5},{8,10},{9,11},{10,... | collective-permute-start | bytes 2359304 | tf_op jit(solution)/shard_map/ppermute | solution.py:350
  4.2 1.1 copy-start.1
  6.5 12.2 %collective-permute-start = (bf16[12,64,256]{2,1,0:T(8,128)(2,1)S(1)}, bf16[12,64,256]{2,1,0:T(8,128)(2,1)S(1)}, u32[]{:S(2)}, u32[]{:S(2)}) collective-permute-start(bf16[12,64,256]{2,1,0:T(8,128)(2,1)S(1)} %constant_dynamic-slice_fusion), channel_id=1, source_target_pairs={{0,4},{4,8},{8,12},{12,16},{16,20},{20,24},{24,28},{1,5},{5,9},{9,... | collective-permute-start | bytes 1179656 | tf_op jit(solution)/shard_map/ppermute | solution.py:356
  9.6 19.2 %collective-permute-start.2 = (bf16[12,64,256]{2,1,0:T(8,128)(2,1)S(1)}, bf16[12,64,256]{2,1,0:T(8,128)(2,1)}, u32[]{:S(2)}, u32[]{:S(2)}) collective-permute-start(bf16[12,64,256]{2,1,0:T(8,128)(2,1)S(1)} %constant_dynamic-slice_fusion), channel_id=1, source_target_pairs={{4,0},{8,4},{12,8},{16,12},{20,16},{24,20},{28,24},{5,1},{9,5},{13... | collective-permute-start | bytes 1179656 | tf_op jit(solution)/shard_map/ppermute | solution.py:359
  18.7 20.3 %collective-permute-start.1 = (bf16[12,64,256]{2,1,0:T(8,128)(2,1)S(1)}, bf16[12,64,256]{2,1,0:T(8,128)(2,1)S(1)}, u32[]{:S(2)}, u32[]{:S(2)}) collective-permute-start(bf16[12,64,256]{2,1,0:T(8,128)(2,1)S(1)} %collective-permute-done.pr), channel_id=1, source_target_pairs={{0,1},{1,0},{2,3},{3,2},{4,5},{5,4},{6,7},{7,6},{8,9},{9,8},{10,11... | collective-permute-start | bytes 1179656 | tf_op jit(solution)/shard_map/ppermute | solution.py:353
  20.9 29.9 %collective-permute-start.6 = (bf16[12,64,512]{2,1,0:T(8,128)(2,1)S(1)}, bf16[12,64,512]{2,1,0:T(8,128)(2,1)}, u32[]{:S(2)}, u32[]{:S(2)}) collective-permute-start(bf16[12,64,512]{2,1,0:T(8,128)(2,1)S(1)} %relayout.2.refs_0_), channel_id=1, source_target_pairs={{0,1},{1,0},{2,3},{3,2},{4,5},{5,4},{6,7},{7,6},{8,9},{9,8},{10,11... | collective-permute-start | bytes 2359304 | tf_op jit(solution)/shard_map/ppermute | solution.py:353
  20.9 34.2 %collective-permute-start.5 = (bf16[12,64,512]{2,1,0:T(8,128)(2,1)}, bf16[12,64,512]{2,1,0:T(8,128)(2,1)}, u32[]{:S(2)}, u32[]{:S(2)}) collective-permute-start(bf16[12,64,512]{2,1,0:T(8,128)(2,1)} %collective-permute-done.4.refs_0_), channel_id=1, source_target_pairs={{0,1},{1,0},{2,3},{3,2},{4,5},{5,4},{6,7},{7,6},{8,9},{9,8},{10,11... | collective-permute-start | bytes 2359304 | tf_op jit(solution)/shard_map/ppermute | solution.py:353
  28.8 35.4 %collective-permute-start.9 = (bf16[12,64,512]{2,1,0:T(8,128)(2,1)S(1)}, bf16[12,64,512]{2,1,0:T(8,128)(2,1)}, u32[]{:S(2)}, u32[]{:S(2)}) collective-permute-start(bf16[12,64,512]{2,1,0:T(8,128)(2,1)S(1)} %relayout.3.refs_0_), channel_id=1, source_target_pairs={{0,1},{1,0},{2,3},{3,2},{4,5},{5,4},{6,7},{7,6},{8,9},{9,8},{10,11... | collective-permute-start | bytes 2359304 | tf_op jit(solution)/shard_map/ppermute | solution.py:353
  37.4 31.1 %collective-permute-start.8 = (bf16[12,64,512]{2,1,0:T(8,128)(2,1)}, bf16[12,64,512]{2,1,0:T(8,128)(2,1)}, u32[]{:S(2)}, u32[]{:S(2)}) collective-permute-start(bf16[12,64,512]{2,1,0:T(8,128)(2,1)} %collective-permute-done.7.refs_0_), channel_id=1, source_target_pairs={{0,1},{1,0},{2,3},{3,2},{4,5},{5,4},{6,7},{7,6},{8,9},{9,8},{10,11... | collective-permute-start | bytes 2359304 | tf_op jit(solution)/shard_map/ppermute | solution.py:353
  39.0 0.7 copy-start.2
  39.7 3.0 %collective-permute-start.3 = (bf16[12,64,256]{2,1,0:T(8,128)(2,1)}, bf16[12,64,256]{2,1,0:T(8,128)(2,1)}, u32[]{:S(2)}, u32[]{:S(2)}) collective-permute-start(bf16[12,64,256]{2,1,0:T(8,128)(2,1)} %collective-permute-done.2.nr), channel_id=1, source_target_pairs={{0,1},{1,0},{2,3},{3,2},{4,5},{5,4},{6,7},{7,6},{8,9},{9,8},{10,11... | collective-permute-start | bytes 1179656 | tf_op jit(solution)/shard_map/ppermute | solution.py:353
  39.7 2.9 %copy-start.6 = (s32[24]{0:T(128)S(1)}, s32[24]{0:T(128)}, u32[]{:S(2)}) copy-start(s32[24]{0:T(128)} %param.7) | copy-start | bytes 292
  39.8 3.0 %copy-start.3 = (bf16[12,64,256]{2,1,0:T(8,128)(2,1)S(1)}, bf16[12,64,256]{2,1,0:T(8,128)(2,1)}, u32[]{:S(2)}) copy-start(bf16[12,64,256]{2,1,0:T(8,128)(2,1)} %copy-done.2) | copy-start | bytes 1179652
  60.5 28.9 %collective-permute-start.11 = (bf16[10,4,4096]{2,1,0:T(4,128)(2,1)S(1)}, bf16[10,4,4096]{2,1,0:T(4,128)(2,1)S(1)}, u32[]{:S(2)}, u32[]{:S(2)}) collective-permute-start(bf16[10,4,4096]{2,1,0:T(4,128)(2,1)S(1)} %coarse.7), channel_id=1, source_target_pairs={{4,0},{8,4},{12,8},{16,12},{20,16},{24,20},{28,24},{5,1},{9,5},{13... | collective-permute-start | bytes 983048 | tf_op jit(solution)/shard_map/ppermute | solution.py:359
  78.5 11.1 %collective-permute-start.17 = (bf16[10,4,2048]{2,1,0:T(4,128)(2,1)S(1)}, bf16[10,4,2048]{2,1,0:T(4,128)(2,1)S(1)}, u32[]{:S(2)}, u32[]{:S(2)}) collective-permute-start(bf16[10,4,2048]{2,1,0:T(4,128)(2,1)S(1)} %get-tuple-element.16), channel_id=1, source_target_pairs={{4,0},{8,4},{12,8},{16,12},{20,16},{24,20},{28,24},{5,1},{9,5},{13... | collective-permute-start | bytes 491528 | tf_op jit(solution)/shard_map/ppermute | solution.py:359
  81.3 10.4 %collective-permute-start.16 = (bf16[10,8,2048]{2,1,0:T(8,128)(2,1)S(1)}, bf16[10,8,2048]{2,1,0:T(8,128)(2,1)S(1)}, u32[]{:S(2)}, u32[]{:S(2)}) collective-permute-start(bf16[10,8,2048]{2,1,0:T(8,128)(2,1)S(1)} %get-tuple-element.15), channel_id=1, source_target_pairs={{0,4},{4,8},{8,12},{12,16},{16,20},{20,24},{24,28},{1,5},{5,9},{9,... | collective-permute-start | bytes 983048 | tf_op jit(solution)/shard_map/ppermute | solution.py:356
  83.8 20.7 %collective-permute-start.12 = (bf16[10,4,2048]{2,1,0:T(4,128)(2,1)S(1)}, bf16[10,4,2048]{2,1,0:T(4,128)(2,1)S(1)}, u32[]{:S(2)}, u32[]{:S(2)}) collective-permute-start(bf16[10,4,2048]{2,1,0:T(4,128)(2,1)S(1)} %get-tuple-element.14), channel_id=1, source_target_pairs={{4,0},{8,4},{12,8},{16,12},{20,16},{24,20},{28,24},{5,1},{9,5},{13... | collective-permute-start | bytes 491528 | tf_op jit(solution)/shard_map/ppermute | solution.py:359
  87.5 17.2 %collective-permute-start.10 = (bf16[10,8,2048]{2,1,0:T(8,128)(2,1)S(1)}, bf16[10,8,2048]{2,1,0:T(8,128)(2,1)S(1)}, u32[]{:S(2)}, u32[]{:S(2)}) collective-permute-start(bf16[10,8,2048]{2,1,0:T(8,128)(2,1)S(1)} %get-tuple-element.13), channel_id=1, source_target_pairs={{0,4},{4,8},{8,12},{12,16},{16,20},{20,24},{24,28},{1,5},{5,9},{9,... | collective-permute-start | bytes 983048 | tf_op jit(solution)/shard_map/ppermute | solution.py:356
  91.8 22.0 %collective-permute-start.19 = (bf16[14,8,2048]{2,1,0:T(8,128)(2,1)S(1)}, bf16[14,8,2048]{2,1,0:T(8,128)(2,1)S(1)}, u32[]{:S(2)}, u32[]{:S(2)}) collective-permute-start(bf16[14,8,2048]{2,1,0:T(8,128)(2,1)S(1)} %bitcast.14), channel_id=1, source_target_pairs={{0,2},{1,3},{2,0},{3,1},{4,6},{5,7},{6,4},{7,5},{8,10},{9,11},{10,... | collective-permute-start | bytes 1376264 | tf_op jit(solution)/shard_map/ppermute | solution.py:350
  104.8 18.8 %collective-permute-start.14 = (bf16[14,8,2048]{2,1,0:T(8,128)(2,1)S(1)}, bf16[14,8,2048]{2,1,0:T(8,128)(2,1)S(1)}, u32[]{:S(2)}, u32[]{:S(2)}) collective-permute-start(bf16[14,8,2048]{2,1,0:T(8,128)(2,1)S(1)} %bitcast.11), channel_id=1, source_target_pairs={{0,2},{1,3},{2,0},{3,1},{4,6},{5,7},{6,4},{7,5},{8,10},{9,11},{10,... | collective-permute-start | bytes 1376264 | tf_op jit(solution)/shard_map/ppermute | solution.py:350
  107.0 22.5 %collective-permute-start.18 = (bf16[14,8,2048]{2,1,0:T(8,128)(2,1)S(1)}, bf16[14,8,2048]{2,1,0:T(8,128)(2,1)S(1)}, u32[]{:S(2)}, u32[]{:S(2)}) collective-permute-start(bf16[14,8,2048]{2,1,0:T(8,128)(2,1)S(1)} %bitcast.15), channel_id=1, source_target_pairs={{0,1},{1,0},{2,3},{3,2},{4,5},{5,4},{6,7},{7,6},{8,9},{9,8},{10,11... | collective-permute-start | bytes 1376264 | tf_op jit(solution)/shard_map/ppermute | solution.py:353
  107.7 17.6 %collective-permute-start.13 = (bf16[14,8,2048]{2,1,0:T(8,128)(2,1)S(1)}, bf16[14,8,2048]{2,1,0:T(8,128)(2,1)S(1)}, u32[]{:S(2)}, u32[]{:S(2)}) collective-permute-start(bf16[14,8,2048]{2,1,0:T(8,128)(2,1)S(1)} %bitcast.12), channel_id=1, source_target_pairs={{0,1},{1,0},{2,3},{3,2},{4,5},{5,4},{6,7},{7,6},{8,9},{9,8},{10,11... | collective-permute-start | bytes 1376264 | tf_op jit(solution)/shard_map/ppermute | solution.py:353
  113.8 15.7 %collective-permute-start.20 = (bf16[14,8,2048]{2,1,0:T(8,128)(2,1)S(1)}, bf16[14,8,2048]{2,1,0:T(8,128)(2,1)S(1)}, u32[]{:S(2)}, u32[]{:S(2)}) collective-permute-start(bf16[14,8,2048]{2,1,0:T(8,128)(2,1)S(1)} %collective-permute-done.19.refs_3_), channel_id=1, source_target_pairs={{0,1},{1,0},{2,3},{3,2},{4,5},{5,4},{6,7},{7,6},{8,9},{9,8},{10,11... | collective-permute-start | bytes 1376264 | tf_op jit(solution)/shard_map/ppermute | solution.py:353
  123.6 3.0 %collective-permute-start.15 = (bf16[14,8,2048]{2,1,0:T(8,128)(2,1)S(1)}, bf16[14,8,2048]{2,1,0:T(8,128)(2,1)S(1)}, u32[]{:S(2)}, u32[]{:S(2)}) collective-permute-start(bf16[14,8,2048]{2,1,0:T(8,128)(2,1)S(1)} %collective-permute-done.14.refs_2_), channel_id=1, source_target_pairs={{0,1},{1,0},{2,3},{3,2},{4,5},{5,4},{6,7},{7,6},{8,9},{9,8},{10,11... | collective-permute-start | bytes 1376264 | tf_op jit(solution)/shard_map/ppermute | solution.py:353

commit v3 on v2

--- a/solution.py
+++ b/solution.py
@@ -24,7 +24,7 @@
 
 
 def cost(us):
-    return pl.CostEstimate(flops=0, bytes_accessed=int(us * 3.7e6), transcendentals=0)
+    return pl.CostEstimate(flops=int(us * 1e8), bytes_accessed=int(us * 3.7e6), transcendentals=0)
 
 
 def low_lanes(rows):
@@ -125,74 +125,77 @@
     )(pct, p_own)
 
 
-def right_kernel(rb, nfb, share, tiles, pct_ref, own, pr, ps, nr, ns, o_ref):
+def column_table(pct, rb, share):
     slab = lax.axis_index("row")
-    col = lax.axis_index("col")
-    core = lax.rem(col, 2)
-    half = rb // 2
-    base = (slab - 1) * rb
-    low = low_lanes(BS)
+    padded = jnp.pad(pct, ((0, 0), (rb, rb)), constant_values=-1000000)
+    near = lax.dynamic_slice_in_dim(padded, slab * rb, 3 * rb, 1)
+    w = near - (slab - 2) * CB
+    e = (w & (CB - 1)) - share * lax.axis_index("col")
+    return jnp.where((w >= 0) & (e >= 0) & (e < share), e * GROUPS + (w >> 3), -1)
+
+
+def right_kernel(rb, tiles, table_ref, *refs):
+    o_ref = refs[-1]
+    core = lax.rem(lax.axis_index("col"), 2)
+    low = lax.broadcasted_iota(jnp.int32, (1, LANES), 1) < BS
+    wants = [jnp.where(low, p, tiles + p) for p in range(tiles)]
 
     def fill(src, count, near_first, out_first):
         def one(jj, carry):
-            fine = base + near_first + jj
-            valid = (fine >= 0) & (fine < nfb)
-            at = jnp.clip(fine, 0, nfb - 1)
-            spot = out_first + jj
+            dups = []
+            for t in range(4):
+                x = src[jj, :, t * BS : (t + 1) * BS]
+                dups.append(jnp.concatenate([x, x], axis=1))
+            at = [table_ref[t, near_first + jj] for t in range(4)]
             for p in range(tiles):
-                o_ref[spot, p] = jnp.zeros((BS, LANES), BF)
-            for t in range(4):
-                w = pct_ref[t, at] - (slab - 2) * CB
-                e = (w & (CB - 1)) - share * col
-
-                @pl.when(valid & (e >= 0) & (e < share))
-                def _():
-                    n = e * GROUPS + (w >> 3)
-                    upper = n >= tiles
-                    tile = jnp.where(upper, n - tiles, n)
-                    pair = src[jj, :, t // 2 * LANES : (t // 2 + 1) * LANES].astype(F32)
-                    other = pltpu.roll(pair, BS, 1)
-                    both = jnp.where(low, pair, other) if t % 2 == 0 else jnp.where(low, other, pair)
-                    keep = jnp.where(low == jnp.logical_not(upper), both, 0.0)
-                    o_ref[spot, tile] = (o_ref[spot, tile].astype(F32) + keep).astype(BF)
-
+                total = None
+                for t in range(4):
+                    keep = dups[t] * jnp.where(wants[p] == at[t], 1.0, 0.0).astype(BF)
+                    total = keep if total is None else total + keep
+                o_ref[out_first + jj, p] = total
             return carry
 
-        lax.fori_loop(0, count, one, 0)
-
-    fill(own, rb, rb, 0)
-    fill(pr, half, half * core, rb)
-    fill(ps, half, half * (1 - core), rb + half)
-    fill(nr, half, 2 * rb + half * core, 2 * rb)
-    fill(ns, half, 2 * rb + half * (1 - core), 2 * rb + half)
-    o_ref[3 * rb] = jnp.zeros((tiles, BS, LANES), BF)
-
-
-def right_factor(pct, pieces, nfb, share, tiles):
-    rb = pieces[0].shape[0]
-    return pl.pallas_call(
-        functools.partial(right_kernel, rb, nfb, share, tiles),
-        out_shape=jax.ShapeDtypeStruct((3 * rb + 1, tiles, BS, LANES), BF),
-        in_specs=[SM] + [VM] * 5,
+        lax.fori_loop(0, count, one, 0, unroll=4)
+
+    if len(refs) == 2:
+        fill(refs[0], rb, rb, 0)
+        o_ref[rb] = jnp.zeros((tiles, BS, LANES), BF)
+    else:
+        done = refs[0].shape[0]
+
+        def copy(jj, carry):
+            o_ref[jj] = refs[0][jj]
+            return carry
+
+        lax.fori_loop(0, done, copy, 0)
+        for z in range(2):
+            there = core if z == 0 else 1 - core
+            fill(refs[1 + z], rb, 2 * rb * there, done + rb * z)
+
+
+def right_factor(table, srcs, tiles, us):
+    rb = table.shape[1] // 3
+    spots = rb + 1 if len(srcs) == 1 else 3 * rb + 1
+    return pl.pallas_call(
+        functools.partial(right_kernel, rb, tiles),
+        out_shape=jax.ShapeDtypeStruct((spots, tiles, BS, LANES), BF),
+        in_specs=[SM] + [VM] * len(srcs),
         out_specs=VM,
         compiler_params=params(24),
-        cost_estimate=cost(4.0),
+        cost_estimate=cost(us),
         name="right_factor",
-    )(pct, *pieces)
+    )(table, *srcs)
 
 
 def slot_places(a_cols, counts):
     rb, ka = a_cols.shape
-    half = rb // 2
     core = lax.axis_index("col") % 2
     near = a_cols - (lax.axis_index("row") - 1) * rb
-    before, behind = near < rb, near >= 2 * rb
-    inside = near - jnp.where(before, 0, jnp.where(behind, 2 * rb, rb))
-    far = (inside >= half).astype(jnp.int32)
-    off = inside - half * far + half * jnp.where(far == core, 0, 1)
-    spot = jnp.where(before, rb + off, jnp.where(behind, 2 * rb + off, inside))
+    before = near + jnp.where(core == 0, rb + 1, 2 * rb + 1)
+    after = near - 2 * rb + jnp.where(core == 0, 2 * rb + 1, rb + 1)
+    spot = jnp.where(near < rb, before, jnp.where(near >= 2 * rb, after, near - rb))
     live = jnp.arange(ka, dtype=jnp.int32)[None, :] < counts[:, None]
-    return jnp.where(live, spot, 3 * rb)
+    return jnp.where(live, spot, rb)
 
 
 def product_kernel(first, shifts, has_acc, ks, place_ref, right_ref, *refs):
@@ -243,7 +246,6 @@
     aps = refs[: -1 - len(sets)]
     scr = refs[-1]
     ac = a1 - a0
-    half = aps[0].shape[0]
     tiles = aps[0].shape[2] // LANES
     for out, (i0, i1) in zip(outs, sets):
         rows = i1 - i0
@@ -251,12 +253,13 @@
         for p0 in range(0, tiles, 2):
             p1 = min(p0 + 2, tiles)
             acc = jnp.zeros((rows * ac, (p1 - p0) * LANES), F32)
-            for side, ap in enumerate(aps):
-                for g in range(0, half // 2, 2):
-                    ip = side * (half // 2) + g
+            ip = 0
+            for ap in aps:
+                for g in range(0, ap.shape[0] // 2, 2):
                     lhs = [left_ref[ip + d, i0:i1, a0:a1].reshape(rows * ac, LANES) for d in range(2)]
                     rhs = ap[2 * g : 2 * g + 4, :, p0 * LANES : p1 * LANES].reshape(4 * BS, (p1 - p0) * LANES)
                     acc = acc + dot(jnp.concatenate(lhs, axis=1), rhs)
+                    ip += 2
             for p in range(p0, p1):
                 scr[p, 0 : rows * ac] = acc[:, (p - p0) * LANES : (p - p0 + 1) * LANES]
         for p in range(tiles):
@@ -342,9 +345,12 @@
     nfb = p_cols.shape[0]
     share = CB // ncol
     tiles = (GROUPS * share + 1) // 2
-    half = rb // 2
+    parts = ((0, rb * 2 // 3), (rb * 2 // 3, rb // 3))
     chunks = ((0, 32), (32, 64))
-    core = lax.axis_index("col") % 2
+
+    def outward(x):
+        pairs = [(r * ncol + c, (r + 1 - 2 * (c % 2)) * ncol + c) for r in range(nrow) for c in range(ncol)]
+        return lax.ppermute(x, ("row", "col"), [(a, b) for a, b in pairs if 0 <= b < nrow * ncol])
 
     def over_y(x, s):
         return lax.ppermute(x, "col", [(y * 2 + c, (y + s) % ny * 2 + c) for y in range(ny) for c in range(2)])
@@ -365,19 +371,30 @@
         got = [x] + [over_y(x, s) for s in range(1, ny)]
         return [z for g in got for z in (g, over_core(g))]
 
-    a_parts = [gather(relayout(a_blocks, h * half, half)) for h in range(2)]
+    own_a, side_a, far_a = [], [], []
+    for h, (first, rows) in enumerate(parts):
+        x = relayout(a_blocks, first, rows)
+        own_a.append(x)
+        far_a.append([over_y(x, s) for s in range(1, ny)])
+        side_a.append(over_core(x))
+        if h == 0:
+            a_blocks, p_blocks, side_a[0] = lax.optimization_barrier((a_blocks, p_blocks, side_a[0]))
     p_mixed, p_own = relayout_both(p_blocks)
-    mine = lax.dynamic_slice_in_dim(p_own, core * half, half, 0)
-    prev, after = upward(mine), downward(mine)
+    beside = outward(p_own)
+    p_mixed, p_own, side_a[1] = lax.optimization_barrier((p_mixed, p_own, side_a[1]))
+    table = column_table(pct, rb, share)
     left = left_factor(pct, p_mixed)
+    right = right_factor(table, [p_own], tiles, 2.0)
     order = assembly_order(shifts, ncol, share)
     place = slot_places(a_cols, counts)
-    pieces = [p_own, prev, over_core(prev), after, over_core(after)]
-    right = right_factor(pct, pieces, nfb, share, tiles)
+    beside, left, right, order, place = lax.optimization_barrier((beside, left, right, order, place))
+    right = right_factor(table, [right, beside, over_core(beside)], tiles, 4.0)
+    near = [product(place, right, [own_a[h], side_a[h]], shifts[:2], parts[h][0], None, F32) for h in range(2)]
+    far_a[1], near = lax.optimization_barrier((far_a[1], near))
     aps = []
     for h in range(2):
-        near = product(place, right, a_parts[h][:2], shifts[:2], h * half, None, F32)
-        aps.append(product(place, right, a_parts[h][2:], shifts[2:], h * half, near, BF))
+        srcs = [z for g in far_a[h] for z in (g, over_core(g))]
+        aps.append(product(place, right, srcs, shifts[2:], parts[h][0], near[h], BF))
         if h == 0:
             early = downward(coarse_rows(left, aps, ((0, CB // 2),), 0, BS, BF, 1.0)[0])
 

time: 132 us -> 115 us (0.87)
  the two profiles are of different devices: /device:TPU:25 before, /device:TPU:9 now
where the time goes in v3:
time: 115 us
  Pallas kernels  41.4 us (36%)
  waiting for transfers between devices  41.2 us (36%)
  starting transfers between devices  29.7 us (26%)
  local copies, waits for them, and re-layouts  1.57 us (1%)
    pallas_call x4, Pallas kernels, product(): pl.pallas_call(functools.partial(product_kernel, first, shifts, acc is no...  16.6 us
    ppermute x4, waiting for transfers between devices, over_y(): lax.ppermute(x, 'col', [(y * 2 + c, (y + s) % ny * 2 + c) for y in range(...  16.4 us
    ppermute x3, waiting for transfers between devices, downward(): return lax.ppermute(x, 'row', [(i + 1, i) for i in range(nrow - 1)])  11.1 us
    ppermute x1, waiting for transfers between devices, outward(): lax.ppermute(x, ('row', 'col'), [(a, b) for a, b in pairs if 0 <= b < nro...  10.4 us
    ppermute x3, starting transfers between devices, downward(): return lax.ppermute(x, 'row', [(i + 1, i) for i in range(nrow - 1)])  8.07 us
    ppermute x2, starting transfers between devices, upward(): return lax.ppermute(x, 'row', [(i, i + 1) for i in range(nrow - 1)])  7.33 us
    ppermute x9, starting transfers between devices, over_core(): return lax.ppermute(x, 'col', [(c, c ^ 1) for c in range(ncol)])  7.2 us
    pallas_call x5, Pallas kernels, coarse_rows(): pl.pallas_call(functools.partial(coarse_kernel, sets, a0, a1), out_shape=...  6.35 us
  transfers between devices with their start and end apart: 19, of which 8 were waited for; matrix products, arithmetic and copies ran while one was open for 1% of the time, Pallas kernels for 33%

profile of v3, /device:TPU:9, one launch (start us, length us, event | category | flops | bytes accessed | tf_op | source)
XLA Modules:
  0.0 115.0 jit_solution(8490111685101988008)
XLA Ops:
  0.0 1.4 %copy-done = bf16[24,8,4096]{2,1,0:T(8,128)(2,1)S(1)} copy-done((bf16[24,8,4096]{2,1,0:T(8,128)(2,1)S(1)}, bf16[24,8,4096]{2,1,0:T(8,128)(2,1)}, u32[]{:S(2)}) %copy-start) | copy-done | bytes 1572888
  1.4 0.8 relayout.2.refs_0_
  2.2 0.7 collective-permute-start
  3.0 1.3 %collective-permute-start.4 = (bf16[16,64,512]{2,1,0:T(8,128)(2,1)S(1)}, bf16[16,64,512]{2,1,0:T(8,128)(2,1)}, u32[]{:S(2)}, u32[]{:S(2)}) collective-permute-start(bf16[16,64,512]{2,1,0:T(8,128)(2,1)S(1)} %relayout.2.refs_0_), channel_id=1, source_target_pairs={{0,2},{1,3},{2,0},{3,1},{4,6},{5,7},{6,4},{7,5},{8,10},{9,11},{10,... | collective-permute-start | bytes 3145736 | tf_op jit(solution)/shard_map/ppermute | solution.py:356
  4.2 0.1 add_select_fusion.4.table_ref
  4.4 1.0 collective-permute-done.refs_1_
  5.4 2.7 %relayout_both.1 = (bf16[24,64,256]{2,1,0:T(8,128)(2,1)S(1)}, bf16[24,64,256]{2,1,0:T(8,128)(2,1)}) custom-call(bf16[24,4,4096]{2,1,0:T(4,128)(2,1)S(1)} %copy-done.4), custom_call_target="tpu_custom_call" | custom-call | flops 150000000 | bytes 5550000 | tf_op jit(solution)/shard_map/relayout_both/pallas_call | solution.py:83
  8.1 3.0 %collective-permute-start.1 = (bf16[24,64,256]{2,1,0:T(8,128)(2,1)}, bf16[24,64,256]{2,1,0:T(8,128)(2,1)}, u32[]{:S(2)}, u32[]{:S(2)}) collective-permute-start(bf16[24,64,256]{2,1,0:T(8,128)(2,1)} %get-tuple-element.30.refs_0_), channel_id=1, source_target_pairs={{0,4},{2,6},{4,8},{5,1},{6,10},{7,3},{8,12},{9,5},{10,14},{11,7},{... | collective-permute-start | bytes 2359304 | tf_op jit(solution)/shard_map/ppermute | solution.py:353
  11.1 0.1 select_select_fusion.1.place_ref
  11.2 0.4 relayout.3.refs_0_
  11.6 0.8 collective-permute-start.2
  12.4 0.2 fusion.12.order_ref
  12.6 1.3 %collective-permute-done.2.refs_1_ = bf16[8,64,512]{2,1,0:T(8,128)(2,1)S(1)} collective-permute-done((bf16[8,64,512]{2,1,0:T(8,128)(2,1)S(1)}, bf16[8,64,512]{2,1,0:T(8,128)(2,1)S(1)}, u32[]{:S(2)}, u32[]{:S(2)}) %collective-permute-start.2) | collective-permute-done | bytes 524320 | tf_op jit(solution)/shard_map/ppermute | solution.py:359
  14.0 2.3 %right_factor.2.refs_0_ = bf16[25,5,64,128]{3,2,1,0:T(8,128)(2,1)S(1)} custom-call(s32[4,72]{1,0:T(4,128)S(1)} %add_select_fusion.4.table_ref, bf16[24,64,256]{2,1,0:T(8,128)(2,1)} %get-tuple-element.30.refs_0_), custom_call_target="tpu_custom_call" | custom-call | flops 200000000 | bytes 7400000 | tf_op jit(solution)/shard_map/right_factor/pallas_call | solution.py:179
  16.3 2.9 %left_factor.1.left_ref = bf16[12,24,64,128]{3,2,1,0:T(8,128)(2,1)S(1)} custom-call(s32[4,192]{1,0:T(4,128)S(1)} %bitcast.18, bf16[24,64,256]{2,1,0:T(8,128)(2,1)S(1)} %copy-done.3), custom_call_target="tpu_custom_call" | custom-call | flops 290000000 | bytes 10730000 | tf_op jit(solution)/shard_map/left_factor/pallas_call | solution.py:117
  19.2 10.4 %collective-permute-done.1.refs_1_ = bf16[24,64,256]{2,1,0:T(8,128)(2,1)} collective-permute-done((bf16[24,64,256]{2,1,0:T(8,128)(2,1)}, bf16[24,64,256]{2,1,0:T(8,128)(2,1)}, u32[]{:S(2)}, u32[]{:S(2)}) %collective-permute-start.1) | collective-permute-done | bytes 786464 | tf_op jit(solution)/shard_map/ppermute | solution.py:353
  29.5 0.5 collective-permute-start.3
  30.1 0.0 collective-permute-done.4.refs_0_
  30.1 0.0 collective-permute-start.5
  30.1 1.2 %collective-permute-start.6 = (bf16[8,64,512]{2,1,0:T(8,128)(2,1)S(1)}, bf16[8,64,512]{2,1,0:T(8,128)(2,1)S(1)}, u32[]{:S(2)}, u32[]{:S(2)}) collective-permute-start(bf16[8,64,512]{2,1,0:T(8,128)(2,1)S(1)} %relayout.3.refs_0_), channel_id=1, source_target_pairs={{0,2},{1,3},{2,0},{3,1},{4,6},{5,7},{6,4},{7,5},{8,10},{9,11},{10,... | collective-permute-start | bytes 1572872 | tf_op jit(solution)/shard_map/ppermute | solution.py:356
  31.3 0.9 collective-permute-done.3.refs_2_
  32.2 3.6 %right_factor.3.right_ref = bf16[73,5,64,128]{3,2,1,0:T(8,128)(2,1)S(1)} custom-call(s32[4,72]{1,0:T(4,128)S(1)} %add_select_fusion.4.table_ref, bf16[25,5,64,128]{3,2,1,0:T(8,128)(2,1)S(1)} %right_factor.2.refs_0_, bf16[24,64,256]{2,1,0:T(8,128)(2,1)} %collective-permute-done.1.refs_1_, bf16[24,64,256]{2,1,0:T(8,128)(2,1)S(1)} %collective-permute-done.3.refs_2_), custom_call_target="tpu_custom_call" | custom-call | flops 400000000 | bytes 14800000 | tf_op jit(solution)/shard_map/right_factor/pallas_call | solution.py:179
  35.8 2.8 %product.5.refs_2_ = f32[8,64,640]{2,1,0:T(8,128)S(1)} custom-call(s32[24,32]{1,0:T(8,128)S(1)} %select_select_fusion.1.place_ref, bf16[73,5,64,128]{3,2,1,0:T(8,128)(2,1)S(1)} %right_factor.3.right_ref, bf16[8,64,512]{2,1,0:T(8,128)(2,1)S(1)} %relayout.3.refs_0_, bf16[8,64,512]{2,1,0:T(8,128)(2,1)S(1)} %collective-permute-done.2.refs_1_), custom_call_target="tpu_custom_call" | custom-call | flops 400000000 | bytes 14800000 | tf_op jit(solution)/shard_map/product/pallas_call | solution.py:233
  38.7 5.4 %product.4.refs_2_ = f32[16,64,640]{2,1,0:T(8,128)S(1)} custom-call(s32[24,32]{1,0:T(8,128)S(1)} %select_select_fusion.1.place_ref, bf16[73,5,64,128]{3,2,1,0:T(8,128)(2,1)S(1)} %right_factor.3.right_ref, bf16[16,64,512]{2,1,0:T(8,128)(2,1)S(1)} %relayout.2.refs_0_, bf16[16,64,512]{2,1,0:T(8,128)(2,1)} %collective-permute-done.refs_1_), custom_call_target="tpu_custom_call" | custom-call | flops 400000000 | bytes 14800000 | tf_op jit(solution)/shard_map/product/pallas_call | solution.py:233
  44.1 0.0 collective-permute-done.6.refs_0_
  44.1 0.4 collective-permute-start.7
  44.6 0.0 collective-permute-done.5.refs_1_
  44.6 5.4 %product.6.refs_0_ = bf16[16,64,640]{2,1,0:T(8,128)(2,1)S(1)} custom-call(s32[24,32]{1,0:T(8,128)S(1)} %select_select_fusion.1.place_ref, bf16[73,5,64,128]{3,2,1,0:T(8,128)(2,1)S(1)} %right_factor.3.right_ref, bf16[16,64,512]{2,1,0:T(8,128)(2,1)} %collective-permute-done.4.refs_0_, bf16[16,64,512]{2,1,0:T(8,128)(2,1)S(1)} %collective-permute-done.5.refs_1_, ...), custom_call_target="tpu_custom_call" | custom-call | flops 400000000 | bytes 14800000 | tf_op jit(solution)/shard_map/product/pallas_call | solution.py:233
  50.0 0.9 coarse.7
  51.0 4.0 %collective-permute-start.9 = (bf16[10,4,4096]{2,1,0:T(4,128)(2,1)S(1)}, bf16[10,4,4096]{2,1,0:T(4,128)(2,1)S(1)}, u32[]{:S(2)}, u32[]{:S(2)}) collective-permute-start(bf16[10,4,4096]{2,1,0:T(4,128)(2,1)S(1)} %coarse.7), channel_id=1, source_target_pairs={{4,0},{8,4},{12,8},{16,12},{20,16},{24,20},{28,24},{5,1},{9,5},{13... | collective-permute-start | bytes 983048 | tf_op jit(solution)/shard_map/ppermute | solution.py:365
  55.0 0.0 collective-permute-done.7.refs_1_
  55.0 2.9 %product.7.refs_1_ = bf16[8,64,640]{2,1,0:T(8,128)(2,1)S(1)} custom-call(s32[24,32]{1,0:T(8,128)S(1)} %select_select_fusion.1.place_ref, bf16[73,5,64,128]{3,2,1,0:T(8,128)(2,1)S(1)} %right_factor.3.right_ref, bf16[8,64,512]{2,1,0:T(8,128)(2,1)S(1)} %collective-permute-done.6.refs_0_, bf16[8,64,512]{2,1,0:T(8,128)(2,1)S(1)} %collective-permute-done.7.refs_1_, ...), custom_call_target="tpu_custom_call" | custom-call | flops 400000000 | bytes 14800000 | tf_op jit(solution)/shard_map/product/pallas_call | solution.py:233
  57.8 1.6 %coarse.8 = (bf16[10,4,2048]{2,1,0:T(4,128)(2,1)S(1)}, bf16[10,8,2048]{2,1,0:T(8,128)(2,1)S(1)}) custom-call(bf16[12,24,64,128]{3,2,1,0:T(8,128)(2,1)S(1)} %left_factor.1.left_ref, bf16[16,64,640]{2,1,0:T(8,128)(2,1)S(1)} %product.6.refs_0_, bf16[8,64,640]{2,1,0:T(8,128)(2,1)S(1)} %product.7.refs_1_), custom_call_target="tpu_custom_call" | custom-call | flops 200000000 | bytes 7400000 | tf_op jit(solution)/shard_map/coarse/pallas_call | solution.py:276
  59.5 1.9 %collective-permute-start.15 = (bf16[10,4,2048]{2,1,0:T(4,128)(2,1)S(1)}, bf16[10,4,2048]{2,1,0:T(4,128)(2,1)S(1)}, u32[]{:S(2)}, u32[]{:S(2)}) collective-permute-start(bf16[10,4,2048]{2,1,0:T(4,128)(2,1)S(1)} %get-tuple-element.44), channel_id=1, source_target_pairs={{4,0},{8,4},{12,8},{16,12},{20,16},{24,20},{28,24},{5,1},{9,5},{13... | collective-permute-start | bytes 491528 | tf_op jit(solution)/shard_map/ppermute | solution.py:365
  61.4 1.6 %collective-permute-done.9 = bf16[10,4,4096]{2,1,0:T(4,128)(2,1)S(1)} collective-permute-done((bf16[10,4,4096]{2,1,0:T(4,128)(2,1)S(1)}, bf16[10,4,4096]{2,1,0:T(4,128)(2,1)S(1)}, u32[]{:S(2)}, u32[]{:S(2)}) %collective-permute-start.9) | collective-permute-done | bytes 327712 | tf_op jit(solution)/shard_map/ppermute | solution.py:365
  63.0 0.1 fusion.24
  63.2 4.0 %collective-permute-start.14 = (bf16[10,8,2048]{2,1,0:T(8,128)(2,1)S(1)}, bf16[10,8,2048]{2,1,0:T(8,128)(2,1)S(1)}, u32[]{:S(2)}, u32[]{:S(2)}) collective-permute-start(bf16[10,8,2048]{2,1,0:T(8,128)(2,1)S(1)} %get-tuple-element.43), channel_id=1, source_target_pairs={{0,4},{4,8},{8,12},{12,16},{16,20},{20,24},{24,28},{1,5},{5,9},{9,... | collective-permute-start | bytes 983048 | tf_op jit(solution)/shard_map/ppermute | solution.py:362
  67.2 1.6 %coarse.5 = (bf16[10,4,2048]{2,1,0:T(4,128)(2,1)S(1)}, bf16[10,8,2048]{2,1,0:T(8,128)(2,1)S(1)}) custom-call(bf16[12,24,64,128]{3,2,1,0:T(8,128)(2,1)S(1)} %left_factor.1.left_ref, bf16[16,64,640]{2,1,0:T(8,128)(2,1)S(1)} %product.6.refs_0_, bf16[8,64,640]{2,1,0:T(8,128)(2,1)S(1)} %product.7.refs_1_), custom_call_target="tpu_custom_call" | custom-call | flops 200000000 | bytes 7400000 | tf_op jit(solution)/shard_map/coarse/pallas_call | solution.py:276
  68.8 2.2 %collective-permute-start.10 = (bf16[10,4,2048]{2,1,0:T(4,128)(2,1)S(1)}, bf16[10,4,2048]{2,1,0:T(4,128)(2,1)S(1)}, u32[]{:S(2)}, u32[]{:S(2)}) collective-permute-start(bf16[10,4,2048]{2,1,0:T(4,128)(2,1)S(1)} %get-tuple-element.42), channel_id=1, source_target_pairs={{4,0},{8,4},{12,8},{16,12},{20,16},{24,20},{28,24},{5,1},{9,5},{13... | collective-permute-start | bytes 491528 | tf_op jit(solution)/shard_map/ppermute | solution.py:365
  71.0 3.3 %collective-permute-start.8 = (bf16[10,8,2048]{2,1,0:T(8,128)(2,1)S(1)}, bf16[10,8,2048]{2,1,0:T(8,128)(2,1)S(1)}, u32[]{:S(2)}, u32[]{:S(2)}) collective-permute-start(bf16[10,8,2048]{2,1,0:T(8,128)(2,1)S(1)} %get-tuple-element.41), channel_id=1, source_target_pairs={{0,4},{4,8},{8,12},{12,16},{16,20},{20,24},{24,28},{1,5},{5,9},{9,... | collective-permute-start | bytes 983048 | tf_op jit(solution)/shard_map/ppermute | solution.py:362
  74.3 1.1 coarse.9
  75.4 1.1 coarse.6
  76.4 0.0 collective-permute-done.15
  76.5 0.2 pad_maximum_fusion.1
  76.6 9.5 %collective-permute-done.10 = bf16[10,4,2048]{2,1,0:T(4,128)(2,1)S(1)} collective-permute-done((bf16[10,4,2048]{2,1,0:T(4,128)(2,1)S(1)}, bf16[10,4,2048]{2,1,0:T(4,128)(2,1)S(1)}, u32[]{:S(2)}, u32[]{:S(2)}) %collective-permute-start.10) | collective-permute-done | bytes 163872 | tf_op jit(solution)/shard_map/ppermute | solution.py:365
  86.1 0.2 pad_maximum_fusion
  86.3 0.0 collective-permute-done.8
  86.3 0.1 add_convert_fusion.1
  86.4 1.3 %collective-permute-start.12 = (bf16[14,8,2048]{2,1,0:T(8,128)(2,1)S(1)}, bf16[14,8,2048]{2,1,0:T(8,128)(2,1)S(1)}, u32[]{:S(2)}, u32[]{:S(2)}) collective-permute-start(bf16[14,8,2048]{2,1,0:T(8,128)(2,1)S(1)} %bitcast.11), channel_id=1, source_target_pairs={{0,2},{1,3},{2,0},{3,1},{4,6},{5,7},{6,4},{7,5},{8,10},{9,11},{10,... | collective-permute-start | bytes 1376264 | tf_op jit(solution)/shard_map/ppermute | solution.py:356
  87.7 0.0 collective-permute-done.14
  87.7 0.1 add_convert_fusion
  87.8 0.3 collective-permute-start.17
  88.1 1.0 collective-permute-start.11
  89.2 8.9 %collective-permute-done.12.refs_2_ = bf16[14,8,2048]{2,1,0:T(8,128)(2,1)S(1)} collective-permute-done((bf16[14,8,2048]{2,1,0:T(8,128)(2,1)S(1)}, bf16[14,8,2048]{2,1,0:T(8,128)(2,1)S(1)}, u32[]{:S(2)}, u32[]{:S(2)}) %collective-permute-start.12) | collective-permute-done | bytes 458784 | tf_op jit(solution)/shard_map/ppermute | solution.py:356
  98.1 2.3 %collective-permute-start.13 = (bf16[14,8,2048]{2,1,0:T(8,128)(2,1)S(1)}, bf16[14,8,2048]{2,1,0:T(8,128)(2,1)S(1)}, u32[]{:S(2)}, u32[]{:S(2)}) collective-permute-start(bf16[14,8,2048]{2,1,0:T(8,128)(2,1)S(1)} %collective-permute-done.12.refs_2_), channel_id=1, source_target_pairs={{0,1},{1,0},{2,3},{3,2},{4,5},{5,4},{6,7},{7,6},{8,9},{9,8},{10,11... | collective-permute-start | bytes 1376264 | tf_op jit(solution)/shard_map/ppermute | solution.py:359
  100.3 0.0 collective-permute-start.16
  100.4 7.5 %collective-permute-done.17.refs_3_ = bf16[14,8,2048]{2,1,0:T(8,128)(2,1)S(1)} collective-permute-done((bf16[14,8,2048]{2,1,0:T(8,128)(2,1)S(1)}, bf16[14,8,2048]{2,1,0:T(8,128)(2,1)S(1)}, u32[]{:S(2)}, u32[]{:S(2)}) %collective-permute-start.17) | collective-permute-done | bytes 458784 | tf_op jit(solution)/shard_map/ppermute | solution.py:356
  107.9 1.3 %collective-permute-start.18 = (bf16[14,8,2048]{2,1,0:T(8,128)(2,1)S(1)}, bf16[14,8,2048]{2,1,0:T(8,128)(2,1)S(1)}, u32[]{:S(2)}, u32[]{:S(2)}) collective-permute-start(bf16[14,8,2048]{2,1,0:T(8,128)(2,1)S(1)} %collective-permute-done.17.refs_3_), channel_id=1, source_target_pairs={{0,1},{1,0},{2,3},{3,2},{4,5},{5,4},{6,7},{7,6},{8,9},{9,8},{10,11... | collective-permute-start | bytes 1376264 | tf_op jit(solution)/shard_map/ppermute | solution.py:359
  109.2 0.0 collective-permute-done.11.refs_1_
  109.2 0.0 collective-permute-done.13.refs_3_
  109.2 2.9 %assemble.2.refs_0_ = bf16[8,56,4096]{2,1,0:T(8,128)(2,1)} custom-call(bf16[448,448]{1,0:T(8,128)(2,1)S(1)} %fusion.12.order_ref, bf16[14,8,2048]{2,1,0:T(8,128)(2,1)S(1)} %bitcast.13, bf16[14,8,2048]{2,1,0:T(8,128)(2,1)S(1)} %collective-permute-done.11.refs_1_, bf16[14,8,2048]{2,1,0:T(8,128)(2,1)S(1)} %collective-permute-done.12.refs_2_, ...), custom_call_target="tpu_custom_call" | custom-call | flops 290000000 | bytes 10730000 | tf_op jit(solution)/shard_map/assemble/pallas_call | solution.py:311
  112.1 0.0 collective-permute-done.16.refs_2_
  112.1 0.0 collective-permute-done.18.refs_4_
  112.1 2.9 %assemble.3 = bf16[8,56,4096]{2,1,0:T(8,128)(2,1)} custom-call(bf16[448,448]{1,0:T(8,128)(2,1)S(1)} %fusion.12.order_ref, bf16[8,56,4096]{2,1,0:T(8,128)(2,1)} %assemble.2.refs_0_, bf16[14,8,2048]{2,1,0:T(8,128)(2,1)S(1)} %bitcast.16, bf16[14,8,2048]{2,1,0:T(8,128)(2,1)S(1)} %collective-permute-done.16.refs_2_, ...), custom_call_target="tpu_custom_call", output_to_operand_aliasing={{}: (1, {})} | custom-call | flops 290000000 | bytes 10730000 | tf_op jit(solution)/shard_map/assemble/pallas_call | solution.py:311
  (18 shorter events, 0.1 us)
Async XLA Ops:
  0.0 1.4 %copy-start = (bf16[24,8,4096]{2,1,0:T(8,128)(2,1)S(1)}, bf16[24,8,4096]{2,1,0:T(8,128)(2,1)}, u32[]{:S(2)}) copy-start(bf16[24,8,4096]{2,1,0:T(8,128)(2,1)} %x_ref.3) | copy-start | bytes 4718596
  1.4 2.8 %copy-start.5 = (s32[192,4]{0,1:T(4,128)S(1)}, s32[192,4]{0,1:T(4,128)}, u32[]{:S(2)}) copy-start(s32[192,4]{0,1:T(4,128)} %param.9) | copy-start | bytes 9220
  1.4 4.0 %copy-start.4 = (bf16[24,4,4096]{2,1,0:T(4,128)(2,1)S(1)}, bf16[24,4,4096]{2,1,0:T(4,128)(2,1)}, u32[]{:S(2)}) copy-start(bf16[24,4,4096]{2,1,0:T(4,128)(2,1)} %x_ref.2) | copy-start | bytes 2359300
  1.4 9.7 %copy-start.6 = (s32[24,32]{1,0:T(8,128)S(1)}, s32[24,32]{1,0:T(8,128)}, u32[]{:S(2)}) copy-start(s32[24,32]{1,0:T(8,128)} %param.6) | copy-start | bytes 9220
  1.4 9.7 %copy-start.7 = (s32[24]{0:T(128)S(1)}, s32[24]{0:T(128)}, u32[]{:S(2)}) copy-start(s32[24]{0:T(128)} %param.7) | copy-start | bytes 292
  1.4 9.8 %copy-start.1 = (bf16[24,8,4096]{2,1,0:T(8,128)(2,1)S(1)}, bf16[24,8,4096]{2,1,0:T(8,128)(2,1)}, u32[]{:S(2)}) copy-start(bf16[24,8,4096]{2,1,0:T(8,128)(2,1)} %x_ref.3) | copy-start | bytes 4718596
  2.2 3.2 %collective-permute-start = (bf16[16,64,512]{2,1,0:T(8,128)(2,1)S(1)}, bf16[16,64,512]{2,1,0:T(8,128)(2,1)}, u32[]{:S(2)}, u32[]{:S(2)}) collective-permute-start(bf16[16,64,512]{2,1,0:T(8,128)(2,1)S(1)} %relayout.2.refs_0_), channel_id=1, source_target_pairs={{0,1},{1,0},{2,3},{3,2},{4,5},{5,4},{6,7},{7,6},{8,9},{9,8},{10,11... | collective-permute-start | bytes 3145736 | tf_op jit(solution)/shard_map/ppermute | solution.py:359
  3.0 27.1 %collective-permute-start.4 = (bf16[16,64,512]{2,1,0:T(8,128)(2,1)S(1)}, bf16[16,64,512]{2,1,0:T(8,128)(2,1)}, u32[]{:S(2)}, u32[]{:S(2)}) collective-permute-start(bf16[16,64,512]{2,1,0:T(8,128)(2,1)S(1)} %relayout.2.refs_0_), channel_id=1, source_target_pairs={{0,2},{1,3},{2,0},{3,1},{4,6},{5,7},{6,4},{7,5},{8,10},{9,11},{10,... | collective-permute-start | bytes 3145736 | tf_op jit(solution)/shard_map/ppermute | solution.py:356
  8.1 3.5 %copy-start.2 = (bf16[24,64,256]{2,1,0:T(8,128)(2,1)}, bf16[24,64,256]{2,1,0:T(8,128)(2,1)S(1)}, u32[]{:S(2)}) copy-start(bf16[24,64,256]{2,1,0:T(8,128)(2,1)S(1)} %get-tuple-element.29.pl_ref) | copy-start | bytes 2359300
  8.1 21.5 %collective-permute-start.1 = (bf16[24,64,256]{2,1,0:T(8,128)(2,1)}, bf16[24,64,256]{2,1,0:T(8,128)(2,1)}, u32[]{:S(2)}, u32[]{:S(2)}) collective-permute-start(bf16[24,64,256]{2,1,0:T(8,128)(2,1)} %get-tuple-element.30.refs_0_), channel_id=1, source_target_pairs={{0,4},{2,6},{4,8},{5,1},{6,10},{7,3},{8,12},{9,5},{10,14},{11,7},{... | collective-permute-start | bytes 2359304 | tf_op jit(solution)/shard_map/ppermute | solution.py:353
  11.6 2.4 %collective-permute-start.2 = (bf16[8,64,512]{2,1,0:T(8,128)(2,1)S(1)}, bf16[8,64,512]{2,1,0:T(8,128)(2,1)S(1)}, u32[]{:S(2)}, u32[]{:S(2)}) collective-permute-start(bf16[8,64,512]{2,1,0:T(8,128)(2,1)S(1)} %relayout.3.refs_0_), channel_id=1, source_target_pairs={{0,1},{1,0},{2,3},{3,2},{4,5},{5,4},{6,7},{7,6},{8,9},{9,8},{10,11... | collective-permute-start | bytes 1572872 | tf_op jit(solution)/shard_map/ppermute | solution.py:359
  12.4 3.9 %copy-start.3 = (bf16[24,64,256]{2,1,0:T(8,128)(2,1)S(1)}, bf16[24,64,256]{2,1,0:T(8,128)(2,1)}, u32[]{:S(2)}) copy-start(bf16[24,64,256]{2,1,0:T(8,128)(2,1)} %copy-done.2) | copy-start | bytes 2359300
  29.5 2.7 %collective-permute-start.3 = (bf16[24,64,256]{2,1,0:T(8,128)(2,1)}, bf16[24,64,256]{2,1,0:T(8,128)(2,1)S(1)}, u32[]{:S(2)}, u32[]{:S(2)}) collective-permute-start(bf16[24,64,256]{2,1,0:T(8,128)(2,1)} %collective-permute-done.1.refs_1_), channel_id=1, source_target_pairs={{0,1},{1,0},{2,3},{3,2},{4,5},{5,4},{6,7},{7,6},{8,9},{9,8},{10,11... | collective-permute-start | bytes 2359304 | tf_op jit(solution)/shard_map/ppermute | solution.py:359
  30.1 14.5 %collective-permute-start.5 = (bf16[16,64,512]{2,1,0:T(8,128)(2,1)}, bf16[16,64,512]{2,1,0:T(8,128)(2,1)S(1)}, u32[]{:S(2)}, u32[]{:S(2)}) collective-permute-start(bf16[16,64,512]{2,1,0:T(8,128)(2,1)} %collective-permute-done.4.refs_0_), channel_id=1, source_target_pairs={{0,1},{1,0},{2,3},{3,2},{4,5},{5,4},{6,7},{7,6},{8,9},{9,8},{10,11... | collective-permute-start | bytes 3145736 | tf_op jit(solution)/shard_map/ppermute | solution.py:359
  30.1 14.1 %collective-permute-start.6 = (bf16[8,64,512]{2,1,0:T(8,128)(2,1)S(1)}, bf16[8,64,512]{2,1,0:T(8,128)(2,1)S(1)}, u32[]{:S(2)}, u32[]{:S(2)}) collective-permute-start(bf16[8,64,512]{2,1,0:T(8,128)(2,1)S(1)} %relayout.3.refs_0_), channel_id=1, source_target_pairs={{0,2},{1,3},{2,0},{3,1},{4,6},{5,7},{6,4},{7,5},{8,10},{9,11},{10,... | collective-permute-start | bytes 1572872 | tf_op jit(solution)/shard_map/ppermute | solution.py:356
  44.1 10.8 %collective-permute-start.7 = (bf16[8,64,512]{2,1,0:T(8,128)(2,1)S(1)}, bf16[8,64,512]{2,1,0:T(8,128)(2,1)S(1)}, u32[]{:S(2)}, u32[]{:S(2)}) collective-permute-start(bf16[8,64,512]{2,1,0:T(8,128)(2,1)S(1)} %collective-permute-done.6.refs_0_), channel_id=1, source_target_pairs={{0,1},{1,0},{2,3},{3,2},{4,5},{5,4},{6,7},{7,6},{8,9},{9,8},{10,11... | collective-permute-start | bytes 1572872 | tf_op jit(solution)/shard_map/ppermute | solution.py:359
  51.0 12.1 %collective-permute-start.9 = (bf16[10,4,4096]{2,1,0:T(4,128)(2,1)S(1)}, bf16[10,4,4096]{2,1,0:T(4,128)(2,1)S(1)}, u32[]{:S(2)}, u32[]{:S(2)}) collective-permute-start(bf16[10,4,4096]{2,1,0:T(4,128)(2,1)S(1)} %coarse.7), channel_id=1, source_target_pairs={{4,0},{8,4},{12,8},{16,12},{20,16},{24,20},{28,24},{5,1},{9,5},{13... | collective-permute-start | bytes 983048 | tf_op jit(solution)/shard_map/ppermute | solution.py:365
  59.5 17.0 %collective-permute-start.15 = (bf16[10,4,2048]{2,1,0:T(4,128)(2,1)S(1)}, bf16[10,4,2048]{2,1,0:T(4,128)(2,1)S(1)}, u32[]{:S(2)}, u32[]{:S(2)}) collective-permute-start(bf16[10,4,2048]{2,1,0:T(4,128)(2,1)S(1)} %get-tuple-element.44), channel_id=1, source_target_pairs={{4,0},{8,4},{12,8},{16,12},{20,16},{24,20},{28,24},{5,1},{9,5},{13... | collective-permute-start | bytes 491528 | tf_op jit(solution)/shard_map/ppermute | solution.py:365
  63.2 24.6 %collective-permute-start.14 = (bf16[10,8,2048]{2,1,0:T(8,128)(2,1)S(1)}, bf16[10,8,2048]{2,1,0:T(8,128)(2,1)S(1)}, u32[]{:S(2)}, u32[]{:S(2)}) collective-permute-start(bf16[10,8,2048]{2,1,0:T(8,128)(2,1)S(1)} %get-tuple-element.43), channel_id=1, source_target_pairs={{0,4},{4,8},{8,12},{12,16},{16,20},{20,24},{24,28},{1,5},{5,9},{9,... | collective-permute-start | bytes 983048 | tf_op jit(solution)/shard_map/ppermute | solution.py:362
  68.8 17.3 %collective-permute-start.10 = (bf16[10,4,2048]{2,1,0:T(4,128)(2,1)S(1)}, bf16[10,4,2048]{2,1,0:T(4,128)(2,1)S(1)}, u32[]{:S(2)}, u32[]{:S(2)}) collective-permute-start(bf16[10,4,2048]{2,1,0:T(4,128)(2,1)S(1)} %get-tuple-element.42), channel_id=1, source_target_pairs={{4,0},{8,4},{12,8},{16,12},{20,16},{24,20},{28,24},{5,1},{9,5},{13... | collective-permute-start | bytes 491528 | tf_op jit(solution)/shard_map/ppermute | solution.py:365
  71.0 15.3 %collective-permute-start.8 = (bf16[10,8,2048]{2,1,0:T(8,128)(2,1)S(1)}, bf16[10,8,2048]{2,1,0:T(8,128)(2,1)S(1)}, u32[]{:S(2)}, u32[]{:S(2)}) collective-permute-start(bf16[10,8,2048]{2,1,0:T(8,128)(2,1)S(1)} %get-tuple-element.41), channel_id=1, source_target_pairs={{0,4},{4,8},{8,12},{12,16},{16,20},{20,24},{24,28},{1,5},{5,9},{9,... | collective-permute-start | bytes 983048 | tf_op jit(solution)/shard_map/ppermute | solution.py:362
  86.4 11.7 %collective-permute-start.12 = (bf16[14,8,2048]{2,1,0:T(8,128)(2,1)S(1)}, bf16[14,8,2048]{2,1,0:T(8,128)(2,1)S(1)}, u32[]{:S(2)}, u32[]{:S(2)}) collective-permute-start(bf16[14,8,2048]{2,1,0:T(8,128)(2,1)S(1)} %bitcast.11), channel_id=1, source_target_pairs={{0,2},{1,3},{2,0},{3,1},{4,6},{5,7},{6,4},{7,5},{8,10},{9,11},{10,... | collective-permute-start | bytes 1376264 | tf_op jit(solution)/shard_map/ppermute | solution.py:356
  87.8 20.1 %collective-permute-start.17 = (bf16[14,8,2048]{2,1,0:T(8,128)(2,1)S(1)}, bf16[14,8,2048]{2,1,0:T(8,128)(2,1)S(1)}, u32[]{:S(2)}, u32[]{:S(2)}) collective-permute-start(bf16[14,8,2048]{2,1,0:T(8,128)(2,1)S(1)} %bitcast.14), channel_id=1, source_target_pairs={{0,2},{1,3},{2,0},{3,1},{4,6},{5,7},{6,4},{7,5},{8,10},{9,11},{10,... | collective-permute-start | bytes 1376264 | tf_op jit(solution)/shard_map/ppermute | solution.py:356
  88.1 21.1 %collective-permute-start.11 = (bf16[14,8,2048]{2,1,0:T(8,128)(2,1)S(1)}, bf16[14,8,2048]{2,1,0:T(8,128)(2,1)S(1)}, u32[]{:S(2)}, u32[]{:S(2)}) collective-permute-start(bf16[14,8,2048]{2,1,0:T(8,128)(2,1)S(1)} %bitcast.12), channel_id=1, source_target_pairs={{0,1},{1,0},{2,3},{3,2},{4,5},{5,4},{6,7},{7,6},{8,9},{9,8},{10,11... | collective-permute-start | bytes 1376264 | tf_op jit(solution)/shard_map/ppermute | solution.py:359
  98.1 11.2 %collective-permute-start.13 = (bf16[14,8,2048]{2,1,0:T(8,128)(2,1)S(1)}, bf16[14,8,2048]{2,1,0:T(8,128)(2,1)S(1)}, u32[]{:S(2)}, u32[]{:S(2)}) collective-permute-start(bf16[14,8,2048]{2,1,0:T(8,128)(2,1)S(1)} %collective-permute-done.12.refs_2_), channel_id=1, source_target_pairs={{0,1},{1,0},{2,3},{3,2},{4,5},{5,4},{6,7},{7,6},{8,9},{9,8},{10,11... | collective-permute-start | bytes 1376264 | tf_op jit(solution)/shard_map/ppermute | solution.py:359
  100.3 11.8 %collective-permute-start.16 = (bf16[14,8,2048]{2,1,0:T(8,128)(2,1)S(1)}, bf16[14,8,2048]{2,1,0:T(8,128)(2,1)S(1)}, u32[]{:S(2)}, u32[]{:S(2)}) collective-permute-start(bf16[14,8,2048]{2,1,0:T(8,128)(2,1)S(1)} %bitcast.15), channel_id=1, source_target_pairs={{0,1},{1,0},{2,3},{3,2},{4,5},{5,4},{6,7},{7,6},{8,9},{9,8},{10,11... | collective-permute-start | bytes 1376264 | tf_op jit(solution)/shard_map/ppermute | solution.py:359
  107.9 4.2 %collective-permute-start.18 = (bf16[14,8,2048]{2,1,0:T(8,128)(2,1)S(1)}, bf16[14,8,2048]{2,1,0:T(8,128)(2,1)S(1)}, u32[]{:S(2)}, u32[]{:S(2)}) collective-permute-start(bf16[14,8,2048]{2,1,0:T(8,128)(2,1)S(1)} %collective-permute-done.17.refs_3_), channel_id=1, source_target_pairs={{0,1},{1,0},{2,3},{3,2},{4,5},{5,4},{6,7},{7,6},{8,9},{9,8},{10,11... | collective-permute-start | bytes 1376264 | tf_op jit(solution)/shard_map/ppermute | solution.py:359

commit v4 on v3

--- a/solution.py
+++ b/solution.py
@@ -58,38 +58,39 @@
         in_specs=[pl.BlockSpec((step, nb, BS * BS), lambda i: (i + first // step, 0, 0))],
         out_specs=pl.BlockSpec((step, BS, nb * BS), lambda i: (i, 0, 0)),
         scratch_shapes=[pltpu.VMEM((step, 256, LANES), F32)],
-        compiler_params=params(16),
+        compiler_params=params(4),
         cost_estimate=cost(0.6),
         name="relayout",
     )(x)
 
 
-def relayout_both_kernel(x_ref, o_ref, nat_ref, scr, mix):
-    relayout_kernel(x_ref, o_ref, scr)
+def relayout_rows_kernel(x_ref, o_ref, scr, mix):
     rows, nb, _ = x_ref.shape
+    low = low_lanes(32)
     for r in range(rows):
+        for q in range(32):
+            scr[r, pl.ds(q * 8, nb), :] = x_ref[r, :, q * LANES : (q + 1) * LANES].astype(F32)
         for k in range(0, nb, 2):
-            at = slice(k * BS, (k + 2) * BS)
-            mix[r, k // 2, pl.ds(0, 32, stride=2), :] = o_ref[r, 0:32, at].astype(F32)
-            mix[r, k // 2, pl.ds(1, 32, stride=2), :] = o_ref[r, 32:64, at].astype(F32)
-            nat_ref[r, :, at] = mix[r, k // 2].astype(BF)
-
-
-def relayout_both(x):
+            x0 = scr[r, pl.ds(k, 32, stride=8), :]
+            x1 = scr[r, pl.ds(k + 1, 32, stride=8), :]
+            mix[r, k // 2, pl.ds(0, 32, stride=2), :] = jnp.where(low, x0, pltpu.roll(x1, BS, 1))
+            mix[r, k // 2, pl.ds(1, 32, stride=2), :] = jnp.where(low, pltpu.roll(x0, BS, 1), x1)
+            o_ref[r, :, k * BS : (k + 2) * BS] = mix[r, k // 2].astype(BF)
+
+
+def relayout_rows(x):
     rows, nb, _ = x.shape
     step = 4
-    shape = jax.ShapeDtypeStruct((rows, BS, nb * BS), BF)
-    spec = pl.BlockSpec((step, BS, nb * BS), lambda i: (i, 0, 0))
-    return pl.pallas_call(
-        relayout_both_kernel,
+    return pl.pallas_call(
+        relayout_rows_kernel,
         grid=(rows // step,),
-        out_shape=(shape, shape),
+        out_shape=jax.ShapeDtypeStruct((rows, BS, nb * BS), BF),
         in_specs=[pl.BlockSpec((step, nb, BS * BS), lambda i: (i, 0, 0))],
-        out_specs=(spec, spec),
+        out_specs=pl.BlockSpec((step, BS, nb * BS), lambda i: (i, 0, 0)),
         scratch_shapes=[pltpu.VMEM((step, 256, LANES), F32), pltpu.VMEM((step, nb // 2, BS, LANES), F32)],
-        compiler_params=params(16),
-        cost_estimate=cost(1.5),
-        name="relayout_both",
+        compiler_params=params(4),
+        cost_estimate=cost(1.0),
+        name="relayout_rows",
     )(x)
 
 
@@ -134,54 +135,60 @@
     return jnp.where((w >= 0) & (e >= 0) & (e < share), e * GROUPS + (w >> 3), -1)
 
 
+def touched(side, tiles):
+    return (side, side + 3) if tiles == GROUPS else (0, tiles)
+
+
 def right_kernel(rb, tiles, table_ref, *refs):
     o_ref = refs[-1]
     core = lax.rem(lax.axis_index("col"), 2)
     low = lax.broadcasted_iota(jnp.int32, (1, LANES), 1) < BS
     wants = [jnp.where(low, p, tiles + p) for p in range(tiles)]
 
-    def fill(src, count, near_first, out_first):
-        def one(jj, carry):
-            dups = []
-            for t in range(4):
-                x = src[jj, :, t * BS : (t + 1) * BS]
-                dups.append(jnp.concatenate([x, x], axis=1))
-            at = [table_ref[t, near_first + jj] for t in range(4)]
-            for p in range(tiles):
-                total = None
+    def fill(src, side, out_first):
+        def four(jq, carry):
+            for d in range(4):
+                jj = 4 * jq + d
+                dups = []
                 for t in range(4):
-                    keep = dups[t] * jnp.where(wants[p] == at[t], 1.0, 0.0).astype(BF)
-                    total = keep if total is None else total + keep
-                o_ref[out_first + jj, p] = total
+                    x = src[jj, :, t * BS : (t + 1) * BS]
+                    dups.append(jnp.concatenate([x, x], axis=1))
+                at = [table_ref[t, side * rb + jj] for t in range(4)]
+                for p in range(*touched(side, tiles)):
+                    total = None
+                    for t in range(4):
+                        keep = dups[t] * jnp.where(wants[p] == at[t], 1.0, 0.0).astype(BF)
+                        total = keep if total is None else total + keep
+                    o_ref[out_first + jq, p, d * BS : (d + 1) * BS] = total
             return carry
 
-        lax.fori_loop(0, count, one, 0, unroll=4)
+        lax.fori_loop(0, rb // 4, four, 0)
 
     if len(refs) == 2:
-        fill(refs[0], rb, rb, 0)
-        o_ref[rb] = jnp.zeros((tiles, BS, LANES), BF)
+        fill(refs[0], 1, 0)
     else:
-        done = refs[0].shape[0]
-
-        def copy(jj, carry):
-            o_ref[jj] = refs[0][jj]
-            return carry
-
-        lax.fori_loop(0, done, copy, 0)
-        for z in range(2):
-            there = core if z == 0 else 1 - core
-            fill(refs[1 + z], rb, 2 * rb * there, done + rb * z)
+        first = refs[0]
+        second = refs[1]
+
+        @pl.when(core == 0)
+        def _():
+            fill(first, 0, 0)
+            fill(second, 2, rb // 4)
+
+        @pl.when(core == 1)
+        def _():
+            fill(second, 0, 0)
+            fill(first, 2, rb // 4)
 
 
 def right_factor(table, srcs, tiles, us):
     rb = table.shape[1] // 3
-    spots = rb + 1 if len(srcs) == 1 else 3 * rb + 1
     return pl.pallas_call(
         functools.partial(right_kernel, rb, tiles),
-        out_shape=jax.ShapeDtypeStruct((spots, tiles, BS, LANES), BF),
+        out_shape=jax.ShapeDtypeStruct((len(srcs) * rb // 4, tiles, 4 * BS, LANES), BF),
         in_specs=[SM] + [VM] * len(srcs),
         out_specs=VM,
-        compiler_params=params(24),
+        compiler_params=params(16),
         cost_estimate=cost(us),
         name="right_factor",
     )(table, *srcs)
@@ -189,56 +196,88 @@
 
 def slot_places(a_cols, counts):
     rb, ka = a_cols.shape
-    core = lax.axis_index("col") % 2
-    near = a_cols - (lax.axis_index("row") - 1) * rb
-    before = near + jnp.where(core == 0, rb + 1, 2 * rb + 1)
-    after = near - 2 * rb + jnp.where(core == 0, 2 * rb + 1, rb + 1)
-    spot = jnp.where(near < rb, before, jnp.where(near >= 2 * rb, after, near - rb))
+    row = jnp.arange(rb, dtype=jnp.int32)[:, None]
+    near = a_cols - (lax.axis_index("row") - 1) * rb - row // 4 * 4
     live = jnp.arange(ka, dtype=jnp.int32)[None, :] < counts[:, None]
-    return jnp.where(live, spot, rb)
-
-
-def product_kernel(first, shifts, has_acc, ks, place_ref, right_ref, *refs):
+    return jnp.where(live, near, -1)
+
+
+def product_kernel(first, rb, shifts, place_ref, own_ref, near_ref, *refs):
     col = lax.axis_index("col")
     ny = lax.axis_size("col") // 2
-    srcs = refs[: len(shifts)]
-    acc_ref = refs[len(shifts)] if has_acc else None
-    o_ref = refs[-1]
+    srcs, o_ref, band, acc = refs[: len(shifts)], refs[-3], refs[-2], refs[-1]
     rows = o_ref.shape[0]
-    tiles = right_ref.shape[1]
+    ks = srcs[0].shape[2] // BS
+    tiles = own_ref.shape[1]
     y, core = col // 2, lax.rem(col, 2)
-    firsts = []
+    wide = band.shape[1]
+    half_of = lax.broadcasted_iota(jnp.int32, (1, LANES), 1) // BS
+    slots = []
     for s, flip in shifts:
         c = core if flip == 0 else 1 - core
-        firsts.append((lax.rem(y - s + ny, ny) * 2 + c) * ks)
-
-    def one(i, carry):
-        spots = [[place_ref[first + i, f + k] for k in range(ks)] for f in firsts]
-        for p0 in range(0, tiles, 2):
-            ps = range(p0, min(p0 + 2, tiles))
-            at = slice(p0 * LANES, (ps[-1] + 1) * LANES)
-            acc = acc_ref[i, :, at] if has_acc else jnp.zeros((BS, len(ps) * LANES), F32)
-            for src, spot in zip(srcs, spots):
-                for k in range(0, ks, 4):
-                    rhs = [jnp.concatenate([right_ref[spot[k + d], p] for d in range(4)], axis=0) for p in ps]
-                    acc = acc + dot(src[i, :, k * BS : (k + 4) * BS], jnp.concatenate(rhs, axis=1))
-            o_ref[i, :, at] = acc.astype(o_ref.dtype)
+        slots.append((lax.rem(y - s + ny, ny) * 2 + c) * ks)
+
+    def lay(g, carry):
+        for t in range(wide):
+            band[g, t] = jnp.zeros((4 * BS, LANES), BF)
+        for src, slot in zip(srcs, slots):
+            for k in range(0, ks, 2):
+                pairs = [src[4 * g + d, :, k * BS : (k + 2) * BS] for d in range(4)]
+                turned = [jnp.concatenate([x[:, BS:], x[:, :BS]], axis=1) for x in pairs]
+                for e in range(2):
+                    at = [place_ref[first + 4 * g + d, slot + k + e] for d in range(4)]
+                    tile = [jnp.maximum(a, 0) >> 1 for a in at]
+                    old = [band[g, tile[d], d * BS : (d + 1) * BS] for d in range(4)]
+                    for d in range(4):
+                        half = jnp.where(at[d] < 0, 2, at[d] & 1)
+                        keep = jnp.where(half_of == half, 1.0, 0.0)
+                        stay = (keep * jnp.where(half_of == e, 1.0, 0.0)).astype(BF)
+                        move = (keep * jnp.where(half_of == e, 0.0, 1.0)).astype(BF)
+                        old[d] = old[d] + (pairs[d] * stay + turned[d] * move)
+                    for d in range(4):
+                        band[g, tile[d], d * BS : (d + 1) * BS] = old[d]
         return carry
 
-    lax.fori_loop(0, rows, one, 0, unroll=4)
-
-
-def product(place, right, srcs, shifts, first, acc, dtype):
-    rows, _, wide = srcs[0].shape
-    return pl.pallas_call(
-        functools.partial(product_kernel, first, shifts, acc is not None, wide // BS),
-        out_shape=jax.ShapeDtypeStruct((rows, BS, right.shape[1] * LANES), dtype),
-        in_specs=[SM, VM] + [VM] * (len(srcs) + (acc is not None)),
+    lax.fori_loop(0, rows // 4, lay, 0)
+
+    quads = rb // 4
+    for g in range(rows // 4):
+        start = first // 4 + g
+        acc[...] = jnp.zeros_like(acc)
+        for side in range(3):
+            k0, k1 = max(start, side * quads), min(start + wide // 2, (side + 1) * quads)
+            if k0 >= k1:
+                continue
+            p0, p1 = touched(side, tiles)
+            ref, base = (own_ref, quads) if side == 1 else (near_ref, 0 if side == 0 else quads)
+            total = None
+            for k in range(k0, k1):
+                lhs = jnp.concatenate([band[g, 2 * (k - start)], band[g, 2 * (k - start) + 1]], axis=1)
+                rhs = jnp.concatenate([ref[k - base, p] for p in range(p0, p1)], axis=1)
+                part = dot(lhs, rhs)
+                total = part if total is None else total + part
+            acc[:, p0 * LANES : p1 * LANES] += total
+        for d in range(4):
+            o_ref[4 * g + d] = acc[d * BS : (d + 1) * BS].astype(BF)
+
+
+def product(place, own, near, srcs, shifts, first, us):
+    rows = srcs[0].shape[0]
+    rb = place.shape[0]
+    tiles = own.shape[1]
+    return pl.pallas_call(
+        functools.partial(product_kernel, first, rb, shifts),
+        out_shape=jax.ShapeDtypeStruct((rows, BS, tiles * LANES), BF),
+        in_specs=[SM] + [VM] * (2 + len(srcs)),
         out_specs=VM,
-        compiler_params=params(24),
-        cost_estimate=cost(4.0),
+        scratch_shapes=[
+            pltpu.VMEM((rows // 4, rb + 2, 4 * BS, LANES), BF),
+            pltpu.VMEM((4 * BS, tiles * LANES), F32),
+        ],
+        compiler_params=params(32),
+        cost_estimate=cost(us),
         name="product",
-    )(place, right, *srcs, *([] if acc is None else [acc]))
+    )(place, own, near, *srcs)
 
 
 def coarse_kernel(sets, a0, a1, left_ref, *refs):
@@ -367,10 +406,6 @@
     shifts = tuple((s, f) for s in range(ny) for f in range(2))
     pct = p_cols.T
 
-    def gather(x):
-        got = [x] + [over_y(x, s) for s in range(1, ny)]
-        return [z for g in got for z in (g, over_core(g))]
-
     own_a, side_a, far_a = [], [], []
     for h, (first, rows) in enumerate(parts):
         x = relayout(a_blocks, first, rows)
@@ -379,37 +414,42 @@
         side_a.append(over_core(x))
         if h == 0:
             a_blocks, p_blocks, side_a[0] = lax.optimization_barrier((a_blocks, p_blocks, side_a[0]))
-    p_mixed, p_own = relayout_both(p_blocks)
+    p_own = relayout_rows(p_blocks)
     beside = outward(p_own)
-    p_mixed, p_own, side_a[1] = lax.optimization_barrier((p_mixed, p_own, side_a[1]))
+    p_blocks, p_own, side_a[1] = lax.optimization_barrier((p_blocks, p_own, side_a[1]))
     table = column_table(pct, rb, share)
-    left = left_factor(pct, p_mixed)
-    right = right_factor(table, [p_own], tiles, 2.0)
+    left = left_factor(pct, relayout(p_blocks, 0, rb))
+    own = right_factor(table, [p_own], tiles, 2.0)
     order = assembly_order(shifts, ncol, share)
     place = slot_places(a_cols, counts)
-    beside, left, right, order, place = lax.optimization_barrier((beside, left, right, order, place))
-    right = right_factor(table, [right, beside, over_core(beside)], tiles, 4.0)
-    near = [product(place, right, [own_a[h], side_a[h]], shifts[:2], parts[h][0], None, F32) for h in range(2)]
-    far_a[1], near = lax.optimization_barrier((far_a[1], near))
+    beside, left, own, order, place = lax.optimization_barrier((beside, left, own, order, place))
+    near = right_factor(table, [beside, over_core(beside)], tiles, 3.0)
     aps = []
     for h in range(2):
-        srcs = [z for g in far_a[h] for z in (g, over_core(g))]
-        aps.append(product(place, right, srcs, shifts[2:], parts[h][0], near[h], BF))
+        srcs = [own_a[h], side_a[h]] + [z for g in far_a[h] for z in (g, over_core(g))]
+        aps.append(product(place, own, near, srcs, shifts, parts[h][0], 0.3 * parts[h][1]))
         if h == 0:
+            far_a[1], aps[0] = lax.optimization_barrier((far_a[1], aps[0]))
             early = downward(coarse_rows(left, aps, ((0, CB // 2),), 0, BS, BF, 1.0)[0])
 
     def columns(x, g):
         y = x[: GROUPS * share].reshape((share, GROUPS) + x.shape[1:])
         return jnp.pad(y.astype(F32), ((0, 0), (g, 2 - g), (0, 0), (0, 0)))
 
-    rims = [coarse_rows(left, aps, ((CB // 2, CB), (2 * CB, 3 * CB)), a0, a1, BF, 2.0) for a0, a1 in chunks]
+    late = downward(coarse_rows(left, aps, ((CB // 2, CB),), 0, BS, BF, 1.0)[0])
+    highs = [upward(coarse_rows(left, aps, ((2 * CB, 3 * CB),), a0, a1, BF, 1.0)[0]) for a0, a1 in chunks]
     mids = [coarse_rows(left, aps, ((CB, 2 * CB),), a0, a1, F32, 1.0)[0] for a0, a1 in chunks]
+    early, mids = lax.optimization_barrier((early, mids))
+    lower = jnp.concatenate([early, late], axis=1)
     out = None
-    for (a0, a1), (low, high), mid in zip(chunks, rims, mids):
-        lower = jnp.concatenate([early[:, :, a0 * BS : a1 * BS], downward(low)], axis=1)
-        total = columns(upward(high), 0) + columns(mid, 1) + columns(lower, 2)
+    for (a0, a1), high, mid in zip(chunks, highs, mids):
+        total = columns(high, 0) + columns(mid, 1) + columns(lower[:, :, a0 * BS : a1 * BS], 2)
         total = total.astype(BF).reshape((share * (GROUPS + 2),) + total.shape[2:])
-        out = assemble(order, gather(total), a0, BS * BS, out)
+        far = [over_y(total, s) for s in range(1, ny)]
+        if out is not None:
+            far, out = lax.optimization_barrier((far, out))
+        srcs = [z for g in [total] + far for z in (g, over_core(g))]
+        out = assemble(order, srcs, a0, BS * BS, out)
     return out
 
 

time: 115 us -> 110 us (0.957)
  waiting for transfers between devices: 41.2 us -> 36.4 us
  Pallas kernels: 41.4 us -> 39 us
  starting transfers between devices: 29.7 us -> 31.1 us
    ppermute x1, waiting for transfers between devices: 10.4 us -> 0.01 us  [outward(): lax.ppermute(x, ('row', 'col'), [(a, b) for a, b in pairs if 0 <= b < nro...]
    ppermute x4, waiting for transfers between devices: 16.4 us -> 23.7 us  [over_y(): lax.ppermute(x, 'col', [(y * 2 + c, (y + s) % ny * 2 + c) for y in range(...]
    ppermute x9, starting transfers between devices: 7.2 us -> 10.6 us  [over_core(): return lax.ppermute(x, 'col', [(c, c ^ 1) for c in range(ncol)])]
    ppermute x3 -> x2, starting transfers between devices: 8.07 us -> 5.15 us  [downward(): return lax.ppermute(x, 'row', [(i + 1, i) for i in range(nrow - 1)])]
    pallas_call x5 -> x3, Pallas kernels: 19.2 us -> 16.8 us  [the longest x2 15.8 us: product(): pl.pallas_call(functools.partial(product_kernel, first, rb, shifts), out_...]
    ppermute x3 -> x2, waiting for transfers between devices: 11.1 us -> 8.93 us  [downward(): return lax.ppermute(x, 'row', [(i + 1, i) for i in range(nrow - 1)])]
    pallas_call x2, Pallas kernels: 5.95 us -> 4.28 us  [right_factor(): pl.pallas_call(functools.partial(right_kernel, rb, tiles), out_shape=jax....]
    pallas_call x2 -> x3, Pallas kernels: 1.21 us -> 2.76 us  [relayout(): pl.pallas_call(relayout_kernel, grid=(rows // step,), out_shape=jax.Shape...]
  transfers between devices with their start and end apart: 19 -> 18, of which waited for: 8 -> 7; matrix products, arithmetic and copies ran while one was open for 1% -> 1% of each run, Pallas kernels for 33% -> 32%
where the time goes in v4:
time: 110 us; the launch traced here: 109 us
  Pallas kernels  39 us (35%)
  waiting for transfers between devices  36.4 us (33%)
  starting transfers between devices  31.1 us (28%)
  local copies, waits for them, and re-layouts  1.43 us (1%)
    ppermute x4, waiting for transfers between devices, over_y(): lax.ppermute(x, 'col', [(y * 2 + c, (y + s) % ny * 2 + c) for y in range(...  23.7 us
    pallas_call x2, Pallas kernels, product(): pl.pallas_call(functools.partial(product_kernel, first, rb, shifts), out_...  15.8 us
    ppermute x9, starting transfers between devices, over_core(): return lax.ppermute(x, 'col', [(c, c ^ 1) for c in range(ncol)])  10.6 us
    ppermute x2, waiting for transfers between devices, downward(): return lax.ppermute(x, 'row', [(i + 1, i) for i in range(nrow - 1)])  8.93 us
    ppermute x2, starting transfers between devices, upward(): return lax.ppermute(x, 'row', [(i, i + 1) for i in range(nrow - 1)])  7.18 us
    pallas_call x6, Pallas kernels, coarse_rows(): pl.pallas_call(functools.partial(coarse_kernel, sets, a0, a1), out_shape=...  6.47 us
    pallas_call x2, Pallas kernels, assemble(): pl.pallas_call(assemble_kernel, grid=(per,), out_shape=jax.ShapeDtypeStru...  5.75 us
    ppermute x4, starting transfers between devices, over_y(): lax.ppermute(x, 'col', [(y * 2 + c, (y + s) % ny * 2 + c) for y in range(...  5.17 us
  transfers between devices with their start and end apart: 18, of which 7 were waited for; matrix products, arithmetic and copies ran while one was open for 1% of the time, Pallas kernels for 32%

profile of v4, /device:TPU:9, one launch (start us, length us, event | category | flops | bytes accessed | tf_op | source)
XLA Modules:
  0.0 109.1 jit_solution(8212458594665794290)
XLA Ops:
  0.0 1.4 %copy-done = bf16[24,8,4096]{2,1,0:T(8,128)(2,1)S(1)} copy-done((bf16[24,8,4096]{2,1,0:T(8,128)(2,1)S(1)}, bf16[24,8,4096]{2,1,0:T(8,128)(2,1)}, u32[]{:S(2)}) %copy-start) | copy-done | bytes 1572888
  1.4 0.0 copy-start.5
  1.4 0.8 relayout.3.refs_0_
  2.2 0.7 collective-permute-start
  3.0 1.3 %collective-permute-start.5 = (bf16[16,64,512]{2,1,0:T(8,128)(2,1)S(1)}, bf16[16,64,512]{2,1,0:T(8,128)(2,1)}, u32[]{:S(2)}, u32[]{:S(2)}) collective-permute-start(bf16[16,64,512]{2,1,0:T(8,128)(2,1)S(1)} %relayout.3.refs_0_), channel_id=1, source_target_pairs={{0,2},{1,3},{2,0},{3,1},{4,6},{5,7},{6,4},{7,5},{8,10},{9,11},{10,... | collective-permute-start | bytes 3145736 | tf_op jit(solution)/shard_map/ppermute | solution.py:395
  4.3 1.1 %collective-permute-done.refs_1_ = bf16[16,64,512]{2,1,0:T(8,128)(2,1)} collective-permute-done((bf16[16,64,512]{2,1,0:T(8,128)(2,1)S(1)}, bf16[16,64,512]{2,1,0:T(8,128)(2,1)}, u32[]{:S(2)}, u32[]{:S(2)}) %collective-permute-start) | collective-permute-done | bytes 1048608 | tf_op jit(solution)/shard_map/ppermute | solution.py:398
  5.4 1.1 %relayout.4.refs_0_ = bf16[8,64,512]{2,1,0:T(8,128)(2,1)} custom-call(bf16[24,8,4096]{2,1,0:T(8,128)(2,1)S(1)} %copy-done.1), custom_call_target="tpu_custom_call" | custom-call | flops 60000000 | bytes 2220000 | tf_op jit(solution)/shard_map/relayout/pallas_call | solution.py:54
  6.5 0.4 collective-permute-start.2
  6.9 0.0 copy-done.2
  6.9 1.0 relayout_rows.1.refs_0_
  7.9 3.0 %collective-permute-start.1 = (bf16[24,64,256]{2,1,0:T(8,128)(2,1)S(1)}, bf16[24,64,256]{2,1,0:T(8,128)(2,1)}, u32[]{:S(2)}, u32[]{:S(2)}) collective-permute-start(bf16[24,64,256]{2,1,0:T(8,128)(2,1)S(1)} %relayout_rows.1.refs_0_), channel_id=1, source_target_pairs={{0,4},{2,6},{4,8},{5,1},{6,10},{7,3},{8,12},{9,5},{10,14},{11,7},{... | collective-permute-start | bytes 2359304 | tf_op jit(solution)/shard_map/ppermute | solution.py:392
  10.9 0.2 fusion.12.order_ref
  11.2 0.0 copy-done.3
  11.2 0.1 add_select_fusion.4.table_ref
  11.3 16.5 %collective-permute-done.5.refs_2_ = bf16[16,64,512]{2,1,0:T(8,128)(2,1)} collective-permute-done((bf16[16,64,512]{2,1,0:T(8,128)(2,1)S(1)}, bf16[16,64,512]{2,1,0:T(8,128)(2,1)}, u32[]{:S(2)}, u32[]{:S(2)}) %collective-permute-start.5) | collective-permute-done | bytes 1048608 | tf_op jit(solution)/shard_map/ppermute | solution.py:395
  27.8 0.8 collective-permute-start.6
  28.7 0.0 copy-done.4
  28.7 0.1 subtract_select_fusion.place_ref
  28.8 0.0 collective-permute-done.2.refs_1_
  28.8 0.9 relayout.5.pl_ref
  29.6 1.4 %right_factor.2.own_ref = bf16[6,5,256,128]{3,2,1,0:T(8,128)(2,1)S(1)} custom-call(s32[4,72]{1,0:T(4,128)S(1)} %add_select_fusion.4.table_ref, bf16[24,64,256]{2,1,0:T(8,128)(2,1)S(1)} %relayout_rows.1.refs_0_), custom_call_target="tpu_custom_call" | custom-call | flops 200000000 | bytes 7400000 | tf_op jit(solution)/shard_map/right_factor/pallas_call | solution.py:186
  31.1 2.9 %left_factor.1.left_ref = bf16[12,24,64,128]{3,2,1,0:T(8,128)(2,1)S(1)} custom-call(s32[4,192]{1,0:T(4,128)S(1)} %bitcast.18, bf16[24,64,256]{2,1,0:T(8,128)(2,1)S(1)} %relayout.5.pl_ref), custom_call_target="tpu_custom_call" | custom-call | flops 290000000 | bytes 10730000 | tf_op jit(solution)/shard_map/left_factor/pallas_call | solution.py:118
  34.0 0.0 collective-permute-done.1.refs_0_
  34.0 0.1 collective-permute-start.4
  34.0 1.3 %collective-permute-start.3 = (bf16[8,64,512]{2,1,0:T(8,128)(2,1)}, bf16[8,64,512]{2,1,0:T(8,128)(2,1)S(1)}, u32[]{:S(2)}, u32[]{:S(2)}) collective-permute-start(bf16[8,64,512]{2,1,0:T(8,128)(2,1)} %relayout.4.refs_0_), channel_id=1, source_target_pairs={{0,2},{1,3},{2,0},{3,1},{4,6},{5,7},{6,4},{7,5},{8,10},{9,11},{10,... | collective-permute-start | bytes 1572872 | tf_op jit(solution)/shard_map/ppermute | solution.py:395
  35.3 1.2 %collective-permute-done.4.refs_1_ = bf16[24,64,256]{2,1,0:T(8,128)(2,1)S(1)} collective-permute-done((bf16[24,64,256]{2,1,0:T(8,128)(2,1)}, bf16[24,64,256]{2,1,0:T(8,128)(2,1)S(1)}, u32[]{:S(2)}, u32[]{:S(2)}) %collective-permute-start.4) | collective-permute-done | bytes 786464 | tf_op jit(solution)/shard_map/ppermute | solution.py:398
  36.5 2.9 %right_factor.3.near_ref = bf16[12,5,256,128]{3,2,1,0:T(8,128)(2,1)S(1)} custom-call(s32[4,72]{1,0:T(4,128)S(1)} %add_select_fusion.4.table_ref, bf16[24,64,256]{2,1,0:T(8,128)(2,1)} %collective-permute-done.1.refs_0_, bf16[24,64,256]{2,1,0:T(8,128)(2,1)S(1)} %collective-permute-done.4.refs_1_), custom_call_target="tpu_custom_call" | custom-call | flops 300000000 | bytes 11100000 | tf_op jit(solution)/shard_map/right_factor/pallas_call | solution.py:186
  39.4 0.0 collective-permute-done.6.refs_3_
  39.4 10.1 %product.2.refs_0_ = bf16[16,64,640]{2,1,0:T(8,128)(2,1)S(1)} custom-call(s32[24,32]{1,0:T(8,128)S(1)} %subtract_select_fusion.place_ref, bf16[6,5,256,128]{3,2,1,0:T(8,128)(2,1)S(1)} %right_factor.2.own_ref, bf16[12,5,256,128]{3,2,1,0:T(8,128)(2,1)S(1)} %right_factor.3.near_ref, bf16[16,64,512]{2,1,0:T(8,128)(2,1)S(1)} %relayout.3.refs_0_, ...), custom_call_target="tpu_custom_call" | custom-call | flops 480000000 | bytes 17760000 | tf_op jit(solution)/shard_map/product/pallas_call | solution.py:268
  49.6 0.0 collective-permute-done.3.refs_2_
  49.6 0.2 collective-permute-start.7
  49.8 0.9 coarse.7
  50.7 3.2 %collective-permute-start.9 = (bf16[10,4,4096]{2,1,0:T(4,128)(2,1)S(1)}, bf16[10,4,4096]{2,1,0:T(4,128)(2,1)S(1)}, u32[]{:S(2)}, u32[]{:S(2)}) collective-permute-start(bf16[10,4,4096]{2,1,0:T(4,128)(2,1)S(1)} %coarse.7), channel_id=1, source_target_pairs={{4,0},{8,4},{12,8},{16,12},{20,16},{24,20},{28,24},{5,1},{9,5},{13... | collective-permute-start | bytes 983048 | tf_op jit(solution)/shard_map/ppermute | solution.py:404
  53.9 0.0 collective-permute-done.7.refs_3_
  53.9 5.6 %product.3.refs_1_ = bf16[8,64,640]{2,1,0:T(8,128)(2,1)S(1)} custom-call(s32[24,32]{1,0:T(8,128)S(1)} %subtract_select_fusion.place_ref, bf16[6,5,256,128]{3,2,1,0:T(8,128)(2,1)S(1)} %right_factor.2.own_ref, bf16[12,5,256,128]{3,2,1,0:T(8,128)(2,1)S(1)} %right_factor.3.near_ref, bf16[8,64,512]{2,1,0:T(8,128)(2,1)} %relayout.4.refs_0_, ...), custom_call_target="tpu_custom_call" | custom-call | flops 240000000 | bytes 8880000 | tf_op jit(solution)/shard_map/product/pallas_call | solution.py:268
  59.6 1.1 %coarse.10 = bf16[10,4,4096]{2,1,0:T(4,128)(2,1)S(1)} custom-call(bf16[12,24,64,128]{3,2,1,0:T(8,128)(2,1)S(1)} %left_factor.1.left_ref, bf16[16,64,640]{2,1,0:T(8,128)(2,1)S(1)} %product.2.refs_0_, bf16[8,64,640]{2,1,0:T(8,128)(2,1)S(1)} %product.3.refs_1_), custom_call_target="tpu_custom_call" | custom-call | flops 100000000 | bytes 3700000 | tf_op jit(solution)/shard_map/coarse/pallas_call | solution.py:315
  60.7 2.0 %collective-permute-start.10 = (bf16[10,4,4096]{2,1,0:T(4,128)(2,1)S(1)}, bf16[10,4,4096]{2,1,0:T(4,128)(2,1)S(1)}, u32[]{:S(2)}, u32[]{:S(2)}) collective-permute-start(bf16[10,4,4096]{2,1,0:T(4,128)(2,1)S(1)} %coarse.10), channel_id=1, source_target_pairs={{4,0},{8,4},{12,8},{16,12},{20,16},{24,20},{28,24},{5,1},{9,5},{13... | collective-permute-start | bytes 983048 | tf_op jit(solution)/shard_map/ppermute | solution.py:404
  62.7 1.1 %coarse.11 = bf16[10,8,2048]{2,1,0:T(8,128)(2,1)S(1)} custom-call(bf16[12,24,64,128]{3,2,1,0:T(8,128)(2,1)S(1)} %left_factor.1.left_ref, bf16[16,64,640]{2,1,0:T(8,128)(2,1)S(1)} %product.2.refs_0_, bf16[8,64,640]{2,1,0:T(8,128)(2,1)S(1)} %product.3.refs_1_), custom_call_target="tpu_custom_call" | custom-call | flops 100000000 | bytes 3700000 | tf_op jit(solution)/shard_map/coarse/pallas_call | solution.py:315
  63.8 3.3 %collective-permute-start.12 = (bf16[10,8,2048]{2,1,0:T(8,128)(2,1)S(1)}, bf16[10,8,2048]{2,1,0:T(8,128)(2,1)S(1)}, u32[]{:S(2)}, u32[]{:S(2)}) collective-permute-start(bf16[10,8,2048]{2,1,0:T(8,128)(2,1)S(1)} %coarse.11), channel_id=1, source_target_pairs={{0,4},{4,8},{8,12},{12,16},{16,20},{20,24},{24,28},{1,5},{5,9},{9,... | collective-permute-start | bytes 983048 | tf_op jit(solution)/shard_map/ppermute | solution.py:401
  67.1 1.1 coarse.9
  68.2 1.1 coarse.8
  69.3 0.0 collective-permute-done.9
  69.3 8.9 %collective-permute-done.10 = bf16[10,4,4096]{2,1,0:T(4,128)(2,1)S(1)} collective-permute-done((bf16[10,4,4096]{2,1,0:T(4,128)(2,1)S(1)}, bf16[10,4,4096]{2,1,0:T(4,128)(2,1)S(1)}, u32[]{:S(2)}, u32[]{:S(2)}) %collective-permute-start.10) | collective-permute-done | bytes 327712 | tf_op jit(solution)/shard_map/ppermute | solution.py:404
  78.2 0.3 pad_maximum_fusion
  78.6 0.0 collective-permute-done.12
  78.6 0.1 add_convert_fusion
  78.7 1.3 %collective-permute-start.14 = (bf16[14,8,2048]{2,1,0:T(8,128)(2,1)S(1)}, bf16[14,8,2048]{2,1,0:T(8,128)(2,1)S(1)}, u32[]{:S(2)}, u32[]{:S(2)}) collective-permute-start(bf16[14,8,2048]{2,1,0:T(8,128)(2,1)S(1)} %bitcast.11), channel_id=1, source_target_pairs={{0,2},{1,3},{2,0},{3,1},{4,6},{5,7},{6,4},{7,5},{8,10},{9,11},{10,... | collective-permute-start | bytes 1376264 | tf_op jit(solution)/shard_map/ppermute | solution.py:395
  80.0 1.1 %coarse.6 = bf16[10,8,2048]{2,1,0:T(8,128)(2,1)S(1)} custom-call(bf16[12,24,64,128]{3,2,1,0:T(8,128)(2,1)S(1)} %left_factor.1.left_ref, bf16[16,64,640]{2,1,0:T(8,128)(2,1)S(1)} %product.2.refs_0_, bf16[8,64,640]{2,1,0:T(8,128)(2,1)S(1)} %product.3.refs_1_), custom_call_target="tpu_custom_call" | custom-call | flops 100000000 | bytes 3700000 | tf_op jit(solution)/shard_map/coarse/pallas_call | solution.py:315
  81.1 3.9 %collective-permute-start.8 = (bf16[10,8,2048]{2,1,0:T(8,128)(2,1)S(1)}, bf16[10,8,2048]{2,1,0:T(8,128)(2,1)S(1)}, u32[]{:S(2)}, u32[]{:S(2)}) collective-permute-start(bf16[10,8,2048]{2,1,0:T(8,128)(2,1)S(1)} %coarse.6), channel_id=1, source_target_pairs={{0,4},{4,8},{8,12},{12,16},{16,20},{20,24},{24,28},{1,5},{5,9},{9,... | collective-permute-start | bytes 983048 | tf_op jit(solution)/shard_map/ppermute | solution.py:401
  85.0 1.1 %collective-permute-start.13 = (bf16[14,8,2048]{2,1,0:T(8,128)(2,1)S(1)}, bf16[14,8,2048]{2,1,0:T(8,128)(2,1)S(1)}, u32[]{:S(2)}, u32[]{:S(2)}) collective-permute-start(bf16[14,8,2048]{2,1,0:T(8,128)(2,1)S(1)} %bitcast.12), channel_id=1, source_target_pairs={{0,1},{1,0},{2,3},{3,2},{4,5},{5,4},{6,7},{7,6},{8,9},{9,8},{10,11... | collective-permute-start | bytes 1376264 | tf_op jit(solution)/shard_map/ppermute | solution.py:398
  86.1 3.1 %collective-permute-done.14.refs_2_ = bf16[14,8,2048]{2,1,0:T(8,128)(2,1)S(1)} collective-permute-done((bf16[14,8,2048]{2,1,0:T(8,128)(2,1)S(1)}, bf16[14,8,2048]{2,1,0:T(8,128)(2,1)S(1)}, u32[]{:S(2)}, u32[]{:S(2)}) %collective-permute-start.14) | collective-permute-done | bytes 458784 | tf_op jit(solution)/shard_map/ppermute | solution.py:395
  89.2 2.4 %collective-permute-start.15 = (bf16[14,8,2048]{2,1,0:T(8,128)(2,1)S(1)}, bf16[14,8,2048]{2,1,0:T(8,128)(2,1)S(1)}, u32[]{:S(2)}, u32[]{:S(2)}) collective-permute-start(bf16[14,8,2048]{2,1,0:T(8,128)(2,1)S(1)} %collective-permute-done.14.refs_2_), channel_id=1, source_target_pairs={{0,1},{1,0},{2,3},{3,2},{4,5},{5,4},{6,7},{7,6},{8,9},{9,8},{10,11... | collective-permute-start | bytes 1376264 | tf_op jit(solution)/shard_map/ppermute | solution.py:398
  91.7 0.0 collective-permute-done.8
  91.7 0.1 add_convert_fusion.1
  91.8 1.3 %collective-permute-start.11 = (bf16[14,8,2048]{2,1,0:T(8,128)(2,1)S(1)}, bf16[14,8,2048]{2,1,0:T(8,128)(2,1)S(1)}, u32[]{:S(2)}, u32[]{:S(2)}) collective-permute-start(bf16[14,8,2048]{2,1,0:T(8,128)(2,1)S(1)} %bitcast.14), channel_id=1, source_target_pairs={{0,2},{1,3},{2,0},{3,1},{4,6},{5,7},{6,4},{7,5},{8,10},{9,11},{10,... | collective-permute-start | bytes 1376264 | tf_op jit(solution)/shard_map/ppermute | solution.py:395
  93.1 1.6 %collective-permute-start.16 = (bf16[14,8,2048]{2,1,0:T(8,128)(2,1)S(1)}, bf16[14,8,2048]{2,1,0:T(8,128)(2,1)S(1)}, u32[]{:S(2)}, u32[]{:S(2)}) collective-permute-start(bf16[14,8,2048]{2,1,0:T(8,128)(2,1)S(1)} %bitcast.15), channel_id=1, source_target_pairs={{0,1},{1,0},{2,3},{3,2},{4,5},{5,4},{6,7},{7,6},{8,9},{9,8},{10,11... | collective-permute-start | bytes 1376264 | tf_op jit(solution)/shard_map/ppermute | solution.py:398
  94.7 0.0 collective-permute-done.13.refs_1_
  94.7 0.0 collective-permute-done.15.refs_3_
  94.7 2.9 %assemble.2.refs_0_ = bf16[8,56,4096]{2,1,0:T(8,128)(2,1)} custom-call(bf16[448,448]{1,0:T(8,128)(2,1)S(1)} %fusion.12.order_ref, bf16[14,8,2048]{2,1,0:T(8,128)(2,1)S(1)} %bitcast.13, bf16[14,8,2048]{2,1,0:T(8,128)(2,1)S(1)} %collective-permute-done.13.refs_1_, bf16[14,8,2048]{2,1,0:T(8,128)(2,1)S(1)} %collective-permute-done.14.refs_2_, ...), custom_call_target="tpu_custom_call" | custom-call | flops 290000000 | bytes 10730000 | tf_op jit(solution)/shard_map/assemble/pallas_call | solution.py:350
  97.6 4.0 %collective-permute-done.11.refs_3_ = bf16[14,8,2048]{2,1,0:T(8,128)(2,1)S(1)} collective-permute-done((bf16[14,8,2048]{2,1,0:T(8,128)(2,1)S(1)}, bf16[14,8,2048]{2,1,0:T(8,128)(2,1)S(1)}, u32[]{:S(2)}, u32[]{:S(2)}) %collective-permute-start.11) | collective-permute-done | bytes 458784 | tf_op jit(solution)/shard_map/ppermute | solution.py:395
  101.6 3.2 %collective-permute-start.17 = (bf16[14,8,2048]{2,1,0:T(8,128)(2,1)S(1)}, bf16[14,8,2048]{2,1,0:T(8,128)(2,1)S(1)}, u32[]{:S(2)}, u32[]{:S(2)}) collective-permute-start(bf16[14,8,2048]{2,1,0:T(8,128)(2,1)S(1)} %collective-permute-done.11.refs_3_), channel_id=1, source_target_pairs={{0,1},{1,0},{2,3},{3,2},{4,5},{5,4},{6,7},{7,6},{8,9},{9,8},{10,11... | collective-permute-start | bytes 1376264 | tf_op jit(solution)/shard_map/ppermute | solution.py:398
  104.8 0.0 collective-permute-done.16.refs_2_
  104.8 1.4 %collective-permute-done.17.refs_4_ = bf16[14,8,2048]{2,1,0:T(8,128)(2,1)S(1)} collective-permute-done((bf16[14,8,2048]{2,1,0:T(8,128)(2,1)S(1)}, bf16[14,8,2048]{2,1,0:T(8,128)(2,1)S(1)}, u32[]{:S(2)}, u32[]{:S(2)}) %collective-permute-start.17) | collective-permute-done | bytes 458784 | tf_op jit(solution)/shard_map/ppermute | solution.py:398
  106.2 2.9 %assemble.3 = bf16[8,56,4096]{2,1,0:T(8,128)(2,1)} custom-call(bf16[448,448]{1,0:T(8,128)(2,1)S(1)} %fusion.12.order_ref, bf16[8,56,4096]{2,1,0:T(8,128)(2,1)} %assemble.2.refs_0_, bf16[14,8,2048]{2,1,0:T(8,128)(2,1)S(1)} %bitcast.16, bf16[14,8,2048]{2,1,0:T(8,128)(2,1)S(1)} %collective-permute-done.16.refs_2_, ...), custom_call_target="tpu_custom_call", output_to_operand_aliasing={{}: (1, {})} | custom-call | flops 290000000 | bytes 10730000 | tf_op jit(solution)/shard_map/assemble/pallas_call | solution.py:350
  (11 shorter events, 0.0 us)
Async XLA Ops:
  0.0 1.4 %copy-start = (bf16[24,8,4096]{2,1,0:T(8,128)(2,1)S(1)}, bf16[24,8,4096]{2,1,0:T(8,128)(2,1)}, u32[]{:S(2)}) copy-start(bf16[24,8,4096]{2,1,0:T(8,128)(2,1)} %x_ref.3) | copy-start | bytes 4718596
  1.4 4.0 %copy-start.1 = (bf16[24,8,4096]{2,1,0:T(8,128)(2,1)S(1)}, bf16[24,8,4096]{2,1,0:T(8,128)(2,1)}, u32[]{:S(2)}) copy-start(bf16[24,8,4096]{2,1,0:T(8,128)(2,1)} %x_ref.3) | copy-start | bytes 4718596
  1.4 5.5 %copy-start.2 = (bf16[24,4,4096]{2,1,0:T(4,128)(2,1)S(1)}, bf16[24,4,4096]{2,1,0:T(4,128)(2,1)}, u32[]{:S(2)}) copy-start(bf16[24,4,4096]{2,1,0:T(4,128)(2,1)} %x_ref.4) | copy-start | bytes 2359300
  1.4 9.8 %copy-start.3 = (s32[192,4]{0,1:T(4,128)S(1)}, s32[192,4]{0,1:T(4,128)}, u32[]{:S(2)}) copy-start(s32[192,4]{0,1:T(4,128)} %param.9) | copy-start | bytes 9220
  1.4 27.3 %copy-start.4 = (s32[24,32]{1,0:T(8,128)S(1)}, s32[24,32]{1,0:T(8,128)}, u32[]{:S(2)}) copy-start(s32[24,32]{1,0:T(8,128)} %param.6) | copy-start | bytes 9220
  1.4 27.3 %copy-start.5 = (s32[24]{0:T(128)S(1)}, s32[24]{0:T(128)}, u32[]{:S(2)}) copy-start(s32[24]{0:T(128)} %param.7) | copy-start | bytes 292
  2.2 3.2 %collective-permute-start = (bf16[16,64,512]{2,1,0:T(8,128)(2,1)S(1)}, bf16[16,64,512]{2,1,0:T(8,128)(2,1)}, u32[]{:S(2)}, u32[]{:S(2)}) collective-permute-start(bf16[16,64,512]{2,1,0:T(8,128)(2,1)S(1)} %relayout.3.refs_0_), channel_id=1, source_target_pairs={{0,1},{1,0},{2,3},{3,2},{4,5},{5,4},{6,7},{7,6},{8,9},{9,8},{10,11... | collective-permute-start | bytes 3145736 | tf_op jit(solution)/shard_map/ppermute | solution.py:398
  3.0 24.8 %collective-permute-start.5 = (bf16[16,64,512]{2,1,0:T(8,128)(2,1)S(1)}, bf16[16,64,512]{2,1,0:T(8,128)(2,1)}, u32[]{:S(2)}, u32[]{:S(2)}) collective-permute-start(bf16[16,64,512]{2,1,0:T(8,128)(2,1)S(1)} %relayout.3.refs_0_), channel_id=1, source_target_pairs={{0,2},{1,3},{2,0},{3,1},{4,6},{5,7},{6,4},{7,5},{8,10},{9,11},{10,... | collective-permute-start | bytes 3145736 | tf_op jit(solution)/shard_map/ppermute | solution.py:395
  6.5 22.3 %collective-permute-start.2 = (bf16[8,64,512]{2,1,0:T(8,128)(2,1)}, bf16[8,64,512]{2,1,0:T(8,128)(2,1)}, u32[]{:S(2)}, u32[]{:S(2)}) collective-permute-start(bf16[8,64,512]{2,1,0:T(8,128)(2,1)} %relayout.4.refs_0_), channel_id=1, source_target_pairs={{0,1},{1,0},{2,3},{3,2},{4,5},{5,4},{6,7},{7,6},{8,9},{9,8},{10,11... | collective-permute-start | bytes 1572872 | tf_op jit(solution)/shard_map/ppermute | solution.py:398
  7.9 26.0 %collective-permute-start.1 = (bf16[24,64,256]{2,1,0:T(8,128)(2,1)S(1)}, bf16[24,64,256]{2,1,0:T(8,128)(2,1)}, u32[]{:S(2)}, u32[]{:S(2)}) collective-permute-start(bf16[24,64,256]{2,1,0:T(8,128)(2,1)S(1)} %relayout_rows.1.refs_0_), channel_id=1, source_target_pairs={{0,4},{2,6},{4,8},{5,1},{6,10},{7,3},{8,12},{9,5},{10,14},{11,7},{... | collective-permute-start | bytes 2359304 | tf_op jit(solution)/shard_map/ppermute | solution.py:392
  27.8 11.6 %collective-permute-start.6 = (bf16[16,64,512]{2,1,0:T(8,128)(2,1)}, bf16[16,64,512]{2,1,0:T(8,128)(2,1)S(1)}, u32[]{:S(2)}, u32[]{:S(2)}) collective-permute-start(bf16[16,64,512]{2,1,0:T(8,128)(2,1)} %collective-permute-done.5.refs_2_), channel_id=1, source_target_pairs={{0,1},{1,0},{2,3},{3,2},{4,5},{5,4},{6,7},{7,6},{8,9},{9,8},{10,11... | collective-permute-start | bytes 3145736 | tf_op jit(solution)/shard_map/ppermute | solution.py:398
  34.0 2.6 %collective-permute-start.4 = (bf16[24,64,256]{2,1,0:T(8,128)(2,1)}, bf16[24,64,256]{2,1,0:T(8,128)(2,1)S(1)}, u32[]{:S(2)}, u32[]{:S(2)}) collective-permute-start(bf16[24,64,256]{2,1,0:T(8,128)(2,1)} %collective-permute-done.1.refs_0_), channel_id=1, source_target_pairs={{0,1},{1,0},{2,3},{3,2},{4,5},{5,4},{6,7},{7,6},{8,9},{9,8},{10,11... | collective-permute-start | bytes 2359304 | tf_op jit(solution)/shard_map/ppermute | solution.py:398
  34.0 15.5 %collective-permute-start.3 = (bf16[8,64,512]{2,1,0:T(8,128)(2,1)}, bf16[8,64,512]{2,1,0:T(8,128)(2,1)S(1)}, u32[]{:S(2)}, u32[]{:S(2)}) collective-permute-start(bf16[8,64,512]{2,1,0:T(8,128)(2,1)} %relayout.4.refs_0_), channel_id=1, source_target_pairs={{0,2},{1,3},{2,0},{3,1},{4,6},{5,7},{6,4},{7,5},{8,10},{9,11},{10,... | collective-permute-start | bytes 1572872 | tf_op jit(solution)/shard_map/ppermute | solution.py:395
  49.6 4.3 %collective-permute-start.7 = (bf16[8,64,512]{2,1,0:T(8,128)(2,1)S(1)}, bf16[8,64,512]{2,1,0:T(8,128)(2,1)S(1)}, u32[]{:S(2)}, u32[]{:S(2)}) collective-permute-start(bf16[8,64,512]{2,1,0:T(8,128)(2,1)S(1)} %collective-permute-done.3.refs_2_), channel_id=1, source_target_pairs={{0,1},{1,0},{2,3},{3,2},{4,5},{5,4},{6,7},{7,6},{8,9},{9,8},{10,11... | collective-permute-start | bytes 1572872 | tf_op jit(solution)/shard_map/ppermute | solution.py:398
  50.7 18.6 %collective-permute-start.9 = (bf16[10,4,4096]{2,1,0:T(4,128)(2,1)S(1)}, bf16[10,4,4096]{2,1,0:T(4,128)(2,1)S(1)}, u32[]{:S(2)}, u32[]{:S(2)}) collective-permute-start(bf16[10,4,4096]{2,1,0:T(4,128)(2,1)S(1)} %coarse.7), channel_id=1, source_target_pairs={{4,0},{8,4},{12,8},{16,12},{20,16},{24,20},{28,24},{5,1},{9,5},{13... | collective-permute-start | bytes 983048 | tf_op jit(solution)/shard_map/ppermute | solution.py:404
  60.7 17.5 %collective-permute-start.10 = (bf16[10,4,4096]{2,1,0:T(4,128)(2,1)S(1)}, bf16[10,4,4096]{2,1,0:T(4,128)(2,1)S(1)}, u32[]{:S(2)}, u32[]{:S(2)}) collective-permute-start(bf16[10,4,4096]{2,1,0:T(4,128)(2,1)S(1)} %coarse.10), channel_id=1, source_target_pairs={{4,0},{8,4},{12,8},{16,12},{20,16},{24,20},{28,24},{5,1},{9,5},{13... | collective-permute-start | bytes 983048 | tf_op jit(solution)/shard_map/ppermute | solution.py:404
  63.8 14.8 %collective-permute-start.12 = (bf16[10,8,2048]{2,1,0:T(8,128)(2,1)S(1)}, bf16[10,8,2048]{2,1,0:T(8,128)(2,1)S(1)}, u32[]{:S(2)}, u32[]{:S(2)}) collective-permute-start(bf16[10,8,2048]{2,1,0:T(8,128)(2,1)S(1)} %coarse.11), channel_id=1, source_target_pairs={{0,4},{4,8},{8,12},{12,16},{16,20},{20,24},{24,28},{1,5},{5,9},{9,... | collective-permute-start | bytes 983048 | tf_op jit(solution)/shard_map/ppermute | solution.py:401
  78.7 10.6 %collective-permute-start.14 = (bf16[14,8,2048]{2,1,0:T(8,128)(2,1)S(1)}, bf16[14,8,2048]{2,1,0:T(8,128)(2,1)S(1)}, u32[]{:S(2)}, u32[]{:S(2)}) collective-permute-start(bf16[14,8,2048]{2,1,0:T(8,128)(2,1)S(1)} %bitcast.11), channel_id=1, source_target_pairs={{0,2},{1,3},{2,0},{3,1},{4,6},{5,7},{6,4},{7,5},{8,10},{9,11},{10,... | collective-permute-start | bytes 1376264 | tf_op jit(solution)/shard_map/ppermute | solution.py:395
  81.1 10.6 %collective-permute-start.8 = (bf16[10,8,2048]{2,1,0:T(8,128)(2,1)S(1)}, bf16[10,8,2048]{2,1,0:T(8,128)(2,1)S(1)}, u32[]{:S(2)}, u32[]{:S(2)}) collective-permute-start(bf16[10,8,2048]{2,1,0:T(8,128)(2,1)S(1)} %coarse.6), channel_id=1, source_target_pairs={{0,4},{4,8},{8,12},{12,16},{16,20},{20,24},{24,28},{1,5},{5,9},{9,... | collective-permute-start | bytes 983048 | tf_op jit(solution)/shard_map/ppermute | solution.py:401
  85.0 9.7 %collective-permute-start.13 = (bf16[14,8,2048]{2,1,0:T(8,128)(2,1)S(1)}, bf16[14,8,2048]{2,1,0:T(8,128)(2,1)S(1)}, u32[]{:S(2)}, u32[]{:S(2)}) collective-permute-start(bf16[14,8,2048]{2,1,0:T(8,128)(2,1)S(1)} %bitcast.12), channel_id=1, source_target_pairs={{0,1},{1,0},{2,3},{3,2},{4,5},{5,4},{6,7},{7,6},{8,9},{9,8},{10,11... | collective-permute-start | bytes 1376264 | tf_op jit(solution)/shard_map/ppermute | solution.py:398
  89.2 5.5 %collective-permute-start.15 = (bf16[14,8,2048]{2,1,0:T(8,128)(2,1)S(1)}, bf16[14,8,2048]{2,1,0:T(8,128)(2,1)S(1)}, u32[]{:S(2)}, u32[]{:S(2)}) collective-permute-start(bf16[14,8,2048]{2,1,0:T(8,128)(2,1)S(1)} %collective-permute-done.14.refs_2_), channel_id=1, source_target_pairs={{0,1},{1,0},{2,3},{3,2},{4,5},{5,4},{6,7},{7,6},{8,9},{9,8},{10,11... | collective-permute-start | bytes 1376264 | tf_op jit(solution)/shard_map/ppermute | solution.py:398
  91.8 9.8 %collective-permute-start.11 = (bf16[14,8,2048]{2,1,0:T(8,128)(2,1)S(1)}, bf16[14,8,2048]{2,1,0:T(8,128)(2,1)S(1)}, u32[]{:S(2)}, u32[]{:S(2)}) collective-permute-start(bf16[14,8,2048]{2,1,0:T(8,128)(2,1)S(1)} %bitcast.14), channel_id=1, source_target_pairs={{0,2},{1,3},{2,0},{3,1},{4,6},{5,7},{6,4},{7,5},{8,10},{9,11},{10,... | collective-permute-start | bytes 1376264 | tf_op jit(solution)/shard_map/ppermute | solution.py:395
  93.1 11.7 %collective-permute-start.16 = (bf16[14,8,2048]{2,1,0:T(8,128)(2,1)S(1)}, bf16[14,8,2048]{2,1,0:T(8,128)(2,1)S(1)}, u32[]{:S(2)}, u32[]{:S(2)}) collective-permute-start(bf16[14,8,2048]{2,1,0:T(8,128)(2,1)S(1)} %bitcast.15), channel_id=1, source_target_pairs={{0,1},{1,0},{2,3},{3,2},{4,5},{5,4},{6,7},{7,6},{8,9},{9,8},{10,11... | collective-permute-start | bytes 1376264 | tf_op jit(solution)/shard_map/ppermute | solution.py:398
  101.6 4.7 %collective-permute-start.17 = (bf16[14,8,2048]{2,1,0:T(8,128)(2,1)S(1)}, bf16[14,8,2048]{2,1,0:T(8,128)(2,1)S(1)}, u32[]{:S(2)}, u32[]{:S(2)}) collective-permute-start(bf16[14,8,2048]{2,1,0:T(8,128)(2,1)S(1)} %collective-permute-done.11.refs_3_), channel_id=1, source_target_pairs={{0,1},{1,0},{2,3},{3,2},{4,5},{5,4},{6,7},{7,6},{8,9},{9,8},{10,11... | collective-permute-start | bytes 1376264 | tf_op jit(solution)/shard_map/ppermute | solution.py:398

commit v5 on v4

--- a/solution.py
+++ b/solution.py
@@ -44,8 +44,8 @@
         for k in range(0, nb, 2):
             x0 = scr[r, pl.ds(k, 32, stride=8), :]
             x1 = scr[r, pl.ds(k + 1, 32, stride=8), :]
-            o_ref[r, 0:32, k * BS : (k + 2) * BS] = jnp.where(low, x0, pltpu.roll(x1, BS, 1)).astype(BF)
-            o_ref[r, 32:64, k * BS : (k + 2) * BS] = jnp.where(low, pltpu.roll(x0, BS, 1), x1).astype(BF)
+            o_ref[r, k // 2, 0:32] = jnp.where(low, x0, pltpu.roll(x1, BS, 1)).astype(BF)
+            o_ref[r, k // 2, 32:64] = jnp.where(low, pltpu.roll(x0, BS, 1), x1).astype(BF)
 
 
 def relayout(x, first, rows):
@@ -54,9 +54,9 @@
     return pl.pallas_call(
         relayout_kernel,
         grid=(rows // step,),
-        out_shape=jax.ShapeDtypeStruct((rows, BS, nb * BS), BF),
+        out_shape=jax.ShapeDtypeStruct((rows, nb // 2, BS, LANES), BF),
         in_specs=[pl.BlockSpec((step, nb, BS * BS), lambda i: (i + first // step, 0, 0))],
-        out_specs=pl.BlockSpec((step, BS, nb * BS), lambda i: (i, 0, 0)),
+        out_specs=pl.BlockSpec((step, nb // 2, BS, LANES), lambda i: (i, 0, 0, 0)),
         scratch_shapes=[pltpu.VMEM((step, 256, LANES), F32)],
         compiler_params=params(4),
         cost_estimate=cost(0.6),
@@ -75,7 +75,7 @@
             x1 = scr[r, pl.ds(k + 1, 32, stride=8), :]
             mix[r, k // 2, pl.ds(0, 32, stride=2), :] = jnp.where(low, x0, pltpu.roll(x1, BS, 1))
             mix[r, k // 2, pl.ds(1, 32, stride=2), :] = jnp.where(low, pltpu.roll(x0, BS, 1), x1)
-            o_ref[r, :, k * BS : (k + 2) * BS] = mix[r, k // 2].astype(BF)
+            o_ref[r, k // 2] = mix[r, k // 2].astype(BF)
 
 
 def relayout_rows(x):
@@ -84,9 +84,9 @@
     return pl.pallas_call(
         relayout_rows_kernel,
         grid=(rows // step,),
-        out_shape=jax.ShapeDtypeStruct((rows, BS, nb * BS), BF),
+        out_shape=jax.ShapeDtypeStruct((rows, nb // 2, BS, LANES), BF),
         in_specs=[pl.BlockSpec((step, nb, BS * BS), lambda i: (i, 0, 0))],
-        out_specs=pl.BlockSpec((step, BS, nb * BS), lambda i: (i, 0, 0)),
+        out_specs=pl.BlockSpec((step, nb // 2, BS, LANES), lambda i: (i, 0, 0, 0)),
         scratch_shapes=[pltpu.VMEM((step, 256, LANES), F32), pltpu.VMEM((step, nb // 2, BS, LANES), F32)],
         compiler_params=params(4),
         cost_estimate=cost(1.0),
@@ -102,7 +102,7 @@
     def pair(ip, carry):
         for half in range(2):
             i = ip * 2 + half
-            x = pl_ref[i].astype(F32)
+            x = jnp.concatenate([pl_ref[i, 0], pl_ref[i, 1]], axis=1).astype(F32)
             xt = jnp.concatenate([x, x], axis=0).T
             keep = jnp.where(low if half == 0 else jnp.logical_not(low), xt, 0.0)
             for s in range(4):
@@ -151,7 +151,7 @@
                 jj = 4 * jq + d
                 dups = []
                 for t in range(4):
-                    x = src[jj, :, t * BS : (t + 1) * BS]
+                    x = src[jj, t // 2, :, t % 2 * BS : (t % 2 + 1) * BS]
                     dups.append(jnp.concatenate([x, x], axis=1))
                 at = [table_ref[t, side * rb + jj] for t in range(4)]
                 for p in range(*touched(side, tiles)):
@@ -199,47 +199,78 @@
     row = jnp.arange(rb, dtype=jnp.int32)[:, None]
     near = a_cols - (lax.axis_index("row") - 1) * rb - row // 4 * 4
     live = jnp.arange(ka, dtype=jnp.int32)[None, :] < counts[:, None]
-    return jnp.where(live, near, -1)
-
-
-def product_kernel(first, rb, shifts, place_ref, own_ref, near_ref, *refs):
+    return jnp.where(live, near, 2 * (rb + 2))
+
+
+def first_slots(shifts, ks):
     col = lax.axis_index("col")
     ny = lax.axis_size("col") // 2
-    srcs, o_ref, band, acc = refs[: len(shifts)], refs[-3], refs[-2], refs[-1]
-    rows = o_ref.shape[0]
-    ks = srcs[0].shape[2] // BS
-    tiles = own_ref.shape[1]
     y, core = col // 2, lax.rem(col, 2)
-    wide = band.shape[1]
-    half_of = lax.broadcasted_iota(jnp.int32, (1, LANES), 1) // BS
     slots = []
     for s, flip in shifts:
         c = core if flip == 0 else 1 - core
         slots.append((lax.rem(y - s + ny, ny) * 2 + c) * ks)
-
-    def lay(g, carry):
-        for t in range(wide):
-            band[g, t] = jnp.zeros((4 * BS, LANES), BF)
+    return slots
+
+
+def lay(first, place_ref, srcs, slots, band, start):
+    low = low_lanes(BS)
+    zero = jnp.zeros((BS, LANES), BF)
+
+    def group(g, carry):
+        for t in range(band.shape[1]):
+            band[g, t] = start(g, t)
         for src, slot in zip(srcs, slots):
-            for k in range(0, ks, 2):
-                pairs = [src[4 * g + d, :, k * BS : (k + 2) * BS] for d in range(4)]
-                turned = [jnp.concatenate([x[:, BS:], x[:, :BS]], axis=1) for x in pairs]
-                for e in range(2):
-                    at = [place_ref[first + 4 * g + d, slot + k + e] for d in range(4)]
-                    tile = [jnp.maximum(a, 0) >> 1 for a in at]
-                    old = [band[g, tile[d], d * BS : (d + 1) * BS] for d in range(4)]
-                    for d in range(4):
-                        half = jnp.where(at[d] < 0, 2, at[d] & 1)
-                        keep = jnp.where(half_of == half, 1.0, 0.0)
-                        stay = (keep * jnp.where(half_of == e, 1.0, 0.0)).astype(BF)
-                        move = (keep * jnp.where(half_of == e, 0.0, 1.0)).astype(BF)
-                        old[d] = old[d] + (pairs[d] * stay + turned[d] * move)
-                    for d in range(4):
-                        band[g, tile[d], d * BS : (d + 1) * BS] = old[d]
+            for k in range(src.shape[1]):
+                for d0 in range(0, 4, 2):
+                    cuts = []
+                    for d in range(d0, d0 + 2):
+                        x = src[4 * g + d, k]
+                        r = jnp.concatenate([x[:, BS:], x[:, :BS]], axis=1)
+                        cuts.append(
+                            (
+                                (jnp.where(low, x, zero), jnp.where(low, zero, r)),
+                                (jnp.where(low, r, zero), jnp.where(low, zero, x)),
+                            )
+                        )
+                    for e in range(2):
+                        at = [place_ref[first + 4 * g + d0 + d, slot + 2 * k + e] for d in range(2)]
+                        spots = [(g, a >> 1, slice((d0 + d) * BS, (d0 + d + 1) * BS)) for d, a in enumerate(at)]
+                        old = [band[spot] for spot in spots]
+                        for spot, a, x, cut in zip(spots, at, old, cuts):
+                            band[spot] = x + jnp.where((a & 1) == 0, cut[e][0], cut[e][1])
         return carry
 
-    lax.fori_loop(0, rows // 4, lay, 0)
-
+    lax.fori_loop(0, band.shape[0], group, 0)
+
+
+def band_kernel(first, shifts, place_ref, *refs):
+    srcs, band = refs[:-1], refs[-1]
+    slots = first_slots(shifts, srcs[0].shape[1] * 2)
+    lay(first, place_ref, srcs, slots, band, lambda g, t: jnp.zeros((4 * BS, LANES), BF))
+
+
+def near_band(place, srcs, shifts, first):
+    rows = srcs[0].shape[0]
+    return pl.pallas_call(
+        functools.partial(band_kernel, first, shifts),
+        out_shape=jax.ShapeDtypeStruct((rows // 4, place.shape[0] + 3, 4 * BS, LANES), BF),
+        in_specs=[SM] + [VM] * len(srcs),
+        out_specs=VM,
+        compiler_params=params(24),
+        cost_estimate=cost(0.16 * rows),
+        name="near_band",
+    )(place, *srcs)
+
+
+def product_kernel(first, rb, shifts, place_ref, own_ref, near_ref, start_ref, *refs):
+    srcs = refs[: len(shifts)]
+    o_ref, band, acc = refs[len(shifts) :]
+    rows = o_ref.shape[0]
+    tiles = own_ref.shape[1]
+    wide = rb + 2
+    slots = first_slots(shifts, srcs[0].shape[1] * 2)
+    lay(first, place_ref, srcs, slots, band, lambda g, t: start_ref[g, t])
     quads = rb // 4
     for g in range(rows // 4):
         start = first // 4 + g
@@ -261,23 +292,23 @@
             o_ref[4 * g + d] = acc[d * BS : (d + 1) * BS].astype(BF)
 
 
-def product(place, own, near, srcs, shifts, first, us):
+def product(place, own, near, start, srcs, shifts, first, us):
     rows = srcs[0].shape[0]
     rb = place.shape[0]
     tiles = own.shape[1]
     return pl.pallas_call(
         functools.partial(product_kernel, first, rb, shifts),
         out_shape=jax.ShapeDtypeStruct((rows, BS, tiles * LANES), BF),
-        in_specs=[SM] + [VM] * (2 + len(srcs)),
+        in_specs=[SM] + [VM] * (3 + len(srcs)),
         out_specs=VM,
         scratch_shapes=[
-            pltpu.VMEM((rows // 4, rb + 2, 4 * BS, LANES), BF),
+            pltpu.VMEM(start.shape, BF),
             pltpu.VMEM((4 * BS, tiles * LANES), F32),
         ],
-        compiler_params=params(32),
+        compiler_params=params(40),
         cost_estimate=cost(us),
         name="product",
-    )(place, own, near, *srcs)
+    )(place, own, near, start, *srcs)
 
 
 def coarse_kernel(sets, a0, a1, left_ref, *refs):
@@ -422,12 +453,13 @@
     own = right_factor(table, [p_own], tiles, 2.0)
     order = assembly_order(shifts, ncol, share)
     place = slot_places(a_cols, counts)
-    beside, left, own, order, place = lax.optimization_barrier((beside, left, own, order, place))
+    bands = [near_band(place, [own_a[h], side_a[h]], shifts[:2], parts[h][0]) for h in range(2)]
+    beside, far_a[0], left, own, order, bands = lax.optimization_barrier((beside, far_a[0], left, own, order, bands))
     near = right_factor(table, [beside, over_core(beside)], tiles, 3.0)
     aps = []
     for h in range(2):
-        srcs = [own_a[h], side_a[h]] + [z for g in far_a[h] for z in (g, over_core(g))]
-        aps.append(product(place, own, near, srcs, shifts, parts[h][0], 0.3 * parts[h][1]))
+        srcs = [z for g in far_a[h] for z in (g, over_core(g))]
+        aps.append(product(place, own, near, bands[h], srcs, shifts[2:], parts[h][0], 0.3 * parts[h][1]))
         if h == 0:
             far_a[1], aps[0] = lax.optimization_barrier((far_a[1], aps[0]))
             early = downward(coarse_rows(left, aps, ((0, CB // 2),), 0, BS, BF, 1.0)[0])
@@ -437,15 +469,20 @@
         return jnp.pad(y.astype(F32), ((0, 0), (g, 2 - g), (0, 0), (0, 0)))
 
     late = downward(coarse_rows(left, aps, ((CB // 2, CB),), 0, BS, BF, 1.0)[0])
-    highs = [upward(coarse_rows(left, aps, ((2 * CB, 3 * CB),), a0, a1, BF, 1.0)[0]) for a0, a1 in chunks]
+    highs = [coarse_rows(left, aps, ((2 * CB, 3 * CB),), a0, a1, BF, 1.0)[0] for a0, a1 in chunks]
+    left, highs = lax.optimization_barrier((left, highs))
+    highs = [upward(x) for x in highs]
     mids = [coarse_rows(left, aps, ((CB, 2 * CB),), a0, a1, F32, 1.0)[0] for a0, a1 in chunks]
     early, mids = lax.optimization_barrier((early, mids))
     lower = jnp.concatenate([early, late], axis=1)
-    out = None
+    totals, fars = [], []
     for (a0, a1), high, mid in zip(chunks, highs, mids):
         total = columns(high, 0) + columns(mid, 1) + columns(lower[:, :, a0 * BS : a1 * BS], 2)
-        total = total.astype(BF).reshape((share * (GROUPS + 2),) + total.shape[2:])
-        far = [over_y(total, s) for s in range(1, ny)]
+        totals.append(total.astype(BF).reshape((share * (GROUPS + 2),) + total.shape[2:]))
+        fars.append([over_y(totals[-1], s) for s in range(1, ny)])
+    fars[0], totals[1] = lax.optimization_barrier((fars[0], totals[1]))
+    out = None
+    for (a0, a1), total, far in zip(chunks, totals, fars):
         if out is not None:
             far, out = lax.optimization_barrier((far, out))
         srcs = [z for g in [total] + far for z in (g, over_core(g))]

time: 110 us -> 111 us (level)
  local copies, waits for them, and re-layouts: 1.43 us -> 5.42 us
  starting transfers between devices: 31.1 us -> 27.9 us
  Pallas kernels: 39 us -> 42 us
  waiting for transfers between devices: 36.4 us -> 33.5 us
    ppermute x4, waiting for transfers between devices: 23.7 us -> 16.9 us  [over_y(): lax.ppermute(x, 'col', [(y * 2 + c, (y + s) % ny * 2 + c) for y in range(...]
    pallas_call x0 -> x2, Pallas kernels: none -> 5.99 us  [near_band(): pl.pallas_call(functools.partial(band_kernel, first, shifts), out_shape=j...]
    unnamed x12 -> x16, local copies, waits for them, and re-layouts: 1.43 us -> 5.42 us
    ppermute x9, starting transfers between devices: 10.6 us -> 7.52 us  [over_core(): return lax.ppermute(x, 'col', [(c, c ^ 1) for c in range(ncol)])]
    ppermute x2, waiting for transfers between devices: 8.93 us -> 11.9 us  [downward(): return lax.ppermute(x, 'row', [(i + 1, i) for i in range(nrow - 1)])]
    pallas_call x2, Pallas kernels: 15.8 us -> 12.9 us  [product(): pl.pallas_call(functools.partial(product_kernel, first, rb, shifts), out_...]
  transfers between devices with their start and end apart: 18 -> 18, of which waited for: 7 -> 8; matrix products, arithmetic and copies ran while one was open for 1% -> 1% of each run, Pallas kernels for 32% -> 34%
where the time goes in v5:
time: 111 us
  Pallas kernels  42 us (38%)
  waiting for transfers between devices  33.5 us (30%)
  starting transfers between devices  27.9 us (25%)
  local copies, waits for them, and re-layouts  5.42 us (5%)
  other arithmetic  1.59 us (1%)
    ppermute x4, waiting for transfers between devices, over_y(): lax.ppermute(x, 'col', [(y * 2 + c, (y + s) % ny * 2 + c) for y in range(...  16.9 us
    pallas_call x2, Pallas kernels, product(): pl.pallas_call(functools.partial(product_kernel, first, rb, shifts), out_...  12.9 us
    ppermute x2, waiting for transfers between devices, downward(): return lax.ppermute(x, 'row', [(i + 1, i) for i in range(nrow - 1)])  11.9 us
    ppermute x9, starting transfers between devices, over_core(): return lax.ppermute(x, 'col', [(c, c ^ 1) for c in range(ncol)])  7.52 us
    pallas_call x6, Pallas kernels, coarse_rows(): pl.pallas_call(functools.partial(coarse_kernel, sets, a0, a1), out_shape=...  6.48 us
    ppermute x2, starting transfers between devices, upward(): return lax.ppermute(x, 'row', [(i, i + 1) for i in range(nrow - 1)])  6.29 us
    ppermute x2, starting transfers between devices, downward(): return lax.ppermute(x, 'row', [(i + 1, i) for i in range(nrow - 1)])  6.11 us
    pallas_call x2, Pallas kernels, near_band(): pl.pallas_call(functools.partial(band_kernel, first, shifts), out_shape=j...  5.99 us
  transfers between devices with their start and end apart: 18, of which 8 were waited for; matrix products, arithmetic and copies ran while one was open for 1% of the time, Pallas kernels for 34%

profile of v5, /device:TPU:9, one launch (start us, length us, event | category | flops | bytes accessed | tf_op | source)
XLA Modules:
  0.0 110.7 jit_solution(5511453843362175664)
XLA Ops:
  0.0 1.4 %copy-done.1 = bf16[24,8,4096]{2,1,0:T(8,128)(2,1)S(1)} copy-done((bf16[24,8,4096]{2,1,0:T(8,128)(2,1)S(1)}, bf16[24,8,4096]{2,1,0:T(8,128)(2,1)}, u32[]{:S(2)}) %copy-start.1) | copy-done | bytes 1572888
  1.4 2.0 %relayout.3.refs_0_ = bf16[16,4,64,128]{3,2,1,0:T(8,128)(2,1)} custom-call(bf16[24,8,4096]{2,1,0:T(8,128)(2,1)S(1)} %copy-done.1), custom_call_target="tpu_custom_call" | custom-call | flops 60000000 | bytes 2220000 | tf_op jit(solution)/shard_map/relayout/pallas_call | solution.py:54
  3.4 0.7 collective-permute-start
  4.1 1.2 %collective-permute-start.2 = (bf16[16,4,64,128]{3,2,1,0:T(8,128)(2,1)}, bf16[16,4,64,128]{3,2,1,0:T(8,128)(2,1)}, u32[]{:S(2)}, u32[]{:S(2)}) collective-permute-start(bf16[16,4,64,128]{3,2,1,0:T(8,128)(2,1)} %relayout.3.refs_0_), channel_id=1, source_target_pairs={{0,2},{1,3},{2,0},{3,1},{4,6},{5,7},{6,4},{7,5},{8,10},{9,11},{10,... | collective-permute-start | bytes 3145736 | tf_op jit(solution)/shard_map/ppermute | solution.py:426
  5.3 0.8 add_select_fusion.4.table_ref
  6.1 0.4 collective-permute-done.refs_1_
  6.6 1.1 %copy-done.3 = bf16[24,4,4096]{2,1,0:T(4,128)(2,1)S(1)} copy-done((bf16[24,4,4096]{2,1,0:T(4,128)(2,1)S(1)}, bf16[24,4,4096]{2,1,0:T(4,128)(2,1)}, u32[]{:S(2)}) %copy-start.3) | copy-done | bytes 786456
  7.7 1.1 relayout_rows.1.refs_0_
  8.8 3.0 %collective-permute-start.1 = (bf16[24,2,64,128]{3,2,1,0:T(8,128)(2,1)S(1)}, bf16[24,2,64,128]{3,2,1,0:T(8,128)(2,1)S(1)}, u32[]{:S(2)}, u32[]{:S(2)}) collective-permute-start(bf16[24,2,64,128]{3,2,1,0:T(8,128)(2,1)S(1)} %relayout_rows.1.refs_0_), channel_id=1, source_target_pairs={{0,4},{2,6},{4,8},{5,1},{6,10},{7,3},{8,12},{9,5},{10,14},{11,7},{... | collective-permute-start | bytes 2359304 | tf_op jit(solution)/shard_map/ppermute | solution.py:423
  11.8 0.1 subtract_select_fusion.place_ref
  11.9 0.4 relayout.4.refs_0_
  12.3 0.8 collective-permute-start.3
  13.1 0.2 fusion.12.order_ref
  13.3 0.0 copy-start.4
  13.3 3.9 %near_band.2.start_ref = bf16[4,27,256,128]{3,2,1,0:T(8,128)(2,1)S(1)} custom-call(s32[24,32]{1,0:T(8,128)S(1)} %subtract_select_fusion.place_ref, bf16[16,4,64,128]{3,2,1,0:T(8,128)(2,1)} %relayout.3.refs_0_, bf16[16,4,64,128]{3,2,1,0:T(8,128)(2,1)S(1)} %collective-permute-done.refs_1_), custom_call_target="tpu_custom_call" | custom-call | flops 256000000 | bytes 9472000 | tf_op jit(solution)/shard_map/near_band/pallas_call | solution.py:255
  17.3 2.9 %copy-done = bf16[4,27,256,128]{3,2,1,0:T(8,128)(2,1)} copy-done((bf16[4,27,256,128]{3,2,1,0:T(8,128)(2,1)}, bf16[4,27,256,128]{3,2,1,0:T(8,128)(2,1)S(1)}, u32[]{:S(2)}) %copy-start) | copy-done | bytes 7077912
  20.1 0.0 collective-permute-done.3.refs_1_
  20.1 0.9 relayout.5.pl_ref
  21.0 0.0 copy-start.5
  21.0 2.1 %near_band.3.start_ref = bf16[2,27,256,128]{3,2,1,0:T(8,128)(2,1)S(1)} custom-call(s32[24,32]{1,0:T(8,128)S(1)} %subtract_select_fusion.place_ref, bf16[8,4,64,128]{3,2,1,0:T(8,128)(2,1)S(1)} %relayout.4.refs_0_, bf16[8,4,64,128]{3,2,1,0:T(8,128)(2,1)S(1)} %collective-permute-done.3.refs_1_), custom_call_target="tpu_custom_call" | custom-call | flops 128000000 | bytes 4736000 | tf_op jit(solution)/shard_map/near_band/pallas_call | solution.py:255
  23.1 1.4 %right_factor.2.own_ref = bf16[6,5,256,128]{3,2,1,0:T(8,128)(2,1)S(1)} custom-call(s32[4,72]{1,0:T(4,128)S(1)} %add_select_fusion.4.table_ref, bf16[24,2,64,128]{3,2,1,0:T(8,128)(2,1)S(1)} %relayout_rows.1.refs_0_), custom_call_target="tpu_custom_call" | custom-call | flops 200000000 | bytes 7400000 | tf_op jit(solution)/shard_map/right_factor/pallas_call | solution.py:186
  24.5 2.9 %left_factor.1.left_ref = bf16[12,24,64,128]{3,2,1,0:T(8,128)(2,1)S(1)} custom-call(s32[4,192]{1,0:T(4,128)S(1)} %bitcast.18, bf16[24,2,64,128]{3,2,1,0:T(8,128)(2,1)S(1)} %relayout.5.pl_ref), custom_call_target="tpu_custom_call" | custom-call | flops 290000000 | bytes 10730000 | tf_op jit(solution)/shard_map/left_factor/pallas_call | solution.py:118
  27.4 1.8 %collective-permute-done.2.refs_0_ = bf16[16,4,64,128]{3,2,1,0:T(8,128)(2,1)} collective-permute-done((bf16[16,4,64,128]{3,2,1,0:T(8,128)(2,1)}, bf16[16,4,64,128]{3,2,1,0:T(8,128)(2,1)}, u32[]{:S(2)}, u32[]{:S(2)}) %collective-permute-start.2) | collective-permute-done | bytes 1048608 | tf_op jit(solution)/shard_map/ppermute | solution.py:426
  29.2 0.7 collective-permute-done.1.refs_0_
  29.9 0.5 collective-permute-start.6
  30.5 0.0 collective-permute-start.5
  30.5 1.2 %collective-permute-start.4 = (bf16[8,4,64,128]{3,2,1,0:T(8,128)(2,1)S(1)}, bf16[8,4,64,128]{3,2,1,0:T(8,128)(2,1)S(1)}, u32[]{:S(2)}, u32[]{:S(2)}) collective-permute-start(bf16[8,4,64,128]{3,2,1,0:T(8,128)(2,1)S(1)} %relayout.4.refs_0_), channel_id=1, source_target_pairs={{0,2},{1,3},{2,0},{3,1},{4,6},{5,7},{6,4},{7,5},{8,10},{9,11},{10,... | collective-permute-start | bytes 1572872 | tf_op jit(solution)/shard_map/ppermute | solution.py:426
  31.7 2.0 %collective-permute-done.5.refs_1_ = bf16[24,2,64,128]{3,2,1,0:T(8,128)(2,1)S(1)} collective-permute-done((bf16[24,2,64,128]{3,2,1,0:T(8,128)(2,1)S(1)}, bf16[24,2,64,128]{3,2,1,0:T(8,128)(2,1)S(1)}, u32[]{:S(2)}, u32[]{:S(2)}) %collective-permute-start.5) | collective-permute-done | bytes 786464 | tf_op jit(solution)/shard_map/ppermute | solution.py:429
  33.7 2.3 %right_factor.3.near_ref = bf16[12,5,256,128]{3,2,1,0:T(8,128)(2,1)S(1)} custom-call(s32[4,72]{1,0:T(4,128)S(1)} %add_select_fusion.4.table_ref, bf16[24,2,64,128]{3,2,1,0:T(8,128)(2,1)S(1)} %collective-permute-done.1.refs_0_, bf16[24,2,64,128]{3,2,1,0:T(8,128)(2,1)S(1)} %collective-permute-done.5.refs_1_), custom_call_target="tpu_custom_call" | custom-call | flops 300000000 | bytes 11100000 | tf_op jit(solution)/shard_map/right_factor/pallas_call | solution.py:186
  36.0 0.0 collective-permute-done.6.refs_1_
  36.0 9.1 %product.2.refs_0_ = bf16[16,64,640]{2,1,0:T(8,128)(2,1)S(1)} custom-call(s32[24,32]{1,0:T(8,128)S(1)} %subtract_select_fusion.place_ref, bf16[6,5,256,128]{3,2,1,0:T(8,128)(2,1)S(1)} %right_factor.2.own_ref, bf16[12,5,256,128]{3,2,1,0:T(8,128)(2,1)S(1)} %right_factor.3.near_ref, bf16[4,27,256,128]{3,2,1,0:T(8,128)(2,1)} %copy-done, ...), custom_call_target="tpu_custom_call" | custom-call | flops 480000000 | bytes 17760000 | tf_op jit(solution)/shard_map/product/pallas_call | solution.py:299
  45.2 0.0 collective-permute-done.4.refs_0_
  45.2 0.2 collective-permute-start.7
  45.4 0.9 coarse.8
  46.3 4.2 %collective-permute-start.9 = (bf16[10,4,4096]{2,1,0:T(4,128)(2,1)S(1)}, bf16[10,4,4096]{2,1,0:T(4,128)(2,1)S(1)}, u32[]{:S(2)}, u32[]{:S(2)}) collective-permute-start(bf16[10,4,4096]{2,1,0:T(4,128)(2,1)S(1)} %coarse.8), channel_id=1, source_target_pairs={{4,0},{8,4},{12,8},{16,12},{20,16},{24,20},{28,24},{5,1},{9,5},{13... | collective-permute-start | bytes 983048 | tf_op jit(solution)/shard_map/ppermute | solution.py:435
  50.5 0.0 collective-permute-done.7.refs_1_
  50.5 3.8 %product.3.refs_1_ = bf16[8,64,640]{2,1,0:T(8,128)(2,1)S(1)} custom-call(s32[24,32]{1,0:T(8,128)S(1)} %subtract_select_fusion.place_ref, bf16[6,5,256,128]{3,2,1,0:T(8,128)(2,1)S(1)} %right_factor.2.own_ref, bf16[12,5,256,128]{3,2,1,0:T(8,128)(2,1)S(1)} %right_factor.3.near_ref, bf16[2,27,256,128]{3,2,1,0:T(8,128)(2,1)S(1)} %near_band.3.start_ref, ...), custom_call_target="tpu_custom_call" | custom-call | flops 240000000 | bytes 8880000 | tf_op jit(solution)/shard_map/product/pallas_call | solution.py:299
  54.3 1.1 %coarse.11 = bf16[10,4,4096]{2,1,0:T(4,128)(2,1)S(1)} custom-call(bf16[12,24,64,128]{3,2,1,0:T(8,128)(2,1)S(1)} %left_factor.1.left_ref, bf16[16,64,640]{2,1,0:T(8,128)(2,1)S(1)} %product.2.refs_0_, bf16[8,64,640]{2,1,0:T(8,128)(2,1)S(1)} %product.3.refs_1_), custom_call_target="tpu_custom_call" | custom-call | flops 100000000 | bytes 3700000 | tf_op jit(solution)/shard_map/coarse/pallas_call | solution.py:346
  55.5 1.9 %collective-permute-start.10 = (bf16[10,4,4096]{2,1,0:T(4,128)(2,1)S(1)}, bf16[10,4,4096]{2,1,0:T(4,128)(2,1)S(1)}, u32[]{:S(2)}, u32[]{:S(2)}) collective-permute-start(bf16[10,4,4096]{2,1,0:T(4,128)(2,1)S(1)} %coarse.11), channel_id=1, source_target_pairs={{4,0},{8,4},{12,8},{16,12},{20,16},{24,20},{28,24},{5,1},{9,5},{13... | collective-permute-start | bytes 983048 | tf_op jit(solution)/shard_map/ppermute | solution.py:435
  57.4 1.1 %coarse.7 = bf16[10,8,2048]{2,1,0:T(8,128)(2,1)S(1)} custom-call(bf16[12,24,64,128]{3,2,1,0:T(8,128)(2,1)S(1)} %left_factor.1.left_ref, bf16[16,64,640]{2,1,0:T(8,128)(2,1)S(1)} %product.2.refs_0_, bf16[8,64,640]{2,1,0:T(8,128)(2,1)S(1)} %product.3.refs_1_), custom_call_target="tpu_custom_call" | custom-call | flops 100000000 | bytes 3700000 | tf_op jit(solution)/shard_map/coarse/pallas_call | solution.py:346
  58.5 1.1 %coarse.6 = bf16[10,8,2048]{2,1,0:T(8,128)(2,1)S(1)} custom-call(bf16[12,24,64,128]{3,2,1,0:T(8,128)(2,1)S(1)} %left_factor.1.left_ref, bf16[16,64,640]{2,1,0:T(8,128)(2,1)S(1)} %product.2.refs_0_, bf16[8,64,640]{2,1,0:T(8,128)(2,1)S(1)} %product.3.refs_1_), custom_call_target="tpu_custom_call" | custom-call | flops 100000000 | bytes 3700000 | tf_op jit(solution)/shard_map/coarse/pallas_call | solution.py:346
  59.6 3.4 %collective-permute-start.12 = (bf16[10,8,2048]{2,1,0:T(8,128)(2,1)S(1)}, bf16[10,8,2048]{2,1,0:T(8,128)(2,1)S(1)}, u32[]{:S(2)}, u32[]{:S(2)}) collective-permute-start(bf16[10,8,2048]{2,1,0:T(8,128)(2,1)S(1)} %coarse.6), channel_id=1, source_target_pairs={{0,4},{4,8},{8,12},{12,16},{16,20},{20,24},{24,28},{1,5},{5,9},{9,... | collective-permute-start | bytes 983048 | tf_op jit(solution)/shard_map/ppermute | solution.py:432
  63.0 1.1 coarse.10
  64.1 1.1 coarse.9
  65.2 0.0 collective-permute-done.9
  65.2 2.9 %collective-permute-start.8 = (bf16[10,8,2048]{2,1,0:T(8,128)(2,1)S(1)}, bf16[10,8,2048]{2,1,0:T(8,128)(2,1)S(1)}, u32[]{:S(2)}, u32[]{:S(2)}) collective-permute-start(bf16[10,8,2048]{2,1,0:T(8,128)(2,1)S(1)} %coarse.7), channel_id=1, source_target_pairs={{0,4},{4,8},{8,12},{12,16},{16,20},{20,24},{24,28},{1,5},{5,9},{9,... | collective-permute-start | bytes 983048 | tf_op jit(solution)/shard_map/ppermute | solution.py:432
  68.1 11.9 %collective-permute-done.10 = bf16[10,4,4096]{2,1,0:T(4,128)(2,1)S(1)} collective-permute-done((bf16[10,4,4096]{2,1,0:T(4,128)(2,1)S(1)}, bf16[10,4,4096]{2,1,0:T(4,128)(2,1)S(1)}, u32[]{:S(2)}, u32[]{:S(2)}) %collective-permute-start.10) | collective-permute-done | bytes 327712 | tf_op jit(solution)/shard_map/ppermute | solution.py:435
  80.0 0.3 pad_maximum_fusion
  80.4 0.0 collective-permute-done.12
  80.4 0.1 add_convert_fusion
  80.5 1.3 %collective-permute-start.14 = (bf16[14,8,2048]{2,1,0:T(8,128)(2,1)S(1)}, bf16[14,8,2048]{2,1,0:T(8,128)(2,1)S(1)}, u32[]{:S(2)}, u32[]{:S(2)}) collective-permute-start(bf16[14,8,2048]{2,1,0:T(8,128)(2,1)S(1)} %bitcast.11), channel_id=1, source_target_pairs={{0,2},{1,3},{2,0},{3,1},{4,6},{5,7},{6,4},{7,5},{8,10},{9,11},{10,... | collective-permute-start | bytes 1376264 | tf_op jit(solution)/shard_map/ppermute | solution.py:426
  81.8 1.8 %collective-permute-start.13 = (bf16[14,8,2048]{2,1,0:T(8,128)(2,1)S(1)}, bf16[14,8,2048]{2,1,0:T(8,128)(2,1)S(1)}, u32[]{:S(2)}, u32[]{:S(2)}) collective-permute-start(bf16[14,8,2048]{2,1,0:T(8,128)(2,1)S(1)} %bitcast.12), channel_id=1, source_target_pairs={{0,1},{1,0},{2,3},{3,2},{4,5},{5,4},{6,7},{7,6},{8,9},{9,8},{10,11... | collective-permute-start | bytes 1376264 | tf_op jit(solution)/shard_map/ppermute | solution.py:429
  83.5 0.0 collective-permute-done.8
  83.5 0.1 add_convert_fusion.1
  83.7 7.4 %collective-permute-done.14.refs_2_ = bf16[14,8,2048]{2,1,0:T(8,128)(2,1)S(1)} collective-permute-done((bf16[14,8,2048]{2,1,0:T(8,128)(2,1)S(1)}, bf16[14,8,2048]{2,1,0:T(8,128)(2,1)S(1)}, u32[]{:S(2)}, u32[]{:S(2)}) %collective-permute-start.14) | collective-permute-done | bytes 458784 | tf_op jit(solution)/shard_map/ppermute | solution.py:426
  91.1 2.4 %collective-permute-start.15 = (bf16[14,8,2048]{2,1,0:T(8,128)(2,1)S(1)}, bf16[14,8,2048]{2,1,0:T(8,128)(2,1)S(1)}, u32[]{:S(2)}, u32[]{:S(2)}) collective-permute-start(bf16[14,8,2048]{2,1,0:T(8,128)(2,1)S(1)} %collective-permute-done.14.refs_2_), channel_id=1, source_target_pairs={{0,1},{1,0},{2,3},{3,2},{4,5},{5,4},{6,7},{7,6},{8,9},{9,8},{10,11... | collective-permute-start | bytes 1376264 | tf_op jit(solution)/shard_map/ppermute | solution.py:429
  93.5 1.2 %collective-permute-start.11 = (bf16[14,8,2048]{2,1,0:T(8,128)(2,1)S(1)}, bf16[14,8,2048]{2,1,0:T(8,128)(2,1)S(1)}, u32[]{:S(2)}, u32[]{:S(2)}) collective-permute-start(bf16[14,8,2048]{2,1,0:T(8,128)(2,1)S(1)} %bitcast.14), channel_id=1, source_target_pairs={{0,2},{1,3},{2,0},{3,1},{4,6},{5,7},{6,4},{7,5},{8,10},{9,11},{10,... | collective-permute-start | bytes 1376264 | tf_op jit(solution)/shard_map/ppermute | solution.py:426
  94.7 0.3 collective-permute-start.16
  95.0 0.0 collective-permute-done.13.refs_1_
  95.0 2.9 %assemble.2.refs_0_ = bf16[8,56,4096]{2,1,0:T(8,128)(2,1)} custom-call(bf16[448,448]{1,0:T(8,128)(2,1)S(1)} %fusion.12.order_ref, bf16[14,8,2048]{2,1,0:T(8,128)(2,1)S(1)} %bitcast.13, bf16[14,8,2048]{2,1,0:T(8,128)(2,1)S(1)} %collective-permute-done.13.refs_1_, bf16[14,8,2048]{2,1,0:T(8,128)(2,1)S(1)} %collective-permute-done.14.refs_2_, ...), custom_call_target="tpu_custom_call" | custom-call | flops 290000000 | bytes 10730000 | tf_op jit(solution)/shard_map/assemble/pallas_call | solution.py:381
  97.9 7.7 %collective-permute-done.11.refs_3_ = bf16[14,8,2048]{2,1,0:T(8,128)(2,1)S(1)} collective-permute-done((bf16[14,8,2048]{2,1,0:T(8,128)(2,1)S(1)}, bf16[14,8,2048]{2,1,0:T(8,128)(2,1)S(1)}, u32[]{:S(2)}, u32[]{:S(2)}) %collective-permute-start.11) | collective-permute-done | bytes 458784 | tf_op jit(solution)/shard_map/ppermute | solution.py:426
  105.6 0.8 collective-permute-start.17
  106.4 1.4 %collective-permute-done.17.refs_4_ = bf16[14,8,2048]{2,1,0:T(8,128)(2,1)S(1)} collective-permute-done((bf16[14,8,2048]{2,1,0:T(8,128)(2,1)S(1)}, bf16[14,8,2048]{2,1,0:T(8,128)(2,1)S(1)}, u32[]{:S(2)}, u32[]{:S(2)}) %collective-permute-start.17) | collective-permute-done | bytes 458784 | tf_op jit(solution)/shard_map/ppermute | solution.py:429
  107.9 2.9 %assemble.3 = bf16[8,56,4096]{2,1,0:T(8,128)(2,1)} custom-call(bf16[448,448]{1,0:T(8,128)(2,1)S(1)} %fusion.12.order_ref, bf16[8,56,4096]{2,1,0:T(8,128)(2,1)} %assemble.2.refs_0_, bf16[14,8,2048]{2,1,0:T(8,128)(2,1)S(1)} %bitcast.16, bf16[14,8,2048]{2,1,0:T(8,128)(2,1)S(1)} %collective-permute-done.16.refs_2_, ...), custom_call_target="tpu_custom_call", output_to_operand_aliasing={{}: (1, {})} | custom-call | flops 290000000 | bytes 10730000 | tf_op jit(solution)/shard_map/assemble/pallas_call | solution.py:381
  (17 shorter events, 0.1 us)
Async XLA Ops:
  0.0 1.4 %copy-start.1 = (bf16[24,8,4096]{2,1,0:T(8,128)(2,1)S(1)}, bf16[24,8,4096]{2,1,0:T(8,128)(2,1)}, u32[]{:S(2)}) copy-start(bf16[24,8,4096]{2,1,0:T(8,128)(2,1)} %x_ref.3) | copy-start | bytes 4718596
  1.4 10.4 %copy-start.6 = (s32[24,32]{1,0:T(8,128)S(1)}, s32[24,32]{1,0:T(8,128)}, u32[]{:S(2)}) copy-start(s32[24,32]{1,0:T(8,128)} %param.6) | copy-start | bytes 9220
  1.4 10.4 %copy-start.7 = (s32[24]{0:T(128)S(1)}, s32[24]{0:T(128)}, u32[]{:S(2)}) copy-start(s32[24]{0:T(128)} %param.7) | copy-start | bytes 292
  1.4 10.5 %copy-start.2 = (bf16[24,8,4096]{2,1,0:T(8,128)(2,1)S(1)}, bf16[24,8,4096]{2,1,0:T(8,128)(2,1)}, u32[]{:S(2)}) copy-start(bf16[24,8,4096]{2,1,0:T(8,128)(2,1)} %x_ref.3) | copy-start | bytes 4718596
  3.4 3.2 %collective-permute-start = (bf16[16,4,64,128]{3,2,1,0:T(8,128)(2,1)}, bf16[16,4,64,128]{3,2,1,0:T(8,128)(2,1)S(1)}, u32[]{:S(2)}, u32[]{:S(2)}) collective-permute-start(bf16[16,4,64,128]{3,2,1,0:T(8,128)(2,1)} %relayout.3.refs_0_), channel_id=1, source_target_pairs={{0,1},{1,0},{2,3},{3,2},{4,5},{5,4},{6,7},{7,6},{8,9},{9,8},{10,11... | collective-permute-start | bytes 3145736 | tf_op jit(solution)/shard_map/ppermute | solution.py:429
  4.1 25.1 %collective-permute-start.2 = (bf16[16,4,64,128]{3,2,1,0:T(8,128)(2,1)}, bf16[16,4,64,128]{3,2,1,0:T(8,128)(2,1)}, u32[]{:S(2)}, u32[]{:S(2)}) collective-permute-start(bf16[16,4,64,128]{3,2,1,0:T(8,128)(2,1)} %relayout.3.refs_0_), channel_id=1, source_target_pairs={{0,2},{1,3},{2,0},{3,1},{4,6},{5,7},{6,4},{7,5},{8,10},{9,11},{10,... | collective-permute-start | bytes 3145736 | tf_op jit(solution)/shard_map/ppermute | solution.py:426
  6.6 1.1 %copy-start.3 = (bf16[24,4,4096]{2,1,0:T(4,128)(2,1)S(1)}, bf16[24,4,4096]{2,1,0:T(4,128)(2,1)}, u32[]{:S(2)}) copy-start(bf16[24,4,4096]{2,1,0:T(4,128)(2,1)} %x_ref.4) | copy-start | bytes 2359300
  8.8 21.2 %collective-permute-start.1 = (bf16[24,2,64,128]{3,2,1,0:T(8,128)(2,1)S(1)}, bf16[24,2,64,128]{3,2,1,0:T(8,128)(2,1)S(1)}, u32[]{:S(2)}, u32[]{:S(2)}) collective-permute-start(bf16[24,2,64,128]{3,2,1,0:T(8,128)(2,1)S(1)} %relayout_rows.1.refs_0_), channel_id=1, source_target_pairs={{0,4},{2,6},{4,8},{5,1},{6,10},{7,3},{8,12},{9,5},{10,14},{11,7},{... | collective-permute-start | bytes 2359304 | tf_op jit(solution)/shard_map/ppermute | solution.py:423
  12.3 7.8 %collective-permute-start.3 = (bf16[8,4,64,128]{3,2,1,0:T(8,128)(2,1)S(1)}, bf16[8,4,64,128]{3,2,1,0:T(8,128)(2,1)S(1)}, u32[]{:S(2)}, u32[]{:S(2)}) collective-permute-start(bf16[8,4,64,128]{3,2,1,0:T(8,128)(2,1)S(1)} %relayout.4.refs_0_), channel_id=1, source_target_pairs={{0,1},{1,0},{2,3},{3,2},{4,5},{5,4},{6,7},{7,6},{8,9},{9,8},{10,11... | collective-permute-start | bytes 1572872 | tf_op jit(solution)/shard_map/ppermute | solution.py:429
  13.3 6.8 %copy-start.4 = (bf16[24,4,4096]{2,1,0:T(4,128)(2,1)S(1)}, bf16[24,4,4096]{2,1,0:T(4,128)(2,1)}, u32[]{:S(2)}) copy-start(bf16[24,4,4096]{2,1,0:T(4,128)(2,1)} %x_ref.4) | copy-start | bytes 2359300
  17.3 2.9 %copy-start = (bf16[4,27,256,128]{3,2,1,0:T(8,128)(2,1)}, bf16[4,27,256,128]{3,2,1,0:T(8,128)(2,1)S(1)}, u32[]{:S(2)}) copy-start(bf16[4,27,256,128]{3,2,1,0:T(8,128)(2,1)S(1)} %near_band.2.start_ref) | copy-start | bytes 21233668
  21.0 3.5 %copy-start.5 = (s32[192,4]{0,1:T(4,128)S(1)}, s32[192,4]{0,1:T(4,128)}, u32[]{:S(2)}) copy-start(s32[192,4]{0,1:T(4,128)} %param.9) | copy-start | bytes 9220
  29.9 6.1 %collective-permute-start.6 = (bf16[16,4,64,128]{3,2,1,0:T(8,128)(2,1)}, bf16[16,4,64,128]{3,2,1,0:T(8,128)(2,1)S(1)}, u32[]{:S(2)}, u32[]{:S(2)}) collective-permute-start(bf16[16,4,64,128]{3,2,1,0:T(8,128)(2,1)} %collective-permute-done.2.refs_0_), channel_id=1, source_target_pairs={{0,1},{1,0},{2,3},{3,2},{4,5},{5,4},{6,7},{7,6},{8,9},{9,8},{10,11... | collective-permute-start | bytes 3145736 | tf_op jit(solution)/shard_map/ppermute | solution.py:429
  30.5 3.3 %collective-permute-start.5 = (bf16[24,2,64,128]{3,2,1,0:T(8,128)(2,1)S(1)}, bf16[24,2,64,128]{3,2,1,0:T(8,128)(2,1)S(1)}, u32[]{:S(2)}, u32[]{:S(2)}) collective-permute-start(bf16[24,2,64,128]{3,2,1,0:T(8,128)(2,1)S(1)} %collective-permute-done.1.refs_0_), channel_id=1, source_target_pairs={{0,1},{1,0},{2,3},{3,2},{4,5},{5,4},{6,7},{7,6},{8,9},{9,8},{10,11... | collective-permute-start | bytes 2359304 | tf_op jit(solution)/shard_map/ppermute | solution.py:429
  30.5 14.7 %collective-permute-start.4 = (bf16[8,4,64,128]{3,2,1,0:T(8,128)(2,1)S(1)}, bf16[8,4,64,128]{3,2,1,0:T(8,128)(2,1)S(1)}, u32[]{:S(2)}, u32[]{:S(2)}) collective-permute-start(bf16[8,4,64,128]{3,2,1,0:T(8,128)(2,1)S(1)} %relayout.4.refs_0_), channel_id=1, source_target_pairs={{0,2},{1,3},{2,0},{3,1},{4,6},{5,7},{6,4},{7,5},{8,10},{9,11},{10,... | collective-permute-start | bytes 1572872 | tf_op jit(solution)/shard_map/ppermute | solution.py:426
  45.2 5.4 %collective-permute-start.7 = (bf16[8,4,64,128]{3,2,1,0:T(8,128)(2,1)S(1)}, bf16[8,4,64,128]{3,2,1,0:T(8,128)(2,1)S(1)}, u32[]{:S(2)}, u32[]{:S(2)}) collective-permute-start(bf16[8,4,64,128]{3,2,1,0:T(8,128)(2,1)S(1)} %collective-permute-done.4.refs_0_), channel_id=1, source_target_pairs={{0,1},{1,0},{2,3},{3,2},{4,5},{5,4},{6,7},{7,6},{8,9},{9,8},{10,11... | collective-permute-start | bytes 1572872 | tf_op jit(solution)/shard_map/ppermute | solution.py:429
  46.3 18.8 %collective-permute-start.9 = (bf16[10,4,4096]{2,1,0:T(4,128)(2,1)S(1)}, bf16[10,4,4096]{2,1,0:T(4,128)(2,1)S(1)}, u32[]{:S(2)}, u32[]{:S(2)}) collective-permute-start(bf16[10,4,4096]{2,1,0:T(4,128)(2,1)S(1)} %coarse.8), channel_id=1, source_target_pairs={{4,0},{8,4},{12,8},{16,12},{20,16},{24,20},{28,24},{5,1},{9,5},{13... | collective-permute-start | bytes 983048 | tf_op jit(solution)/shard_map/ppermute | solution.py:435
  55.5 24.6 %collective-permute-start.10 = (bf16[10,4,4096]{2,1,0:T(4,128)(2,1)S(1)}, bf16[10,4,4096]{2,1,0:T(4,128)(2,1)S(1)}, u32[]{:S(2)}, u32[]{:S(2)}) collective-permute-start(bf16[10,4,4096]{2,1,0:T(4,128)(2,1)S(1)} %coarse.11), channel_id=1, source_target_pairs={{4,0},{8,4},{12,8},{16,12},{20,16},{24,20},{28,24},{5,1},{9,5},{13... | collective-permute-start | bytes 983048 | tf_op jit(solution)/shard_map/ppermute | solution.py:435
  59.6 20.7 %collective-permute-start.12 = (bf16[10,8,2048]{2,1,0:T(8,128)(2,1)S(1)}, bf16[10,8,2048]{2,1,0:T(8,128)(2,1)S(1)}, u32[]{:S(2)}, u32[]{:S(2)}) collective-permute-start(bf16[10,8,2048]{2,1,0:T(8,128)(2,1)S(1)} %coarse.6), channel_id=1, source_target_pairs={{0,4},{4,8},{8,12},{12,16},{16,20},{20,24},{24,28},{1,5},{5,9},{9,... | collective-permute-start | bytes 983048 | tf_op jit(solution)/shard_map/ppermute | solution.py:432
  65.2 18.4 %collective-permute-start.8 = (bf16[10,8,2048]{2,1,0:T(8,128)(2,1)S(1)}, bf16[10,8,2048]{2,1,0:T(8,128)(2,1)S(1)}, u32[]{:S(2)}, u32[]{:S(2)}) collective-permute-start(bf16[10,8,2048]{2,1,0:T(8,128)(2,1)S(1)} %coarse.7), channel_id=1, source_target_pairs={{0,4},{4,8},{8,12},{12,16},{16,20},{20,24},{24,28},{1,5},{5,9},{9,... | collective-permute-start | bytes 983048 | tf_op jit(solution)/shard_map/ppermute | solution.py:432
  80.5 10.6 %collective-permute-start.14 = (bf16[14,8,2048]{2,1,0:T(8,128)(2,1)S(1)}, bf16[14,8,2048]{2,1,0:T(8,128)(2,1)S(1)}, u32[]{:S(2)}, u32[]{:S(2)}) collective-permute-start(bf16[14,8,2048]{2,1,0:T(8,128)(2,1)S(1)} %bitcast.11), channel_id=1, source_target_pairs={{0,2},{1,3},{2,0},{3,1},{4,6},{5,7},{6,4},{7,5},{8,10},{9,11},{10,... | collective-permute-start | bytes 1376264 | tf_op jit(solution)/shard_map/ppermute | solution.py:426
  81.8 13.2 %collective-permute-start.13 = (bf16[14,8,2048]{2,1,0:T(8,128)(2,1)S(1)}, bf16[14,8,2048]{2,1,0:T(8,128)(2,1)S(1)}, u32[]{:S(2)}, u32[]{:S(2)}) collective-permute-start(bf16[14,8,2048]{2,1,0:T(8,128)(2,1)S(1)} %bitcast.12), channel_id=1, source_target_pairs={{0,1},{1,0},{2,3},{3,2},{4,5},{5,4},{6,7},{7,6},{8,9},{9,8},{10,11... | collective-permute-start | bytes 1376264 | tf_op jit(solution)/shard_map/ppermute | solution.py:429
  91.1 3.9 %collective-permute-start.15 = (bf16[14,8,2048]{2,1,0:T(8,128)(2,1)S(1)}, bf16[14,8,2048]{2,1,0:T(8,128)(2,1)S(1)}, u32[]{:S(2)}, u32[]{:S(2)}) collective-permute-start(bf16[14,8,2048]{2,1,0:T(8,128)(2,1)S(1)} %collective-permute-done.14.refs_2_), channel_id=1, source_target_pairs={{0,1},{1,0},{2,3},{3,2},{4,5},{5,4},{6,7},{7,6},{8,9},{9,8},{10,11... | collective-permute-start | bytes 1376264 | tf_op jit(solution)/shard_map/ppermute | solution.py:429
  93.5 12.2 %collective-permute-start.11 = (bf16[14,8,2048]{2,1,0:T(8,128)(2,1)S(1)}, bf16[14,8,2048]{2,1,0:T(8,128)(2,1)S(1)}, u32[]{:S(2)}, u32[]{:S(2)}) collective-permute-start(bf16[14,8,2048]{2,1,0:T(8,128)(2,1)S(1)} %bitcast.14), channel_id=1, source_target_pairs={{0,2},{1,3},{2,0},{3,1},{4,6},{5,7},{6,4},{7,5},{8,10},{9,11},{10,... | collective-permute-start | bytes 1376264 | tf_op jit(solution)/shard_map/ppermute | solution.py:426
  94.7 11.7 %collective-permute-start.16 = (bf16[14,8,2048]{2,1,0:T(8,128)(2,1)S(1)}, bf16[14,8,2048]{2,1,0:T(8,128)(2,1)S(1)}, u32[]{:S(2)}, u32[]{:S(2)}) collective-permute-start(bf16[14,8,2048]{2,1,0:T(8,128)(2,1)S(1)} %bitcast.15), channel_id=1, source_target_pairs={{0,1},{1,0},{2,3},{3,2},{4,5},{5,4},{6,7},{7,6},{8,9},{9,8},{10,11... | collective-permute-start | bytes 1376264 | tf_op jit(solution)/shard_map/ppermute | solution.py:429
  105.6 2.2 %collective-permute-start.17 = (bf16[14,8,2048]{2,1,0:T(8,128)(2,1)S(1)}, bf16[14,8,2048]{2,1,0:T(8,128)(2,1)S(1)}, u32[]{:S(2)}, u32[]{:S(2)}) collective-permute-start(bf16[14,8,2048]{2,1,0:T(8,128)(2,1)S(1)} %collective-permute-done.11.refs_3_), channel_id=1, source_target_pairs={{0,1},{1,0},{2,3},{3,2},{4,5},{5,4},{6,7},{7,6},{8,9},{9,8},{10,11... | collective-permute-start | bytes 1376264 | tf_op jit(solution)/shard_map/ppermute | solution.py:429

commit v6 on v5

--- a/solution.py
+++ b/solution.py
@@ -120,7 +120,7 @@
         out_shape=jax.ShapeDtypeStruct((rb // 2, 3 * CB, BS, LANES), BF),
         in_specs=[SM, VM],
         out_specs=VM,
-        compiler_params=params(24),
+        compiler_params=params(12),
         cost_estimate=cost(2.9),
         name="left_factor",
     )(pct, p_own)
@@ -188,7 +188,7 @@
         out_shape=jax.ShapeDtypeStruct((len(srcs) * rb // 4, tiles, 4 * BS, LANES), BF),
         in_specs=[SM] + [VM] * len(srcs),
         out_specs=VM,
-        compiler_params=params(16),
+        compiler_params=params(8),
         cost_estimate=cost(us),
         name="right_factor",
     )(table, *srcs)
@@ -257,7 +257,7 @@
         out_shape=jax.ShapeDtypeStruct((rows // 4, place.shape[0] + 3, 4 * BS, LANES), BF),
         in_specs=[SM] + [VM] * len(srcs),
         out_specs=VM,
-        compiler_params=params(24),
+        compiler_params=params(12),
         cost_estimate=cost(0.16 * rows),
         name="near_band",
     )(place, *srcs)
@@ -305,7 +305,7 @@
             pltpu.VMEM(start.shape, BF),
             pltpu.VMEM((4 * BS, tiles * LANES), F32),
         ],
-        compiler_params=params(40),
+        compiler_params=params(16),
         cost_estimate=cost(us),
         name="product",
     )(place, own, near, start, *srcs)
@@ -349,7 +349,7 @@
         in_specs=[VM] * (1 + len(aps)),
         out_specs=[VM] * len(sets),
         scratch_shapes=[pltpu.VMEM((tiles, max(i1 - i0 for i0, i1 in sets) * (a1 - a0), LANES), F32)],
-        compiler_params=params(32),
+        compiler_params=params(12),
         cost_estimate=cost(us),
         name="coarse",
     )(left, *aps)
@@ -385,7 +385,7 @@
         in_specs=specs,
         out_specs=pl.BlockSpec((CB, wide, step), lambda i: (0, 0, a0 * BS // step + i)),
         input_output_aliases=alias,
-        compiler_params=params(24),
+        compiler_params=params(12),
         cost_estimate=cost(2.9),
         name="assemble",
     )(*args, *srcs)
@@ -471,6 +471,7 @@
     late = downward(coarse_rows(left, aps, ((CB // 2, CB),), 0, BS, BF, 1.0)[0])
     highs = [coarse_rows(left, aps, ((2 * CB, 3 * CB),), a0, a1, BF, 1.0)[0] for a0, a1 in chunks]
     left, highs = lax.optimization_barrier((left, highs))
+    highs[1], late = lax.optimization_barrier((highs[1], late))
     highs = [upward(x) for x in highs]
     mids = [coarse_rows(left, aps, ((CB, 2 * CB),), a0, a1, F32, 1.0)[0] for a0, a1 in chunks]
     early, mids = lax.optimization_barrier((early, mids))

time: 111 us -> 106 us (0.955); the launches traced: 111 us -> 104 us
  Pallas kernels: 42 us -> 38.8 us
  local copies, waits for them, and re-layouts: 5.42 us -> 2.56 us
    ppermute x2, waiting for transfers between devices: 0.01 us -> 5.84 us  [upward(): return lax.ppermute(x, 'row', [(i, i + 1) for i in range(nrow - 1)])]
    ppermute x2, waiting for transfers between devices: 11.9 us -> 8.22 us  [downward(): return lax.ppermute(x, 'row', [(i + 1, i) for i in range(nrow - 1)])]
    unnamed x16 -> x14, local copies, waits for them, and re-layouts: 5.42 us -> 2.56 us
    ppermute x4, waiting for transfers between devices: 16.9 us -> 14.8 us  [over_y(): lax.ppermute(x, 'col', [(y * 2 + c, (y + s) % ny * 2 + c) for y in range(...]
    pallas_call x2, Pallas kernels: 12.9 us -> 10.9 us  [product(): pl.pallas_call(functools.partial(product_kernel, first, rb, shifts), out_...]
    pallas_call x3, Pallas kernels: 3.24 us -> 2.06 us  [relayout(): pl.pallas_call(relayout_kernel, grid=(rows // step,), out_shape=jax.Shape...]
  transfers between devices with their start and end apart: 18 -> 18, of which waited for: 8 -> 10; matrix products, arithmetic and copies ran while one was open for 1% -> 2% of each run, Pallas kernels for 34% -> 34%
where the time goes in v6:
time: 106 us; the launch traced here: 104 us
  Pallas kernels  38.8 us (37%)
  waiting for transfers between devices  33.6 us (32%)
  starting transfers between devices  27.4 us (26%)
  local copies, waits for them, and re-layouts  2.56 us (2%)
  other arithmetic  1.57 us (1%)
    ppermute x4, waiting for transfers between devices, over_y(): lax.ppermute(x, 'col', [(y * 2 + c, (y + s) % ny * 2 + c) for y in range(...  14.8 us
    pallas_call x2, Pallas kernels, product(): pl.pallas_call(functools.partial(product_kernel, first, rb, shifts), out_...  10.9 us
    ppermute x2, waiting for transfers between devices, downward(): return lax.ppermute(x, 'row', [(i + 1, i) for i in range(nrow - 1)])  8.22 us
    ppermute x9, starting transfers between devices, over_core(): return lax.ppermute(x, 'col', [(c, c ^ 1) for c in range(ncol)])  7.94 us
    pallas_call x6, Pallas kernels, coarse_rows(): pl.pallas_call(functools.partial(coarse_kernel, sets, a0, a1), out_shape=...  6.48 us
    ppermute x2, starting transfers between devices, downward(): return lax.ppermute(x, 'row', [(i + 1, i) for i in range(nrow - 1)])  6.1 us
    pallas_call x2, Pallas kernels, near_band(): pl.pallas_call(functools.partial(band_kernel, first, shifts), out_shape=j...  5.98 us
    ppermute x2, waiting for transfers between devices, upward(): return lax.ppermute(x, 'row', [(i, i + 1) for i in range(nrow - 1)])  5.84 us
  transfers between devices with their start and end apart: 18, of which 10 were waited for; matrix products, arithmetic and copies ran while one was open for 2% of the time, Pallas kernels for 34%

profile of v6, /device:TPU:9, one launch (start us, length us, event | category | flops | bytes accessed | tf_op | source)
XLA Modules:
  0.0 104.2 jit_solution(17378663341464618555)
XLA Ops:
  0.0 1.4 %copy-done = bf16[24,8,4096]{2,1,0:T(8,128)(2,1)S(1)} copy-done((bf16[24,8,4096]{2,1,0:T(8,128)(2,1)S(1)}, bf16[24,8,4096]{2,1,0:T(8,128)(2,1)}, u32[]{:S(2)}) %copy-start) | copy-done | bytes 1572888
  1.4 0.8 relayout.3.refs_0_
  2.2 0.7 collective-permute-start
  3.0 1.3 %collective-permute-start.2 = (bf16[16,4,64,128]{3,2,1,0:T(8,128)(2,1)S(1)}, bf16[16,4,64,128]{3,2,1,0:T(8,128)(2,1)}, u32[]{:S(2)}, u32[]{:S(2)}) collective-permute-start(bf16[16,4,64,128]{3,2,1,0:T(8,128)(2,1)S(1)} %relayout.3.refs_0_), channel_id=1, source_target_pairs={{0,2},{1,3},{2,0},{3,1},{4,6},{5,7},{6,4},{7,5},{8,10},{9,11},{10,... | collective-permute-start | bytes 3145736 | tf_op jit(solution)/shard_map/ppermute | solution.py:426
  4.2 0.8 add_select_fusion.4.table_ref
  5.0 0.3 collective-permute-done.refs_1_
  5.4 1.1 %copy-done.2 = bf16[24,4,4096]{2,1,0:T(4,128)(2,1)S(1)} copy-done((bf16[24,4,4096]{2,1,0:T(4,128)(2,1)S(1)}, bf16[24,4,4096]{2,1,0:T(4,128)(2,1)}, u32[]{:S(2)}) %copy-start.2) | copy-done | bytes 786456
  6.5 1.1 %relayout_rows.1.refs_0_ = bf16[24,2,64,128]{3,2,1,0:T(8,128)(2,1)S(1)} custom-call(bf16[24,4,4096]{2,1,0:T(4,128)(2,1)S(1)} %copy-done.2), custom_call_target="tpu_custom_call" | custom-call | flops 100000000 | bytes 3700000 | tf_op jit(solution)/shard_map/relayout_rows/pallas_call | solution.py:84
  7.6 3.0 %collective-permute-start.1 = (bf16[24,2,64,128]{3,2,1,0:T(8,128)(2,1)S(1)}, bf16[24,2,64,128]{3,2,1,0:T(8,128)(2,1)S(1)}, u32[]{:S(2)}, u32[]{:S(2)}) collective-permute-start(bf16[24,2,64,128]{3,2,1,0:T(8,128)(2,1)S(1)} %relayout_rows.1.refs_0_), channel_id=1, source_target_pairs={{0,4},{2,6},{4,8},{5,1},{6,10},{7,3},{8,12},{9,5},{10,14},{11,7},{... | collective-permute-start | bytes 2359304 | tf_op jit(solution)/shard_map/ppermute | solution.py:423
  10.6 0.1 subtract_select_fusion.place_ref
  10.7 0.4 relayout.4.refs_0_
  11.1 0.8 collective-permute-start.3
  11.9 0.2 fusion.12.order_ref
  12.1 0.0 copy-start.3
  12.1 3.9 %near_band.2.start_ref = bf16[4,27,256,128]{3,2,1,0:T(8,128)(2,1)S(1)} custom-call(s32[24,32]{1,0:T(8,128)S(1)} %subtract_select_fusion.place_ref, bf16[16,4,64,128]{3,2,1,0:T(8,128)(2,1)S(1)} %relayout.3.refs_0_, bf16[16,4,64,128]{3,2,1,0:T(8,128)(2,1)} %collective-permute-done.refs_1_), custom_call_target="tpu_custom_call" | custom-call | flops 256000000 | bytes 9472000 | tf_op jit(solution)/shard_map/near_band/pallas_call | solution.py:255
  16.1 0.0 collective-permute-done.3.refs_1_
  16.1 0.9 relayout.5.pl_ref
  17.0 0.0 copy-start.4
  17.0 2.1 %near_band.3.start_ref = bf16[2,27,256,128]{3,2,1,0:T(8,128)(2,1)S(1)} custom-call(s32[24,32]{1,0:T(8,128)S(1)} %subtract_select_fusion.place_ref, bf16[8,4,64,128]{3,2,1,0:T(8,128)(2,1)S(1)} %relayout.4.refs_0_, bf16[8,4,64,128]{3,2,1,0:T(8,128)(2,1)S(1)} %collective-permute-done.3.refs_1_), custom_call_target="tpu_custom_call" | custom-call | flops 128000000 | bytes 4736000 | tf_op jit(solution)/shard_map/near_band/pallas_call | solution.py:255
  19.0 1.4 %right_factor.2.own_ref = bf16[6,5,256,128]{3,2,1,0:T(8,128)(2,1)S(1)} custom-call(s32[4,72]{1,0:T(4,128)S(1)} %add_select_fusion.4.table_ref, bf16[24,2,64,128]{3,2,1,0:T(8,128)(2,1)S(1)} %relayout_rows.1.refs_0_), custom_call_target="tpu_custom_call" | custom-call | flops 200000000 | bytes 7400000 | tf_op jit(solution)/shard_map/right_factor/pallas_call | solution.py:186
  20.5 2.9 %left_factor.1.left_ref = bf16[12,24,64,128]{3,2,1,0:T(8,128)(2,1)S(1)} custom-call(s32[4,192]{1,0:T(4,128)S(1)} %bitcast.18, bf16[24,2,64,128]{3,2,1,0:T(8,128)(2,1)S(1)} %relayout.5.pl_ref), custom_call_target="tpu_custom_call" | custom-call | flops 290000000 | bytes 10730000 | tf_op jit(solution)/shard_map/left_factor/pallas_call | solution.py:118
  23.4 4.4 %collective-permute-done.2.refs_0_ = bf16[16,4,64,128]{3,2,1,0:T(8,128)(2,1)} collective-permute-done((bf16[16,4,64,128]{3,2,1,0:T(8,128)(2,1)S(1)}, bf16[16,4,64,128]{3,2,1,0:T(8,128)(2,1)}, u32[]{:S(2)}, u32[]{:S(2)}) %collective-permute-start.2) | collective-permute-done | bytes 1048608 | tf_op jit(solution)/shard_map/ppermute | solution.py:426
  27.8 0.9 collective-permute-done.1.refs_0_
  28.7 0.5 collective-permute-start.6
  29.3 0.0 collective-permute-start.5
  29.3 1.2 %collective-permute-start.4 = (bf16[8,4,64,128]{3,2,1,0:T(8,128)(2,1)S(1)}, bf16[8,4,64,128]{3,2,1,0:T(8,128)(2,1)S(1)}, u32[]{:S(2)}, u32[]{:S(2)}) collective-permute-start(bf16[8,4,64,128]{3,2,1,0:T(8,128)(2,1)S(1)} %relayout.4.refs_0_), channel_id=1, source_target_pairs={{0,2},{1,3},{2,0},{3,1},{4,6},{5,7},{6,4},{7,5},{8,10},{9,11},{10,... | collective-permute-start | bytes 1572872 | tf_op jit(solution)/shard_map/ppermute | solution.py:426
  30.5 2.0 %collective-permute-done.5.refs_1_ = bf16[24,2,64,128]{3,2,1,0:T(8,128)(2,1)S(1)} collective-permute-done((bf16[24,2,64,128]{3,2,1,0:T(8,128)(2,1)S(1)}, bf16[24,2,64,128]{3,2,1,0:T(8,128)(2,1)S(1)}, u32[]{:S(2)}, u32[]{:S(2)}) %collective-permute-start.5) | collective-permute-done | bytes 786464 | tf_op jit(solution)/shard_map/ppermute | solution.py:429
  32.5 2.3 %right_factor.3.near_ref = bf16[12,5,256,128]{3,2,1,0:T(8,128)(2,1)S(1)} custom-call(s32[4,72]{1,0:T(4,128)S(1)} %add_select_fusion.4.table_ref, bf16[24,2,64,128]{3,2,1,0:T(8,128)(2,1)S(1)} %collective-permute-done.1.refs_0_, bf16[24,2,64,128]{3,2,1,0:T(8,128)(2,1)S(1)} %collective-permute-done.5.refs_1_), custom_call_target="tpu_custom_call" | custom-call | flops 300000000 | bytes 11100000 | tf_op jit(solution)/shard_map/right_factor/pallas_call | solution.py:186
  34.8 0.0 collective-permute-done.6.refs_1_
  34.8 7.1 %product.2.refs_0_ = bf16[16,64,640]{2,1,0:T(8,128)(2,1)S(1)} custom-call(s32[24,32]{1,0:T(8,128)S(1)} %subtract_select_fusion.place_ref, bf16[6,5,256,128]{3,2,1,0:T(8,128)(2,1)S(1)} %right_factor.2.own_ref, bf16[12,5,256,128]{3,2,1,0:T(8,128)(2,1)S(1)} %right_factor.3.near_ref, bf16[4,27,256,128]{3,2,1,0:T(8,128)(2,1)S(1)} %near_band.2.start_ref, ...), custom_call_target="tpu_custom_call" | custom-call | flops 480000000 | bytes 17760000 | tf_op jit(solution)/shard_map/product/pallas_call | solution.py:299
  42.0 0.3 collective-permute-done.4.refs_0_
  42.2 1.4 %collective-permute-start.7 = (bf16[8,4,64,128]{3,2,1,0:T(8,128)(2,1)S(1)}, bf16[8,4,64,128]{3,2,1,0:T(8,128)(2,1)S(1)}, u32[]{:S(2)}, u32[]{:S(2)}) collective-permute-start(bf16[8,4,64,128]{3,2,1,0:T(8,128)(2,1)S(1)} %collective-permute-done.4.refs_0_), channel_id=1, source_target_pairs={{0,1},{1,0},{2,3},{3,2},{4,5},{5,4},{6,7},{7,6},{8,9},{9,8},{10,11... | collective-permute-start | bytes 1572872 | tf_op jit(solution)/shard_map/ppermute | solution.py:429
  43.6 0.9 coarse.9
  44.6 4.2 %collective-permute-start.10 = (bf16[10,4,4096]{2,1,0:T(4,128)(2,1)S(1)}, bf16[10,4,4096]{2,1,0:T(4,128)(2,1)S(1)}, u32[]{:S(2)}, u32[]{:S(2)}) collective-permute-start(bf16[10,4,4096]{2,1,0:T(4,128)(2,1)S(1)} %coarse.9), channel_id=1, source_target_pairs={{4,0},{8,4},{12,8},{16,12},{20,16},{24,20},{28,24},{5,1},{9,5},{13... | collective-permute-start | bytes 983048 | tf_op jit(solution)/shard_map/ppermute | solution.py:435
  48.7 0.0 collective-permute-done.7.refs_1_
  48.7 3.8 %product.3.refs_1_ = bf16[8,64,640]{2,1,0:T(8,128)(2,1)S(1)} custom-call(s32[24,32]{1,0:T(8,128)S(1)} %subtract_select_fusion.place_ref, bf16[6,5,256,128]{3,2,1,0:T(8,128)(2,1)S(1)} %right_factor.2.own_ref, bf16[12,5,256,128]{3,2,1,0:T(8,128)(2,1)S(1)} %right_factor.3.near_ref, bf16[2,27,256,128]{3,2,1,0:T(8,128)(2,1)S(1)} %near_band.3.start_ref, ...), custom_call_target="tpu_custom_call" | custom-call | flops 240000000 | bytes 8880000 | tf_op jit(solution)/shard_map/product/pallas_call | solution.py:299
  52.5 1.1 %coarse.8 = bf16[10,4,4096]{2,1,0:T(4,128)(2,1)S(1)} custom-call(bf16[12,24,64,128]{3,2,1,0:T(8,128)(2,1)S(1)} %left_factor.1.left_ref, bf16[16,64,640]{2,1,0:T(8,128)(2,1)S(1)} %product.2.refs_0_, bf16[8,64,640]{2,1,0:T(8,128)(2,1)S(1)} %product.3.refs_1_), custom_call_target="tpu_custom_call" | custom-call | flops 100000000 | bytes 3700000 | tf_op jit(solution)/shard_map/coarse/pallas_call | solution.py:346
  53.7 1.9 %collective-permute-start.8 = (bf16[10,4,4096]{2,1,0:T(4,128)(2,1)S(1)}, bf16[10,4,4096]{2,1,0:T(4,128)(2,1)S(1)}, u32[]{:S(2)}, u32[]{:S(2)}) collective-permute-start(bf16[10,4,4096]{2,1,0:T(4,128)(2,1)S(1)} %coarse.8), channel_id=1, source_target_pairs={{4,0},{8,4},{12,8},{16,12},{20,16},{24,20},{28,24},{5,1},{9,5},{13... | collective-permute-start | bytes 983048 | tf_op jit(solution)/shard_map/ppermute | solution.py:435
  55.6 1.1 %coarse.7 = bf16[10,8,2048]{2,1,0:T(8,128)(2,1)S(1)} custom-call(bf16[12,24,64,128]{3,2,1,0:T(8,128)(2,1)S(1)} %left_factor.1.left_ref, bf16[16,64,640]{2,1,0:T(8,128)(2,1)S(1)} %product.2.refs_0_, bf16[8,64,640]{2,1,0:T(8,128)(2,1)S(1)} %product.3.refs_1_), custom_call_target="tpu_custom_call" | custom-call | flops 100000000 | bytes 3700000 | tf_op jit(solution)/shard_map/coarse/pallas_call | solution.py:346
  56.7 1.1 %coarse.6 = bf16[10,8,2048]{2,1,0:T(8,128)(2,1)S(1)} custom-call(bf16[12,24,64,128]{3,2,1,0:T(8,128)(2,1)S(1)} %left_factor.1.left_ref, bf16[16,64,640]{2,1,0:T(8,128)(2,1)S(1)} %product.2.refs_0_, bf16[8,64,640]{2,1,0:T(8,128)(2,1)S(1)} %product.3.refs_1_), custom_call_target="tpu_custom_call" | custom-call | flops 100000000 | bytes 3700000 | tf_op jit(solution)/shard_map/coarse/pallas_call | solution.py:346
  57.8 3.4 %collective-permute-start.12 = (bf16[10,8,2048]{2,1,0:T(8,128)(2,1)S(1)}, bf16[10,8,2048]{2,1,0:T(8,128)(2,1)S(1)}, u32[]{:S(2)}, u32[]{:S(2)}) collective-permute-start(bf16[10,8,2048]{2,1,0:T(8,128)(2,1)S(1)} %coarse.6), channel_id=1, source_target_pairs={{0,4},{4,8},{8,12},{12,16},{16,20},{20,24},{24,28},{1,5},{5,9},{9,... | collective-permute-start | bytes 983048 | tf_op jit(solution)/shard_map/ppermute | solution.py:432
  61.2 1.1 %coarse.11 = f32[10,8,2048]{2,1,0:T(8,128)S(1)} custom-call(bf16[12,24,64,128]{3,2,1,0:T(8,128)(2,1)S(1)} %left_factor.1.left_ref, bf16[16,64,640]{2,1,0:T(8,128)(2,1)S(1)} %product.2.refs_0_, bf16[8,64,640]{2,1,0:T(8,128)(2,1)S(1)} %product.3.refs_1_), custom_call_target="tpu_custom_call" | custom-call | flops 100000000 | bytes 3700000 | tf_op jit(solution)/shard_map/coarse/pallas_call | solution.py:346
  62.3 1.1 %coarse.10 = f32[10,8,2048]{2,1,0:T(8,128)S(1)} custom-call(bf16[12,24,64,128]{3,2,1,0:T(8,128)(2,1)S(1)} %left_factor.1.left_ref, bf16[16,64,640]{2,1,0:T(8,128)(2,1)S(1)} %product.2.refs_0_, bf16[8,64,640]{2,1,0:T(8,128)(2,1)S(1)} %product.3.refs_1_), custom_call_target="tpu_custom_call" | custom-call | flops 100000000 | bytes 3700000 | tf_op jit(solution)/shard_map/coarse/pallas_call | solution.py:346
  63.4 0.0 collective-permute-done.10
  63.4 8.2 %collective-permute-done.8 = bf16[10,4,4096]{2,1,0:T(4,128)(2,1)S(1)} collective-permute-done((bf16[10,4,4096]{2,1,0:T(4,128)(2,1)S(1)}, bf16[10,4,4096]{2,1,0:T(4,128)(2,1)S(1)}, u32[]{:S(2)}, u32[]{:S(2)}) %collective-permute-start.8) | collective-permute-done | bytes 327712 | tf_op jit(solution)/shard_map/ppermute | solution.py:435
  71.6 1.9 %collective-permute-start.9 = (bf16[10,8,2048]{2,1,0:T(8,128)(2,1)S(1)}, bf16[10,8,2048]{2,1,0:T(8,128)(2,1)S(1)}, u32[]{:S(2)}, u32[]{:S(2)}) collective-permute-start(bf16[10,8,2048]{2,1,0:T(8,128)(2,1)S(1)} %coarse.7), channel_id=1, source_target_pairs={{0,4},{4,8},{8,12},{12,16},{16,20},{20,24},{24,28},{1,5},{5,9},{9,... | collective-permute-start | bytes 983048 | tf_op jit(solution)/shard_map/ppermute | solution.py:432
  73.5 0.3 pad_maximum_fusion
  73.9 0.0 collective-permute-done.12
  73.9 0.1 add_convert_fusion
  74.0 1.3 %collective-permute-start.14 = (bf16[14,8,2048]{2,1,0:T(8,128)(2,1)S(1)}, bf16[14,8,2048]{2,1,0:T(8,128)(2,1)S(1)}, u32[]{:S(2)}, u32[]{:S(2)}) collective-permute-start(bf16[14,8,2048]{2,1,0:T(8,128)(2,1)S(1)} %bitcast.11), channel_id=1, source_target_pairs={{0,2},{1,3},{2,0},{3,1},{4,6},{5,7},{6,4},{7,5},{8,10},{9,11},{10,... | collective-permute-start | bytes 1376264 | tf_op jit(solution)/shard_map/ppermute | solution.py:426
  75.3 1.4 %collective-permute-start.13 = (bf16[14,8,2048]{2,1,0:T(8,128)(2,1)S(1)}, bf16[14,8,2048]{2,1,0:T(8,128)(2,1)S(1)}, u32[]{:S(2)}, u32[]{:S(2)}) collective-permute-start(bf16[14,8,2048]{2,1,0:T(8,128)(2,1)S(1)} %bitcast.12), channel_id=1, source_target_pairs={{0,1},{1,0},{2,3},{3,2},{4,5},{5,4},{6,7},{7,6},{8,9},{9,8},{10,11... | collective-permute-start | bytes 1376264 | tf_op jit(solution)/shard_map/ppermute | solution.py:429
  76.6 5.8 %collective-permute-done.9 = bf16[10,8,2048]{2,1,0:T(8,128)(2,1)S(1)} collective-permute-done((bf16[10,8,2048]{2,1,0:T(8,128)(2,1)S(1)}, bf16[10,8,2048]{2,1,0:T(8,128)(2,1)S(1)}, u32[]{:S(2)}, u32[]{:S(2)}) %collective-permute-start.9) | collective-permute-done | bytes 327712 | tf_op jit(solution)/shard_map/ppermute | solution.py:432
  82.5 0.1 add_convert_fusion.1
  82.6 2.4 %collective-permute-done.14.refs_2_ = bf16[14,8,2048]{2,1,0:T(8,128)(2,1)S(1)} collective-permute-done((bf16[14,8,2048]{2,1,0:T(8,128)(2,1)S(1)}, bf16[14,8,2048]{2,1,0:T(8,128)(2,1)S(1)}, u32[]{:S(2)}, u32[]{:S(2)}) %collective-permute-start.14) | collective-permute-done | bytes 458784 | tf_op jit(solution)/shard_map/ppermute | solution.py:426
  84.9 2.0 %collective-permute-start.15 = (bf16[14,8,2048]{2,1,0:T(8,128)(2,1)S(1)}, bf16[14,8,2048]{2,1,0:T(8,128)(2,1)S(1)}, u32[]{:S(2)}, u32[]{:S(2)}) collective-permute-start(bf16[14,8,2048]{2,1,0:T(8,128)(2,1)S(1)} %collective-permute-done.14.refs_2_), channel_id=1, source_target_pairs={{0,1},{1,0},{2,3},{3,2},{4,5},{5,4},{6,7},{7,6},{8,9},{9,8},{10,11... | collective-permute-start | bytes 1376264 | tf_op jit(solution)/shard_map/ppermute | solution.py:429
  87.0 1.2 %collective-permute-start.11 = (bf16[14,8,2048]{2,1,0:T(8,128)(2,1)S(1)}, bf16[14,8,2048]{2,1,0:T(8,128)(2,1)S(1)}, u32[]{:S(2)}, u32[]{:S(2)}) collective-permute-start(bf16[14,8,2048]{2,1,0:T(8,128)(2,1)S(1)} %bitcast.14), channel_id=1, source_target_pairs={{0,2},{1,3},{2,0},{3,1},{4,6},{5,7},{6,4},{7,5},{8,10},{9,11},{10,... | collective-permute-start | bytes 1376264 | tf_op jit(solution)/shard_map/ppermute | solution.py:426
  88.2 0.3 collective-permute-start.16
  88.5 0.0 collective-permute-done.13.refs_1_
  88.5 2.9 %assemble.2.refs_0_ = bf16[8,56,4096]{2,1,0:T(8,128)(2,1)} custom-call(bf16[448,448]{1,0:T(8,128)(2,1)S(1)} %fusion.12.order_ref, bf16[14,8,2048]{2,1,0:T(8,128)(2,1)S(1)} %bitcast.13, bf16[14,8,2048]{2,1,0:T(8,128)(2,1)S(1)} %collective-permute-done.13.refs_1_, bf16[14,8,2048]{2,1,0:T(8,128)(2,1)S(1)} %collective-permute-done.14.refs_2_, ...), custom_call_target="tpu_custom_call" | custom-call | flops 290000000 | bytes 10730000 | tf_op jit(solution)/shard_map/assemble/pallas_call | solution.py:381
  91.4 7.7 %collective-permute-done.11.refs_3_ = bf16[14,8,2048]{2,1,0:T(8,128)(2,1)S(1)} collective-permute-done((bf16[14,8,2048]{2,1,0:T(8,128)(2,1)S(1)}, bf16[14,8,2048]{2,1,0:T(8,128)(2,1)S(1)}, u32[]{:S(2)}, u32[]{:S(2)}) %collective-permute-start.11) | collective-permute-done | bytes 458784 | tf_op jit(solution)/shard_map/ppermute | solution.py:426
  99.1 0.8 collective-permute-start.17
  99.9 0.0 collective-permute-done.16.refs_2_
  99.9 1.4 %collective-permute-done.17.refs_4_ = bf16[14,8,2048]{2,1,0:T(8,128)(2,1)S(1)} collective-permute-done((bf16[14,8,2048]{2,1,0:T(8,128)(2,1)S(1)}, bf16[14,8,2048]{2,1,0:T(8,128)(2,1)S(1)}, u32[]{:S(2)}, u32[]{:S(2)}) %collective-permute-start.17) | collective-permute-done | bytes 458784 | tf_op jit(solution)/shard_map/ppermute | solution.py:429
  101.3 2.9 %assemble.3 = bf16[8,56,4096]{2,1,0:T(8,128)(2,1)} custom-call(bf16[448,448]{1,0:T(8,128)(2,1)S(1)} %fusion.12.order_ref, bf16[8,56,4096]{2,1,0:T(8,128)(2,1)} %assemble.2.refs_0_, bf16[14,8,2048]{2,1,0:T(8,128)(2,1)S(1)} %bitcast.16, bf16[14,8,2048]{2,1,0:T(8,128)(2,1)S(1)} %collective-permute-done.16.refs_2_, ...), custom_call_target="tpu_custom_call", output_to_operand_aliasing={{}: (1, {})} | custom-call | flops 290000000 | bytes 10730000 | tf_op jit(solution)/shard_map/assemble/pallas_call | solution.py:381
  (15 shorter events, 0.1 us)
Async XLA Ops:
  0.0 1.4 %copy-start = (bf16[24,8,4096]{2,1,0:T(8,128)(2,1)S(1)}, bf16[24,8,4096]{2,1,0:T(8,128)(2,1)}, u32[]{:S(2)}) copy-start(bf16[24,8,4096]{2,1,0:T(8,128)(2,1)} %x_ref.3) | copy-start | bytes 4718596
  1.4 9.2 %copy-start.5 = (s32[24,32]{1,0:T(8,128)S(1)}, s32[24,32]{1,0:T(8,128)}, u32[]{:S(2)}) copy-start(s32[24,32]{1,0:T(8,128)} %param.6) | copy-start | bytes 9220
  1.4 9.2 %copy-start.6 = (s32[24]{0:T(128)S(1)}, s32[24]{0:T(128)}, u32[]{:S(2)}) copy-start(s32[24]{0:T(128)} %param.7) | copy-start | bytes 292
  1.4 9.3 %copy-start.1 = (bf16[24,8,4096]{2,1,0:T(8,128)(2,1)S(1)}, bf16[24,8,4096]{2,1,0:T(8,128)(2,1)}, u32[]{:S(2)}) copy-start(bf16[24,8,4096]{2,1,0:T(8,128)(2,1)} %x_ref.3) | copy-start | bytes 4718596
  2.2 3.2 %collective-permute-start = (bf16[16,4,64,128]{3,2,1,0:T(8,128)(2,1)S(1)}, bf16[16,4,64,128]{3,2,1,0:T(8,128)(2,1)}, u32[]{:S(2)}, u32[]{:S(2)}) collective-permute-start(bf16[16,4,64,128]{3,2,1,0:T(8,128)(2,1)S(1)} %relayout.3.refs_0_), channel_id=1, source_target_pairs={{0,1},{1,0},{2,3},{3,2},{4,5},{5,4},{6,7},{7,6},{8,9},{9,8},{10,11... | collective-permute-start | bytes 3145736 | tf_op jit(solution)/shard_map/ppermute | solution.py:429
  3.0 24.8 %collective-permute-start.2 = (bf16[16,4,64,128]{3,2,1,0:T(8,128)(2,1)S(1)}, bf16[16,4,64,128]{3,2,1,0:T(8,128)(2,1)}, u32[]{:S(2)}, u32[]{:S(2)}) collective-permute-start(bf16[16,4,64,128]{3,2,1,0:T(8,128)(2,1)S(1)} %relayout.3.refs_0_), channel_id=1, source_target_pairs={{0,2},{1,3},{2,0},{3,1},{4,6},{5,7},{6,4},{7,5},{8,10},{9,11},{10,... | collective-permute-start | bytes 3145736 | tf_op jit(solution)/shard_map/ppermute | solution.py:426
  5.4 1.1 %copy-start.2 = (bf16[24,4,4096]{2,1,0:T(4,128)(2,1)S(1)}, bf16[24,4,4096]{2,1,0:T(4,128)(2,1)}, u32[]{:S(2)}) copy-start(bf16[24,4,4096]{2,1,0:T(4,128)(2,1)} %x_ref.4) | copy-start | bytes 2359300
  7.6 21.2 %collective-permute-start.1 = (bf16[24,2,64,128]{3,2,1,0:T(8,128)(2,1)S(1)}, bf16[24,2,64,128]{3,2,1,0:T(8,128)(2,1)S(1)}, u32[]{:S(2)}, u32[]{:S(2)}) collective-permute-start(bf16[24,2,64,128]{3,2,1,0:T(8,128)(2,1)S(1)} %relayout_rows.1.refs_0_), channel_id=1, source_target_pairs={{0,4},{2,6},{4,8},{5,1},{6,10},{7,3},{8,12},{9,5},{10,14},{11,7},{... | collective-permute-start | bytes 2359304 | tf_op jit(solution)/shard_map/ppermute | solution.py:423
  11.1 5.0 %collective-permute-start.3 = (bf16[8,4,64,128]{3,2,1,0:T(8,128)(2,1)S(1)}, bf16[8,4,64,128]{3,2,1,0:T(8,128)(2,1)S(1)}, u32[]{:S(2)}, u32[]{:S(2)}) collective-permute-start(bf16[8,4,64,128]{3,2,1,0:T(8,128)(2,1)S(1)} %relayout.4.refs_0_), channel_id=1, source_target_pairs={{0,1},{1,0},{2,3},{3,2},{4,5},{5,4},{6,7},{7,6},{8,9},{9,8},{10,11... | collective-permute-start | bytes 1572872 | tf_op jit(solution)/shard_map/ppermute | solution.py:429
  12.1 4.0 %copy-start.3 = (bf16[24,4,4096]{2,1,0:T(4,128)(2,1)S(1)}, bf16[24,4,4096]{2,1,0:T(4,128)(2,1)}, u32[]{:S(2)}) copy-start(bf16[24,4,4096]{2,1,0:T(4,128)(2,1)} %x_ref.4) | copy-start | bytes 2359300
  17.0 3.5 %copy-start.4 = (s32[192,4]{0,1:T(4,128)S(1)}, s32[192,4]{0,1:T(4,128)}, u32[]{:S(2)}) copy-start(s32[192,4]{0,1:T(4,128)} %param.9) | copy-start | bytes 9220
  28.7 6.1 %collective-permute-start.6 = (bf16[16,4,64,128]{3,2,1,0:T(8,128)(2,1)}, bf16[16,4,64,128]{3,2,1,0:T(8,128)(2,1)S(1)}, u32[]{:S(2)}, u32[]{:S(2)}) collective-permute-start(bf16[16,4,64,128]{3,2,1,0:T(8,128)(2,1)} %collective-permute-done.2.refs_0_), channel_id=1, source_target_pairs={{0,1},{1,0},{2,3},{3,2},{4,5},{5,4},{6,7},{7,6},{8,9},{9,8},{10,11... | collective-permute-start | bytes 3145736 | tf_op jit(solution)/shard_map/ppermute | solution.py:429
  29.3 3.3 %collective-permute-start.5 = (bf16[24,2,64,128]{3,2,1,0:T(8,128)(2,1)S(1)}, bf16[24,2,64,128]{3,2,1,0:T(8,128)(2,1)S(1)}, u32[]{:S(2)}, u32[]{:S(2)}) collective-permute-start(bf16[24,2,64,128]{3,2,1,0:T(8,128)(2,1)S(1)} %collective-permute-done.1.refs_0_), channel_id=1, source_target_pairs={{0,1},{1,0},{2,3},{3,2},{4,5},{5,4},{6,7},{7,6},{8,9},{9,8},{10,11... | collective-permute-start | bytes 2359304 | tf_op jit(solution)/shard_map/ppermute | solution.py:429
  29.3 13.0 %collective-permute-start.4 = (bf16[8,4,64,128]{3,2,1,0:T(8,128)(2,1)S(1)}, bf16[8,4,64,128]{3,2,1,0:T(8,128)(2,1)S(1)}, u32[]{:S(2)}, u32[]{:S(2)}) collective-permute-start(bf16[8,4,64,128]{3,2,1,0:T(8,128)(2,1)S(1)} %relayout.4.refs_0_), channel_id=1, source_target_pairs={{0,2},{1,3},{2,0},{3,1},{4,6},{5,7},{6,4},{7,5},{8,10},{9,11},{10,... | collective-permute-start | bytes 1572872 | tf_op jit(solution)/shard_map/ppermute | solution.py:426
  42.2 6.5 %collective-permute-start.7 = (bf16[8,4,64,128]{3,2,1,0:T(8,128)(2,1)S(1)}, bf16[8,4,64,128]{3,2,1,0:T(8,128)(2,1)S(1)}, u32[]{:S(2)}, u32[]{:S(2)}) collective-permute-start(bf16[8,4,64,128]{3,2,1,0:T(8,128)(2,1)S(1)} %collective-permute-done.4.refs_0_), channel_id=1, source_target_pairs={{0,1},{1,0},{2,3},{3,2},{4,5},{5,4},{6,7},{7,6},{8,9},{9,8},{10,11... | collective-permute-start | bytes 1572872 | tf_op jit(solution)/shard_map/ppermute | solution.py:429
  44.6 18.8 %collective-permute-start.10 = (bf16[10,4,4096]{2,1,0:T(4,128)(2,1)S(1)}, bf16[10,4,4096]{2,1,0:T(4,128)(2,1)S(1)}, u32[]{:S(2)}, u32[]{:S(2)}) collective-permute-start(bf16[10,4,4096]{2,1,0:T(4,128)(2,1)S(1)} %coarse.9), channel_id=1, source_target_pairs={{4,0},{8,4},{12,8},{16,12},{20,16},{24,20},{28,24},{5,1},{9,5},{13... | collective-permute-start | bytes 983048 | tf_op jit(solution)/shard_map/ppermute | solution.py:435
  53.7 17.9 %collective-permute-start.8 = (bf16[10,4,4096]{2,1,0:T(4,128)(2,1)S(1)}, bf16[10,4,4096]{2,1,0:T(4,128)(2,1)S(1)}, u32[]{:S(2)}, u32[]{:S(2)}) collective-permute-start(bf16[10,4,4096]{2,1,0:T(4,128)(2,1)S(1)} %coarse.8), channel_id=1, source_target_pairs={{4,0},{8,4},{12,8},{16,12},{20,16},{24,20},{28,24},{5,1},{9,5},{13... | collective-permute-start | bytes 983048 | tf_op jit(solution)/shard_map/ppermute | solution.py:435
  57.8 16.0 %collective-permute-start.12 = (bf16[10,8,2048]{2,1,0:T(8,128)(2,1)S(1)}, bf16[10,8,2048]{2,1,0:T(8,128)(2,1)S(1)}, u32[]{:S(2)}, u32[]{:S(2)}) collective-permute-start(bf16[10,8,2048]{2,1,0:T(8,128)(2,1)S(1)} %coarse.6), channel_id=1, source_target_pairs={{0,4},{4,8},{8,12},{12,16},{16,20},{20,24},{24,28},{1,5},{5,9},{9,... | collective-permute-start | bytes 983048 | tf_op jit(solution)/shard_map/ppermute | solution.py:432
  71.6 10.9 %collective-permute-start.9 = (bf16[10,8,2048]{2,1,0:T(8,128)(2,1)S(1)}, bf16[10,8,2048]{2,1,0:T(8,128)(2,1)S(1)}, u32[]{:S(2)}, u32[]{:S(2)}) collective-permute-start(bf16[10,8,2048]{2,1,0:T(8,128)(2,1)S(1)} %coarse.7), channel_id=1, source_target_pairs={{0,4},{4,8},{8,12},{12,16},{16,20},{20,24},{24,28},{1,5},{5,9},{9,... | collective-permute-start | bytes 983048 | tf_op jit(solution)/shard_map/ppermute | solution.py:432
  74.0 11.0 %collective-permute-start.14 = (bf16[14,8,2048]{2,1,0:T(8,128)(2,1)S(1)}, bf16[14,8,2048]{2,1,0:T(8,128)(2,1)S(1)}, u32[]{:S(2)}, u32[]{:S(2)}) collective-permute-start(bf16[14,8,2048]{2,1,0:T(8,128)(2,1)S(1)} %bitcast.11), channel_id=1, source_target_pairs={{0,2},{1,3},{2,0},{3,1},{4,6},{5,7},{6,4},{7,5},{8,10},{9,11},{10,... | collective-permute-start | bytes 1376264 | tf_op jit(solution)/shard_map/ppermute | solution.py:426
  75.3 13.2 %collective-permute-start.13 = (bf16[14,8,2048]{2,1,0:T(8,128)(2,1)S(1)}, bf16[14,8,2048]{2,1,0:T(8,128)(2,1)S(1)}, u32[]{:S(2)}, u32[]{:S(2)}) collective-permute-start(bf16[14,8,2048]{2,1,0:T(8,128)(2,1)S(1)} %bitcast.12), channel_id=1, source_target_pairs={{0,1},{1,0},{2,3},{3,2},{4,5},{5,4},{6,7},{7,6},{8,9},{9,8},{10,11... | collective-permute-start | bytes 1376264 | tf_op jit(solution)/shard_map/ppermute | solution.py:429
  84.9 3.6 %collective-permute-start.15 = (bf16[14,8,2048]{2,1,0:T(8,128)(2,1)S(1)}, bf16[14,8,2048]{2,1,0:T(8,128)(2,1)S(1)}, u32[]{:S(2)}, u32[]{:S(2)}) collective-permute-start(bf16[14,8,2048]{2,1,0:T(8,128)(2,1)S(1)} %collective-permute-done.14.refs_2_), channel_id=1, source_target_pairs={{0,1},{1,0},{2,3},{3,2},{4,5},{5,4},{6,7},{7,6},{8,9},{9,8},{10,11... | collective-permute-start | bytes 1376264 | tf_op jit(solution)/shard_map/ppermute | solution.py:429
  87.0 12.2 %collective-permute-start.11 = (bf16[14,8,2048]{2,1,0:T(8,128)(2,1)S(1)}, bf16[14,8,2048]{2,1,0:T(8,128)(2,1)S(1)}, u32[]{:S(2)}, u32[]{:S(2)}) collective-permute-start(bf16[14,8,2048]{2,1,0:T(8,128)(2,1)S(1)} %bitcast.14), channel_id=1, source_target_pairs={{0,2},{1,3},{2,0},{3,1},{4,6},{5,7},{6,4},{7,5},{8,10},{9,11},{10,... | collective-permute-start | bytes 1376264 | tf_op jit(solution)/shard_map/ppermute | solution.py:426
  88.2 11.7 %collective-permute-start.16 = (bf16[14,8,2048]{2,1,0:T(8,128)(2,1)S(1)}, bf16[14,8,2048]{2,1,0:T(8,128)(2,1)S(1)}, u32[]{:S(2)}, u32[]{:S(2)}) collective-permute-start(bf16[14,8,2048]{2,1,0:T(8,128)(2,1)S(1)} %bitcast.15), channel_id=1, source_target_pairs={{0,1},{1,0},{2,3},{3,2},{4,5},{5,4},{6,7},{7,6},{8,9},{9,8},{10,11... | collective-permute-start | bytes 1376264 | tf_op jit(solution)/shard_map/ppermute | solution.py:429
  99.1 2.2 %collective-permute-start.17 = (bf16[14,8,2048]{2,1,0:T(8,128)(2,1)S(1)}, bf16[14,8,2048]{2,1,0:T(8,128)(2,1)S(1)}, u32[]{:S(2)}, u32[]{:S(2)}) collective-permute-start(bf16[14,8,2048]{2,1,0:T(8,128)(2,1)S(1)} %collective-permute-done.11.refs_3_), channel_id=1, source_target_pairs={{0,1},{1,0},{2,3},{3,2},{4,5},{5,4},{6,7},{7,6},{8,9},{9,8},{10,11... | collective-permute-start | bytes 1376264 | tf_op jit(solution)/shard_map/ppermute | solution.py:429

commit v7 on v6

--- a/solution.py
+++ b/solution.py
@@ -468,25 +468,26 @@
         y = x[: GROUPS * share].reshape((share, GROUPS) + x.shape[1:])
         return jnp.pad(y.astype(F32), ((0, 0), (g, 2 - g), (0, 0), (0, 0)))
 
-    late = downward(coarse_rows(left, aps, ((CB // 2, CB),), 0, BS, BF, 1.0)[0])
-    highs = [coarse_rows(left, aps, ((2 * CB, 3 * CB),), a0, a1, BF, 1.0)[0] for a0, a1 in chunks]
-    left, highs = lax.optimization_barrier((left, highs))
-    highs[1], late = lax.optimization_barrier((highs[1], late))
-    highs = [upward(x) for x in highs]
+    rims = []
+    for a0, a1 in chunks:
+        low = coarse_rows(left, aps, ((CB // 2, CB),), a0, a1, BF, 1.0)[0]
+        high = coarse_rows(left, aps, ((2 * CB, 3 * CB),), a0, a1, BF, 1.0)[0]
+        rims.append((downward(low), upward(high)))
     mids = [coarse_rows(left, aps, ((CB, 2 * CB),), a0, a1, F32, 1.0)[0] for a0, a1 in chunks]
-    early, mids = lax.optimization_barrier((early, mids))
-    lower = jnp.concatenate([early, late], axis=1)
     totals, fars = [], []
-    for (a0, a1), high, mid in zip(chunks, highs, mids):
-        total = columns(high, 0) + columns(mid, 1) + columns(lower[:, :, a0 * BS : a1 * BS], 2)
+    for (a0, a1), (low, high), mid in zip(chunks, rims, mids):
+        lower = jnp.concatenate([early[:, :, a0 * BS : a1 * BS], low], axis=1)
+        total = columns(high, 0) + columns(mid, 1) + columns(lower, 2)
         totals.append(total.astype(BF).reshape((share * (GROUPS + 2),) + total.shape[2:]))
         fars.append([over_y(totals[-1], s) for s in range(1, ny)])
     fars[0], totals[1] = lax.optimization_barrier((fars[0], totals[1]))
+    sides = [over_core(x) for x in totals]
+    beyond = [over_core(x) for x in fars[0]]
+    fars[1], beyond = lax.optimization_barrier((fars[1], beyond))
+    beyond = [beyond, [over_core(x) for x in fars[1]]]
     out = None
-    for (a0, a1), total, far in zip(chunks, totals, fars):
-        if out is not None:
-            far, out = lax.optimization_barrier((far, out))
-        srcs = [z for g in [total] + far for z in (g, over_core(g))]
+    for z, (a0, a1) in enumerate(chunks):
+        srcs = [totals[z], sides[z]] + [q for pair in zip(fars[z], beyond[z]) for q in pair]
         out = assemble(order, srcs, a0, BS * BS, out)
     return out
 

time: 106 us -> 106 us (level); the launches traced: 104 us -> 106 us
  starting transfers between devices: 27.4 us -> 32.4 us
  waiting for transfers between devices: 33.6 us -> 29.5 us
    ppermute x2 -> x3, starting transfers between devices: 6.1 us -> 12.5 us  [downward(): return lax.ppermute(x, 'row', [(i + 1, i) for i in range(nrow - 1)])]
    ppermute x2, waiting for transfers between devices: 5.84 us -> 0.01 us  [upward(): return lax.ppermute(x, 'row', [(i, i + 1) for i in range(nrow - 1)])]
    ppermute x4, waiting for transfers between devices: 14.8 us -> 18.5 us  [over_y(): lax.ppermute(x, 'col', [(y * 2 + c, (y + s) % ny * 2 + c) for y in range(...]
    ppermute x9, waiting for transfers between devices: 3.83 us -> 2.39 us  [over_core(): return lax.ppermute(x, 'col', [(c, c ^ 1) for c in range(ncol)])]
    ppermute x2, starting transfers between devices: 5.27 us -> 4.07 us  [upward(): return lax.ppermute(x, 'row', [(i, i + 1) for i in range(nrow - 1)])]
    ppermute x2 -> x3, waiting for transfers between devices: 8.22 us -> 7.7 us  [downward(): return lax.ppermute(x, 'row', [(i + 1, i) for i in range(nrow - 1)])]
    pallas_call x6 -> x7, Pallas kernels: 6.48 us -> 6.72 us  [coarse_rows(): pl.pallas_call(functools.partial(coarse_kernel, sets, a0, a1), out_shape=...]
  transfers between devices with their start and end apart: 18 -> 19, of which waited for: 10 -> 9; matrix products, arithmetic and copies ran while one was open for 2% -> 2% of each run, Pallas kernels for 34% -> 34%
where the time goes in v7:
time: 106 us
  Pallas kernels  39.1 us (37%)
  starting transfers between devices  32.4 us (31%)
  waiting for transfers between devices  29.5 us (28%)
  local copies, waits for them, and re-layouts  2.7 us (3%)
  other arithmetic  1.57 us (1%)
    ppermute x4, waiting for transfers between devices, over_y(): lax.ppermute(x, 'col', [(y * 2 + c, (y + s) % ny * 2 + c) for y in range(...  18.5 us
    ppermute x3, starting transfers between devices, downward(): return lax.ppermute(x, 'row', [(i + 1, i) for i in range(nrow - 1)])  12.5 us
    pallas_call x2, Pallas kernels, product(): pl.pallas_call(functools.partial(product_kernel, first, rb, shifts), out_...  10.9 us
    ppermute x9, starting transfers between devices, over_core(): return lax.ppermute(x, 'col', [(c, c ^ 1) for c in range(ncol)])  7.73 us
    ppermute x3, waiting for transfers between devices, downward(): return lax.ppermute(x, 'row', [(i + 1, i) for i in range(nrow - 1)])  7.7 us
    pallas_call x7, Pallas kernels, coarse_rows(): pl.pallas_call(functools.partial(coarse_kernel, sets, a0, a1), out_shape=...  6.72 us
    pallas_call x2, Pallas kernels, near_band(): pl.pallas_call(functools.partial(band_kernel, first, shifts), out_shape=j...  5.98 us
    pallas_call x2, Pallas kernels, assemble(): pl.pallas_call(assemble_kernel, grid=(per,), out_shape=jax.ShapeDtypeStru...  5.77 us
  transfers between devices with their start and end apart: 19, of which 9 were waited for; matrix products, arithmetic and copies ran while one was open for 2% of the time, Pallas kernels for 34%

profile of v7, /device:TPU:9, one launch (start us, length us, event | category | flops | bytes accessed | tf_op | source)
XLA Modules:
  0.0 105.5 jit_solution(16881596122943001870)
XLA Ops:
  0.0 1.4 %copy-done = bf16[24,8,4096]{2,1,0:T(8,128)(2,1)S(1)} copy-done((bf16[24,8,4096]{2,1,0:T(8,128)(2,1)S(1)}, bf16[24,8,4096]{2,1,0:T(8,128)(2,1)}, u32[]{:S(2)}) %copy-start) | copy-done | bytes 1572888
  1.4 0.8 relayout.3.refs_0_
  2.2 0.7 collective-permute-start
  3.0 1.3 %collective-permute-start.2 = (bf16[16,4,64,128]{3,2,1,0:T(8,128)(2,1)S(1)}, bf16[16,4,64,128]{3,2,1,0:T(8,128)(2,1)}, u32[]{:S(2)}, u32[]{:S(2)}) collective-permute-start(bf16[16,4,64,128]{3,2,1,0:T(8,128)(2,1)S(1)} %relayout.3.refs_0_), channel_id=1, source_target_pairs={{0,2},{1,3},{2,0},{3,1},{4,6},{5,7},{6,4},{7,5},{8,10},{9,11},{10,... | collective-permute-start | bytes 3145736 | tf_op jit(solution)/shard_map/ppermute | solution.py:426
  4.2 0.8 add_select_fusion.4.table_ref
  5.0 0.3 collective-permute-done.refs_1_
  5.4 1.1 %copy-done.2 = bf16[24,4,4096]{2,1,0:T(4,128)(2,1)S(1)} copy-done((bf16[24,4,4096]{2,1,0:T(4,128)(2,1)S(1)}, bf16[24,4,4096]{2,1,0:T(4,128)(2,1)}, u32[]{:S(2)}) %copy-start.2) | copy-done | bytes 786456
  6.5 1.1 relayout_rows.1.refs_0_
  7.6 3.0 %collective-permute-start.1 = (bf16[24,2,64,128]{3,2,1,0:T(8,128)(2,1)S(1)}, bf16[24,2,64,128]{3,2,1,0:T(8,128)(2,1)S(1)}, u32[]{:S(2)}, u32[]{:S(2)}) collective-permute-start(bf16[24,2,64,128]{3,2,1,0:T(8,128)(2,1)S(1)} %relayout_rows.1.refs_0_), channel_id=1, source_target_pairs={{0,4},{2,6},{4,8},{5,1},{6,10},{7,3},{8,12},{9,5},{10,14},{11,7},{... | collective-permute-start | bytes 2359304 | tf_op jit(solution)/shard_map/ppermute | solution.py:423
  10.6 0.1 subtract_select_fusion.place_ref
  10.7 0.4 relayout.4.refs_0_
  11.1 0.8 collective-permute-start.3
  11.9 0.2 fusion.12.order_ref
  12.1 0.0 copy-start.3
  12.1 3.9 %near_band.2.start_ref = bf16[4,27,256,128]{3,2,1,0:T(8,128)(2,1)S(1)} custom-call(s32[24,32]{1,0:T(8,128)S(1)} %subtract_select_fusion.place_ref, bf16[16,4,64,128]{3,2,1,0:T(8,128)(2,1)S(1)} %relayout.3.refs_0_, bf16[16,4,64,128]{3,2,1,0:T(8,128)(2,1)} %collective-permute-done.refs_1_), custom_call_target="tpu_custom_call" | custom-call | flops 256000000 | bytes 9472000 | tf_op jit(solution)/shard_map/near_band/pallas_call | solution.py:255
  16.1 0.0 collective-permute-done.3.refs_1_
  16.1 0.9 relayout.5.pl_ref
  17.0 0.0 copy-start.4
  17.0 2.1 %near_band.3.start_ref = bf16[2,27,256,128]{3,2,1,0:T(8,128)(2,1)S(1)} custom-call(s32[24,32]{1,0:T(8,128)S(1)} %subtract_select_fusion.place_ref, bf16[8,4,64,128]{3,2,1,0:T(8,128)(2,1)S(1)} %relayout.4.refs_0_, bf16[8,4,64,128]{3,2,1,0:T(8,128)(2,1)S(1)} %collective-permute-done.3.refs_1_), custom_call_target="tpu_custom_call" | custom-call | flops 128000000 | bytes 4736000 | tf_op jit(solution)/shard_map/near_band/pallas_call | solution.py:255
  19.0 1.4 %right_factor.2.own_ref = bf16[6,5,256,128]{3,2,1,0:T(8,128)(2,1)S(1)} custom-call(s32[4,72]{1,0:T(4,128)S(1)} %add_select_fusion.4.table_ref, bf16[24,2,64,128]{3,2,1,0:T(8,128)(2,1)S(1)} %relayout_rows.1.refs_0_), custom_call_target="tpu_custom_call" | custom-call | flops 200000000 | bytes 7400000 | tf_op jit(solution)/shard_map/right_factor/pallas_call | solution.py:186
  20.5 2.9 %left_factor.1.left_ref = bf16[12,24,64,128]{3,2,1,0:T(8,128)(2,1)S(1)} custom-call(s32[4,192]{1,0:T(4,128)S(1)} %bitcast.18, bf16[24,2,64,128]{3,2,1,0:T(8,128)(2,1)S(1)} %relayout.5.pl_ref), custom_call_target="tpu_custom_call" | custom-call | flops 290000000 | bytes 10730000 | tf_op jit(solution)/shard_map/left_factor/pallas_call | solution.py:118
  23.4 4.4 %collective-permute-done.2.refs_0_ = bf16[16,4,64,128]{3,2,1,0:T(8,128)(2,1)} collective-permute-done((bf16[16,4,64,128]{3,2,1,0:T(8,128)(2,1)S(1)}, bf16[16,4,64,128]{3,2,1,0:T(8,128)(2,1)}, u32[]{:S(2)}, u32[]{:S(2)}) %collective-permute-start.2) | collective-permute-done | bytes 1048608 | tf_op jit(solution)/shard_map/ppermute | solution.py:426
  27.8 0.9 collective-permute-done.1.refs_0_
  28.7 0.5 collective-permute-start.6
  29.3 0.0 collective-permute-start.5
  29.3 1.2 %collective-permute-start.4 = (bf16[8,4,64,128]{3,2,1,0:T(8,128)(2,1)S(1)}, bf16[8,4,64,128]{3,2,1,0:T(8,128)(2,1)S(1)}, u32[]{:S(2)}, u32[]{:S(2)}) collective-permute-start(bf16[8,4,64,128]{3,2,1,0:T(8,128)(2,1)S(1)} %relayout.4.refs_0_), channel_id=1, source_target_pairs={{0,2},{1,3},{2,0},{3,1},{4,6},{5,7},{6,4},{7,5},{8,10},{9,11},{10,... | collective-permute-start | bytes 1572872 | tf_op jit(solution)/shard_map/ppermute | solution.py:426
  30.5 2.0 %collective-permute-done.5.refs_1_ = bf16[24,2,64,128]{3,2,1,0:T(8,128)(2,1)S(1)} collective-permute-done((bf16[24,2,64,128]{3,2,1,0:T(8,128)(2,1)S(1)}, bf16[24,2,64,128]{3,2,1,0:T(8,128)(2,1)S(1)}, u32[]{:S(2)}, u32[]{:S(2)}) %collective-permute-start.5) | collective-permute-done | bytes 786464 | tf_op jit(solution)/shard_map/ppermute | solution.py:429
  32.5 2.3 %right_factor.3.near_ref = bf16[12,5,256,128]{3,2,1,0:T(8,128)(2,1)S(1)} custom-call(s32[4,72]{1,0:T(4,128)S(1)} %add_select_fusion.4.table_ref, bf16[24,2,64,128]{3,2,1,0:T(8,128)(2,1)S(1)} %collective-permute-done.1.refs_0_, bf16[24,2,64,128]{3,2,1,0:T(8,128)(2,1)S(1)} %collective-permute-done.5.refs_1_), custom_call_target="tpu_custom_call" | custom-call | flops 300000000 | bytes 11100000 | tf_op jit(solution)/shard_map/right_factor/pallas_call | solution.py:186
  34.8 0.0 collective-permute-done.6.refs_1_
  34.8 7.1 %product.2.refs_0_ = bf16[16,64,640]{2,1,0:T(8,128)(2,1)S(1)} custom-call(s32[24,32]{1,0:T(8,128)S(1)} %subtract_select_fusion.place_ref, bf16[6,5,256,128]{3,2,1,0:T(8,128)(2,1)S(1)} %right_factor.2.own_ref, bf16[12,5,256,128]{3,2,1,0:T(8,128)(2,1)S(1)} %right_factor.3.near_ref, bf16[4,27,256,128]{3,2,1,0:T(8,128)(2,1)S(1)} %near_band.2.start_ref, ...), custom_call_target="tpu_custom_call" | custom-call | flops 480000000 | bytes 17760000 | tf_op jit(solution)/shard_map/product/pallas_call | solution.py:299
  42.0 0.3 collective-permute-done.4.refs_0_
  42.2 1.4 %collective-permute-start.7 = (bf16[8,4,64,128]{3,2,1,0:T(8,128)(2,1)S(1)}, bf16[8,4,64,128]{3,2,1,0:T(8,128)(2,1)S(1)}, u32[]{:S(2)}, u32[]{:S(2)}) collective-permute-start(bf16[8,4,64,128]{3,2,1,0:T(8,128)(2,1)S(1)} %collective-permute-done.4.refs_0_), channel_id=1, source_target_pairs={{0,1},{1,0},{2,3},{3,2},{4,5},{5,4},{6,7},{7,6},{8,9},{9,8},{10,11... | collective-permute-start | bytes 1572872 | tf_op jit(solution)/shard_map/ppermute | solution.py:429
  43.6 0.9 coarse.9
  44.6 4.2 %collective-permute-start.9 = (bf16[10,4,4096]{2,1,0:T(4,128)(2,1)S(1)}, bf16[10,4,4096]{2,1,0:T(4,128)(2,1)S(1)}, u32[]{:S(2)}, u32[]{:S(2)}) collective-permute-start(bf16[10,4,4096]{2,1,0:T(4,128)(2,1)S(1)} %coarse.9), channel_id=1, source_target_pairs={{4,0},{8,4},{12,8},{16,12},{20,16},{24,20},{28,24},{5,1},{9,5},{13... | collective-permute-start | bytes 983048 | tf_op jit(solution)/shard_map/ppermute | solution.py:435
  48.7 0.0 collective-permute-done.7.refs_1_
  48.7 3.8 %product.3.refs_1_ = bf16[8,64,640]{2,1,0:T(8,128)(2,1)S(1)} custom-call(s32[24,32]{1,0:T(8,128)S(1)} %subtract_select_fusion.place_ref, bf16[6,5,256,128]{3,2,1,0:T(8,128)(2,1)S(1)} %right_factor.2.own_ref, bf16[12,5,256,128]{3,2,1,0:T(8,128)(2,1)S(1)} %right_factor.3.near_ref, bf16[2,27,256,128]{3,2,1,0:T(8,128)(2,1)S(1)} %near_band.3.start_ref, ...), custom_call_target="tpu_custom_call" | custom-call | flops 240000000 | bytes 8880000 | tf_op jit(solution)/shard_map/product/pallas_call | solution.py:299
  52.5 1.1 %coarse.7 = bf16[10,8,2048]{2,1,0:T(8,128)(2,1)S(1)} custom-call(bf16[12,24,64,128]{3,2,1,0:T(8,128)(2,1)S(1)} %left_factor.1.left_ref, bf16[16,64,640]{2,1,0:T(8,128)(2,1)S(1)} %product.2.refs_0_, bf16[8,64,640]{2,1,0:T(8,128)(2,1)S(1)} %product.3.refs_1_), custom_call_target="tpu_custom_call" | custom-call | flops 100000000 | bytes 3700000 | tf_op jit(solution)/shard_map/coarse/pallas_call | solution.py:346
  53.6 2.0 %collective-permute-start.8 = (bf16[10,8,2048]{2,1,0:T(8,128)(2,1)S(1)}, bf16[10,8,2048]{2,1,0:T(8,128)(2,1)S(1)}, u32[]{:S(2)}, u32[]{:S(2)}) collective-permute-start(bf16[10,8,2048]{2,1,0:T(8,128)(2,1)S(1)} %coarse.7), channel_id=1, source_target_pairs={{0,4},{4,8},{8,12},{12,16},{16,20},{20,24},{24,28},{1,5},{5,9},{9,... | collective-permute-start | bytes 983048 | tf_op jit(solution)/shard_map/ppermute | solution.py:432
  55.7 0.7 coarse.10
  56.4 4.1 %collective-permute-start.10 = (bf16[10,4,2048]{2,1,0:T(4,128)(2,1)S(1)}, bf16[10,4,2048]{2,1,0:T(4,128)(2,1)S(1)}, u32[]{:S(2)}, u32[]{:S(2)}) collective-permute-start(bf16[10,4,2048]{2,1,0:T(4,128)(2,1)S(1)} %coarse.10), channel_id=1, source_target_pairs={{4,0},{8,4},{12,8},{16,12},{20,16},{24,20},{28,24},{5,1},{9,5},{13... | collective-permute-start | bytes 491528 | tf_op jit(solution)/shard_map/ppermute | solution.py:435
  60.6 0.1 fusion.25
  60.7 1.1 %coarse.11 = bf16[10,8,2048]{2,1,0:T(8,128)(2,1)S(1)} custom-call(bf16[12,24,64,128]{3,2,1,0:T(8,128)(2,1)S(1)} %left_factor.1.left_ref, bf16[16,64,640]{2,1,0:T(8,128)(2,1)S(1)} %product.2.refs_0_, bf16[8,64,640]{2,1,0:T(8,128)(2,1)S(1)} %product.3.refs_1_), custom_call_target="tpu_custom_call" | custom-call | flops 100000000 | bytes 3700000 | tf_op jit(solution)/shard_map/coarse/pallas_call | solution.py:346
  61.8 2.0 %collective-permute-start.13 = (bf16[10,8,2048]{2,1,0:T(8,128)(2,1)S(1)}, bf16[10,8,2048]{2,1,0:T(8,128)(2,1)S(1)}, u32[]{:S(2)}, u32[]{:S(2)}) collective-permute-start(bf16[10,8,2048]{2,1,0:T(8,128)(2,1)S(1)} %coarse.11), channel_id=1, source_target_pairs={{0,4},{4,8},{8,12},{12,16},{16,20},{20,24},{24,28},{1,5},{5,9},{9,... | collective-permute-start | bytes 983048 | tf_op jit(solution)/shard_map/ppermute | solution.py:432
  63.9 0.7 coarse.13
  64.6 4.1 %collective-permute-start.14 = (bf16[10,4,2048]{2,1,0:T(4,128)(2,1)S(1)}, bf16[10,4,2048]{2,1,0:T(4,128)(2,1)S(1)}, u32[]{:S(2)}, u32[]{:S(2)}) collective-permute-start(bf16[10,4,2048]{2,1,0:T(4,128)(2,1)S(1)} %coarse.13), channel_id=1, source_target_pairs={{4,0},{8,4},{12,8},{16,12},{20,16},{24,20},{28,24},{5,1},{9,5},{13... | collective-permute-start | bytes 491528 | tf_op jit(solution)/shard_map/ppermute | solution.py:435
  68.7 1.1 %coarse.12 = f32[10,8,2048]{2,1,0:T(8,128)S(1)} custom-call(bf16[12,24,64,128]{3,2,1,0:T(8,128)(2,1)S(1)} %left_factor.1.left_ref, bf16[16,64,640]{2,1,0:T(8,128)(2,1)S(1)} %product.2.refs_0_, bf16[8,64,640]{2,1,0:T(8,128)(2,1)S(1)} %product.3.refs_1_), custom_call_target="tpu_custom_call" | custom-call | flops 100000000 | bytes 3700000 | tf_op jit(solution)/shard_map/coarse/pallas_call | solution.py:346
  69.8 1.1 %coarse.8 = f32[10,8,2048]{2,1,0:T(8,128)S(1)} custom-call(bf16[12,24,64,128]{3,2,1,0:T(8,128)(2,1)S(1)} %left_factor.1.left_ref, bf16[16,64,640]{2,1,0:T(8,128)(2,1)S(1)} %product.2.refs_0_, bf16[8,64,640]{2,1,0:T(8,128)(2,1)S(1)} %product.3.refs_1_), custom_call_target="tpu_custom_call" | custom-call | flops 100000000 | bytes 3700000 | tf_op jit(solution)/shard_map/coarse/pallas_call | solution.py:346
  70.9 5.8 %collective-permute-done.10 = bf16[10,4,2048]{2,1,0:T(4,128)(2,1)S(1)} collective-permute-done((bf16[10,4,2048]{2,1,0:T(4,128)(2,1)S(1)}, bf16[10,4,2048]{2,1,0:T(4,128)(2,1)S(1)}, u32[]{:S(2)}, u32[]{:S(2)}) %collective-permute-start.10) | collective-permute-done | bytes 163872 | tf_op jit(solution)/shard_map/ppermute | solution.py:435
  76.6 0.2 pad_maximum_fusion
  76.8 0.1 add_convert_fusion.1
  76.9 1.3 %collective-permute-start.12 = (bf16[14,8,2048]{2,1,0:T(8,128)(2,1)S(1)}, bf16[14,8,2048]{2,1,0:T(8,128)(2,1)S(1)}, u32[]{:S(2)}, u32[]{:S(2)}) collective-permute-start(bf16[14,8,2048]{2,1,0:T(8,128)(2,1)S(1)} %bitcast.11), channel_id=1, source_target_pairs={{0,2},{1,3},{2,0},{3,1},{4,6},{5,7},{6,4},{7,5},{8,10},{9,11},{10,... | collective-permute-start | bytes 1376264 | tf_op jit(solution)/shard_map/ppermute | solution.py:426
  78.2 1.9 %collective-permute-done.14 = bf16[10,4,2048]{2,1,0:T(4,128)(2,1)S(1)} collective-permute-done((bf16[10,4,2048]{2,1,0:T(4,128)(2,1)S(1)}, bf16[10,4,2048]{2,1,0:T(4,128)(2,1)S(1)}, u32[]{:S(2)}, u32[]{:S(2)}) %collective-permute-start.14) | collective-permute-done | bytes 163872 | tf_op jit(solution)/shard_map/ppermute | solution.py:435
  80.1 0.2 pad_maximum_fusion.1
  80.3 0.0 collective-permute-done.13
  80.3 0.1 add_convert_fusion
  80.4 1.3 %collective-permute-start.15 = (bf16[14,8,2048]{2,1,0:T(8,128)(2,1)S(1)}, bf16[14,8,2048]{2,1,0:T(8,128)(2,1)S(1)}, u32[]{:S(2)}, u32[]{:S(2)}) collective-permute-start(bf16[14,8,2048]{2,1,0:T(8,128)(2,1)S(1)} %bitcast.14), channel_id=1, source_target_pairs={{0,2},{1,3},{2,0},{3,1},{4,6},{5,7},{6,4},{7,5},{8,10},{9,11},{10,... | collective-permute-start | bytes 1376264 | tf_op jit(solution)/shard_map/ppermute | solution.py:426
  81.7 6.8 %collective-permute-done.12.refs_2_ = bf16[14,8,2048]{2,1,0:T(8,128)(2,1)S(1)} collective-permute-done((bf16[14,8,2048]{2,1,0:T(8,128)(2,1)S(1)}, bf16[14,8,2048]{2,1,0:T(8,128)(2,1)S(1)}, u32[]{:S(2)}, u32[]{:S(2)}) %collective-permute-start.12) | collective-permute-done | bytes 458784 | tf_op jit(solution)/shard_map/ppermute | solution.py:426
  88.5 2.4 %collective-permute-start.16 = (bf16[14,8,2048]{2,1,0:T(8,128)(2,1)S(1)}, bf16[14,8,2048]{2,1,0:T(8,128)(2,1)S(1)}, u32[]{:S(2)}, u32[]{:S(2)}) collective-permute-start(bf16[14,8,2048]{2,1,0:T(8,128)(2,1)S(1)} %collective-permute-done.12.refs_2_), channel_id=1, source_target_pairs={{0,1},{1,0},{2,3},{3,2},{4,5},{5,4},{6,7},{7,6},{8,9},{9,8},{10,11... | collective-permute-start | bytes 1376264 | tf_op jit(solution)/shard_map/ppermute | solution.py:429
  90.9 0.0 collective-permute-start.11
  90.9 0.5 collective-permute-start.17
  91.4 7.0 %collective-permute-done.15.refs_3_ = bf16[14,8,2048]{2,1,0:T(8,128)(2,1)S(1)} collective-permute-done((bf16[14,8,2048]{2,1,0:T(8,128)(2,1)S(1)}, bf16[14,8,2048]{2,1,0:T(8,128)(2,1)S(1)}, u32[]{:S(2)}, u32[]{:S(2)}) %collective-permute-start.15) | collective-permute-done | bytes 458784 | tf_op jit(solution)/shard_map/ppermute | solution.py:426
  98.4 1.4 %collective-permute-start.18 = (bf16[14,8,2048]{2,1,0:T(8,128)(2,1)S(1)}, bf16[14,8,2048]{2,1,0:T(8,128)(2,1)S(1)}, u32[]{:S(2)}, u32[]{:S(2)}) collective-permute-start(bf16[14,8,2048]{2,1,0:T(8,128)(2,1)S(1)} %collective-permute-done.15.refs_3_), channel_id=1, source_target_pairs={{0,1},{1,0},{2,3},{3,2},{4,5},{5,4},{6,7},{7,6},{8,9},{9,8},{10,11... | collective-permute-start | bytes 1376264 | tf_op jit(solution)/shard_map/ppermute | solution.py:429
  99.7 2.9 %assemble.2.refs_0_ = bf16[8,56,4096]{2,1,0:T(8,128)(2,1)} custom-call(bf16[448,448]{1,0:T(8,128)(2,1)S(1)} %fusion.12.order_ref, bf16[14,8,2048]{2,1,0:T(8,128)(2,1)S(1)} %bitcast.13, bf16[14,8,2048]{2,1,0:T(8,128)(2,1)S(1)} %collective-permute-done.11.refs_1_, bf16[14,8,2048]{2,1,0:T(8,128)(2,1)S(1)} %collective-permute-done.12.refs_2_, ...), custom_call_target="tpu_custom_call" | custom-call | flops 290000000 | bytes 10730000 | tf_op jit(solution)/shard_map/assemble/pallas_call | solution.py:381
  102.6 2.9 %assemble.3 = bf16[8,56,4096]{2,1,0:T(8,128)(2,1)} custom-call(bf16[448,448]{1,0:T(8,128)(2,1)S(1)} %fusion.12.order_ref, bf16[8,56,4096]{2,1,0:T(8,128)(2,1)} %assemble.2.refs_0_, bf16[14,8,2048]{2,1,0:T(8,128)(2,1)S(1)} %bitcast.16, bf16[14,8,2048]{2,1,0:T(8,128)(2,1)S(1)} %collective-permute-done.17.refs_2_, ...), custom_call_target="tpu_custom_call", output_to_operand_aliasing={{}: (1, {})} | custom-call | flops 290000000 | bytes 10730000 | tf_op jit(solution)/shard_map/assemble/pallas_call | solution.py:381
  (20 shorter events, 0.1 us)
Async XLA Ops:
  0.0 1.4 %copy-start = (bf16[24,8,4096]{2,1,0:T(8,128)(2,1)S(1)}, bf16[24,8,4096]{2,1,0:T(8,128)(2,1)}, u32[]{:S(2)}) copy-start(bf16[24,8,4096]{2,1,0:T(8,128)(2,1)} %x_ref.3) | copy-start | bytes 4718596
  1.4 9.2 %copy-start.5 = (s32[24,32]{1,0:T(8,128)S(1)}, s32[24,32]{1,0:T(8,128)}, u32[]{:S(2)}) copy-start(s32[24,32]{1,0:T(8,128)} %param.6) | copy-start | bytes 9220
  1.4 9.2 %copy-start.6 = (s32[24]{0:T(128)S(1)}, s32[24]{0:T(128)}, u32[]{:S(2)}) copy-start(s32[24]{0:T(128)} %param.7) | copy-start | bytes 292
  1.4 9.3 %copy-start.1 = (bf16[24,8,4096]{2,1,0:T(8,128)(2,1)S(1)}, bf16[24,8,4096]{2,1,0:T(8,128)(2,1)}, u32[]{:S(2)}) copy-start(bf16[24,8,4096]{2,1,0:T(8,128)(2,1)} %x_ref.3) | copy-start | bytes 4718596
  2.2 3.2 %collective-permute-start = (bf16[16,4,64,128]{3,2,1,0:T(8,128)(2,1)S(1)}, bf16[16,4,64,128]{3,2,1,0:T(8,128)(2,1)}, u32[]{:S(2)}, u32[]{:S(2)}) collective-permute-start(bf16[16,4,64,128]{3,2,1,0:T(8,128)(2,1)S(1)} %relayout.3.refs_0_), channel_id=1, source_target_pairs={{0,1},{1,0},{2,3},{3,2},{4,5},{5,4},{6,7},{7,6},{8,9},{9,8},{10,11... | collective-permute-start | bytes 3145736 | tf_op jit(solution)/shard_map/ppermute | solution.py:429
  3.0 24.8 %collective-permute-start.2 = (bf16[16,4,64,128]{3,2,1,0:T(8,128)(2,1)S(1)}, bf16[16,4,64,128]{3,2,1,0:T(8,128)(2,1)}, u32[]{:S(2)}, u32[]{:S(2)}) collective-permute-start(bf16[16,4,64,128]{3,2,1,0:T(8,128)(2,1)S(1)} %relayout.3.refs_0_), channel_id=1, source_target_pairs={{0,2},{1,3},{2,0},{3,1},{4,6},{5,7},{6,4},{7,5},{8,10},{9,11},{10,... | collective-permute-start | bytes 3145736 | tf_op jit(solution)/shard_map/ppermute | solution.py:426
  5.4 1.1 %copy-start.2 = (bf16[24,4,4096]{2,1,0:T(4,128)(2,1)S(1)}, bf16[24,4,4096]{2,1,0:T(4,128)(2,1)}, u32[]{:S(2)}) copy-start(bf16[24,4,4096]{2,1,0:T(4,128)(2,1)} %x_ref.4) | copy-start | bytes 2359300
  7.6 21.2 %collective-permute-start.1 = (bf16[24,2,64,128]{3,2,1,0:T(8,128)(2,1)S(1)}, bf16[24,2,64,128]{3,2,1,0:T(8,128)(2,1)S(1)}, u32[]{:S(2)}, u32[]{:S(2)}) collective-permute-start(bf16[24,2,64,128]{3,2,1,0:T(8,128)(2,1)S(1)} %relayout_rows.1.refs_0_), channel_id=1, source_target_pairs={{0,4},{2,6},{4,8},{5,1},{6,10},{7,3},{8,12},{9,5},{10,14},{11,7},{... | collective-permute-start | bytes 2359304 | tf_op jit(solution)/shard_map/ppermute | solution.py:423
  11.1 5.0 %collective-permute-start.3 = (bf16[8,4,64,128]{3,2,1,0:T(8,128)(2,1)S(1)}, bf16[8,4,64,128]{3,2,1,0:T(8,128)(2,1)S(1)}, u32[]{:S(2)}, u32[]{:S(2)}) collective-permute-start(bf16[8,4,64,128]{3,2,1,0:T(8,128)(2,1)S(1)} %relayout.4.refs_0_), channel_id=1, source_target_pairs={{0,1},{1,0},{2,3},{3,2},{4,5},{5,4},{6,7},{7,6},{8,9},{9,8},{10,11... | collective-permute-start | bytes 1572872 | tf_op jit(solution)/shard_map/ppermute | solution.py:429
  12.1 4.0 %copy-start.3 = (bf16[24,4,4096]{2,1,0:T(4,128)(2,1)S(1)}, bf16[24,4,4096]{2,1,0:T(4,128)(2,1)}, u32[]{:S(2)}) copy-start(bf16[24,4,4096]{2,1,0:T(4,128)(2,1)} %x_ref.4) | copy-start | bytes 2359300
  17.0 3.5 %copy-start.4 = (s32[192,4]{0,1:T(4,128)S(1)}, s32[192,4]{0,1:T(4,128)}, u32[]{:S(2)}) copy-start(s32[192,4]{0,1:T(4,128)} %param.9) | copy-start | bytes 9220
  28.7 6.1 %collective-permute-start.6 = (bf16[16,4,64,128]{3,2,1,0:T(8,128)(2,1)}, bf16[16,4,64,128]{3,2,1,0:T(8,128)(2,1)S(1)}, u32[]{:S(2)}, u32[]{:S(2)}) collective-permute-start(bf16[16,4,64,128]{3,2,1,0:T(8,128)(2,1)} %collective-permute-done.2.refs_0_), channel_id=1, source_target_pairs={{0,1},{1,0},{2,3},{3,2},{4,5},{5,4},{6,7},{7,6},{8,9},{9,8},{10,11... | collective-permute-start | bytes 3145736 | tf_op jit(solution)/shard_map/ppermute | solution.py:429
  29.3 3.3 %collective-permute-start.5 = (bf16[24,2,64,128]{3,2,1,0:T(8,128)(2,1)S(1)}, bf16[24,2,64,128]{3,2,1,0:T(8,128)(2,1)S(1)}, u32[]{:S(2)}, u32[]{:S(2)}) collective-permute-start(bf16[24,2,64,128]{3,2,1,0:T(8,128)(2,1)S(1)} %collective-permute-done.1.refs_0_), channel_id=1, source_target_pairs={{0,1},{1,0},{2,3},{3,2},{4,5},{5,4},{6,7},{7,6},{8,9},{9,8},{10,11... | collective-permute-start | bytes 2359304 | tf_op jit(solution)/shard_map/ppermute | solution.py:429
  29.3 13.0 %collective-permute-start.4 = (bf16[8,4,64,128]{3,2,1,0:T(8,128)(2,1)S(1)}, bf16[8,4,64,128]{3,2,1,0:T(8,128)(2,1)S(1)}, u32[]{:S(2)}, u32[]{:S(2)}) collective-permute-start(bf16[8,4,64,128]{3,2,1,0:T(8,128)(2,1)S(1)} %relayout.4.refs_0_), channel_id=1, source_target_pairs={{0,2},{1,3},{2,0},{3,1},{4,6},{5,7},{6,4},{7,5},{8,10},{9,11},{10,... | collective-permute-start | bytes 1572872 | tf_op jit(solution)/shard_map/ppermute | solution.py:426
  42.2 6.5 %collective-permute-start.7 = (bf16[8,4,64,128]{3,2,1,0:T(8,128)(2,1)S(1)}, bf16[8,4,64,128]{3,2,1,0:T(8,128)(2,1)S(1)}, u32[]{:S(2)}, u32[]{:S(2)}) collective-permute-start(bf16[8,4,64,128]{3,2,1,0:T(8,128)(2,1)S(1)} %collective-permute-done.4.refs_0_), channel_id=1, source_target_pairs={{0,1},{1,0},{2,3},{3,2},{4,5},{5,4},{6,7},{7,6},{8,9},{9,8},{10,11... | collective-permute-start | bytes 1572872 | tf_op jit(solution)/shard_map/ppermute | solution.py:429
  44.6 16.0 %collective-permute-start.9 = (bf16[10,4,4096]{2,1,0:T(4,128)(2,1)S(1)}, bf16[10,4,4096]{2,1,0:T(4,128)(2,1)S(1)}, u32[]{:S(2)}, u32[]{:S(2)}) collective-permute-start(bf16[10,4,4096]{2,1,0:T(4,128)(2,1)S(1)} %coarse.9), channel_id=1, source_target_pairs={{4,0},{8,4},{12,8},{16,12},{20,16},{24,20},{28,24},{5,1},{9,5},{13... | collective-permute-start | bytes 983048 | tf_op jit(solution)/shard_map/ppermute | solution.py:435
  53.6 23.2 %collective-permute-start.8 = (bf16[10,8,2048]{2,1,0:T(8,128)(2,1)S(1)}, bf16[10,8,2048]{2,1,0:T(8,128)(2,1)S(1)}, u32[]{:S(2)}, u32[]{:S(2)}) collective-permute-start(bf16[10,8,2048]{2,1,0:T(8,128)(2,1)S(1)} %coarse.7), channel_id=1, source_target_pairs={{0,4},{4,8},{8,12},{12,16},{16,20},{20,24},{24,28},{1,5},{5,9},{9,... | collective-permute-start | bytes 983048 | tf_op jit(solution)/shard_map/ppermute | solution.py:432
  56.4 20.2 %collective-permute-start.10 = (bf16[10,4,2048]{2,1,0:T(4,128)(2,1)S(1)}, bf16[10,4,2048]{2,1,0:T(4,128)(2,1)S(1)}, u32[]{:S(2)}, u32[]{:S(2)}) collective-permute-start(bf16[10,4,2048]{2,1,0:T(4,128)(2,1)S(1)} %coarse.10), channel_id=1, source_target_pairs={{4,0},{8,4},{12,8},{16,12},{20,16},{24,20},{28,24},{5,1},{9,5},{13... | collective-permute-start | bytes 491528 | tf_op jit(solution)/shard_map/ppermute | solution.py:435
  61.8 18.5 %collective-permute-start.13 = (bf16[10,8,2048]{2,1,0:T(8,128)(2,1)S(1)}, bf16[10,8,2048]{2,1,0:T(8,128)(2,1)S(1)}, u32[]{:S(2)}, u32[]{:S(2)}) collective-permute-start(bf16[10,8,2048]{2,1,0:T(8,128)(2,1)S(1)} %coarse.11), channel_id=1, source_target_pairs={{0,4},{4,8},{8,12},{12,16},{16,20},{20,24},{24,28},{1,5},{5,9},{9,... | collective-permute-start | bytes 983048 | tf_op jit(solution)/shard_map/ppermute | solution.py:432
  64.6 15.6 %collective-permute-start.14 = (bf16[10,4,2048]{2,1,0:T(4,128)(2,1)S(1)}, bf16[10,4,2048]{2,1,0:T(4,128)(2,1)S(1)}, u32[]{:S(2)}, u32[]{:S(2)}) collective-permute-start(bf16[10,4,2048]{2,1,0:T(4,128)(2,1)S(1)} %coarse.13), channel_id=1, source_target_pairs={{4,0},{8,4},{12,8},{16,12},{20,16},{24,20},{28,24},{5,1},{9,5},{13... | collective-permute-start | bytes 491528 | tf_op jit(solution)/shard_map/ppermute | solution.py:435
  76.9 11.6 %collective-permute-start.12 = (bf16[14,8,2048]{2,1,0:T(8,128)(2,1)S(1)}, bf16[14,8,2048]{2,1,0:T(8,128)(2,1)S(1)}, u32[]{:S(2)}, u32[]{:S(2)}) collective-permute-start(bf16[14,8,2048]{2,1,0:T(8,128)(2,1)S(1)} %bitcast.11), channel_id=1, source_target_pairs={{0,2},{1,3},{2,0},{3,1},{4,6},{5,7},{6,4},{7,5},{8,10},{9,11},{10,... | collective-permute-start | bytes 1376264 | tf_op jit(solution)/shard_map/ppermute | solution.py:426
  80.4 17.9 %collective-permute-start.15 = (bf16[14,8,2048]{2,1,0:T(8,128)(2,1)S(1)}, bf16[14,8,2048]{2,1,0:T(8,128)(2,1)S(1)}, u32[]{:S(2)}, u32[]{:S(2)}) collective-permute-start(bf16[14,8,2048]{2,1,0:T(8,128)(2,1)S(1)} %bitcast.14), channel_id=1, source_target_pairs={{0,2},{1,3},{2,0},{3,1},{4,6},{5,7},{6,4},{7,5},{8,10},{9,11},{10,... | collective-permute-start | bytes 1376264 | tf_op jit(solution)/shard_map/ppermute | solution.py:426
  88.5 9.8 %collective-permute-start.16 = (bf16[14,8,2048]{2,1,0:T(8,128)(2,1)S(1)}, bf16[14,8,2048]{2,1,0:T(8,128)(2,1)S(1)}, u32[]{:S(2)}, u32[]{:S(2)}) collective-permute-start(bf16[14,8,2048]{2,1,0:T(8,128)(2,1)S(1)} %collective-permute-done.12.refs_2_), channel_id=1, source_target_pairs={{0,1},{1,0},{2,3},{3,2},{4,5},{5,4},{6,7},{7,6},{8,9},{9,8},{10,11... | collective-permute-start | bytes 1376264 | tf_op jit(solution)/shard_map/ppermute | solution.py:429
  90.9 8.9 %collective-permute-start.11 = (bf16[14,8,2048]{2,1,0:T(8,128)(2,1)S(1)}, bf16[14,8,2048]{2,1,0:T(8,128)(2,1)S(1)}, u32[]{:S(2)}, u32[]{:S(2)}) collective-permute-start(bf16[14,8,2048]{2,1,0:T(8,128)(2,1)S(1)} %bitcast.12), channel_id=1, source_target_pairs={{0,1},{1,0},{2,3},{3,2},{4,5},{5,4},{6,7},{7,6},{8,9},{9,8},{10,11... | collective-permute-start | bytes 1376264 | tf_op jit(solution)/shard_map/ppermute | solution.py:429
  90.9 11.7 %collective-permute-start.17 = (bf16[14,8,2048]{2,1,0:T(8,128)(2,1)S(1)}, bf16[14,8,2048]{2,1,0:T(8,128)(2,1)S(1)}, u32[]{:S(2)}, u32[]{:S(2)}) collective-permute-start(bf16[14,8,2048]{2,1,0:T(8,128)(2,1)S(1)} %bitcast.15), channel_id=1, source_target_pairs={{0,1},{1,0},{2,3},{3,2},{4,5},{5,4},{6,7},{7,6},{8,9},{9,8},{10,11... | collective-permute-start | bytes 1376264 | tf_op jit(solution)/shard_map/ppermute | solution.py:429
  98.4 4.3 %collective-permute-start.18 = (bf16[14,8,2048]{2,1,0:T(8,128)(2,1)S(1)}, bf16[14,8,2048]{2,1,0:T(8,128)(2,1)S(1)}, u32[]{:S(2)}, u32[]{:S(2)}) collective-permute-start(bf16[14,8,2048]{2,1,0:T(8,128)(2,1)S(1)} %collective-permute-done.15.refs_3_), channel_id=1, source_target_pairs={{0,1},{1,0},{2,3},{3,2},{4,5},{5,4},{6,7},{7,6},{8,9},{9,8},{10,11... | collective-permute-start | bytes 1376264 | tf_op jit(solution)/shard_map/ppermute | solution.py:429

commit v8 on v6

--- a/solution.py
+++ b/solution.py
@@ -416,7 +416,7 @@
     share = CB // ncol
     tiles = (GROUPS * share + 1) // 2
     parts = ((0, rb * 2 // 3), (rb * 2 // 3, rb // 3))
-    chunks = ((0, 32), (32, 64))
+    chunks = ((0, 16), (16, 40), (40, 64))
 
     def outward(x):
         pairs = [(r * ncol + c, (r + 1 - 2 * (c % 2)) * ncol + c) for r in range(nrow) for c in range(ncol)]
@@ -469,24 +469,25 @@
         return jnp.pad(y.astype(F32), ((0, 0), (g, 2 - g), (0, 0), (0, 0)))
 
     late = downward(coarse_rows(left, aps, ((CB // 2, CB),), 0, BS, BF, 1.0)[0])
-    highs = [coarse_rows(left, aps, ((2 * CB, 3 * CB),), a0, a1, BF, 1.0)[0] for a0, a1 in chunks]
-    left, highs = lax.optimization_barrier((left, highs))
-    highs[1], late = lax.optimization_barrier((highs[1], late))
-    highs = [upward(x) for x in highs]
+    highs = [upward(coarse_rows(left, aps, ((2 * CB, 3 * CB),), a0, a1, BF, 1.0)[0]) for a0, a1 in chunks]
     mids = [coarse_rows(left, aps, ((CB, 2 * CB),), a0, a1, F32, 1.0)[0] for a0, a1 in chunks]
-    early, mids = lax.optimization_barrier((early, mids))
     lower = jnp.concatenate([early, late], axis=1)
-    totals, fars = [], []
-    for (a0, a1), high, mid in zip(chunks, highs, mids):
-        total = columns(high, 0) + columns(mid, 1) + columns(lower[:, :, a0 * BS : a1 * BS], 2)
-        totals.append(total.astype(BF).reshape((share * (GROUPS + 2),) + total.shape[2:]))
-        fars.append([over_y(totals[-1], s) for s in range(1, ny)])
-    fars[0], totals[1] = lax.optimization_barrier((fars[0], totals[1]))
+    totals, sides, fars, beyond = [], [], [], []
+    for z, (a0, a1) in enumerate(chunks):
+        total = columns(highs[z], 0) + columns(mids[z], 1) + columns(lower[:, :, a0 * BS : a1 * BS], 2)
+        total = total.astype(BF).reshape((share * (GROUPS + 2),) + total.shape[2:])
+        if z > 0:
+            fars[-1], total = lax.optimization_barrier((fars[-1], total))
+            beyond.append([over_core(x) for x in fars[-1]])
+        totals.append(total)
+        sides.append(over_core(total))
+        fars.append([over_y(total, s) for s in range(1, ny)])
     out = None
-    for (a0, a1), total, far in zip(chunks, totals, fars):
-        if out is not None:
-            far, out = lax.optimization_barrier((far, out))
-        srcs = [z for g in [total] + far for z in (g, over_core(g))]
+    for z, (a0, a1) in enumerate(chunks):
+        if z == len(chunks) - 1:
+            fars[z], out = lax.optimization_barrier((fars[z], out))
+            beyond.append([over_core(x) for x in fars[z]])
+        srcs = [totals[z], sides[z]] + [q for pair in zip(fars[z], beyond[z]) for q in pair]
         out = assemble(order, srcs, a0, BS * BS, out)
     return out
 

time: 106 us -> 110 us (1.038); the launches traced: 104 us -> 110 us
  starting transfers between devices: 27.4 us -> 35.4 us
  waiting for transfers between devices: 33.6 us -> 30.3 us
    ppermute x2 -> x3, waiting for transfers between devices: 5.84 us -> 0.01 us  [upward(): return lax.ppermute(x, 'row', [(i, i + 1) for i in range(nrow - 1)])]
    ppermute x2 -> x3, starting transfers between devices: 5.27 us -> 9.66 us  [upward(): return lax.ppermute(x, 'row', [(i, i + 1) for i in range(nrow - 1)])]
    ppermute x9 -> x11, starting transfers between devices: 7.94 us -> 10.4 us  [over_core(): return lax.ppermute(x, 'col', [(c, c ^ 1) for c in range(ncol)])]
    ppermute x2, waiting for transfers between devices: 8.22 us -> 9.92 us  [downward(): return lax.ppermute(x, 'row', [(i + 1, i) for i in range(nrow - 1)])]
    ppermute x4 -> x5, starting transfers between devices: 5.04 us -> 6.3 us  [over_y(): lax.ppermute(x, 'col', [(y * 2 + c, (y + s) % ny * 2 + c) for y in range(...]
    ppermute x9 -> x11, waiting for transfers between devices: 3.83 us -> 4.97 us  [over_core(): return lax.ppermute(x, 'col', [(c, c ^ 1) for c in range(ncol)])]
    pallas_call x2 -> x3, Pallas kernels: 5.76 us -> 6.56 us  [assemble(): pl.pallas_call(assemble_kernel, grid=(per,), out_shape=jax.ShapeDtypeStru...]
    ppermute x4 -> x5, waiting for transfers between devices: 14.8 us -> 14.4 us  [over_y(): lax.ppermute(x, 'col', [(y * 2 + c, (y + s) % ny * 2 + c) for y in range(...]
  transfers between devices with their start and end apart: 18 -> 22, of which waited for: 10 -> 12; matrix products, arithmetic and copies ran while one was open for 2% -> 1% of each run, Pallas kernels for 34% -> 33%
where the time goes in v8:
time: 110 us
  Pallas kernels  39.3 us (36%)
  starting transfers between devices  35.4 us (32%)
  waiting for transfers between devices  30.3 us (28%)
  local copies, waits for them, and re-layouts  2.56 us (2%)
  other arithmetic  1.6 us (1%)
    ppermute x5, waiting for transfers between devices, over_y(): lax.ppermute(x, 'col', [(y * 2 + c, (y + s) % ny * 2 + c) for y in range(...  14.4 us
    pallas_call x2, Pallas kernels, product(): pl.pallas_call(functools.partial(product_kernel, first, rb, shifts), out_...  10.9 us
    ppermute x11, starting transfers between devices, over_core(): return lax.ppermute(x, 'col', [(c, c ^ 1) for c in range(ncol)])  10.4 us
    ppermute x2, waiting for transfers between devices, downward(): return lax.ppermute(x, 'row', [(i + 1, i) for i in range(nrow - 1)])  9.92 us
    ppermute x3, starting transfers between devices, upward(): return lax.ppermute(x, 'row', [(i, i + 1) for i in range(nrow - 1)])  9.66 us
    pallas_call x3, Pallas kernels, assemble(): pl.pallas_call(assemble_kernel, grid=(per,), out_shape=jax.ShapeDtypeStru...  6.56 us
    ppermute x5, starting transfers between devices, over_y(): lax.ppermute(x, 'col', [(y * 2 + c, (y + s) % ny * 2 + c) for y in range(...  6.3 us
    pallas_call x8, Pallas kernels, coarse_rows(): pl.pallas_call(functools.partial(coarse_kernel, sets, a0, a1), out_shape=...  6.18 us
  transfers between devices with their start and end apart: 22, of which 12 were waited for; matrix products, arithmetic and copies ran while one was open for 1% of the time, Pallas kernels for 33%

profile of v8, /device:TPU:9, one launch (start us, length us, event | category | flops | bytes accessed | tf_op | source)
XLA Modules:
  0.0 109.5 jit_solution(7159355963169281709)
XLA Ops:
  0.0 1.4 %copy-done = bf16[24,8,4096]{2,1,0:T(8,128)(2,1)S(1)} copy-done((bf16[24,8,4096]{2,1,0:T(8,128)(2,1)S(1)}, bf16[24,8,4096]{2,1,0:T(8,128)(2,1)}, u32[]{:S(2)}) %copy-start) | copy-done | bytes 1572888
  1.4 0.8 relayout.3.refs_0_
  2.2 0.7 collective-permute-start
  3.0 1.3 %collective-permute-start.2 = (bf16[16,4,64,128]{3,2,1,0:T(8,128)(2,1)S(1)}, bf16[16,4,64,128]{3,2,1,0:T(8,128)(2,1)}, u32[]{:S(2)}, u32[]{:S(2)}) collective-permute-start(bf16[16,4,64,128]{3,2,1,0:T(8,128)(2,1)S(1)} %relayout.3.refs_0_), channel_id=1, source_target_pairs={{0,2},{1,3},{2,0},{3,1},{4,6},{5,7},{6,4},{7,5},{8,10},{9,11},{10,... | collective-permute-start | bytes 3145736 | tf_op jit(solution)/shard_map/ppermute | solution.py:426
  4.2 0.8 add_select_fusion.4.table_ref
  5.0 0.3 collective-permute-done.refs_1_
  5.4 1.1 %copy-done.2 = bf16[24,4,4096]{2,1,0:T(4,128)(2,1)S(1)} copy-done((bf16[24,4,4096]{2,1,0:T(4,128)(2,1)S(1)}, bf16[24,4,4096]{2,1,0:T(4,128)(2,1)}, u32[]{:S(2)}) %copy-start.2) | copy-done | bytes 786456
  6.5 1.1 relayout_rows.1.refs_0_
  7.6 3.0 %collective-permute-start.1 = (bf16[24,2,64,128]{3,2,1,0:T(8,128)(2,1)S(1)}, bf16[24,2,64,128]{3,2,1,0:T(8,128)(2,1)S(1)}, u32[]{:S(2)}, u32[]{:S(2)}) collective-permute-start(bf16[24,2,64,128]{3,2,1,0:T(8,128)(2,1)S(1)} %relayout_rows.1.refs_0_), channel_id=1, source_target_pairs={{0,4},{2,6},{4,8},{5,1},{6,10},{7,3},{8,12},{9,5},{10,14},{11,7},{... | collective-permute-start | bytes 2359304 | tf_op jit(solution)/shard_map/ppermute | solution.py:423
  10.6 0.1 subtract_select_fusion.place_ref
  10.7 0.4 relayout.4.refs_0_
  11.1 0.8 collective-permute-start.3
  11.9 0.2 fusion.12.order_ref
  12.1 3.9 %near_band.2.start_ref = bf16[4,27,256,128]{3,2,1,0:T(8,128)(2,1)S(1)} custom-call(s32[24,32]{1,0:T(8,128)S(1)} %subtract_select_fusion.place_ref, bf16[16,4,64,128]{3,2,1,0:T(8,128)(2,1)S(1)} %relayout.3.refs_0_, bf16[16,4,64,128]{3,2,1,0:T(8,128)(2,1)} %collective-permute-done.refs_1_), custom_call_target="tpu_custom_call" | custom-call | flops 256000000 | bytes 9472000 | tf_op jit(solution)/shard_map/near_band/pallas_call | solution.py:255
  16.1 0.9 relayout.5.pl_ref
  17.0 2.1 %near_band.3.start_ref = bf16[2,27,256,128]{3,2,1,0:T(8,128)(2,1)S(1)} custom-call(s32[24,32]{1,0:T(8,128)S(1)} %subtract_select_fusion.place_ref, bf16[8,4,64,128]{3,2,1,0:T(8,128)(2,1)S(1)} %relayout.4.refs_0_, bf16[8,4,64,128]{3,2,1,0:T(8,128)(2,1)S(1)} %collective-permute-done.3.refs_1_), custom_call_target="tpu_custom_call" | custom-call | flops 128000000 | bytes 4736000 | tf_op jit(solution)/shard_map/near_band/pallas_call | solution.py:255
  19.0 1.4 %right_factor.2.own_ref = bf16[6,5,256,128]{3,2,1,0:T(8,128)(2,1)S(1)} custom-call(s32[4,72]{1,0:T(4,128)S(1)} %add_select_fusion.4.table_ref, bf16[24,2,64,128]{3,2,1,0:T(8,128)(2,1)S(1)} %relayout_rows.1.refs_0_), custom_call_target="tpu_custom_call" | custom-call | flops 200000000 | bytes 7400000 | tf_op jit(solution)/shard_map/right_factor/pallas_call | solution.py:186
  20.5 2.9 %left_factor.1.left_ref = bf16[12,24,64,128]{3,2,1,0:T(8,128)(2,1)S(1)} custom-call(s32[4,192]{1,0:T(4,128)S(1)} %bitcast.26, bf16[24,2,64,128]{3,2,1,0:T(8,128)(2,1)S(1)} %relayout.5.pl_ref), custom_call_target="tpu_custom_call" | custom-call | flops 290000000 | bytes 10730000 | tf_op jit(solution)/shard_map/left_factor/pallas_call | solution.py:118
  23.4 4.4 %collective-permute-done.2.refs_0_ = bf16[16,4,64,128]{3,2,1,0:T(8,128)(2,1)} collective-permute-done((bf16[16,4,64,128]{3,2,1,0:T(8,128)(2,1)S(1)}, bf16[16,4,64,128]{3,2,1,0:T(8,128)(2,1)}, u32[]{:S(2)}, u32[]{:S(2)}) %collective-permute-start.2) | collective-permute-done | bytes 1048608 | tf_op jit(solution)/shard_map/ppermute | solution.py:426
  27.8 0.9 collective-permute-done.1.refs_0_
  28.7 0.5 collective-permute-start.6
  29.3 1.2 %collective-permute-start.4 = (bf16[8,4,64,128]{3,2,1,0:T(8,128)(2,1)S(1)}, bf16[8,4,64,128]{3,2,1,0:T(8,128)(2,1)S(1)}, u32[]{:S(2)}, u32[]{:S(2)}) collective-permute-start(bf16[8,4,64,128]{3,2,1,0:T(8,128)(2,1)S(1)} %relayout.4.refs_0_), channel_id=1, source_target_pairs={{0,2},{1,3},{2,0},{3,1},{4,6},{5,7},{6,4},{7,5},{8,10},{9,11},{10,... | collective-permute-start | bytes 1572872 | tf_op jit(solution)/shard_map/ppermute | solution.py:426
  30.5 2.0 %collective-permute-done.5.refs_1_ = bf16[24,2,64,128]{3,2,1,0:T(8,128)(2,1)S(1)} collective-permute-done((bf16[24,2,64,128]{3,2,1,0:T(8,128)(2,1)S(1)}, bf16[24,2,64,128]{3,2,1,0:T(8,128)(2,1)S(1)}, u32[]{:S(2)}, u32[]{:S(2)}) %collective-permute-start.5) | collective-permute-done | bytes 786464 | tf_op jit(solution)/shard_map/ppermute | solution.py:429
  32.5 2.3 %right_factor.3.near_ref = bf16[12,5,256,128]{3,2,1,0:T(8,128)(2,1)S(1)} custom-call(s32[4,72]{1,0:T(4,128)S(1)} %add_select_fusion.4.table_ref, bf16[24,2,64,128]{3,2,1,0:T(8,128)(2,1)S(1)} %collective-permute-done.1.refs_0_, bf16[24,2,64,128]{3,2,1,0:T(8,128)(2,1)S(1)} %collective-permute-done.5.refs_1_), custom_call_target="tpu_custom_call" | custom-call | flops 300000000 | bytes 11100000 | tf_op jit(solution)/shard_map/right_factor/pallas_call | solution.py:186
  34.8 7.1 %product.2.refs_0_ = bf16[16,64,640]{2,1,0:T(8,128)(2,1)S(1)} custom-call(s32[24,32]{1,0:T(8,128)S(1)} %subtract_select_fusion.place_ref, bf16[6,5,256,128]{3,2,1,0:T(8,128)(2,1)S(1)} %right_factor.2.own_ref, bf16[12,5,256,128]{3,2,1,0:T(8,128)(2,1)S(1)} %right_factor.3.near_ref, bf16[4,27,256,128]{3,2,1,0:T(8,128)(2,1)S(1)} %near_band.2.start_ref, ...), custom_call_target="tpu_custom_call" | custom-call | flops 480000000 | bytes 17760000 | tf_op jit(solution)/shard_map/product/pallas_call | solution.py:299
  42.0 0.3 collective-permute-done.4.refs_0_
  42.2 1.4 %collective-permute-start.7 = (bf16[8,4,64,128]{3,2,1,0:T(8,128)(2,1)S(1)}, bf16[8,4,64,128]{3,2,1,0:T(8,128)(2,1)S(1)}, u32[]{:S(2)}, u32[]{:S(2)}) collective-permute-start(bf16[8,4,64,128]{3,2,1,0:T(8,128)(2,1)S(1)} %collective-permute-done.4.refs_0_), channel_id=1, source_target_pairs={{0,1},{1,0},{2,3},{3,2},{4,5},{5,4},{6,7},{7,6},{8,9},{9,8},{10,11... | collective-permute-start | bytes 1572872 | tf_op jit(solution)/shard_map/ppermute | solution.py:429
  43.6 0.9 coarse.10
  44.6 4.2 %collective-permute-start.9 = (bf16[10,4,4096]{2,1,0:T(4,128)(2,1)S(1)}, bf16[10,4,4096]{2,1,0:T(4,128)(2,1)S(1)}, u32[]{:S(2)}, u32[]{:S(2)}) collective-permute-start(bf16[10,4,4096]{2,1,0:T(4,128)(2,1)S(1)} %coarse.10), channel_id=1, source_target_pairs={{4,0},{8,4},{12,8},{16,12},{20,16},{24,20},{28,24},{5,1},{9,5},{13... | collective-permute-start | bytes 983048 | tf_op jit(solution)/shard_map/ppermute | solution.py:435
  48.7 3.8 %product.3.refs_1_ = bf16[8,64,640]{2,1,0:T(8,128)(2,1)S(1)} custom-call(s32[24,32]{1,0:T(8,128)S(1)} %subtract_select_fusion.place_ref, bf16[6,5,256,128]{3,2,1,0:T(8,128)(2,1)S(1)} %right_factor.2.own_ref, bf16[12,5,256,128]{3,2,1,0:T(8,128)(2,1)S(1)} %right_factor.3.near_ref, bf16[2,27,256,128]{3,2,1,0:T(8,128)(2,1)S(1)} %near_band.3.start_ref, ...), custom_call_target="tpu_custom_call" | custom-call | flops 240000000 | bytes 8880000 | tf_op jit(solution)/shard_map/product/pallas_call | solution.py:299
  52.5 1.1 %coarse.11 = bf16[10,4,4096]{2,1,0:T(4,128)(2,1)S(1)} custom-call(bf16[12,24,64,128]{3,2,1,0:T(8,128)(2,1)S(1)} %left_factor.1.left_ref, bf16[16,64,640]{2,1,0:T(8,128)(2,1)S(1)} %product.2.refs_0_, bf16[8,64,640]{2,1,0:T(8,128)(2,1)S(1)} %product.3.refs_1_), custom_call_target="tpu_custom_call" | custom-call | flops 100000000 | bytes 3700000 | tf_op jit(solution)/shard_map/coarse/pallas_call | solution.py:346
  53.7 1.9 %collective-permute-start.10 = (bf16[10,4,4096]{2,1,0:T(4,128)(2,1)S(1)}, bf16[10,4,4096]{2,1,0:T(4,128)(2,1)S(1)}, u32[]{:S(2)}, u32[]{:S(2)}) collective-permute-start(bf16[10,4,4096]{2,1,0:T(4,128)(2,1)S(1)} %coarse.11), channel_id=1, source_target_pairs={{4,0},{8,4},{12,8},{16,12},{20,16},{24,20},{28,24},{5,1},{9,5},{13... | collective-permute-start | bytes 983048 | tf_op jit(solution)/shard_map/ppermute | solution.py:435
  55.6 0.6 coarse.8
  56.2 3.4 %collective-permute-start.8 = (bf16[10,8,1024]{2,1,0:T(8,128)(2,1)S(1)}, bf16[10,8,1024]{2,1,0:T(8,128)(2,1)S(1)}, u32[]{:S(2)}, u32[]{:S(2)}) collective-permute-start(bf16[10,8,1024]{2,1,0:T(8,128)(2,1)S(1)} %coarse.8), channel_id=1, source_target_pairs={{0,4},{4,8},{8,12},{12,16},{16,20},{20,24},{24,28},{1,5},{5,9},{9,... | collective-permute-start | bytes 491528 | tf_op jit(solution)/shard_map/ppermute | solution.py:432
  59.6 0.7 coarse.12
  60.3 2.9 %collective-permute-start.12 = (bf16[10,8,1536]{2,1,0:T(8,128)(2,1)S(1)}, bf16[10,8,1536]{2,1,0:T(8,128)(2,1)S(1)}, u32[]{:S(2)}, u32[]{:S(2)}) collective-permute-start(bf16[10,8,1536]{2,1,0:T(8,128)(2,1)S(1)} %coarse.12), channel_id=1, source_target_pairs={{0,4},{4,8},{8,12},{12,16},{16,20},{20,24},{24,28},{1,5},{5,9},{9,... | collective-permute-start | bytes 737288 | tf_op jit(solution)/shard_map/ppermute | solution.py:432
  63.2 0.7 coarse.14
  64.0 3.4 %collective-permute-start.14 = (bf16[10,8,1536]{2,1,0:T(8,128)(2,1)S(1)}, bf16[10,8,1536]{2,1,0:T(8,128)(2,1)S(1)}, u32[]{:S(2)}, u32[]{:S(2)}) collective-permute-start(bf16[10,8,1536]{2,1,0:T(8,128)(2,1)S(1)} %coarse.14), channel_id=1, source_target_pairs={{0,4},{4,8},{8,12},{12,16},{16,20},{20,24},{24,28},{1,5},{5,9},{9,... | collective-permute-start | bytes 737288 | tf_op jit(solution)/shard_map/ppermute | solution.py:432
  67.4 0.7 coarse.13
  68.1 0.6 coarse.9
  68.7 9.9 %collective-permute-done.10 = bf16[10,4,4096]{2,1,0:T(4,128)(2,1)S(1)} collective-permute-done((bf16[10,4,4096]{2,1,0:T(4,128)(2,1)S(1)}, bf16[10,4,4096]{2,1,0:T(4,128)(2,1)S(1)}, u32[]{:S(2)}, u32[]{:S(2)}) %collective-permute-start.10) | collective-permute-done | bytes 327712 | tf_op jit(solution)/shard_map/ppermute | solution.py:435
  78.6 0.1 pad_maximum_fusion.2
  78.8 1.3 %collective-permute-start.11 = (bf16[14,8,1024]{2,1,0:T(8,128)(2,1)S(1)}, bf16[14,8,1024]{2,1,0:T(8,128)(2,1)S(1)}, u32[]{:S(2)}, u32[]{:S(2)}) collective-permute-start(bf16[14,8,1024]{2,1,0:T(8,128)(2,1)S(1)} %bitcast.22), channel_id=1, source_target_pairs={{0,2},{1,3},{2,0},{3,1},{4,6},{5,7},{6,4},{7,5},{8,10},{9,11},{10,... | collective-permute-start | bytes 688136 | tf_op jit(solution)/shard_map/ppermute | solution.py:426
  80.1 0.2 pad_maximum_fusion
  80.3 0.1 add_convert_fusion.1
  80.4 4.4 %collective-permute-done.11.refs_2_ = bf16[14,8,1024]{2,1,0:T(8,128)(2,1)S(1)} collective-permute-done((bf16[14,8,1024]{2,1,0:T(8,128)(2,1)S(1)}, bf16[14,8,1024]{2,1,0:T(8,128)(2,1)S(1)}, u32[]{:S(2)}, u32[]{:S(2)}) %collective-permute-start.11) | collective-permute-done | bytes 229408 | tf_op jit(solution)/shard_map/ppermute | solution.py:426
  84.8 1.2 %collective-permute-start.13 = (bf16[14,8,1536]{2,1,0:T(8,128)(2,1)S(1)}, bf16[14,8,1536]{2,1,0:T(8,128)(2,1)S(1)}, u32[]{:S(2)}, u32[]{:S(2)}) collective-permute-start(bf16[14,8,1536]{2,1,0:T(8,128)(2,1)S(1)} %bitcast.15), channel_id=1, source_target_pairs={{0,2},{1,3},{2,0},{3,1},{4,6},{5,7},{6,4},{7,5},{8,10},{9,11},{10,... | collective-permute-start | bytes 1032200 | tf_op jit(solution)/shard_map/ppermute | solution.py:426
  86.1 0.7 coarse.15
  86.8 0.1 add_convert_fusion
  86.9 2.4 %collective-permute-start.18 = (bf16[14,8,1536]{2,1,0:T(8,128)(2,1)S(1)}, bf16[14,8,1536]{2,1,0:T(8,128)(2,1)S(1)}, u32[]{:S(2)}, u32[]{:S(2)}) collective-permute-start(bf16[14,8,1536]{2,1,0:T(8,128)(2,1)S(1)} %bitcast.16), channel_id=1, source_target_pairs={{0,1},{1,0},{2,3},{3,2},{4,5},{5,4},{6,7},{7,6},{8,9},{9,8},{10,11... | collective-permute-start | bytes 1032200 | tf_op jit(solution)/shard_map/ppermute | solution.py:429
  89.3 3.1 %collective-permute-done.13.refs_3_ = bf16[14,8,1536]{2,1,0:T(8,128)(2,1)S(1)} collective-permute-done((bf16[14,8,1536]{2,1,0:T(8,128)(2,1)S(1)}, bf16[14,8,1536]{2,1,0:T(8,128)(2,1)S(1)}, u32[]{:S(2)}, u32[]{:S(2)}) %collective-permute-start.13) | collective-permute-done | bytes 344096 | tf_op jit(solution)/shard_map/ppermute | solution.py:426
  92.4 3.0 %collective-permute-start.19 = (bf16[14,8,1536]{2,1,0:T(8,128)(2,1)S(1)}, bf16[14,8,1536]{2,1,0:T(8,128)(2,1)S(1)}, u32[]{:S(2)}, u32[]{:S(2)}) collective-permute-start(bf16[14,8,1536]{2,1,0:T(8,128)(2,1)S(1)} %collective-permute-done.13.refs_3_), channel_id=1, source_target_pairs={{0,1},{1,0},{2,3},{3,2},{4,5},{5,4},{6,7},{7,6},{8,9},{9,8},{10,11... | collective-permute-start | bytes 1032200 | tf_op jit(solution)/shard_map/ppermute | solution.py:429
  95.3 1.2 %collective-permute-start.15 = (bf16[14,8,1536]{2,1,0:T(8,128)(2,1)S(1)}, bf16[14,8,1536]{2,1,0:T(8,128)(2,1)S(1)}, u32[]{:S(2)}, u32[]{:S(2)}) collective-permute-start(bf16[14,8,1536]{2,1,0:T(8,128)(2,1)S(1)} %bitcast.18), channel_id=1, source_target_pairs={{0,2},{1,3},{2,0},{3,1},{4,6},{5,7},{6,4},{7,5},{8,10},{9,11},{10,... | collective-permute-start | bytes 1032200 | tf_op jit(solution)/shard_map/ppermute | solution.py:426
  96.6 0.3 collective-permute-start.16
  96.9 0.2 collective-permute-start.17
  97.1 1.0 collective-permute-done.16.refs_1_
  98.1 0.3 collective-permute-done.17.refs_3_
  98.4 1.7 %assemble.3.refs_0_ = bf16[8,56,4096]{2,1,0:T(8,128)(2,1)} custom-call(bf16[448,448]{1,0:T(8,128)(2,1)S(1)} %fusion.12.order_ref, bf16[14,8,1024]{2,1,0:T(8,128)(2,1)S(1)} %bitcast.24, bf16[14,8,1024]{2,1,0:T(8,128)(2,1)S(1)} %collective-permute-done.16.refs_1_, bf16[14,8,1024]{2,1,0:T(8,128)(2,1)S(1)} %collective-permute-done.11.refs_2_, ...), custom_call_target="tpu_custom_call" | custom-call | flops 290000000 | bytes 10730000 | tf_op jit(solution)/shard_map/assemble/pallas_call | solution.py:381
  100.1 0.3 collective-permute-start.20
  100.3 2.4 %assemble.4.refs_0_ = bf16[8,56,4096]{2,1,0:T(8,128)(2,1)} custom-call(bf16[448,448]{1,0:T(8,128)(2,1)S(1)} %fusion.12.order_ref, bf16[8,56,4096]{2,1,0:T(8,128)(2,1)} %assemble.3.refs_0_, bf16[14,8,1536]{2,1,0:T(8,128)(2,1)S(1)} %bitcast.17, bf16[14,8,1536]{2,1,0:T(8,128)(2,1)S(1)} %collective-permute-done.18.refs_2_, ...), custom_call_target="tpu_custom_call", output_to_operand_aliasing={{}: (1, {})} | custom-call | flops 290000000 | bytes 10730000 | tf_op jit(solution)/shard_map/assemble/pallas_call | solution.py:381
  102.8 2.2 %collective-permute-done.15.refs_3_ = bf16[14,8,1536]{2,1,0:T(8,128)(2,1)S(1)} collective-permute-done((bf16[14,8,1536]{2,1,0:T(8,128)(2,1)S(1)}, bf16[14,8,1536]{2,1,0:T(8,128)(2,1)S(1)}, u32[]{:S(2)}, u32[]{:S(2)}) %collective-permute-start.15) | collective-permute-done | bytes 344096 | tf_op jit(solution)/shard_map/ppermute | solution.py:426
  105.0 0.8 collective-permute-start.21
  105.8 1.3 %collective-permute-done.21.refs_4_ = bf16[14,8,1536]{2,1,0:T(8,128)(2,1)S(1)} collective-permute-done((bf16[14,8,1536]{2,1,0:T(8,128)(2,1)S(1)}, bf16[14,8,1536]{2,1,0:T(8,128)(2,1)S(1)}, u32[]{:S(2)}, u32[]{:S(2)}) %collective-permute-start.21) | collective-permute-done | bytes 344096 | tf_op jit(solution)/shard_map/ppermute | solution.py:429
  107.1 2.4 %assemble.5 = bf16[8,56,4096]{2,1,0:T(8,128)(2,1)} custom-call(bf16[448,448]{1,0:T(8,128)(2,1)S(1)} %fusion.12.order_ref, bf16[8,56,4096]{2,1,0:T(8,128)(2,1)} %assemble.4.refs_0_, bf16[14,8,1536]{2,1,0:T(8,128)(2,1)S(1)} %bitcast.20, bf16[14,8,1536]{2,1,0:T(8,128)(2,1)S(1)} %collective-permute-done.20.refs_2_, ...), custom_call_target="tpu_custom_call", output_to_operand_aliasing={{}: (1, {})} | custom-call | flops 290000000 | bytes 10730000 | tf_op jit(solution)/shard_map/assemble/pallas_call | solution.py:381
  (28 shorter events, 0.2 us)
Async XLA Ops:
  0.0 1.4 %copy-start = (bf16[24,8,4096]{2,1,0:T(8,128)(2,1)S(1)}, bf16[24,8,4096]{2,1,0:T(8,128)(2,1)}, u32[]{:S(2)}) copy-start(bf16[24,8,4096]{2,1,0:T(8,128)(2,1)} %x_ref.3) | copy-start | bytes 4718596
  1.4 9.2 %copy-start.5 = (s32[24,32]{1,0:T(8,128)S(1)}, s32[24,32]{1,0:T(8,128)}, u32[]{:S(2)}) copy-start(s32[24,32]{1,0:T(8,128)} %param.6) | copy-start | bytes 9220
  1.4 9.2 %copy-start.6 = (s32[24]{0:T(128)S(1)}, s32[24]{0:T(128)}, u32[]{:S(2)}) copy-start(s32[24]{0:T(128)} %param.7) | copy-start | bytes 292
  1.4 9.3 %copy-start.1 = (bf16[24,8,4096]{2,1,0:T(8,128)(2,1)S(1)}, bf16[24,8,4096]{2,1,0:T(8,128)(2,1)}, u32[]{:S(2)}) copy-start(bf16[24,8,4096]{2,1,0:T(8,128)(2,1)} %x_ref.3) | copy-start | bytes 4718596
  2.2 3.2 %collective-permute-start = (bf16[16,4,64,128]{3,2,1,0:T(8,128)(2,1)S(1)}, bf16[16,4,64,128]{3,2,1,0:T(8,128)(2,1)}, u32[]{:S(2)}, u32[]{:S(2)}) collective-permute-start(bf16[16,4,64,128]{3,2,1,0:T(8,128)(2,1)S(1)} %relayout.3.refs_0_), channel_id=1, source_target_pairs={{0,1},{1,0},{2,3},{3,2},{4,5},{5,4},{6,7},{7,6},{8,9},{9,8},{10,11... | collective-permute-start | bytes 3145736 | tf_op jit(solution)/shard_map/ppermute | solution.py:429
  3.0 24.8 %collective-permute-start.2 = (bf16[16,4,64,128]{3,2,1,0:T(8,128)(2,1)S(1)}, bf16[16,4,64,128]{3,2,1,0:T(8,128)(2,1)}, u32[]{:S(2)}, u32[]{:S(2)}) collective-permute-start(bf16[16,4,64,128]{3,2,1,0:T(8,128)(2,1)S(1)} %relayout.3.refs_0_), channel_id=1, source_target_pairs={{0,2},{1,3},{2,0},{3,1},{4,6},{5,7},{6,4},{7,5},{8,10},{9,11},{10,... | collective-permute-start | bytes 3145736 | tf_op jit(solution)/shard_map/ppermute | solution.py:426
  5.4 1.1 %copy-start.2 = (bf16[24,4,4096]{2,1,0:T(4,128)(2,1)S(1)}, bf16[24,4,4096]{2,1,0:T(4,128)(2,1)}, u32[]{:S(2)}) copy-start(bf16[24,4,4096]{2,1,0:T(4,128)(2,1)} %x_ref.4) | copy-start | bytes 2359300
  7.6 21.2 %collective-permute-start.1 = (bf16[24,2,64,128]{3,2,1,0:T(8,128)(2,1)S(1)}, bf16[24,2,64,128]{3,2,1,0:T(8,128)(2,1)S(1)}, u32[]{:S(2)}, u32[]{:S(2)}) collective-permute-start(bf16[24,2,64,128]{3,2,1,0:T(8,128)(2,1)S(1)} %relayout_rows.1.refs_0_), channel_id=1, source_target_pairs={{0,4},{2,6},{4,8},{5,1},{6,10},{7,3},{8,12},{9,5},{10,14},{11,7},{... | collective-permute-start | bytes 2359304 | tf_op jit(solution)/shard_map/ppermute | solution.py:423
  11.1 5.0 %collective-permute-start.3 = (bf16[8,4,64,128]{3,2,1,0:T(8,128)(2,1)S(1)}, bf16[8,4,64,128]{3,2,1,0:T(8,128)(2,1)S(1)}, u32[]{:S(2)}, u32[]{:S(2)}) collective-permute-start(bf16[8,4,64,128]{3,2,1,0:T(8,128)(2,1)S(1)} %relayout.4.refs_0_), channel_id=1, source_target_pairs={{0,1},{1,0},{2,3},{3,2},{4,5},{5,4},{6,7},{7,6},{8,9},{9,8},{10,11... | collective-permute-start | bytes 1572872 | tf_op jit(solution)/shard_map/ppermute | solution.py:429
  12.1 4.0 %copy-start.3 = (bf16[24,4,4096]{2,1,0:T(4,128)(2,1)S(1)}, bf16[24,4,4096]{2,1,0:T(4,128)(2,1)}, u32[]{:S(2)}) copy-start(bf16[24,4,4096]{2,1,0:T(4,128)(2,1)} %x_ref.4) | copy-start | bytes 2359300
  17.0 3.5 %copy-start.4 = (s32[192,4]{0,1:T(4,128)S(1)}, s32[192,4]{0,1:T(4,128)}, u32[]{:S(2)}) copy-start(s32[192,4]{0,1:T(4,128)} %param.9) | copy-start | bytes 9220
  28.7 6.1 %collective-permute-start.6 = (bf16[16,4,64,128]{3,2,1,0:T(8,128)(2,1)}, bf16[16,4,64,128]{3,2,1,0:T(8,128)(2,1)S(1)}, u32[]{:S(2)}, u32[]{:S(2)}) collective-permute-start(bf16[16,4,64,128]{3,2,1,0:T(8,128)(2,1)} %collective-permute-done.2.refs_0_), channel_id=1, source_target_pairs={{0,1},{1,0},{2,3},{3,2},{4,5},{5,4},{6,7},{7,6},{8,9},{9,8},{10,11... | collective-permute-start | bytes 3145736 | tf_op jit(solution)/shard_map/ppermute | solution.py:429
  29.3 3.3 %collective-permute-start.5 = (bf16[24,2,64,128]{3,2,1,0:T(8,128)(2,1)S(1)}, bf16[24,2,64,128]{3,2,1,0:T(8,128)(2,1)S(1)}, u32[]{:S(2)}, u32[]{:S(2)}) collective-permute-start(bf16[24,2,64,128]{3,2,1,0:T(8,128)(2,1)S(1)} %collective-permute-done.1.refs_0_), channel_id=1, source_target_pairs={{0,1},{1,0},{2,3},{3,2},{4,5},{5,4},{6,7},{7,6},{8,9},{9,8},{10,11... | collective-permute-start | bytes 2359304 | tf_op jit(solution)/shard_map/ppermute | solution.py:429
  29.3 13.0 %collective-permute-start.4 = (bf16[8,4,64,128]{3,2,1,0:T(8,128)(2,1)S(1)}, bf16[8,4,64,128]{3,2,1,0:T(8,128)(2,1)S(1)}, u32[]{:S(2)}, u32[]{:S(2)}) collective-permute-start(bf16[8,4,64,128]{3,2,1,0:T(8,128)(2,1)S(1)} %relayout.4.refs_0_), channel_id=1, source_target_pairs={{0,2},{1,3},{2,0},{3,1},{4,6},{5,7},{6,4},{7,5},{8,10},{9,11},{10,... | collective-permute-start | bytes 1572872 | tf_op jit(solution)/shard_map/ppermute | solution.py:426
  42.2 6.5 %collective-permute-start.7 = (bf16[8,4,64,128]{3,2,1,0:T(8,128)(2,1)S(1)}, bf16[8,4,64,128]{3,2,1,0:T(8,128)(2,1)S(1)}, u32[]{:S(2)}, u32[]{:S(2)}) collective-permute-start(bf16[8,4,64,128]{3,2,1,0:T(8,128)(2,1)S(1)} %collective-permute-done.4.refs_0_), channel_id=1, source_target_pairs={{0,1},{1,0},{2,3},{3,2},{4,5},{5,4},{6,7},{7,6},{8,9},{9,8},{10,11... | collective-permute-start | bytes 1572872 | tf_op jit(solution)/shard_map/ppermute | solution.py:429
  44.6 24.1 %collective-permute-start.9 = (bf16[10,4,4096]{2,1,0:T(4,128)(2,1)S(1)}, bf16[10,4,4096]{2,1,0:T(4,128)(2,1)S(1)}, u32[]{:S(2)}, u32[]{:S(2)}) collective-permute-start(bf16[10,4,4096]{2,1,0:T(4,128)(2,1)S(1)} %coarse.10), channel_id=1, source_target_pairs={{4,0},{8,4},{12,8},{16,12},{20,16},{24,20},{28,24},{5,1},{9,5},{13... | collective-permute-start | bytes 983048 | tf_op jit(solution)/shard_map/ppermute | solution.py:435
  53.7 25.0 %collective-permute-start.10 = (bf16[10,4,4096]{2,1,0:T(4,128)(2,1)S(1)}, bf16[10,4,4096]{2,1,0:T(4,128)(2,1)S(1)}, u32[]{:S(2)}, u32[]{:S(2)}) collective-permute-start(bf16[10,4,4096]{2,1,0:T(4,128)(2,1)S(1)} %coarse.11), channel_id=1, source_target_pairs={{4,0},{8,4},{12,8},{16,12},{20,16},{24,20},{28,24},{5,1},{9,5},{13... | collective-permute-start | bytes 983048 | tf_op jit(solution)/shard_map/ppermute | solution.py:435
  56.2 22.5 %collective-permute-start.8 = (bf16[10,8,1024]{2,1,0:T(8,128)(2,1)S(1)}, bf16[10,8,1024]{2,1,0:T(8,128)(2,1)S(1)}, u32[]{:S(2)}, u32[]{:S(2)}) collective-permute-start(bf16[10,8,1024]{2,1,0:T(8,128)(2,1)S(1)} %coarse.8), channel_id=1, source_target_pairs={{0,4},{4,8},{8,12},{12,16},{16,20},{20,24},{24,28},{1,5},{5,9},{9,... | collective-permute-start | bytes 491528 | tf_op jit(solution)/shard_map/ppermute | solution.py:432
  60.3 20.0 %collective-permute-start.12 = (bf16[10,8,1536]{2,1,0:T(8,128)(2,1)S(1)}, bf16[10,8,1536]{2,1,0:T(8,128)(2,1)S(1)}, u32[]{:S(2)}, u32[]{:S(2)}) collective-permute-start(bf16[10,8,1536]{2,1,0:T(8,128)(2,1)S(1)} %coarse.12), channel_id=1, source_target_pairs={{0,4},{4,8},{8,12},{12,16},{16,20},{20,24},{24,28},{1,5},{5,9},{9,... | collective-permute-start | bytes 737288 | tf_op jit(solution)/shard_map/ppermute | solution.py:432
  64.0 22.8 %collective-permute-start.14 = (bf16[10,8,1536]{2,1,0:T(8,128)(2,1)S(1)}, bf16[10,8,1536]{2,1,0:T(8,128)(2,1)S(1)}, u32[]{:S(2)}, u32[]{:S(2)}) collective-permute-start(bf16[10,8,1536]{2,1,0:T(8,128)(2,1)S(1)} %coarse.14), channel_id=1, source_target_pairs={{0,4},{4,8},{8,12},{12,16},{16,20},{20,24},{24,28},{1,5},{5,9},{9,... | collective-permute-start | bytes 737288 | tf_op jit(solution)/shard_map/ppermute | solution.py:432
  78.8 6.1 %collective-permute-start.11 = (bf16[14,8,1024]{2,1,0:T(8,128)(2,1)S(1)}, bf16[14,8,1024]{2,1,0:T(8,128)(2,1)S(1)}, u32[]{:S(2)}, u32[]{:S(2)}) collective-permute-start(bf16[14,8,1024]{2,1,0:T(8,128)(2,1)S(1)} %bitcast.22), channel_id=1, source_target_pairs={{0,2},{1,3},{2,0},{3,1},{4,6},{5,7},{6,4},{7,5},{8,10},{9,11},{10,... | collective-permute-start | bytes 688136 | tf_op jit(solution)/shard_map/ppermute | solution.py:426
  84.8 7.5 %collective-permute-start.13 = (bf16[14,8,1536]{2,1,0:T(8,128)(2,1)S(1)}, bf16[14,8,1536]{2,1,0:T(8,128)(2,1)S(1)}, u32[]{:S(2)}, u32[]{:S(2)}) collective-permute-start(bf16[14,8,1536]{2,1,0:T(8,128)(2,1)S(1)} %bitcast.15), channel_id=1, source_target_pairs={{0,2},{1,3},{2,0},{3,1},{4,6},{5,7},{6,4},{7,5},{8,10},{9,11},{10,... | collective-permute-start | bytes 1032200 | tf_op jit(solution)/shard_map/ppermute | solution.py:426
  86.9 13.4 %collective-permute-start.18 = (bf16[14,8,1536]{2,1,0:T(8,128)(2,1)S(1)}, bf16[14,8,1536]{2,1,0:T(8,128)(2,1)S(1)}, u32[]{:S(2)}, u32[]{:S(2)}) collective-permute-start(bf16[14,8,1536]{2,1,0:T(8,128)(2,1)S(1)} %bitcast.16), channel_id=1, source_target_pairs={{0,1},{1,0},{2,3},{3,2},{4,5},{5,4},{6,7},{7,6},{8,9},{9,8},{10,11... | collective-permute-start | bytes 1032200 | tf_op jit(solution)/shard_map/ppermute | solution.py:429
  92.4 8.0 %collective-permute-start.19 = (bf16[14,8,1536]{2,1,0:T(8,128)(2,1)S(1)}, bf16[14,8,1536]{2,1,0:T(8,128)(2,1)S(1)}, u32[]{:S(2)}, u32[]{:S(2)}) collective-permute-start(bf16[14,8,1536]{2,1,0:T(8,128)(2,1)S(1)} %collective-permute-done.13.refs_3_), channel_id=1, source_target_pairs={{0,1},{1,0},{2,3},{3,2},{4,5},{5,4},{6,7},{7,6},{8,9},{9,8},{10,11... | collective-permute-start | bytes 1032200 | tf_op jit(solution)/shard_map/ppermute | solution.py:429
  95.3 9.7 %collective-permute-start.15 = (bf16[14,8,1536]{2,1,0:T(8,128)(2,1)S(1)}, bf16[14,8,1536]{2,1,0:T(8,128)(2,1)S(1)}, u32[]{:S(2)}, u32[]{:S(2)}) collective-permute-start(bf16[14,8,1536]{2,1,0:T(8,128)(2,1)S(1)} %bitcast.18), channel_id=1, source_target_pairs={{0,2},{1,3},{2,0},{3,1},{4,6},{5,7},{6,4},{7,5},{8,10},{9,11},{10,... | collective-permute-start | bytes 1032200 | tf_op jit(solution)/shard_map/ppermute | solution.py:426
  96.6 1.5 %collective-permute-start.16 = (bf16[14,8,1024]{2,1,0:T(8,128)(2,1)S(1)}, bf16[14,8,1024]{2,1,0:T(8,128)(2,1)S(1)}, u32[]{:S(2)}, u32[]{:S(2)}) collective-permute-start(bf16[14,8,1024]{2,1,0:T(8,128)(2,1)S(1)} %bitcast.23), channel_id=1, source_target_pairs={{0,1},{1,0},{2,3},{3,2},{4,5},{5,4},{6,7},{7,6},{8,9},{9,8},{10,11... | collective-permute-start | bytes 688136 | tf_op jit(solution)/shard_map/ppermute | solution.py:429
  96.9 1.5 %collective-permute-start.17 = (bf16[14,8,1024]{2,1,0:T(8,128)(2,1)S(1)}, bf16[14,8,1024]{2,1,0:T(8,128)(2,1)S(1)}, u32[]{:S(2)}, u32[]{:S(2)}) collective-permute-start(bf16[14,8,1024]{2,1,0:T(8,128)(2,1)S(1)} %collective-permute-done.11.refs_2_), channel_id=1, source_target_pairs={{0,1},{1,0},{2,3},{3,2},{4,5},{5,4},{6,7},{7,6},{8,9},{9,8},{10,11... | collective-permute-start | bytes 688136 | tf_op jit(solution)/shard_map/ppermute | solution.py:429
  100.1 5.7 %collective-permute-start.20 = (bf16[14,8,1536]{2,1,0:T(8,128)(2,1)S(1)}, bf16[14,8,1536]{2,1,0:T(8,128)(2,1)S(1)}, u32[]{:S(2)}, u32[]{:S(2)}) collective-permute-start(bf16[14,8,1536]{2,1,0:T(8,128)(2,1)S(1)} %bitcast.19), channel_id=1, source_target_pairs={{0,1},{1,0},{2,3},{3,2},{4,5},{5,4},{6,7},{7,6},{8,9},{9,8},{10,11... | collective-permute-start | bytes 1032200 | tf_op jit(solution)/shard_map/ppermute | solution.py:429
  105.0 2.1 %collective-permute-start.21 = (bf16[14,8,1536]{2,1,0:T(8,128)(2,1)S(1)}, bf16[14,8,1536]{2,1,0:T(8,128)(2,1)S(1)}, u32[]{:S(2)}, u32[]{:S(2)}) collective-permute-start(bf16[14,8,1536]{2,1,0:T(8,128)(2,1)S(1)} %collective-permute-done.15.refs_3_), channel_id=1, source_target_pairs={{0,1},{1,0},{2,3},{3,2},{4,5},{5,4},{6,7},{7,6},{8,9},{9,8},{10,11... | collective-permute-start | bytes 1032200 | tf_op jit(solution)/shard_map/ppermute | solution.py:429

commit v9 on v8

--- a/solution.py
+++ b/solution.py
@@ -469,7 +469,13 @@
         return jnp.pad(y.astype(F32), ((0, 0), (g, 2 - g), (0, 0), (0, 0)))
 
     late = downward(coarse_rows(left, aps, ((CB // 2, CB),), 0, BS, BF, 1.0)[0])
-    highs = [upward(coarse_rows(left, aps, ((2 * CB, 3 * CB),), a0, a1, BF, 1.0)[0]) for a0, a1 in chunks]
+    raw = [coarse_rows(left, aps, ((2 * CB, 3 * CB),), a0, a1, BF, 1.0)[0] for a0, a1 in chunks]
+    early, raw[0] = lax.optimization_barrier((early, raw[0]))
+    highs = [upward(raw[0])]
+    highs[0], raw[1] = lax.optimization_barrier((highs[0], raw[1]))
+    highs.append(upward(raw[1]))
+    late, raw[2] = lax.optimization_barrier((late, raw[2]))
+    highs.append(upward(raw[2]))
     mids = [coarse_rows(left, aps, ((CB, 2 * CB),), a0, a1, F32, 1.0)[0] for a0, a1 in chunks]
     lower = jnp.concatenate([early, late], axis=1)
     totals, sides, fars, beyond = [], [], [], []

time: 110 us -> 104 us (0.945)
  waiting for transfers between devices: 30.3 us -> 23.7 us
    ppermute x2, waiting for transfers between devices: 9.92 us -> 0.56 us  [downward(): return lax.ppermute(x, 'row', [(i + 1, i) for i in range(nrow - 1)])]
    ppermute x3, waiting for transfers between devices: 0.01 us -> 5.78 us  [upward(): return lax.ppermute(x, 'row', [(i, i + 1) for i in range(nrow - 1)])]
    ppermute x5, waiting for transfers between devices: 14.4 us -> 11.5 us  [over_y(): lax.ppermute(x, 'col', [(y * 2 + c, (y + s) % ny * 2 + c) for y in range(...]
  transfers between devices with their start and end apart: 22 -> 22, of which waited for: 12 -> 15; matrix products, arithmetic and copies ran while one was open for 1% -> 2% of each run, Pallas kernels for 33% -> 35%
where the time goes in v9:
time: 104 us; the launch traced here: 103 us
  Pallas kernels  39.3 us (38%)
  starting transfers between devices  35.3 us (34%)
  waiting for transfers between devices  23.7 us (23%)
  local copies, waits for them, and re-layouts  2.56 us (2%)
  other arithmetic  1.6 us (2%)
    ppermute x5, waiting for transfers between devices, over_y(): lax.ppermute(x, 'col', [(y * 2 + c, (y + s) % ny * 2 + c) for y in range(...  11.5 us
    pallas_call x2, Pallas kernels, product(): pl.pallas_call(functools.partial(product_kernel, first, rb, shifts), out_...  10.9 us
    ppermute x3, starting transfers between devices, upward(): return lax.ppermute(x, 'row', [(i, i + 1) for i in range(nrow - 1)])  10.3 us
    ppermute x11, starting transfers between devices, over_core(): return lax.ppermute(x, 'col', [(c, c ^ 1) for c in range(ncol)])  9.63 us
    pallas_call x3, Pallas kernels, assemble(): pl.pallas_call(assemble_kernel, grid=(per,), out_shape=jax.ShapeDtypeStru...  6.55 us
    ppermute x5, starting transfers between devices, over_y(): lax.ppermute(x, 'col', [(y * 2 + c, (y + s) % ny * 2 + c) for y in range(...  6.28 us
    pallas_call x8, Pallas kernels, coarse_rows(): pl.pallas_call(functools.partial(coarse_kernel, sets, a0, a1), out_shape=...  6.2 us
    ppermute x2, starting transfers between devices, downward(): return lax.ppermute(x, 'row', [(i + 1, i) for i in range(nrow - 1)])  6.1 us
  transfers between devices with their start and end apart: 22, of which 15 were waited for; matrix products, arithmetic and copies ran while one was open for 2% of the time, Pallas kernels for 35%

profile of v9, /device:TPU:9, one launch (start us, length us, event | category | flops | bytes accessed | tf_op | source)
XLA Modules:
  0.0 102.9 jit_solution(8545307045891039487)
XLA Ops:
  0.0 1.4 %copy-done = bf16[24,8,4096]{2,1,0:T(8,128)(2,1)S(1)} copy-done((bf16[24,8,4096]{2,1,0:T(8,128)(2,1)S(1)}, bf16[24,8,4096]{2,1,0:T(8,128)(2,1)}, u32[]{:S(2)}) %copy-start) | copy-done | bytes 1572888
  1.4 0.8 relayout.3.refs_0_
  2.2 0.7 collective-permute-start
  3.0 1.3 %collective-permute-start.2 = (bf16[16,4,64,128]{3,2,1,0:T(8,128)(2,1)S(1)}, bf16[16,4,64,128]{3,2,1,0:T(8,128)(2,1)}, u32[]{:S(2)}, u32[]{:S(2)}) collective-permute-start(bf16[16,4,64,128]{3,2,1,0:T(8,128)(2,1)S(1)} %relayout.3.refs_0_), channel_id=1, source_target_pairs={{0,2},{1,3},{2,0},{3,1},{4,6},{5,7},{6,4},{7,5},{8,10},{9,11},{10,... | collective-permute-start | bytes 3145736 | tf_op jit(solution)/shard_map/ppermute | solution.py:426
  4.2 0.8 add_select_fusion.4.table_ref
  5.0 0.3 collective-permute-done.refs_1_
  5.4 1.1 %copy-done.2 = bf16[24,4,4096]{2,1,0:T(4,128)(2,1)S(1)} copy-done((bf16[24,4,4096]{2,1,0:T(4,128)(2,1)S(1)}, bf16[24,4,4096]{2,1,0:T(4,128)(2,1)}, u32[]{:S(2)}) %copy-start.2) | copy-done | bytes 786456
  6.5 1.1 %relayout_rows.1.refs_0_ = bf16[24,2,64,128]{3,2,1,0:T(8,128)(2,1)S(1)} custom-call(bf16[24,4,4096]{2,1,0:T(4,128)(2,1)S(1)} %copy-done.2), custom_call_target="tpu_custom_call" | custom-call | flops 100000000 | bytes 3700000 | tf_op jit(solution)/shard_map/relayout_rows/pallas_call | solution.py:84
  7.6 3.0 %collective-permute-start.1 = (bf16[24,2,64,128]{3,2,1,0:T(8,128)(2,1)S(1)}, bf16[24,2,64,128]{3,2,1,0:T(8,128)(2,1)S(1)}, u32[]{:S(2)}, u32[]{:S(2)}) collective-permute-start(bf16[24,2,64,128]{3,2,1,0:T(8,128)(2,1)S(1)} %relayout_rows.1.refs_0_), channel_id=1, source_target_pairs={{0,4},{2,6},{4,8},{5,1},{6,10},{7,3},{8,12},{9,5},{10,14},{11,7},{... | collective-permute-start | bytes 2359304 | tf_op jit(solution)/shard_map/ppermute | solution.py:423
  10.7 0.4 relayout.4.refs_0_
  11.1 0.8 collective-permute-start.3
  11.9 0.2 fusion.12.order_ref
  12.1 3.9 %near_band.2.start_ref = bf16[4,27,256,128]{3,2,1,0:T(8,128)(2,1)S(1)} custom-call(s32[24,32]{1,0:T(8,128)S(1)} %subtract_select_fusion.place_ref, bf16[16,4,64,128]{3,2,1,0:T(8,128)(2,1)S(1)} %relayout.3.refs_0_, bf16[16,4,64,128]{3,2,1,0:T(8,128)(2,1)} %collective-permute-done.refs_1_), custom_call_target="tpu_custom_call" | custom-call | flops 256000000 | bytes 9472000 | tf_op jit(solution)/shard_map/near_band/pallas_call | solution.py:255
  16.1 0.9 relayout.5.pl_ref
  17.0 2.1 %near_band.3.start_ref = bf16[2,27,256,128]{3,2,1,0:T(8,128)(2,1)S(1)} custom-call(s32[24,32]{1,0:T(8,128)S(1)} %subtract_select_fusion.place_ref, bf16[8,4,64,128]{3,2,1,0:T(8,128)(2,1)S(1)} %relayout.4.refs_0_, bf16[8,4,64,128]{3,2,1,0:T(8,128)(2,1)S(1)} %collective-permute-done.3.refs_1_), custom_call_target="tpu_custom_call" | custom-call | flops 128000000 | bytes 4736000 | tf_op jit(solution)/shard_map/near_band/pallas_call | solution.py:255
  19.0 1.4 %right_factor.2.own_ref = bf16[6,5,256,128]{3,2,1,0:T(8,128)(2,1)S(1)} custom-call(s32[4,72]{1,0:T(4,128)S(1)} %add_select_fusion.4.table_ref, bf16[24,2,64,128]{3,2,1,0:T(8,128)(2,1)S(1)} %relayout_rows.1.refs_0_), custom_call_target="tpu_custom_call" | custom-call | flops 200000000 | bytes 7400000 | tf_op jit(solution)/shard_map/right_factor/pallas_call | solution.py:186
  20.5 2.9 %left_factor.1.left_ref = bf16[12,24,64,128]{3,2,1,0:T(8,128)(2,1)S(1)} custom-call(s32[4,192]{1,0:T(4,128)S(1)} %bitcast.26, bf16[24,2,64,128]{3,2,1,0:T(8,128)(2,1)S(1)} %relayout.5.pl_ref), custom_call_target="tpu_custom_call" | custom-call | flops 290000000 | bytes 10730000 | tf_op jit(solution)/shard_map/left_factor/pallas_call | solution.py:118
  23.4 4.4 %collective-permute-done.2.refs_0_ = bf16[16,4,64,128]{3,2,1,0:T(8,128)(2,1)} collective-permute-done((bf16[16,4,64,128]{3,2,1,0:T(8,128)(2,1)S(1)}, bf16[16,4,64,128]{3,2,1,0:T(8,128)(2,1)}, u32[]{:S(2)}, u32[]{:S(2)}) %collective-permute-start.2) | collective-permute-done | bytes 1048608 | tf_op jit(solution)/shard_map/ppermute | solution.py:426
  27.8 0.9 collective-permute-done.1.refs_0_
  28.7 0.5 collective-permute-start.6
  29.3 1.2 %collective-permute-start.4 = (bf16[8,4,64,128]{3,2,1,0:T(8,128)(2,1)S(1)}, bf16[8,4,64,128]{3,2,1,0:T(8,128)(2,1)S(1)}, u32[]{:S(2)}, u32[]{:S(2)}) collective-permute-start(bf16[8,4,64,128]{3,2,1,0:T(8,128)(2,1)S(1)} %relayout.4.refs_0_), channel_id=1, source_target_pairs={{0,2},{1,3},{2,0},{3,1},{4,6},{5,7},{6,4},{7,5},{8,10},{9,11},{10,... | collective-permute-start | bytes 1572872 | tf_op jit(solution)/shard_map/ppermute | solution.py:426
  30.5 2.0 %collective-permute-done.5.refs_1_ = bf16[24,2,64,128]{3,2,1,0:T(8,128)(2,1)S(1)} collective-permute-done((bf16[24,2,64,128]{3,2,1,0:T(8,128)(2,1)S(1)}, bf16[24,2,64,128]{3,2,1,0:T(8,128)(2,1)S(1)}, u32[]{:S(2)}, u32[]{:S(2)}) %collective-permute-start.5) | collective-permute-done | bytes 786464 | tf_op jit(solution)/shard_map/ppermute | solution.py:429
  32.5 2.3 %right_factor.3.near_ref = bf16[12,5,256,128]{3,2,1,0:T(8,128)(2,1)S(1)} custom-call(s32[4,72]{1,0:T(4,128)S(1)} %add_select_fusion.4.table_ref, bf16[24,2,64,128]{3,2,1,0:T(8,128)(2,1)S(1)} %collective-permute-done.1.refs_0_, bf16[24,2,64,128]{3,2,1,0:T(8,128)(2,1)S(1)} %collective-permute-done.5.refs_1_), custom_call_target="tpu_custom_call" | custom-call | flops 300000000 | bytes 11100000 | tf_op jit(solution)/shard_map/right_factor/pallas_call | solution.py:186
  34.8 7.1 %product.2.refs_0_ = bf16[16,64,640]{2,1,0:T(8,128)(2,1)S(1)} custom-call(s32[24,32]{1,0:T(8,128)S(1)} %subtract_select_fusion.place_ref, bf16[6,5,256,128]{3,2,1,0:T(8,128)(2,1)S(1)} %right_factor.2.own_ref, bf16[12,5,256,128]{3,2,1,0:T(8,128)(2,1)S(1)} %right_factor.3.near_ref, bf16[4,27,256,128]{3,2,1,0:T(8,128)(2,1)S(1)} %near_band.2.start_ref, ...), custom_call_target="tpu_custom_call" | custom-call | flops 480000000 | bytes 17760000 | tf_op jit(solution)/shard_map/product/pallas_call | solution.py:299
  42.0 0.3 collective-permute-done.4.refs_0_
  42.2 1.4 %collective-permute-start.8 = (bf16[8,4,64,128]{3,2,1,0:T(8,128)(2,1)S(1)}, bf16[8,4,64,128]{3,2,1,0:T(8,128)(2,1)S(1)}, u32[]{:S(2)}, u32[]{:S(2)}) collective-permute-start(bf16[8,4,64,128]{3,2,1,0:T(8,128)(2,1)S(1)} %collective-permute-done.4.refs_0_), channel_id=1, source_target_pairs={{0,1},{1,0},{2,3},{3,2},{4,5},{5,4},{6,7},{7,6},{8,9},{9,8},{10,11... | collective-permute-start | bytes 1572872 | tf_op jit(solution)/shard_map/ppermute | solution.py:429
  43.6 0.9 coarse.8
  44.6 4.2 %collective-permute-start.7 = (bf16[10,4,4096]{2,1,0:T(4,128)(2,1)S(1)}, bf16[10,4,4096]{2,1,0:T(4,128)(2,1)S(1)}, u32[]{:S(2)}, u32[]{:S(2)}) collective-permute-start(bf16[10,4,4096]{2,1,0:T(4,128)(2,1)S(1)} %coarse.8), channel_id=1, source_target_pairs={{4,0},{8,4},{12,8},{16,12},{20,16},{24,20},{28,24},{5,1},{9,5},{13... | collective-permute-start | bytes 983048 | tf_op jit(solution)/shard_map/ppermute | solution.py:435
  48.7 3.8 %product.3.refs_1_ = bf16[8,64,640]{2,1,0:T(8,128)(2,1)S(1)} custom-call(s32[24,32]{1,0:T(8,128)S(1)} %subtract_select_fusion.place_ref, bf16[6,5,256,128]{3,2,1,0:T(8,128)(2,1)S(1)} %right_factor.2.own_ref, bf16[12,5,256,128]{3,2,1,0:T(8,128)(2,1)S(1)} %right_factor.3.near_ref, bf16[2,27,256,128]{3,2,1,0:T(8,128)(2,1)S(1)} %near_band.3.start_ref, ...), custom_call_target="tpu_custom_call" | custom-call | flops 240000000 | bytes 8880000 | tf_op jit(solution)/shard_map/product/pallas_call | solution.py:299
  52.5 1.1 %coarse.12 = bf16[10,4,4096]{2,1,0:T(4,128)(2,1)S(1)} custom-call(bf16[12,24,64,128]{3,2,1,0:T(8,128)(2,1)S(1)} %left_factor.1.left_ref, bf16[16,64,640]{2,1,0:T(8,128)(2,1)S(1)} %product.2.refs_0_, bf16[8,64,640]{2,1,0:T(8,128)(2,1)S(1)} %product.3.refs_1_), custom_call_target="tpu_custom_call" | custom-call | flops 100000000 | bytes 3700000 | tf_op jit(solution)/shard_map/coarse/pallas_call | solution.py:346
  53.7 1.9 %collective-permute-start.10 = (bf16[10,4,4096]{2,1,0:T(4,128)(2,1)S(1)}, bf16[10,4,4096]{2,1,0:T(4,128)(2,1)S(1)}, u32[]{:S(2)}, u32[]{:S(2)}) collective-permute-start(bf16[10,4,4096]{2,1,0:T(4,128)(2,1)S(1)} %coarse.12), channel_id=1, source_target_pairs={{4,0},{8,4},{12,8},{16,12},{20,16},{24,20},{28,24},{5,1},{9,5},{13... | collective-permute-start | bytes 983048 | tf_op jit(solution)/shard_map/ppermute | solution.py:435
  55.6 0.6 coarse.9
  56.2 0.6 collective-permute-done.7
  56.7 4.0 %collective-permute-start.9 = (bf16[10,8,1024]{2,1,0:T(8,128)(2,1)S(1)}, bf16[10,8,1024]{2,1,0:T(8,128)(2,1)S(1)}, u32[]{:S(2)}, u32[]{:S(2)}) collective-permute-start(bf16[10,8,1024]{2,1,0:T(8,128)(2,1)S(1)} %coarse.9), channel_id=1, source_target_pairs={{0,4},{4,8},{8,12},{12,16},{16,20},{20,24},{24,28},{1,5},{5,9},{9,... | collective-permute-start | bytes 491528 | tf_op jit(solution)/shard_map/ppermute | solution.py:432
  60.8 0.7 coarse.13
  61.5 0.7 coarse.14
  62.3 0.7 coarse.10
  63.0 0.6 coarse.11
  63.6 3.9 %collective-permute-done.9 = bf16[10,8,1024]{2,1,0:T(8,128)(2,1)S(1)} collective-permute-done((bf16[10,8,1024]{2,1,0:T(8,128)(2,1)S(1)}, bf16[10,8,1024]{2,1,0:T(8,128)(2,1)S(1)}, u32[]{:S(2)}, u32[]{:S(2)}) %collective-permute-start.9) | collective-permute-done | bytes 163872 | tf_op jit(solution)/shard_map/ppermute | solution.py:432
  67.5 4.1 %collective-permute-start.12 = (bf16[10,8,1536]{2,1,0:T(8,128)(2,1)S(1)}, bf16[10,8,1536]{2,1,0:T(8,128)(2,1)S(1)}, u32[]{:S(2)}, u32[]{:S(2)}) collective-permute-start(bf16[10,8,1536]{2,1,0:T(8,128)(2,1)S(1)} %coarse.10), channel_id=1, source_target_pairs={{0,4},{4,8},{8,12},{12,16},{16,20},{20,24},{24,28},{1,5},{5,9},{9,... | collective-permute-start | bytes 737288 | tf_op jit(solution)/shard_map/ppermute | solution.py:432
  71.6 0.1 pad_maximum_fusion.2
  71.8 1.3 %collective-permute-start.11 = (bf16[14,8,1024]{2,1,0:T(8,128)(2,1)S(1)}, bf16[14,8,1024]{2,1,0:T(8,128)(2,1)S(1)}, u32[]{:S(2)}, u32[]{:S(2)}) collective-permute-start(bf16[14,8,1024]{2,1,0:T(8,128)(2,1)S(1)} %bitcast.22), channel_id=1, source_target_pairs={{0,2},{1,3},{2,0},{3,1},{4,6},{5,7},{6,4},{7,5},{8,10},{9,11},{10,... | collective-permute-start | bytes 688136 | tf_op jit(solution)/shard_map/ppermute | solution.py:426
  73.1 2.2 %collective-permute-start.14 = (bf16[10,8,1536]{2,1,0:T(8,128)(2,1)S(1)}, bf16[10,8,1536]{2,1,0:T(8,128)(2,1)S(1)}, u32[]{:S(2)}, u32[]{:S(2)}) collective-permute-start(bf16[10,8,1536]{2,1,0:T(8,128)(2,1)S(1)} %coarse.13), channel_id=1, source_target_pairs={{0,4},{4,8},{8,12},{12,16},{16,20},{20,24},{24,28},{1,5},{5,9},{9,... | collective-permute-start | bytes 737288 | tf_op jit(solution)/shard_map/ppermute | solution.py:432
  75.3 0.2 pad_maximum_fusion
  75.5 1.8 %collective-permute-done.12 = bf16[10,8,1536]{2,1,0:T(8,128)(2,1)S(1)} collective-permute-done((bf16[10,8,1536]{2,1,0:T(8,128)(2,1)S(1)}, bf16[10,8,1536]{2,1,0:T(8,128)(2,1)S(1)}, u32[]{:S(2)}, u32[]{:S(2)}) %collective-permute-start.12) | collective-permute-done | bytes 245792 | tf_op jit(solution)/shard_map/ppermute | solution.py:432
  77.4 0.8 collective-permute-done.11.refs_2_
  78.2 1.2 %collective-permute-start.13 = (bf16[14,8,1536]{2,1,0:T(8,128)(2,1)S(1)}, bf16[14,8,1536]{2,1,0:T(8,128)(2,1)S(1)}, u32[]{:S(2)}, u32[]{:S(2)}) collective-permute-start(bf16[14,8,1536]{2,1,0:T(8,128)(2,1)S(1)} %bitcast.15), channel_id=1, source_target_pairs={{0,2},{1,3},{2,0},{3,1},{4,6},{5,7},{6,4},{7,5},{8,10},{9,11},{10,... | collective-permute-start | bytes 1032200 | tf_op jit(solution)/shard_map/ppermute | solution.py:426
  79.5 0.7 coarse.15
  80.2 2.0 %collective-permute-start.18 = (bf16[14,8,1536]{2,1,0:T(8,128)(2,1)S(1)}, bf16[14,8,1536]{2,1,0:T(8,128)(2,1)S(1)}, u32[]{:S(2)}, u32[]{:S(2)}) collective-permute-start(bf16[14,8,1536]{2,1,0:T(8,128)(2,1)S(1)} %bitcast.16), channel_id=1, source_target_pairs={{0,1},{1,0},{2,3},{3,2},{4,5},{5,4},{6,7},{7,6},{8,9},{9,8},{10,11... | collective-permute-start | bytes 1032200 | tf_op jit(solution)/shard_map/ppermute | solution.py:429
  82.2 0.1 collective-permute-done.14
  82.3 3.8 %collective-permute-done.13.refs_3_ = bf16[14,8,1536]{2,1,0:T(8,128)(2,1)S(1)} collective-permute-done((bf16[14,8,1536]{2,1,0:T(8,128)(2,1)S(1)}, bf16[14,8,1536]{2,1,0:T(8,128)(2,1)S(1)}, u32[]{:S(2)}, u32[]{:S(2)}) %collective-permute-start.13) | collective-permute-done | bytes 344096 | tf_op jit(solution)/shard_map/ppermute | solution.py:426
  86.1 2.6 %collective-permute-start.19 = (bf16[14,8,1536]{2,1,0:T(8,128)(2,1)S(1)}, bf16[14,8,1536]{2,1,0:T(8,128)(2,1)S(1)}, u32[]{:S(2)}, u32[]{:S(2)}) collective-permute-start(bf16[14,8,1536]{2,1,0:T(8,128)(2,1)S(1)} %collective-permute-done.13.refs_3_), channel_id=1, source_target_pairs={{0,1},{1,0},{2,3},{3,2},{4,5},{5,4},{6,7},{7,6},{8,9},{9,8},{10,11... | collective-permute-start | bytes 1032200 | tf_op jit(solution)/shard_map/ppermute | solution.py:429
  88.7 1.2 %collective-permute-start.15 = (bf16[14,8,1536]{2,1,0:T(8,128)(2,1)S(1)}, bf16[14,8,1536]{2,1,0:T(8,128)(2,1)S(1)}, u32[]{:S(2)}, u32[]{:S(2)}) collective-permute-start(bf16[14,8,1536]{2,1,0:T(8,128)(2,1)S(1)} %bitcast.18), channel_id=1, source_target_pairs={{0,2},{1,3},{2,0},{3,1},{4,6},{5,7},{6,4},{7,5},{8,10},{9,11},{10,... | collective-permute-start | bytes 1032200 | tf_op jit(solution)/shard_map/ppermute | solution.py:426
  89.9 0.3 collective-permute-start.16
  90.2 0.2 collective-permute-start.17
  90.5 1.0 collective-permute-done.16.refs_1_
  91.4 0.3 collective-permute-done.17.refs_3_
  91.8 1.7 %assemble.3.refs_0_ = bf16[8,56,4096]{2,1,0:T(8,128)(2,1)} custom-call(bf16[448,448]{1,0:T(8,128)(2,1)S(1)} %fusion.12.order_ref, bf16[14,8,1024]{2,1,0:T(8,128)(2,1)S(1)} %bitcast.24, bf16[14,8,1024]{2,1,0:T(8,128)(2,1)S(1)} %collective-permute-done.16.refs_1_, bf16[14,8,1024]{2,1,0:T(8,128)(2,1)S(1)} %collective-permute-done.11.refs_2_, ...), custom_call_target="tpu_custom_call" | custom-call | flops 290000000 | bytes 10730000 | tf_op jit(solution)/shard_map/assemble/pallas_call | solution.py:381
  93.4 0.3 collective-permute-start.20
  93.7 2.4 %assemble.4.refs_0_ = bf16[8,56,4096]{2,1,0:T(8,128)(2,1)} custom-call(bf16[448,448]{1,0:T(8,128)(2,1)S(1)} %fusion.12.order_ref, bf16[8,56,4096]{2,1,0:T(8,128)(2,1)} %assemble.3.refs_0_, bf16[14,8,1536]{2,1,0:T(8,128)(2,1)S(1)} %bitcast.17, bf16[14,8,1536]{2,1,0:T(8,128)(2,1)S(1)} %collective-permute-done.18.refs_2_, ...), custom_call_target="tpu_custom_call", output_to_operand_aliasing={{}: (1, {})} | custom-call | flops 290000000 | bytes 10730000 | tf_op jit(solution)/shard_map/assemble/pallas_call | solution.py:381
  96.2 2.2 %collective-permute-done.15.refs_3_ = bf16[14,8,1536]{2,1,0:T(8,128)(2,1)S(1)} collective-permute-done((bf16[14,8,1536]{2,1,0:T(8,128)(2,1)S(1)}, bf16[14,8,1536]{2,1,0:T(8,128)(2,1)S(1)}, u32[]{:S(2)}, u32[]{:S(2)}) %collective-permute-start.15) | collective-permute-done | bytes 344096 | tf_op jit(solution)/shard_map/ppermute | solution.py:426
  98.4 0.8 collective-permute-start.21
  99.2 1.3 %collective-permute-done.21.refs_4_ = bf16[14,8,1536]{2,1,0:T(8,128)(2,1)S(1)} collective-permute-done((bf16[14,8,1536]{2,1,0:T(8,128)(2,1)S(1)}, bf16[14,8,1536]{2,1,0:T(8,128)(2,1)S(1)}, u32[]{:S(2)}, u32[]{:S(2)}) %collective-permute-start.21) | collective-permute-done | bytes 344096 | tf_op jit(solution)/shard_map/ppermute | solution.py:429
  100.5 2.4 %assemble.5 = bf16[8,56,4096]{2,1,0:T(8,128)(2,1)} custom-call(bf16[448,448]{1,0:T(8,128)(2,1)S(1)} %fusion.12.order_ref, bf16[8,56,4096]{2,1,0:T(8,128)(2,1)} %assemble.4.refs_0_, bf16[14,8,1536]{2,1,0:T(8,128)(2,1)S(1)} %bitcast.20, bf16[14,8,1536]{2,1,0:T(8,128)(2,1)S(1)} %collective-permute-done.20.refs_2_, ...), custom_call_target="tpu_custom_call", output_to_operand_aliasing={{}: (1, {})} | custom-call | flops 290000000 | bytes 10730000 | tf_op jit(solution)/shard_map/assemble/pallas_call | solution.py:381
  (28 shorter events, 0.4 us)
Async XLA Ops:
  0.0 1.4 %copy-start = (bf16[24,8,4096]{2,1,0:T(8,128)(2,1)S(1)}, bf16[24,8,4096]{2,1,0:T(8,128)(2,1)}, u32[]{:S(2)}) copy-start(bf16[24,8,4096]{2,1,0:T(8,128)(2,1)} %x_ref.3) | copy-start | bytes 4718596
  1.4 9.2 %copy-start.5 = (s32[24,32]{1,0:T(8,128)S(1)}, s32[24,32]{1,0:T(8,128)}, u32[]{:S(2)}) copy-start(s32[24,32]{1,0:T(8,128)} %param.6) | copy-start | bytes 9220
  1.4 9.2 %copy-start.6 = (s32[24]{0:T(128)S(1)}, s32[24]{0:T(128)}, u32[]{:S(2)}) copy-start(s32[24]{0:T(128)} %param.7) | copy-start | bytes 292
  1.4 9.3 %copy-start.1 = (bf16[24,8,4096]{2,1,0:T(8,128)(2,1)S(1)}, bf16[24,8,4096]{2,1,0:T(8,128)(2,1)}, u32[]{:S(2)}) copy-start(bf16[24,8,4096]{2,1,0:T(8,128)(2,1)} %x_ref.3) | copy-start | bytes 4718596
  2.2 3.2 %collective-permute-start = (bf16[16,4,64,128]{3,2,1,0:T(8,128)(2,1)S(1)}, bf16[16,4,64,128]{3,2,1,0:T(8,128)(2,1)}, u32[]{:S(2)}, u32[]{:S(2)}) collective-permute-start(bf16[16,4,64,128]{3,2,1,0:T(8,128)(2,1)S(1)} %relayout.3.refs_0_), channel_id=1, source_target_pairs={{0,1},{1,0},{2,3},{3,2},{4,5},{5,4},{6,7},{7,6},{8,9},{9,8},{10,11... | collective-permute-start | bytes 3145736 | tf_op jit(solution)/shard_map/ppermute | solution.py:429
  3.0 24.8 %collective-permute-start.2 = (bf16[16,4,64,128]{3,2,1,0:T(8,128)(2,1)S(1)}, bf16[16,4,64,128]{3,2,1,0:T(8,128)(2,1)}, u32[]{:S(2)}, u32[]{:S(2)}) collective-permute-start(bf16[16,4,64,128]{3,2,1,0:T(8,128)(2,1)S(1)} %relayout.3.refs_0_), channel_id=1, source_target_pairs={{0,2},{1,3},{2,0},{3,1},{4,6},{5,7},{6,4},{7,5},{8,10},{9,11},{10,... | collective-permute-start | bytes 3145736 | tf_op jit(solution)/shard_map/ppermute | solution.py:426
  5.4 1.1 %copy-start.2 = (bf16[24,4,4096]{2,1,0:T(4,128)(2,1)S(1)}, bf16[24,4,4096]{2,1,0:T(4,128)(2,1)}, u32[]{:S(2)}) copy-start(bf16[24,4,4096]{2,1,0:T(4,128)(2,1)} %x_ref.4) | copy-start | bytes 2359300
  7.6 21.2 %collective-permute-start.1 = (bf16[24,2,64,128]{3,2,1,0:T(8,128)(2,1)S(1)}, bf16[24,2,64,128]{3,2,1,0:T(8,128)(2,1)S(1)}, u32[]{:S(2)}, u32[]{:S(2)}) collective-permute-start(bf16[24,2,64,128]{3,2,1,0:T(8,128)(2,1)S(1)} %relayout_rows.1.refs_0_), channel_id=1, source_target_pairs={{0,4},{2,6},{4,8},{5,1},{6,10},{7,3},{8,12},{9,5},{10,14},{11,7},{... | collective-permute-start | bytes 2359304 | tf_op jit(solution)/shard_map/ppermute | solution.py:423
  11.1 5.0 %collective-permute-start.3 = (bf16[8,4,64,128]{3,2,1,0:T(8,128)(2,1)S(1)}, bf16[8,4,64,128]{3,2,1,0:T(8,128)(2,1)S(1)}, u32[]{:S(2)}, u32[]{:S(2)}) collective-permute-start(bf16[8,4,64,128]{3,2,1,0:T(8,128)(2,1)S(1)} %relayout.4.refs_0_), channel_id=1, source_target_pairs={{0,1},{1,0},{2,3},{3,2},{4,5},{5,4},{6,7},{7,6},{8,9},{9,8},{10,11... | collective-permute-start | bytes 1572872 | tf_op jit(solution)/shard_map/ppermute | solution.py:429
  12.1 4.0 %copy-start.3 = (bf16[24,4,4096]{2,1,0:T(4,128)(2,1)S(1)}, bf16[24,4,4096]{2,1,0:T(4,128)(2,1)}, u32[]{:S(2)}) copy-start(bf16[24,4,4096]{2,1,0:T(4,128)(2,1)} %x_ref.4) | copy-start | bytes 2359300
  17.0 3.5 %copy-start.4 = (s32[192,4]{0,1:T(4,128)S(1)}, s32[192,4]{0,1:T(4,128)}, u32[]{:S(2)}) copy-start(s32[192,4]{0,1:T(4,128)} %param.9) | copy-start | bytes 9220
  28.7 6.1 %collective-permute-start.6 = (bf16[16,4,64,128]{3,2,1,0:T(8,128)(2,1)}, bf16[16,4,64,128]{3,2,1,0:T(8,128)(2,1)S(1)}, u32[]{:S(2)}, u32[]{:S(2)}) collective-permute-start(bf16[16,4,64,128]{3,2,1,0:T(8,128)(2,1)} %collective-permute-done.2.refs_0_), channel_id=1, source_target_pairs={{0,1},{1,0},{2,3},{3,2},{4,5},{5,4},{6,7},{7,6},{8,9},{9,8},{10,11... | collective-permute-start | bytes 3145736 | tf_op jit(solution)/shard_map/ppermute | solution.py:429
  29.3 3.3 %collective-permute-start.5 = (bf16[24,2,64,128]{3,2,1,0:T(8,128)(2,1)S(1)}, bf16[24,2,64,128]{3,2,1,0:T(8,128)(2,1)S(1)}, u32[]{:S(2)}, u32[]{:S(2)}) collective-permute-start(bf16[24,2,64,128]{3,2,1,0:T(8,128)(2,1)S(1)} %collective-permute-done.1.refs_0_), channel_id=1, source_target_pairs={{0,1},{1,0},{2,3},{3,2},{4,5},{5,4},{6,7},{7,6},{8,9},{9,8},{10,11... | collective-permute-start | bytes 2359304 | tf_op jit(solution)/shard_map/ppermute | solution.py:429
  29.3 13.0 %collective-permute-start.4 = (bf16[8,4,64,128]{3,2,1,0:T(8,128)(2,1)S(1)}, bf16[8,4,64,128]{3,2,1,0:T(8,128)(2,1)S(1)}, u32[]{:S(2)}, u32[]{:S(2)}) collective-permute-start(bf16[8,4,64,128]{3,2,1,0:T(8,128)(2,1)S(1)} %relayout.4.refs_0_), channel_id=1, source_target_pairs={{0,2},{1,3},{2,0},{3,1},{4,6},{5,7},{6,4},{7,5},{8,10},{9,11},{10,... | collective-permute-start | bytes 1572872 | tf_op jit(solution)/shard_map/ppermute | solution.py:426
  42.2 6.5 %collective-permute-start.8 = (bf16[8,4,64,128]{3,2,1,0:T(8,128)(2,1)S(1)}, bf16[8,4,64,128]{3,2,1,0:T(8,128)(2,1)S(1)}, u32[]{:S(2)}, u32[]{:S(2)}) collective-permute-start(bf16[8,4,64,128]{3,2,1,0:T(8,128)(2,1)S(1)} %collective-permute-done.4.refs_0_), channel_id=1, source_target_pairs={{0,1},{1,0},{2,3},{3,2},{4,5},{5,4},{6,7},{7,6},{8,9},{9,8},{10,11... | collective-permute-start | bytes 1572872 | tf_op jit(solution)/shard_map/ppermute | solution.py:429
  44.6 12.2 %collective-permute-start.7 = (bf16[10,4,4096]{2,1,0:T(4,128)(2,1)S(1)}, bf16[10,4,4096]{2,1,0:T(4,128)(2,1)S(1)}, u32[]{:S(2)}, u32[]{:S(2)}) collective-permute-start(bf16[10,4,4096]{2,1,0:T(4,128)(2,1)S(1)} %coarse.8), channel_id=1, source_target_pairs={{4,0},{8,4},{12,8},{16,12},{20,16},{24,20},{28,24},{5,1},{9,5},{13... | collective-permute-start | bytes 983048 | tf_op jit(solution)/shard_map/ppermute | solution.py:435
  53.7 18.0 %collective-permute-start.10 = (bf16[10,4,4096]{2,1,0:T(4,128)(2,1)S(1)}, bf16[10,4,4096]{2,1,0:T(4,128)(2,1)S(1)}, u32[]{:S(2)}, u32[]{:S(2)}) collective-permute-start(bf16[10,4,4096]{2,1,0:T(4,128)(2,1)S(1)} %coarse.12), channel_id=1, source_target_pairs={{4,0},{8,4},{12,8},{16,12},{20,16},{24,20},{28,24},{5,1},{9,5},{13... | collective-permute-start | bytes 983048 | tf_op jit(solution)/shard_map/ppermute | solution.py:435
  56.7 10.8 %collective-permute-start.9 = (bf16[10,8,1024]{2,1,0:T(8,128)(2,1)S(1)}, bf16[10,8,1024]{2,1,0:T(8,128)(2,1)S(1)}, u32[]{:S(2)}, u32[]{:S(2)}) collective-permute-start(bf16[10,8,1024]{2,1,0:T(8,128)(2,1)S(1)} %coarse.9), channel_id=1, source_target_pairs={{0,4},{4,8},{8,12},{12,16},{16,20},{20,24},{24,28},{1,5},{5,9},{9,... | collective-permute-start | bytes 491528 | tf_op jit(solution)/shard_map/ppermute | solution.py:432
  67.5 9.8 %collective-permute-start.12 = (bf16[10,8,1536]{2,1,0:T(8,128)(2,1)S(1)}, bf16[10,8,1536]{2,1,0:T(8,128)(2,1)S(1)}, u32[]{:S(2)}, u32[]{:S(2)}) collective-permute-start(bf16[10,8,1536]{2,1,0:T(8,128)(2,1)S(1)} %coarse.10), channel_id=1, source_target_pairs={{0,4},{4,8},{8,12},{12,16},{16,20},{20,24},{24,28},{1,5},{5,9},{9,... | collective-permute-start | bytes 737288 | tf_op jit(solution)/shard_map/ppermute | solution.py:432
  71.8 6.4 %collective-permute-start.11 = (bf16[14,8,1024]{2,1,0:T(8,128)(2,1)S(1)}, bf16[14,8,1024]{2,1,0:T(8,128)(2,1)S(1)}, u32[]{:S(2)}, u32[]{:S(2)}) collective-permute-start(bf16[14,8,1024]{2,1,0:T(8,128)(2,1)S(1)} %bitcast.22), channel_id=1, source_target_pairs={{0,2},{1,3},{2,0},{3,1},{4,6},{5,7},{6,4},{7,5},{8,10},{9,11},{10,... | collective-permute-start | bytes 688136 | tf_op jit(solution)/shard_map/ppermute | solution.py:426
  73.1 9.2 %collective-permute-start.14 = (bf16[10,8,1536]{2,1,0:T(8,128)(2,1)S(1)}, bf16[10,8,1536]{2,1,0:T(8,128)(2,1)S(1)}, u32[]{:S(2)}, u32[]{:S(2)}) collective-permute-start(bf16[10,8,1536]{2,1,0:T(8,128)(2,1)S(1)} %coarse.13), channel_id=1, source_target_pairs={{0,4},{4,8},{8,12},{12,16},{16,20},{20,24},{24,28},{1,5},{5,9},{9,... | collective-permute-start | bytes 737288 | tf_op jit(solution)/shard_map/ppermute | solution.py:432
  78.2 7.9 %collective-permute-start.13 = (bf16[14,8,1536]{2,1,0:T(8,128)(2,1)S(1)}, bf16[14,8,1536]{2,1,0:T(8,128)(2,1)S(1)}, u32[]{:S(2)}, u32[]{:S(2)}) collective-permute-start(bf16[14,8,1536]{2,1,0:T(8,128)(2,1)S(1)} %bitcast.15), channel_id=1, source_target_pairs={{0,2},{1,3},{2,0},{3,1},{4,6},{5,7},{6,4},{7,5},{8,10},{9,11},{10,... | collective-permute-start | bytes 1032200 | tf_op jit(solution)/shard_map/ppermute | solution.py:426
  80.2 13.5 %collective-permute-start.18 = (bf16[14,8,1536]{2,1,0:T(8,128)(2,1)S(1)}, bf16[14,8,1536]{2,1,0:T(8,128)(2,1)S(1)}, u32[]{:S(2)}, u32[]{:S(2)}) collective-permute-start(bf16[14,8,1536]{2,1,0:T(8,128)(2,1)S(1)} %bitcast.16), channel_id=1, source_target_pairs={{0,1},{1,0},{2,3},{3,2},{4,5},{5,4},{6,7},{7,6},{8,9},{9,8},{10,11... | collective-permute-start | bytes 1032200 | tf_op jit(solution)/shard_map/ppermute | solution.py:429
  86.1 7.6 %collective-permute-start.19 = (bf16[14,8,1536]{2,1,0:T(8,128)(2,1)S(1)}, bf16[14,8,1536]{2,1,0:T(8,128)(2,1)S(1)}, u32[]{:S(2)}, u32[]{:S(2)}) collective-permute-start(bf16[14,8,1536]{2,1,0:T(8,128)(2,1)S(1)} %collective-permute-done.13.refs_3_), channel_id=1, source_target_pairs={{0,1},{1,0},{2,3},{3,2},{4,5},{5,4},{6,7},{7,6},{8,9},{9,8},{10,11... | collective-permute-start | bytes 1032200 | tf_op jit(solution)/shard_map/ppermute | solution.py:429
  88.7 9.7 %collective-permute-start.15 = (bf16[14,8,1536]{2,1,0:T(8,128)(2,1)S(1)}, bf16[14,8,1536]{2,1,0:T(8,128)(2,1)S(1)}, u32[]{:S(2)}, u32[]{:S(2)}) collective-permute-start(bf16[14,8,1536]{2,1,0:T(8,128)(2,1)S(1)} %bitcast.18), channel_id=1, source_target_pairs={{0,2},{1,3},{2,0},{3,1},{4,6},{5,7},{6,4},{7,5},{8,10},{9,11},{10,... | collective-permute-start | bytes 1032200 | tf_op jit(solution)/shard_map/ppermute | solution.py:426
  89.9 1.5 %collective-permute-start.16 = (bf16[14,8,1024]{2,1,0:T(8,128)(2,1)S(1)}, bf16[14,8,1024]{2,1,0:T(8,128)(2,1)S(1)}, u32[]{:S(2)}, u32[]{:S(2)}) collective-permute-start(bf16[14,8,1024]{2,1,0:T(8,128)(2,1)S(1)} %bitcast.23), channel_id=1, source_target_pairs={{0,1},{1,0},{2,3},{3,2},{4,5},{5,4},{6,7},{7,6},{8,9},{9,8},{10,11... | collective-permute-start | bytes 688136 | tf_op jit(solution)/shard_map/ppermute | solution.py:429
  90.2 1.5 %collective-permute-start.17 = (bf16[14,8,1024]{2,1,0:T(8,128)(2,1)S(1)}, bf16[14,8,1024]{2,1,0:T(8,128)(2,1)S(1)}, u32[]{:S(2)}, u32[]{:S(2)}) collective-permute-start(bf16[14,8,1024]{2,1,0:T(8,128)(2,1)S(1)} %collective-permute-done.11.refs_2_), channel_id=1, source_target_pairs={{0,1},{1,0},{2,3},{3,2},{4,5},{5,4},{6,7},{7,6},{8,9},{9,8},{10,11... | collective-permute-start | bytes 688136 | tf_op jit(solution)/shard_map/ppermute | solution.py:429
  93.4 5.7 %collective-permute-start.20 = (bf16[14,8,1536]{2,1,0:T(8,128)(2,1)S(1)}, bf16[14,8,1536]{2,1,0:T(8,128)(2,1)S(1)}, u32[]{:S(2)}, u32[]{:S(2)}) collective-permute-start(bf16[14,8,1536]{2,1,0:T(8,128)(2,1)S(1)} %bitcast.19), channel_id=1, source_target_pairs={{0,1},{1,0},{2,3},{3,2},{4,5},{5,4},{6,7},{7,6},{8,9},{9,8},{10,11... | collective-permute-start | bytes 1032200 | tf_op jit(solution)/shard_map/ppermute | solution.py:429
  98.4 2.1 %collective-permute-start.21 = (bf16[14,8,1536]{2,1,0:T(8,128)(2,1)S(1)}, bf16[14,8,1536]{2,1,0:T(8,128)(2,1)S(1)}, u32[]{:S(2)}, u32[]{:S(2)}) collective-permute-start(bf16[14,8,1536]{2,1,0:T(8,128)(2,1)S(1)} %collective-permute-done.15.refs_3_), channel_id=1, source_target_pairs={{0,1},{1,0},{2,3},{3,2},{4,5},{5,4},{6,7},{7,6},{8,9},{9,8},{10,11... | collective-permute-start | bytes 1032200 | tf_op jit(solution)/shard_map/ppermute | solution.py:429

commit v10 on v9

--- a/solution.py
+++ b/solution.py
@@ -444,8 +444,8 @@
         far_a.append([over_y(x, s) for s in range(1, ny)])
         side_a.append(over_core(x))
         if h == 0:
-            a_blocks, p_blocks, side_a[0] = lax.optimization_barrier((a_blocks, p_blocks, side_a[0]))
-    p_own = relayout_rows(p_blocks)
+            p_own = relayout_rows(p_blocks)
+            a_blocks, p_own, side_a[0] = lax.optimization_barrier((a_blocks, p_own, side_a[0]))
     beside = outward(p_own)
     p_blocks, p_own, side_a[1] = lax.optimization_barrier((p_blocks, p_own, side_a[1]))
     table = column_table(pct, rb, share)
@@ -478,22 +478,20 @@
     highs.append(upward(raw[2]))
     mids = [coarse_rows(left, aps, ((CB, 2 * CB),), a0, a1, F32, 1.0)[0] for a0, a1 in chunks]
     lower = jnp.concatenate([early, late], axis=1)
-    totals, sides, fars, beyond = [], [], [], []
+    totals, sides, fars = [], [], []
     for z, (a0, a1) in enumerate(chunks):
         total = columns(highs[z], 0) + columns(mids[z], 1) + columns(lower[:, :, a0 * BS : a1 * BS], 2)
         total = total.astype(BF).reshape((share * (GROUPS + 2),) + total.shape[2:])
-        if z > 0:
-            fars[-1], total = lax.optimization_barrier((fars[-1], total))
-            beyond.append([over_core(x) for x in fars[-1]])
         totals.append(total)
         sides.append(over_core(total))
         fars.append([over_y(total, s) for s in range(1, ny)])
+    for z in range(len(chunks) - 1):
+        fars[z], _ = lax.optimization_barrier((fars[z], totals[z + 1]))
     out = None
     for z, (a0, a1) in enumerate(chunks):
-        if z == len(chunks) - 1:
-            fars[z], out = lax.optimization_barrier((fars[z], out))
-            beyond.append([over_core(x) for x in fars[z]])
-        srcs = [totals[z], sides[z]] + [q for pair in zip(fars[z], beyond[z]) for q in pair]
+        if z == 1:
+            fars[1:], out = lax.optimization_barrier((fars[1:], out))
+        srcs = [totals[z], sides[z]] + [q for x in fars[z] for q in (x, over_core(x))]
         out = assemble(order, srcs, a0, BS * BS, out)
     return out
 

time: 104 us -> 104 us (level)
  waiting for transfers between devices: 23.7 us -> 26.6 us
  starting transfers between devices: 35.3 us -> 32.5 us
    ppermute x3, waiting for transfers between devices: 5.78 us -> 9.49 us  [upward(): return lax.ppermute(x, 'row', [(i, i + 1) for i in range(nrow - 1)])]
    ppermute x11, waiting for transfers between devices: 4.97 us -> 2.82 us  [over_core(): return lax.ppermute(x, 'col', [(c, c ^ 1) for c in range(ncol)])]
    ppermute x5, waiting for transfers between devices: 11.5 us -> 13.4 us  [over_y(): lax.ppermute(x, 'col', [(y * 2 + c, (y + s) % ny * 2 + c) for y in range(...]
    ppermute x11, starting transfers between devices: 9.63 us -> 8.05 us  [over_core(): return lax.ppermute(x, 'col', [(c, c ^ 1) for c in range(ncol)])]
  transfers between devices with their start and end apart: 22 -> 22, of which waited for: 15 -> 11; matrix products, arithmetic and copies ran while one was open for 2% -> 1% of each run, Pallas kernels for 35% -> 35%
where the time goes in v10:
time: 104 us; the launch traced here: 102 us
  Pallas kernels  39.3 us (38%)
  starting transfers between devices  32.5 us (31%)
  waiting for transfers between devices  26.6 us (26%)
  local copies, waits for them, and re-layouts  2.56 us (2%)
    ppermute x5, waiting for transfers between devices, over_y(): lax.ppermute(x, 'col', [(y * 2 + c, (y + s) % ny * 2 + c) for y in range(...  13.4 us
    pallas_call x2, Pallas kernels, product(): pl.pallas_call(functools.partial(product_kernel, first, rb, shifts), out_...  10.9 us
    ppermute x3, starting transfers between devices, upward(): return lax.ppermute(x, 'row', [(i, i + 1) for i in range(nrow - 1)])  10.3 us
    ppermute x3, waiting for transfers between devices, upward(): return lax.ppermute(x, 'row', [(i, i + 1) for i in range(nrow - 1)])  9.49 us
    ppermute x11, starting transfers between devices, over_core(): return lax.ppermute(x, 'col', [(c, c ^ 1) for c in range(ncol)])  8.05 us
    pallas_call x3, Pallas kernels, assemble(): pl.pallas_call(assemble_kernel, grid=(per,), out_shape=jax.ShapeDtypeStru...  6.56 us
    pallas_call x8, Pallas kernels, coarse_rows(): pl.pallas_call(functools.partial(coarse_kernel, sets, a0, a1), out_shape=...  6.19 us
    pallas_call x2, Pallas kernels, near_band(): pl.pallas_call(functools.partial(band_kernel, first, shifts), out_shape=j...  5.98 us
  transfers between devices with their start and end apart: 22, of which 11 were waited for; matrix products, arithmetic and copies ran while one was open for 1% of the time, Pallas kernels for 35%

profile of v10, /device:TPU:9, one launch (start us, length us, event | category | flops | bytes accessed | tf_op | source)
XLA Modules:
  0.0 102.2 jit_solution(3604852750055736441)
XLA Ops:
  0.0 1.4 %copy-done = bf16[24,8,4096]{2,1,0:T(8,128)(2,1)S(1)} copy-done((bf16[24,8,4096]{2,1,0:T(8,128)(2,1)S(1)}, bf16[24,8,4096]{2,1,0:T(8,128)(2,1)}, u32[]{:S(2)}) %copy-start) | copy-done | bytes 1572888
  1.4 0.8 relayout.3.refs_0_
  2.2 0.7 collective-permute-start
  3.0 1.3 %collective-permute-start.2 = (bf16[16,4,64,128]{3,2,1,0:T(8,128)(2,1)S(1)}, bf16[16,4,64,128]{3,2,1,0:T(8,128)(2,1)}, u32[]{:S(2)}, u32[]{:S(2)}) collective-permute-start(bf16[16,4,64,128]{3,2,1,0:T(8,128)(2,1)S(1)} %relayout.3.refs_0_), channel_id=1, source_target_pairs={{0,2},{1,3},{2,0},{3,1},{4,6},{5,7},{6,4},{7,5},{8,10},{9,11},{10,... | collective-permute-start | bytes 3145736 | tf_op jit(solution)/shard_map/ppermute | solution.py:426
  4.2 1.1 %copy-done.2 = bf16[24,4,4096]{2,1,0:T(4,128)(2,1)S(1)} copy-done((bf16[24,4,4096]{2,1,0:T(4,128)(2,1)S(1)}, bf16[24,4,4096]{2,1,0:T(4,128)(2,1)}, u32[]{:S(2)}) %copy-start.2) | copy-done | bytes 786456
  5.4 1.1 %relayout_rows.1.refs_0_ = bf16[24,2,64,128]{3,2,1,0:T(8,128)(2,1)S(1)} custom-call(bf16[24,4,4096]{2,1,0:T(4,128)(2,1)S(1)} %copy-done.2), custom_call_target="tpu_custom_call" | custom-call | flops 100000000 | bytes 3700000 | tf_op jit(solution)/shard_map/relayout_rows/pallas_call | solution.py:84
  6.5 0.1 add_select_fusion.4.table_ref
  6.6 3.0 %collective-permute-start.1 = (bf16[24,2,64,128]{3,2,1,0:T(8,128)(2,1)S(1)}, bf16[24,2,64,128]{3,2,1,0:T(8,128)(2,1)S(1)}, u32[]{:S(2)}, u32[]{:S(2)}) collective-permute-start(bf16[24,2,64,128]{3,2,1,0:T(8,128)(2,1)S(1)} %relayout_rows.1.refs_0_), channel_id=1, source_target_pairs={{0,4},{2,6},{4,8},{5,1},{6,10},{7,3},{8,12},{9,5},{10,14},{11,7},{... | collective-permute-start | bytes 2359304 | tf_op jit(solution)/shard_map/ppermute | solution.py:423
  9.6 0.1 subtract_select_fusion.place_ref
  9.7 0.4 relayout.4.refs_0_
  10.1 0.8 collective-permute-start.3
  10.9 0.2 fusion.12.order_ref
  11.1 0.0 copy-start.3
  11.1 3.9 %near_band.2.start_ref = bf16[4,27,256,128]{3,2,1,0:T(8,128)(2,1)S(1)} custom-call(s32[24,32]{1,0:T(8,128)S(1)} %subtract_select_fusion.place_ref, bf16[16,4,64,128]{3,2,1,0:T(8,128)(2,1)S(1)} %relayout.3.refs_0_, bf16[16,4,64,128]{3,2,1,0:T(8,128)(2,1)} %collective-permute-done.refs_1_), custom_call_target="tpu_custom_call" | custom-call | flops 256000000 | bytes 9472000 | tf_op jit(solution)/shard_map/near_band/pallas_call | solution.py:255
  15.1 0.9 relayout.5.pl_ref
  16.0 2.1 %near_band.3.start_ref = bf16[2,27,256,128]{3,2,1,0:T(8,128)(2,1)S(1)} custom-call(s32[24,32]{1,0:T(8,128)S(1)} %subtract_select_fusion.place_ref, bf16[8,4,64,128]{3,2,1,0:T(8,128)(2,1)S(1)} %relayout.4.refs_0_, bf16[8,4,64,128]{3,2,1,0:T(8,128)(2,1)S(1)} %collective-permute-done.3.refs_1_), custom_call_target="tpu_custom_call" | custom-call | flops 128000000 | bytes 4736000 | tf_op jit(solution)/shard_map/near_band/pallas_call | solution.py:255
  18.0 1.4 %right_factor.2.own_ref = bf16[6,5,256,128]{3,2,1,0:T(8,128)(2,1)S(1)} custom-call(s32[4,72]{1,0:T(4,128)S(1)} %add_select_fusion.4.table_ref, bf16[24,2,64,128]{3,2,1,0:T(8,128)(2,1)S(1)} %relayout_rows.1.refs_0_), custom_call_target="tpu_custom_call" | custom-call | flops 200000000 | bytes 7400000 | tf_op jit(solution)/shard_map/right_factor/pallas_call | solution.py:186
  19.4 2.9 %left_factor.1.left_ref = bf16[12,24,64,128]{3,2,1,0:T(8,128)(2,1)S(1)} custom-call(s32[4,192]{1,0:T(4,128)S(1)} %bitcast.26, bf16[24,2,64,128]{3,2,1,0:T(8,128)(2,1)S(1)} %relayout.5.pl_ref), custom_call_target="tpu_custom_call" | custom-call | flops 290000000 | bytes 10730000 | tf_op jit(solution)/shard_map/left_factor/pallas_call | solution.py:118
  22.3 5.5 %collective-permute-done.2.refs_0_ = bf16[16,4,64,128]{3,2,1,0:T(8,128)(2,1)} collective-permute-done((bf16[16,4,64,128]{3,2,1,0:T(8,128)(2,1)S(1)}, bf16[16,4,64,128]{3,2,1,0:T(8,128)(2,1)}, u32[]{:S(2)}, u32[]{:S(2)}) %collective-permute-start.2) | collective-permute-done | bytes 1048608 | tf_op jit(solution)/shard_map/ppermute | solution.py:426
  27.8 0.3 collective-permute-done.1.refs_0_
  28.2 0.5 collective-permute-start.6
  28.7 1.2 %collective-permute-start.4 = (bf16[8,4,64,128]{3,2,1,0:T(8,128)(2,1)S(1)}, bf16[8,4,64,128]{3,2,1,0:T(8,128)(2,1)S(1)}, u32[]{:S(2)}, u32[]{:S(2)}) collective-permute-start(bf16[8,4,64,128]{3,2,1,0:T(8,128)(2,1)S(1)} %relayout.4.refs_0_), channel_id=1, source_target_pairs={{0,2},{1,3},{2,0},{3,1},{4,6},{5,7},{6,4},{7,5},{8,10},{9,11},{10,... | collective-permute-start | bytes 1572872 | tf_op jit(solution)/shard_map/ppermute | solution.py:426
  29.9 2.0 %collective-permute-done.5.refs_1_ = bf16[24,2,64,128]{3,2,1,0:T(8,128)(2,1)S(1)} collective-permute-done((bf16[24,2,64,128]{3,2,1,0:T(8,128)(2,1)S(1)}, bf16[24,2,64,128]{3,2,1,0:T(8,128)(2,1)S(1)}, u32[]{:S(2)}, u32[]{:S(2)}) %collective-permute-start.5) | collective-permute-done | bytes 786464 | tf_op jit(solution)/shard_map/ppermute | solution.py:429
  32.0 2.3 %right_factor.3.near_ref = bf16[12,5,256,128]{3,2,1,0:T(8,128)(2,1)S(1)} custom-call(s32[4,72]{1,0:T(4,128)S(1)} %add_select_fusion.4.table_ref, bf16[24,2,64,128]{3,2,1,0:T(8,128)(2,1)S(1)} %collective-permute-done.1.refs_0_, bf16[24,2,64,128]{3,2,1,0:T(8,128)(2,1)S(1)} %collective-permute-done.5.refs_1_), custom_call_target="tpu_custom_call" | custom-call | flops 300000000 | bytes 11100000 | tf_op jit(solution)/shard_map/right_factor/pallas_call | solution.py:186
  34.3 7.1 %product.2.refs_0_ = bf16[16,64,640]{2,1,0:T(8,128)(2,1)S(1)} custom-call(s32[24,32]{1,0:T(8,128)S(1)} %subtract_select_fusion.place_ref, bf16[6,5,256,128]{3,2,1,0:T(8,128)(2,1)S(1)} %right_factor.2.own_ref, bf16[12,5,256,128]{3,2,1,0:T(8,128)(2,1)S(1)} %right_factor.3.near_ref, bf16[4,27,256,128]{3,2,1,0:T(8,128)(2,1)S(1)} %near_band.2.start_ref, ...), custom_call_target="tpu_custom_call" | custom-call | flops 480000000 | bytes 17760000 | tf_op jit(solution)/shard_map/product/pallas_call | solution.py:299
  41.4 0.3 collective-permute-done.4.refs_0_
  41.7 1.4 %collective-permute-start.8 = (bf16[8,4,64,128]{3,2,1,0:T(8,128)(2,1)S(1)}, bf16[8,4,64,128]{3,2,1,0:T(8,128)(2,1)S(1)}, u32[]{:S(2)}, u32[]{:S(2)}) collective-permute-start(bf16[8,4,64,128]{3,2,1,0:T(8,128)(2,1)S(1)} %collective-permute-done.4.refs_0_), channel_id=1, source_target_pairs={{0,1},{1,0},{2,3},{3,2},{4,5},{5,4},{6,7},{7,6},{8,9},{9,8},{10,11... | collective-permute-start | bytes 1572872 | tf_op jit(solution)/shard_map/ppermute | solution.py:429
  43.0 0.9 coarse.8
  44.0 3.8 %collective-permute-start.7 = (bf16[10,4,4096]{2,1,0:T(4,128)(2,1)S(1)}, bf16[10,4,4096]{2,1,0:T(4,128)(2,1)S(1)}, u32[]{:S(2)}, u32[]{:S(2)}) collective-permute-start(bf16[10,4,4096]{2,1,0:T(4,128)(2,1)S(1)} %coarse.8), channel_id=1, source_target_pairs={{4,0},{8,4},{12,8},{16,12},{20,16},{24,20},{28,24},{5,1},{9,5},{13... | collective-permute-start | bytes 983048 | tf_op jit(solution)/shard_map/ppermute | solution.py:435
  47.7 3.8 %product.3.refs_1_ = bf16[8,64,640]{2,1,0:T(8,128)(2,1)S(1)} custom-call(s32[24,32]{1,0:T(8,128)S(1)} %subtract_select_fusion.place_ref, bf16[6,5,256,128]{3,2,1,0:T(8,128)(2,1)S(1)} %right_factor.2.own_ref, bf16[12,5,256,128]{3,2,1,0:T(8,128)(2,1)S(1)} %right_factor.3.near_ref, bf16[2,27,256,128]{3,2,1,0:T(8,128)(2,1)S(1)} %near_band.3.start_ref, ...), custom_call_target="tpu_custom_call" | custom-call | flops 240000000 | bytes 8880000 | tf_op jit(solution)/shard_map/product/pallas_call | solution.py:299
  51.5 1.1 %coarse.12 = bf16[10,4,4096]{2,1,0:T(4,128)(2,1)S(1)} custom-call(bf16[12,24,64,128]{3,2,1,0:T(8,128)(2,1)S(1)} %left_factor.1.left_ref, bf16[16,64,640]{2,1,0:T(8,128)(2,1)S(1)} %product.2.refs_0_, bf16[8,64,640]{2,1,0:T(8,128)(2,1)S(1)} %product.3.refs_1_), custom_call_target="tpu_custom_call" | custom-call | flops 100000000 | bytes 3700000 | tf_op jit(solution)/shard_map/coarse/pallas_call | solution.py:346
  52.7 1.9 %collective-permute-start.11 = (bf16[10,4,4096]{2,1,0:T(4,128)(2,1)S(1)}, bf16[10,4,4096]{2,1,0:T(4,128)(2,1)S(1)}, u32[]{:S(2)}, u32[]{:S(2)}) collective-permute-start(bf16[10,4,4096]{2,1,0:T(4,128)(2,1)S(1)} %coarse.12), channel_id=1, source_target_pairs={{4,0},{8,4},{12,8},{16,12},{20,16},{24,20},{28,24},{5,1},{9,5},{13... | collective-permute-start | bytes 983048 | tf_op jit(solution)/shard_map/ppermute | solution.py:435
  54.6 0.6 coarse.9
  55.2 0.6 collective-permute-done.7
  55.7 4.0 %collective-permute-start.9 = (bf16[10,8,1024]{2,1,0:T(8,128)(2,1)S(1)}, bf16[10,8,1024]{2,1,0:T(8,128)(2,1)S(1)}, u32[]{:S(2)}, u32[]{:S(2)}) collective-permute-start(bf16[10,8,1024]{2,1,0:T(8,128)(2,1)S(1)} %coarse.9), channel_id=1, source_target_pairs={{0,4},{4,8},{8,12},{12,16},{16,20},{20,24},{24,28},{1,5},{5,9},{9,... | collective-permute-start | bytes 491528 | tf_op jit(solution)/shard_map/ppermute | solution.py:432
  59.8 0.7 coarse.13
  60.5 0.6 coarse.15
  61.1 0.7 coarse.10
  61.9 0.7 coarse.11
  62.6 0.7 coarse.14
  63.4 3.2 %collective-permute-done.9 = bf16[10,8,1024]{2,1,0:T(8,128)(2,1)S(1)} collective-permute-done((bf16[10,8,1024]{2,1,0:T(8,128)(2,1)S(1)}, bf16[10,8,1024]{2,1,0:T(8,128)(2,1)S(1)}, u32[]{:S(2)}, u32[]{:S(2)}) %collective-permute-start.9) | collective-permute-done | bytes 163872 | tf_op jit(solution)/shard_map/ppermute | solution.py:432
  66.5 4.1 %collective-permute-start.10 = (bf16[10,8,1536]{2,1,0:T(8,128)(2,1)S(1)}, bf16[10,8,1536]{2,1,0:T(8,128)(2,1)S(1)}, u32[]{:S(2)}, u32[]{:S(2)}) collective-permute-start(bf16[10,8,1536]{2,1,0:T(8,128)(2,1)S(1)} %coarse.10), channel_id=1, source_target_pairs={{0,4},{4,8},{8,12},{12,16},{16,20},{20,24},{24,28},{1,5},{5,9},{9,... | collective-permute-start | bytes 737288 | tf_op jit(solution)/shard_map/ppermute | solution.py:432
  70.6 2.2 %collective-permute-start.13 = (bf16[10,8,1536]{2,1,0:T(8,128)(2,1)S(1)}, bf16[10,8,1536]{2,1,0:T(8,128)(2,1)S(1)}, u32[]{:S(2)}, u32[]{:S(2)}) collective-permute-start(bf16[10,8,1536]{2,1,0:T(8,128)(2,1)S(1)} %coarse.13), channel_id=1, source_target_pairs={{0,4},{4,8},{8,12},{12,16},{16,20},{20,24},{24,28},{1,5},{5,9},{9,... | collective-permute-start | bytes 737288 | tf_op jit(solution)/shard_map/ppermute | solution.py:432
  72.8 0.2 fusion.13
  73.1 0.1 pad_maximum_fusion
  73.2 0.1 add_convert_fusion.2
  73.2 1.0 collective-permute-start.16
  74.2 2.1 %collective-permute-done.10 = bf16[10,8,1536]{2,1,0:T(8,128)(2,1)S(1)} collective-permute-done((bf16[10,8,1536]{2,1,0:T(8,128)(2,1)S(1)}, bf16[10,8,1536]{2,1,0:T(8,128)(2,1)S(1)}, u32[]{:S(2)}, u32[]{:S(2)}) %collective-permute-start.10) | collective-permute-done | bytes 245792 | tf_op jit(solution)/shard_map/ppermute | solution.py:432
  76.3 0.1 add_convert_fusion.1
  76.4 1.0 collective-permute-start.12
  77.4 4.2 %collective-permute-done.13 = bf16[10,8,1536]{2,1,0:T(8,128)(2,1)S(1)} collective-permute-done((bf16[10,8,1536]{2,1,0:T(8,128)(2,1)S(1)}, bf16[10,8,1536]{2,1,0:T(8,128)(2,1)S(1)}, u32[]{:S(2)}, u32[]{:S(2)}) %collective-permute-start.13) | collective-permute-done | bytes 245792 | tf_op jit(solution)/shard_map/ppermute | solution.py:432
  81.6 0.1 add_convert_fusion
  81.7 1.0 collective-permute-start.14
  82.7 1.6 %collective-permute-start.15 = (bf16[14,8,1024]{2,1,0:T(8,128)(2,1)S(1)}, bf16[14,8,1024]{2,1,0:T(8,128)(2,1)S(1)}, u32[]{:S(2)}, u32[]{:S(2)}) collective-permute-start(bf16[14,8,1024]{2,1,0:T(8,128)(2,1)S(1)} %bitcast.23), channel_id=1, source_target_pairs={{0,1},{1,0},{2,3},{3,2},{4,5},{5,4},{6,7},{7,6},{8,9},{9,8},{10,11... | collective-permute-start | bytes 688136 | tf_op jit(solution)/shard_map/ppermute | solution.py:429
  84.3 0.0 collective-permute-start.17
  84.3 0.5 collective-permute-start.18
  84.8 1.9 %collective-permute-done.12.refs_3_ = bf16[14,8,1536]{2,1,0:T(8,128)(2,1)S(1)} collective-permute-done((bf16[14,8,1536]{2,1,0:T(8,128)(2,1)S(1)}, bf16[14,8,1536]{2,1,0:T(8,128)(2,1)S(1)}, u32[]{:S(2)}, u32[]{:S(2)}) %collective-permute-start.12) | collective-permute-done | bytes 344096 | tf_op jit(solution)/shard_map/ppermute | solution.py:426
  86.7 1.7 %assemble.3.refs_0_ = bf16[8,56,4096]{2,1,0:T(8,128)(2,1)} custom-call(bf16[448,448]{1,0:T(8,128)(2,1)S(1)} %fusion.12.order_ref, bf16[14,8,1024]{2,1,0:T(8,128)(2,1)S(1)} %bitcast.24, bf16[14,8,1024]{2,1,0:T(8,128)(2,1)S(1)} %collective-permute-done.15.refs_1_, bf16[14,8,1024]{2,1,0:T(8,128)(2,1)S(1)} %collective-permute-done.16.refs_2_, ...), custom_call_target="tpu_custom_call" | custom-call | flops 290000000 | bytes 10730000 | tf_op jit(solution)/shard_map/assemble/pallas_call | solution.py:381
  88.4 5.7 %collective-permute-done.14.refs_3_ = bf16[14,8,1536]{2,1,0:T(8,128)(2,1)S(1)} collective-permute-done((bf16[14,8,1536]{2,1,0:T(8,128)(2,1)S(1)}, bf16[14,8,1536]{2,1,0:T(8,128)(2,1)S(1)}, u32[]{:S(2)}, u32[]{:S(2)}) %collective-permute-start.14) | collective-permute-done | bytes 344096 | tf_op jit(solution)/shard_map/ppermute | solution.py:426
  94.1 2.0 %collective-permute-start.19 = (bf16[14,8,1536]{2,1,0:T(8,128)(2,1)S(1)}, bf16[14,8,1536]{2,1,0:T(8,128)(2,1)S(1)}, u32[]{:S(2)}, u32[]{:S(2)}) collective-permute-start(bf16[14,8,1536]{2,1,0:T(8,128)(2,1)S(1)} %collective-permute-done.12.refs_3_), channel_id=1, source_target_pairs={{0,1},{1,0},{2,3},{3,2},{4,5},{5,4},{6,7},{7,6},{8,9},{9,8},{10,11... | collective-permute-start | bytes 1032200 | tf_op jit(solution)/shard_map/ppermute | solution.py:429
  96.1 0.5 collective-permute-start.21
  96.6 0.8 collective-permute-done.19.refs_4_
  97.4 2.4 %assemble.4.refs_0_ = bf16[8,56,4096]{2,1,0:T(8,128)(2,1)} custom-call(bf16[448,448]{1,0:T(8,128)(2,1)S(1)} %fusion.12.order_ref, bf16[8,56,4096]{2,1,0:T(8,128)(2,1)} %assemble.3.refs_0_, bf16[14,8,1536]{2,1,0:T(8,128)(2,1)S(1)} %bitcast.17, bf16[14,8,1536]{2,1,0:T(8,128)(2,1)S(1)} %collective-permute-done.18.refs_2_, ...), custom_call_target="tpu_custom_call", output_to_operand_aliasing={{}: (1, {})} | custom-call | flops 290000000 | bytes 10730000 | tf_op jit(solution)/shard_map/assemble/pallas_call | solution.py:381
  99.8 2.4 %assemble.5 = bf16[8,56,4096]{2,1,0:T(8,128)(2,1)} custom-call(bf16[448,448]{1,0:T(8,128)(2,1)S(1)} %fusion.12.order_ref, bf16[8,56,4096]{2,1,0:T(8,128)(2,1)} %assemble.4.refs_0_, bf16[14,8,1536]{2,1,0:T(8,128)(2,1)S(1)} %bitcast.20, bf16[14,8,1536]{2,1,0:T(8,128)(2,1)S(1)} %collective-permute-done.20.refs_2_, ...), custom_call_target="tpu_custom_call", output_to_operand_aliasing={{}: (1, {})} | custom-call | flops 290000000 | bytes 10730000 | tf_op jit(solution)/shard_map/assemble/pallas_call | solution.py:381
  (28 shorter events, 0.1 us)
Async XLA Ops:
  0.0 1.4 %copy-start = (bf16[24,8,4096]{2,1,0:T(8,128)(2,1)S(1)}, bf16[24,8,4096]{2,1,0:T(8,128)(2,1)}, u32[]{:S(2)}) copy-start(bf16[24,8,4096]{2,1,0:T(8,128)(2,1)} %x_ref.4) | copy-start | bytes 4718596
  1.4 5.0 %copy-start.4 = (s32[192,4]{0,1:T(4,128)S(1)}, s32[192,4]{0,1:T(4,128)}, u32[]{:S(2)}) copy-start(s32[192,4]{0,1:T(4,128)} %param.9) | copy-start | bytes 9220
  1.4 8.2 %copy-start.5 = (s32[24,32]{1,0:T(8,128)S(1)}, s32[24,32]{1,0:T(8,128)}, u32[]{:S(2)}) copy-start(s32[24,32]{1,0:T(8,128)} %param.6) | copy-start | bytes 9220
  1.4 8.2 %copy-start.6 = (s32[24]{0:T(128)S(1)}, s32[24]{0:T(128)}, u32[]{:S(2)}) copy-start(s32[24]{0:T(128)} %param.7) | copy-start | bytes 292
  1.4 8.3 %copy-start.1 = (bf16[24,8,4096]{2,1,0:T(8,128)(2,1)S(1)}, bf16[24,8,4096]{2,1,0:T(8,128)(2,1)}, u32[]{:S(2)}) copy-start(bf16[24,8,4096]{2,1,0:T(8,128)(2,1)} %x_ref.4) | copy-start | bytes 4718596
  2.2 4.3 %collective-permute-start = (bf16[16,4,64,128]{3,2,1,0:T(8,128)(2,1)S(1)}, bf16[16,4,64,128]{3,2,1,0:T(8,128)(2,1)}, u32[]{:S(2)}, u32[]{:S(2)}) collective-permute-start(bf16[16,4,64,128]{3,2,1,0:T(8,128)(2,1)S(1)} %relayout.3.refs_0_), channel_id=1, source_target_pairs={{0,1},{1,0},{2,3},{3,2},{4,5},{5,4},{6,7},{7,6},{8,9},{9,8},{10,11... | collective-permute-start | bytes 3145736 | tf_op jit(solution)/shard_map/ppermute | solution.py:429
  3.0 24.8 %collective-permute-start.2 = (bf16[16,4,64,128]{3,2,1,0:T(8,128)(2,1)S(1)}, bf16[16,4,64,128]{3,2,1,0:T(8,128)(2,1)}, u32[]{:S(2)}, u32[]{:S(2)}) collective-permute-start(bf16[16,4,64,128]{3,2,1,0:T(8,128)(2,1)S(1)} %relayout.3.refs_0_), channel_id=1, source_target_pairs={{0,2},{1,3},{2,0},{3,1},{4,6},{5,7},{6,4},{7,5},{8,10},{9,11},{10,... | collective-permute-start | bytes 3145736 | tf_op jit(solution)/shard_map/ppermute | solution.py:426
  4.2 1.1 %copy-start.2 = (bf16[24,4,4096]{2,1,0:T(4,128)(2,1)S(1)}, bf16[24,4,4096]{2,1,0:T(4,128)(2,1)}, u32[]{:S(2)}) copy-start(bf16[24,4,4096]{2,1,0:T(4,128)(2,1)} %x_ref.5) | copy-start | bytes 2359300
  6.6 21.6 %collective-permute-start.1 = (bf16[24,2,64,128]{3,2,1,0:T(8,128)(2,1)S(1)}, bf16[24,2,64,128]{3,2,1,0:T(8,128)(2,1)S(1)}, u32[]{:S(2)}, u32[]{:S(2)}) collective-permute-start(bf16[24,2,64,128]{3,2,1,0:T(8,128)(2,1)S(1)} %relayout_rows.1.refs_0_), channel_id=1, source_target_pairs={{0,4},{2,6},{4,8},{5,1},{6,10},{7,3},{8,12},{9,5},{10,14},{11,7},{... | collective-permute-start | bytes 2359304 | tf_op jit(solution)/shard_map/ppermute | solution.py:423
  10.1 4.9 %collective-permute-start.3 = (bf16[8,4,64,128]{3,2,1,0:T(8,128)(2,1)S(1)}, bf16[8,4,64,128]{3,2,1,0:T(8,128)(2,1)S(1)}, u32[]{:S(2)}, u32[]{:S(2)}) collective-permute-start(bf16[8,4,64,128]{3,2,1,0:T(8,128)(2,1)S(1)} %relayout.4.refs_0_), channel_id=1, source_target_pairs={{0,1},{1,0},{2,3},{3,2},{4,5},{5,4},{6,7},{7,6},{8,9},{9,8},{10,11... | collective-permute-start | bytes 1572872 | tf_op jit(solution)/shard_map/ppermute | solution.py:429
  11.1 4.0 %copy-start.3 = (bf16[24,4,4096]{2,1,0:T(4,128)(2,1)S(1)}, bf16[24,4,4096]{2,1,0:T(4,128)(2,1)}, u32[]{:S(2)}) copy-start(bf16[24,4,4096]{2,1,0:T(4,128)(2,1)} %x_ref.5) | copy-start | bytes 2359300
  28.2 6.1 %collective-permute-start.6 = (bf16[16,4,64,128]{3,2,1,0:T(8,128)(2,1)}, bf16[16,4,64,128]{3,2,1,0:T(8,128)(2,1)S(1)}, u32[]{:S(2)}, u32[]{:S(2)}) collective-permute-start(bf16[16,4,64,128]{3,2,1,0:T(8,128)(2,1)} %collective-permute-done.2.refs_0_), channel_id=1, source_target_pairs={{0,1},{1,0},{2,3},{3,2},{4,5},{5,4},{6,7},{7,6},{8,9},{9,8},{10,11... | collective-permute-start | bytes 3145736 | tf_op jit(solution)/shard_map/ppermute | solution.py:429
  28.7 3.3 %collective-permute-start.5 = (bf16[24,2,64,128]{3,2,1,0:T(8,128)(2,1)S(1)}, bf16[24,2,64,128]{3,2,1,0:T(8,128)(2,1)S(1)}, u32[]{:S(2)}, u32[]{:S(2)}) collective-permute-start(bf16[24,2,64,128]{3,2,1,0:T(8,128)(2,1)S(1)} %collective-permute-done.1.refs_0_), channel_id=1, source_target_pairs={{0,1},{1,0},{2,3},{3,2},{4,5},{5,4},{6,7},{7,6},{8,9},{9,8},{10,11... | collective-permute-start | bytes 2359304 | tf_op jit(solution)/shard_map/ppermute | solution.py:429
  28.7 13.0 %collective-permute-start.4 = (bf16[8,4,64,128]{3,2,1,0:T(8,128)(2,1)S(1)}, bf16[8,4,64,128]{3,2,1,0:T(8,128)(2,1)S(1)}, u32[]{:S(2)}, u32[]{:S(2)}) collective-permute-start(bf16[8,4,64,128]{3,2,1,0:T(8,128)(2,1)S(1)} %relayout.4.refs_0_), channel_id=1, source_target_pairs={{0,2},{1,3},{2,0},{3,1},{4,6},{5,7},{6,4},{7,5},{8,10},{9,11},{10,... | collective-permute-start | bytes 1572872 | tf_op jit(solution)/shard_map/ppermute | solution.py:426
  41.7 6.1 %collective-permute-start.8 = (bf16[8,4,64,128]{3,2,1,0:T(8,128)(2,1)S(1)}, bf16[8,4,64,128]{3,2,1,0:T(8,128)(2,1)S(1)}, u32[]{:S(2)}, u32[]{:S(2)}) collective-permute-start(bf16[8,4,64,128]{3,2,1,0:T(8,128)(2,1)S(1)} %collective-permute-done.4.refs_0_), channel_id=1, source_target_pairs={{0,1},{1,0},{2,3},{3,2},{4,5},{5,4},{6,7},{7,6},{8,9},{9,8},{10,11... | collective-permute-start | bytes 1572872 | tf_op jit(solution)/shard_map/ppermute | solution.py:429
  44.0 11.8 %collective-permute-start.7 = (bf16[10,4,4096]{2,1,0:T(4,128)(2,1)S(1)}, bf16[10,4,4096]{2,1,0:T(4,128)(2,1)S(1)}, u32[]{:S(2)}, u32[]{:S(2)}) collective-permute-start(bf16[10,4,4096]{2,1,0:T(4,128)(2,1)S(1)} %coarse.8), channel_id=1, source_target_pairs={{4,0},{8,4},{12,8},{16,12},{20,16},{24,20},{28,24},{5,1},{9,5},{13... | collective-permute-start | bytes 983048 | tf_op jit(solution)/shard_map/ppermute | solution.py:435
  52.7 18.0 %collective-permute-start.11 = (bf16[10,4,4096]{2,1,0:T(4,128)(2,1)S(1)}, bf16[10,4,4096]{2,1,0:T(4,128)(2,1)S(1)}, u32[]{:S(2)}, u32[]{:S(2)}) collective-permute-start(bf16[10,4,4096]{2,1,0:T(4,128)(2,1)S(1)} %coarse.12), channel_id=1, source_target_pairs={{4,0},{8,4},{12,8},{16,12},{20,16},{24,20},{28,24},{5,1},{9,5},{13... | collective-permute-start | bytes 983048 | tf_op jit(solution)/shard_map/ppermute | solution.py:435
  55.7 10.8 %collective-permute-start.9 = (bf16[10,8,1024]{2,1,0:T(8,128)(2,1)S(1)}, bf16[10,8,1024]{2,1,0:T(8,128)(2,1)S(1)}, u32[]{:S(2)}, u32[]{:S(2)}) collective-permute-start(bf16[10,8,1024]{2,1,0:T(8,128)(2,1)S(1)} %coarse.9), channel_id=1, source_target_pairs={{0,4},{4,8},{8,12},{12,16},{16,20},{20,24},{24,28},{1,5},{5,9},{9,... | collective-permute-start | bytes 491528 | tf_op jit(solution)/shard_map/ppermute | solution.py:432
  66.5 9.8 %collective-permute-start.10 = (bf16[10,8,1536]{2,1,0:T(8,128)(2,1)S(1)}, bf16[10,8,1536]{2,1,0:T(8,128)(2,1)S(1)}, u32[]{:S(2)}, u32[]{:S(2)}) collective-permute-start(bf16[10,8,1536]{2,1,0:T(8,128)(2,1)S(1)} %coarse.10), channel_id=1, source_target_pairs={{0,4},{4,8},{8,12},{12,16},{16,20},{20,24},{24,28},{1,5},{5,9},{9,... | collective-permute-start | bytes 737288 | tf_op jit(solution)/shard_map/ppermute | solution.py:432
  70.6 11.0 %collective-permute-start.13 = (bf16[10,8,1536]{2,1,0:T(8,128)(2,1)S(1)}, bf16[10,8,1536]{2,1,0:T(8,128)(2,1)S(1)}, u32[]{:S(2)}, u32[]{:S(2)}) collective-permute-start(bf16[10,8,1536]{2,1,0:T(8,128)(2,1)S(1)} %coarse.13), channel_id=1, source_target_pairs={{0,4},{4,8},{8,12},{12,16},{16,20},{20,24},{24,28},{1,5},{5,9},{9,... | collective-permute-start | bytes 737288 | tf_op jit(solution)/shard_map/ppermute | solution.py:432
  73.2 11.0 %collective-permute-start.16 = (bf16[14,8,1024]{2,1,0:T(8,128)(2,1)S(1)}, bf16[14,8,1024]{2,1,0:T(8,128)(2,1)S(1)}, u32[]{:S(2)}, u32[]{:S(2)}) collective-permute-start(bf16[14,8,1024]{2,1,0:T(8,128)(2,1)S(1)} %bitcast.22), channel_id=1, source_target_pairs={{0,2},{1,3},{2,0},{3,1},{4,6},{5,7},{6,4},{7,5},{8,10},{9,11},{10,... | collective-permute-start | bytes 688136 | tf_op jit(solution)/shard_map/ppermute | solution.py:426
  76.4 10.3 %collective-permute-start.12 = (bf16[14,8,1536]{2,1,0:T(8,128)(2,1)S(1)}, bf16[14,8,1536]{2,1,0:T(8,128)(2,1)S(1)}, u32[]{:S(2)}, u32[]{:S(2)}) collective-permute-start(bf16[14,8,1536]{2,1,0:T(8,128)(2,1)S(1)} %bitcast.15), channel_id=1, source_target_pairs={{0,2},{1,3},{2,0},{3,1},{4,6},{5,7},{6,4},{7,5},{8,10},{9,11},{10,... | collective-permute-start | bytes 1032200 | tf_op jit(solution)/shard_map/ppermute | solution.py:426
  81.7 12.4 %collective-permute-start.14 = (bf16[14,8,1536]{2,1,0:T(8,128)(2,1)S(1)}, bf16[14,8,1536]{2,1,0:T(8,128)(2,1)S(1)}, u32[]{:S(2)}, u32[]{:S(2)}) collective-permute-start(bf16[14,8,1536]{2,1,0:T(8,128)(2,1)S(1)} %bitcast.18), channel_id=1, source_target_pairs={{0,2},{1,3},{2,0},{3,1},{4,6},{5,7},{6,4},{7,5},{8,10},{9,11},{10,... | collective-permute-start | bytes 1032200 | tf_op jit(solution)/shard_map/ppermute | solution.py:426
  82.7 4.1 %collective-permute-start.15 = (bf16[14,8,1024]{2,1,0:T(8,128)(2,1)S(1)}, bf16[14,8,1024]{2,1,0:T(8,128)(2,1)S(1)}, u32[]{:S(2)}, u32[]{:S(2)}) collective-permute-start(bf16[14,8,1024]{2,1,0:T(8,128)(2,1)S(1)} %bitcast.23), channel_id=1, source_target_pairs={{0,1},{1,0},{2,3},{3,2},{4,5},{5,4},{6,7},{7,6},{8,9},{9,8},{10,11... | collective-permute-start | bytes 688136 | tf_op jit(solution)/shard_map/ppermute | solution.py:429
  84.3 2.5 %collective-permute-start.17 = (bf16[14,8,1024]{2,1,0:T(8,128)(2,1)S(1)}, bf16[14,8,1024]{2,1,0:T(8,128)(2,1)S(1)}, u32[]{:S(2)}, u32[]{:S(2)}) collective-permute-start(bf16[14,8,1024]{2,1,0:T(8,128)(2,1)S(1)} %collective-permute-done.16.refs_2_), channel_id=1, source_target_pairs={{0,1},{1,0},{2,3},{3,2},{4,5},{5,4},{6,7},{7,6},{8,9},{9,8},{10,11... | collective-permute-start | bytes 688136 | tf_op jit(solution)/shard_map/ppermute | solution.py:429
  84.3 12.3 %collective-permute-start.18 = (bf16[14,8,1536]{2,1,0:T(8,128)(2,1)S(1)}, bf16[14,8,1536]{2,1,0:T(8,128)(2,1)S(1)}, u32[]{:S(2)}, u32[]{:S(2)}) collective-permute-start(bf16[14,8,1536]{2,1,0:T(8,128)(2,1)S(1)} %bitcast.16), channel_id=1, source_target_pairs={{0,1},{1,0},{2,3},{3,2},{4,5},{5,4},{6,7},{7,6},{8,9},{9,8},{10,11... | collective-permute-start | bytes 1032200 | tf_op jit(solution)/shard_map/ppermute | solution.py:429
  94.1 3.3 %collective-permute-start.19 = (bf16[14,8,1536]{2,1,0:T(8,128)(2,1)S(1)}, bf16[14,8,1536]{2,1,0:T(8,128)(2,1)S(1)}, u32[]{:S(2)}, u32[]{:S(2)}) collective-permute-start(bf16[14,8,1536]{2,1,0:T(8,128)(2,1)S(1)} %collective-permute-done.12.refs_3_), channel_id=1, source_target_pairs={{0,1},{1,0},{2,3},{3,2},{4,5},{5,4},{6,7},{7,6},{8,9},{9,8},{10,11... | collective-permute-start | bytes 1032200 | tf_op jit(solution)/shard_map/ppermute | solution.py:429
  96.1 3.7 %collective-permute-start.20 = (bf16[14,8,1536]{2,1,0:T(8,128)(2,1)S(1)}, bf16[14,8,1536]{2,1,0:T(8,128)(2,1)S(1)}, u32[]{:S(2)}, u32[]{:S(2)}) collective-permute-start(bf16[14,8,1536]{2,1,0:T(8,128)(2,1)S(1)} %bitcast.19), channel_id=1, source_target_pairs={{0,1},{1,0},{2,3},{3,2},{4,5},{5,4},{6,7},{7,6},{8,9},{9,8},{10,11... | collective-permute-start | bytes 1032200 | tf_op jit(solution)/shard_map/ppermute | solution.py:429
  96.1 3.7 %collective-permute-start.21 = (bf16[14,8,1536]{2,1,0:T(8,128)(2,1)S(1)}, bf16[14,8,1536]{2,1,0:T(8,128)(2,1)S(1)}, u32[]{:S(2)}, u32[]{:S(2)}) collective-permute-start(bf16[14,8,1536]{2,1,0:T(8,128)(2,1)S(1)} %collective-permute-done.14.refs_3_), channel_id=1, source_target_pairs={{0,1},{1,0},{2,3},{3,2},{4,5},{5,4},{6,7},{7,6},{8,9},{9,8},{10,11... | collective-permute-start | bytes 1032200 | tf_op jit(solution)/shard_map/ppermute | solution.py:429

commit v11 on v10

--- a/solution.py
+++ b/solution.py
@@ -416,7 +416,7 @@
     share = CB // ncol
     tiles = (GROUPS * share + 1) // 2
     parts = ((0, rb * 2 // 3), (rb * 2 // 3, rb // 3))
-    chunks = ((0, 16), (16, 40), (40, 64))
+    chunks = ((0, 24), (24, 48), (48, 64))
 
     def outward(x):
         pairs = [(r * ncol + c, (r + 1 - 2 * (c % 2)) * ncol + c) for r in range(nrow) for c in range(ncol)]
@@ -468,19 +468,27 @@
         y = x[: GROUPS * share].reshape((share, GROUPS) + x.shape[1:])
         return jnp.pad(y.astype(F32), ((0, 0), (g, 2 - g), (0, 0), (0, 0)))
 
-    late = downward(coarse_rows(left, aps, ((CB // 2, CB),), 0, BS, BF, 1.0)[0])
+    cut = chunks[0][1]
+    lows = [coarse_rows(left, aps, ((CB // 2, CB),), a0, a1, BF, 1.0)[0] for a0, a1 in ((0, cut), (cut, BS))]
     raw = [coarse_rows(left, aps, ((2 * CB, 3 * CB),), a0, a1, BF, 1.0)[0] for a0, a1 in chunks]
+    late = [downward(lows[0])]
     early, raw[0] = lax.optimization_barrier((early, raw[0]))
     highs = [upward(raw[0])]
+    late[0], lows[1] = lax.optimization_barrier((late[0], lows[1]))
+    late.append(downward(lows[1]))
     highs[0], raw[1] = lax.optimization_barrier((highs[0], raw[1]))
     highs.append(upward(raw[1]))
-    late, raw[2] = lax.optimization_barrier((late, raw[2]))
+    late[1], raw[2] = lax.optimization_barrier((late[1], raw[2]))
     highs.append(upward(raw[2]))
     mids = [coarse_rows(left, aps, ((CB, 2 * CB),), a0, a1, F32, 1.0)[0] for a0, a1 in chunks]
-    lower = jnp.concatenate([early, late], axis=1)
+    lower = [
+        jnp.concatenate([early[:, :, : cut * BS], late[0]], axis=1),
+        jnp.concatenate([early[:, :, cut * BS :], late[1]], axis=1),
+    ]
     totals, sides, fars = [], [], []
     for z, (a0, a1) in enumerate(chunks):
-        total = columns(highs[z], 0) + columns(mids[z], 1) + columns(lower[:, :, a0 * BS : a1 * BS], 2)
+        low = lower[0] if z == 0 else lower[1][:, :, (a0 - cut) * BS : (a1 - cut) * BS]
+        total = columns(highs[z], 0) + columns(mids[z], 1) + columns(low, 2)
         total = total.astype(BF).reshape((share * (GROUPS + 2),) + total.shape[2:])
         totals.append(total)
         sides.append(over_core(total))

time: 104 us -> 102 us (0.981)
  waiting for transfers between devices: 26.6 us -> 11.6 us
  starting transfers between devices: 32.5 us -> 45.2 us
    ppermute x11, starting transfers between devices: 8.05 us -> 18.5 us  [over_core(): return lax.ppermute(x, 'col', [(c, c ^ 1) for c in range(ncol)])]
    ppermute x3, waiting for transfers between devices: 9.49 us -> 1.7 us  [upward(): return lax.ppermute(x, 'row', [(i, i + 1) for i in range(nrow - 1)])]
    ppermute x5, waiting for transfers between devices: 13.4 us -> 5.77 us  [over_y(): lax.ppermute(x, 'col', [(y * 2 + c, (y + s) % ny * 2 + c) for y in range(...]
    ppermute x2 -> x3, starting transfers between devices: 5.67 us -> 7.8 us  [downward(): return lax.ppermute(x, 'row', [(i + 1, i) for i in range(nrow - 1)])]
    pallas_call x8 -> x9, Pallas kernels: 6.19 us -> 6.27 us  [coarse_rows(): pl.pallas_call(functools.partial(coarse_kernel, sets, a0, a1), out_shape=...]
    unnamed x14 -> x16, local copies, waits for them, and re-layouts: 2.56 us -> 2.56 us
  transfers between devices with their start and end apart: 22 -> 23, of which waited for: 11 -> 7; matrix products, arithmetic and copies ran while one was open for 1% -> 1% of each run, Pallas kernels for 35% -> 37%
where the time goes in v11:
time: 102 us; the launch traced here: 100 us
  starting transfers between devices  45.2 us (44%)
  Pallas kernels  39.4 us (39%)
  waiting for transfers between devices  11.6 us (11%)
  local copies, waits for them, and re-layouts  2.64 us (3%)
    ppermute x11, starting transfers between devices, over_core(): return lax.ppermute(x, 'col', [(c, c ^ 1) for c in range(ncol)])  18.5 us
    pallas_call x2, Pallas kernels, product(): pl.pallas_call(functools.partial(product_kernel, first, rb, shifts), out_...  10.9 us
    ppermute x3, starting transfers between devices, upward(): return lax.ppermute(x, 'row', [(i, i + 1) for i in range(nrow - 1)])  10.1 us
    ppermute x3, starting transfers between devices, downward(): return lax.ppermute(x, 'row', [(i + 1, i) for i in range(nrow - 1)])  7.8 us
    pallas_call x3, Pallas kernels, assemble(): pl.pallas_call(assemble_kernel, grid=(per,), out_shape=jax.ShapeDtypeStru...  6.56 us
    pallas_call x9, Pallas kernels, coarse_rows(): pl.pallas_call(functools.partial(coarse_kernel, sets, a0, a1), out_shape=...  6.27 us
    pallas_call x2, Pallas kernels, near_band(): pl.pallas_call(functools.partial(band_kernel, first, shifts), out_shape=j...  5.98 us
    ppermute x5, waiting for transfers between devices, over_y(): lax.ppermute(x, 'col', [(y * 2 + c, (y + s) % ny * 2 + c) for y in range(...  5.77 us
  transfers between devices with their start and end apart: 23, of which 7 were waited for; matrix products, arithmetic and copies ran while one was open for 1% of the time, Pallas kernels for 37%

profile of v11, /device:TPU:9, one launch (start us, length us, event | category | flops | bytes accessed | tf_op | source)
XLA Modules:
  0.0 100.1 jit_solution(8571194826001753485)
XLA Ops:
  0.0 1.4 %copy-done = bf16[24,8,4096]{2,1,0:T(8,128)(2,1)S(1)} copy-done((bf16[24,8,4096]{2,1,0:T(8,128)(2,1)S(1)}, bf16[24,8,4096]{2,1,0:T(8,128)(2,1)}, u32[]{:S(2)}) %copy-start) | copy-done | bytes 1572888
  1.4 0.8 relayout.3.refs_0_
  2.2 0.7 collective-permute-start
  3.0 1.3 %collective-permute-start.2 = (bf16[16,4,64,128]{3,2,1,0:T(8,128)(2,1)S(1)}, bf16[16,4,64,128]{3,2,1,0:T(8,128)(2,1)}, u32[]{:S(2)}, u32[]{:S(2)}) collective-permute-start(bf16[16,4,64,128]{3,2,1,0:T(8,128)(2,1)S(1)} %relayout.3.refs_0_), channel_id=1, source_target_pairs={{0,2},{1,3},{2,0},{3,1},{4,6},{5,7},{6,4},{7,5},{8,10},{9,11},{10,... | collective-permute-start | bytes 3145736 | tf_op jit(solution)/shard_map/ppermute | solution.py:426
  4.2 1.1 %copy-done.2 = bf16[24,4,4096]{2,1,0:T(4,128)(2,1)S(1)} copy-done((bf16[24,4,4096]{2,1,0:T(4,128)(2,1)S(1)}, bf16[24,4,4096]{2,1,0:T(4,128)(2,1)}, u32[]{:S(2)}) %copy-start.2) | copy-done | bytes 786456
  5.4 1.1 %relayout_rows.1.refs_0_ = bf16[24,2,64,128]{3,2,1,0:T(8,128)(2,1)S(1)} custom-call(bf16[24,4,4096]{2,1,0:T(4,128)(2,1)S(1)} %copy-done.2), custom_call_target="tpu_custom_call" | custom-call | flops 100000000 | bytes 3700000 | tf_op jit(solution)/shard_map/relayout_rows/pallas_call | solution.py:84
  6.5 0.1 add_select_fusion.4.table_ref
  6.6 3.0 %collective-permute-start.1 = (bf16[24,2,64,128]{3,2,1,0:T(8,128)(2,1)S(1)}, bf16[24,2,64,128]{3,2,1,0:T(8,128)(2,1)S(1)}, u32[]{:S(2)}, u32[]{:S(2)}) collective-permute-start(bf16[24,2,64,128]{3,2,1,0:T(8,128)(2,1)S(1)} %relayout_rows.1.refs_0_), channel_id=1, source_target_pairs={{0,4},{2,6},{4,8},{5,1},{6,10},{7,3},{8,12},{9,5},{10,14},{11,7},{... | collective-permute-start | bytes 2359304 | tf_op jit(solution)/shard_map/ppermute | solution.py:423
  9.6 0.1 subtract_select_fusion.place_ref
  9.7 0.4 relayout.4.refs_0_
  10.1 0.8 collective-permute-start.3
  10.9 0.2 fusion.12.order_ref
  11.1 0.0 copy-start.3
  11.1 3.9 %near_band.2.start_ref = bf16[4,27,256,128]{3,2,1,0:T(8,128)(2,1)S(1)} custom-call(s32[24,32]{1,0:T(8,128)S(1)} %subtract_select_fusion.place_ref, bf16[16,4,64,128]{3,2,1,0:T(8,128)(2,1)S(1)} %relayout.3.refs_0_, bf16[16,4,64,128]{3,2,1,0:T(8,128)(2,1)} %collective-permute-done.refs_1_), custom_call_target="tpu_custom_call" | custom-call | flops 256000000 | bytes 9472000 | tf_op jit(solution)/shard_map/near_band/pallas_call | solution.py:255
  15.1 0.9 relayout.5.pl_ref
  16.0 2.1 %near_band.3.start_ref = bf16[2,27,256,128]{3,2,1,0:T(8,128)(2,1)S(1)} custom-call(s32[24,32]{1,0:T(8,128)S(1)} %subtract_select_fusion.place_ref, bf16[8,4,64,128]{3,2,1,0:T(8,128)(2,1)S(1)} %relayout.4.refs_0_, bf16[8,4,64,128]{3,2,1,0:T(8,128)(2,1)S(1)} %collective-permute-done.3.refs_1_), custom_call_target="tpu_custom_call" | custom-call | flops 128000000 | bytes 4736000 | tf_op jit(solution)/shard_map/near_band/pallas_call | solution.py:255
  18.0 1.4 %right_factor.2.own_ref = bf16[6,5,256,128]{3,2,1,0:T(8,128)(2,1)S(1)} custom-call(s32[4,72]{1,0:T(4,128)S(1)} %add_select_fusion.4.table_ref, bf16[24,2,64,128]{3,2,1,0:T(8,128)(2,1)S(1)} %relayout_rows.1.refs_0_), custom_call_target="tpu_custom_call" | custom-call | flops 200000000 | bytes 7400000 | tf_op jit(solution)/shard_map/right_factor/pallas_call | solution.py:186
  19.4 2.9 %left_factor.1.left_ref = bf16[12,24,64,128]{3,2,1,0:T(8,128)(2,1)S(1)} custom-call(s32[4,192]{1,0:T(4,128)S(1)} %bitcast.26, bf16[24,2,64,128]{3,2,1,0:T(8,128)(2,1)S(1)} %relayout.5.pl_ref), custom_call_target="tpu_custom_call" | custom-call | flops 290000000 | bytes 10730000 | tf_op jit(solution)/shard_map/left_factor/pallas_call | solution.py:118
  22.3 5.5 %collective-permute-done.2.refs_0_ = bf16[16,4,64,128]{3,2,1,0:T(8,128)(2,1)} collective-permute-done((bf16[16,4,64,128]{3,2,1,0:T(8,128)(2,1)S(1)}, bf16[16,4,64,128]{3,2,1,0:T(8,128)(2,1)}, u32[]{:S(2)}, u32[]{:S(2)}) %collective-permute-start.2) | collective-permute-done | bytes 1048608 | tf_op jit(solution)/shard_map/ppermute | solution.py:426
  27.8 0.3 collective-permute-done.1.refs_0_
  28.2 0.5 collective-permute-start.6
  28.7 1.2 %collective-permute-start.4 = (bf16[8,4,64,128]{3,2,1,0:T(8,128)(2,1)S(1)}, bf16[8,4,64,128]{3,2,1,0:T(8,128)(2,1)S(1)}, u32[]{:S(2)}, u32[]{:S(2)}) collective-permute-start(bf16[8,4,64,128]{3,2,1,0:T(8,128)(2,1)S(1)} %relayout.4.refs_0_), channel_id=1, source_target_pairs={{0,2},{1,3},{2,0},{3,1},{4,6},{5,7},{6,4},{7,5},{8,10},{9,11},{10,... | collective-permute-start | bytes 1572872 | tf_op jit(solution)/shard_map/ppermute | solution.py:426
  29.9 2.0 %collective-permute-done.5.refs_1_ = bf16[24,2,64,128]{3,2,1,0:T(8,128)(2,1)S(1)} collective-permute-done((bf16[24,2,64,128]{3,2,1,0:T(8,128)(2,1)S(1)}, bf16[24,2,64,128]{3,2,1,0:T(8,128)(2,1)S(1)}, u32[]{:S(2)}, u32[]{:S(2)}) %collective-permute-start.5) | collective-permute-done | bytes 786464 | tf_op jit(solution)/shard_map/ppermute | solution.py:429
  32.0 2.3 %right_factor.3.near_ref = bf16[12,5,256,128]{3,2,1,0:T(8,128)(2,1)S(1)} custom-call(s32[4,72]{1,0:T(4,128)S(1)} %add_select_fusion.4.table_ref, bf16[24,2,64,128]{3,2,1,0:T(8,128)(2,1)S(1)} %collective-permute-done.1.refs_0_, bf16[24,2,64,128]{3,2,1,0:T(8,128)(2,1)S(1)} %collective-permute-done.5.refs_1_), custom_call_target="tpu_custom_call" | custom-call | flops 300000000 | bytes 11100000 | tf_op jit(solution)/shard_map/right_factor/pallas_call | solution.py:186
  34.3 7.1 %product.2.refs_0_ = bf16[16,64,640]{2,1,0:T(8,128)(2,1)S(1)} custom-call(s32[24,32]{1,0:T(8,128)S(1)} %subtract_select_fusion.place_ref, bf16[6,5,256,128]{3,2,1,0:T(8,128)(2,1)S(1)} %right_factor.2.own_ref, bf16[12,5,256,128]{3,2,1,0:T(8,128)(2,1)S(1)} %right_factor.3.near_ref, bf16[4,27,256,128]{3,2,1,0:T(8,128)(2,1)S(1)} %near_band.2.start_ref, ...), custom_call_target="tpu_custom_call" | custom-call | flops 480000000 | bytes 17760000 | tf_op jit(solution)/shard_map/product/pallas_call | solution.py:299
  41.4 0.3 collective-permute-done.4.refs_0_
  41.7 1.4 %collective-permute-start.8 = (bf16[8,4,64,128]{3,2,1,0:T(8,128)(2,1)S(1)}, bf16[8,4,64,128]{3,2,1,0:T(8,128)(2,1)S(1)}, u32[]{:S(2)}, u32[]{:S(2)}) collective-permute-start(bf16[8,4,64,128]{3,2,1,0:T(8,128)(2,1)S(1)} %collective-permute-done.4.refs_0_), channel_id=1, source_target_pairs={{0,1},{1,0},{2,3},{3,2},{4,5},{5,4},{6,7},{7,6},{8,9},{9,8},{10,11... | collective-permute-start | bytes 1572872 | tf_op jit(solution)/shard_map/ppermute | solution.py:429
  43.0 0.9 coarse.9
  44.0 3.8 %collective-permute-start.7 = (bf16[10,4,4096]{2,1,0:T(4,128)(2,1)S(1)}, bf16[10,4,4096]{2,1,0:T(4,128)(2,1)S(1)}, u32[]{:S(2)}, u32[]{:S(2)}) collective-permute-start(bf16[10,4,4096]{2,1,0:T(4,128)(2,1)S(1)} %coarse.9), channel_id=1, source_target_pairs={{4,0},{8,4},{12,8},{16,12},{20,16},{24,20},{28,24},{5,1},{9,5},{13... | collective-permute-start | bytes 983048 | tf_op jit(solution)/shard_map/ppermute | solution.py:435
  47.7 3.8 %product.3.refs_1_ = bf16[8,64,640]{2,1,0:T(8,128)(2,1)S(1)} custom-call(s32[24,32]{1,0:T(8,128)S(1)} %subtract_select_fusion.place_ref, bf16[6,5,256,128]{3,2,1,0:T(8,128)(2,1)S(1)} %right_factor.2.own_ref, bf16[12,5,256,128]{3,2,1,0:T(8,128)(2,1)S(1)} %right_factor.3.near_ref, bf16[2,27,256,128]{3,2,1,0:T(8,128)(2,1)S(1)} %near_band.3.start_ref, ...), custom_call_target="tpu_custom_call" | custom-call | flops 240000000 | bytes 8880000 | tf_op jit(solution)/shard_map/product/pallas_call | solution.py:299
  51.5 0.6 coarse.13
  52.1 1.9 %collective-permute-start.11 = (bf16[10,4,1536]{2,1,0:T(4,128)(2,1)S(1)}, bf16[10,4,1536]{2,1,0:T(4,128)(2,1)S(1)}, u32[]{:S(2)}, u32[]{:S(2)}) collective-permute-start(bf16[10,4,1536]{2,1,0:T(4,128)(2,1)S(1)} %coarse.13), channel_id=1, source_target_pairs={{4,0},{8,4},{12,8},{16,12},{20,16},{24,20},{28,24},{5,1},{9,5},{13... | collective-permute-start | bytes 368648 | tf_op jit(solution)/shard_map/ppermute | solution.py:435
  54.0 0.7 coarse.10
  54.8 1.0 collective-permute-done.7
  55.7 4.0 %collective-permute-start.9 = (bf16[10,8,1536]{2,1,0:T(8,128)(2,1)S(1)}, bf16[10,8,1536]{2,1,0:T(8,128)(2,1)S(1)}, u32[]{:S(2)}, u32[]{:S(2)}) collective-permute-start(bf16[10,8,1536]{2,1,0:T(8,128)(2,1)S(1)} %coarse.10), channel_id=1, source_target_pairs={{0,4},{4,8},{8,12},{12,16},{16,20},{20,24},{24,28},{1,5},{5,9},{9,... | collective-permute-start | bytes 737288 | tf_op jit(solution)/shard_map/ppermute | solution.py:432
  59.8 0.7 coarse.14
  60.5 0.7 coarse.17
  61.2 0.7 coarse.11
  61.9 0.6 coarse.15
  62.5 0.7 coarse.12
  63.3 0.1 slice.12
  63.4 0.0 slice-start
  63.4 0.6 coarse.16
  64.0 2.1 %collective-permute-start.12 = (bf16[10,4,2560]{2,1,0:T(4,128)(2,1)S(1)}, bf16[10,4,2560]{2,1,0:T(4,128)(2,1)S(1)}, u32[]{:S(2)}, u32[]{:S(2)}) collective-permute-start(bf16[10,4,2560]{2,1,0:T(4,128)(2,1)S(1)} %coarse.14), channel_id=1, source_target_pairs={{4,0},{8,4},{12,8},{16,12},{20,16},{24,20},{28,24},{5,1},{9,5},{13... | collective-permute-start | bytes 614408 | tf_op jit(solution)/shard_map/ppermute | solution.py:435
  66.1 0.1 pad_maximum_fusion
  66.3 3.2 %collective-permute-start.10 = (bf16[10,8,1536]{2,1,0:T(8,128)(2,1)S(1)}, bf16[10,8,1536]{2,1,0:T(8,128)(2,1)S(1)}, u32[]{:S(2)}, u32[]{:S(2)}) collective-permute-start(bf16[10,8,1536]{2,1,0:T(8,128)(2,1)S(1)} %coarse.11), channel_id=1, source_target_pairs={{0,4},{4,8},{8,12},{12,16},{16,20},{20,24},{24,28},{1,5},{5,9},{9,... | collective-permute-start | bytes 737288 | tf_op jit(solution)/shard_map/ppermute | solution.py:432
  69.4 0.1 add_convert_fusion
  69.5 0.7 collective-permute-start.17
  70.2 2.2 %collective-permute-start.16 = (bf16[14,8,1536]{2,1,0:T(8,128)(2,1)S(1)}, bf16[14,8,1536]{2,1,0:T(8,128)(2,1)S(1)}, u32[]{:S(2)}, u32[]{:S(2)}) collective-permute-start(bf16[14,8,1536]{2,1,0:T(8,128)(2,1)S(1)} %bitcast.19), channel_id=1, source_target_pairs={{0,1},{1,0},{2,3},{3,2},{4,5},{5,4},{6,7},{7,6},{8,9},{9,8},{10,11... | collective-permute-start | bytes 1032200 | tf_op jit(solution)/shard_map/ppermute | solution.py:429
  72.4 2.9 %collective-permute-start.14 = (bf16[10,8,1024]{2,1,0:T(8,128)(2,1)S(1)}, bf16[10,8,1024]{2,1,0:T(8,128)(2,1)S(1)}, u32[]{:S(2)}, u32[]{:S(2)}) collective-permute-start(bf16[10,8,1024]{2,1,0:T(8,128)(2,1)S(1)} %coarse.15), channel_id=1, source_target_pairs={{0,4},{4,8},{8,12},{12,16},{16,20},{20,24},{24,28},{1,5},{5,9},{9,... | collective-permute-start | bytes 491528 | tf_op jit(solution)/shard_map/ppermute | solution.py:432
  75.3 0.1 fusion.13
  75.5 1.7 %collective-permute-done.10 = bf16[10,8,1536]{2,1,0:T(8,128)(2,1)S(1)} collective-permute-done((bf16[10,8,1536]{2,1,0:T(8,128)(2,1)S(1)}, bf16[10,8,1536]{2,1,0:T(8,128)(2,1)S(1)}, u32[]{:S(2)}, u32[]{:S(2)}) %collective-permute-start.10) | collective-permute-done | bytes 245792 | tf_op jit(solution)/shard_map/ppermute | solution.py:432
  77.2 0.1 add_convert_fusion.1
  77.2 0.8 collective-permute-start.13
  78.0 4.7 %collective-permute-start.18 = (bf16[14,8,1536]{2,1,0:T(8,128)(2,1)S(1)}, bf16[14,8,1536]{2,1,0:T(8,128)(2,1)S(1)}, u32[]{:S(2)}, u32[]{:S(2)}) collective-permute-start(bf16[14,8,1536]{2,1,0:T(8,128)(2,1)S(1)} %collective-permute-done.17.refs_2_), channel_id=1, source_target_pairs={{0,1},{1,0},{2,3},{3,2},{4,5},{5,4},{6,7},{7,6},{8,9},{9,8},{10,11... | collective-permute-start | bytes 1032200 | tf_op jit(solution)/shard_map/ppermute | solution.py:429
  82.7 0.1 pad_maximum_fusion.1
  82.8 1.7 %collective-permute-start.15 = (bf16[14,8,1024]{2,1,0:T(8,128)(2,1)S(1)}, bf16[14,8,1024]{2,1,0:T(8,128)(2,1)S(1)}, u32[]{:S(2)}, u32[]{:S(2)}) collective-permute-start(bf16[14,8,1024]{2,1,0:T(8,128)(2,1)S(1)} %bitcast.22), channel_id=1, source_target_pairs={{0,2},{1,3},{2,0},{3,1},{4,6},{5,7},{6,4},{7,5},{8,10},{9,11},{10,... | collective-permute-start | bytes 688136 | tf_op jit(solution)/shard_map/ppermute | solution.py:426
  84.5 4.1 %collective-permute-start.19 = (bf16[14,8,1536]{2,1,0:T(8,128)(2,1)S(1)}, bf16[14,8,1536]{2,1,0:T(8,128)(2,1)S(1)}, u32[]{:S(2)}, u32[]{:S(2)}) collective-permute-start(bf16[14,8,1536]{2,1,0:T(8,128)(2,1)S(1)} %bitcast.16), channel_id=1, source_target_pairs={{0,1},{1,0},{2,3},{3,2},{4,5},{5,4},{6,7},{7,6},{8,9},{9,8},{10,11... | collective-permute-start | bytes 1032200 | tf_op jit(solution)/shard_map/ppermute | solution.py:429
  88.7 2.4 %assemble.3.refs_0_ = bf16[8,56,4096]{2,1,0:T(8,128)(2,1)} custom-call(bf16[448,448]{1,0:T(8,128)(2,1)S(1)} %fusion.12.order_ref, bf16[14,8,1536]{2,1,0:T(8,128)(2,1)S(1)} %bitcast.20, bf16[14,8,1536]{2,1,0:T(8,128)(2,1)S(1)} %collective-permute-done.16.refs_1_, bf16[14,8,1536]{2,1,0:T(8,128)(2,1)S(1)} %collective-permute-done.17.refs_2_, ...), custom_call_target="tpu_custom_call" | custom-call | flops 290000000 | bytes 10730000 | tf_op jit(solution)/shard_map/assemble/pallas_call | solution.py:381
  91.1 3.6 %collective-permute-start.20 = (bf16[14,8,1536]{2,1,0:T(8,128)(2,1)S(1)}, bf16[14,8,1536]{2,1,0:T(8,128)(2,1)S(1)}, u32[]{:S(2)}, u32[]{:S(2)}) collective-permute-start(bf16[14,8,1536]{2,1,0:T(8,128)(2,1)S(1)} %collective-permute-done.13.refs_3_), channel_id=1, source_target_pairs={{0,1},{1,0},{2,3},{3,2},{4,5},{5,4},{6,7},{7,6},{8,9},{9,8},{10,11... | collective-permute-start | bytes 1032200 | tf_op jit(solution)/shard_map/ppermute | solution.py:429
  94.7 0.5 collective-permute-start.22
  95.3 0.8 collective-permute-done.20.refs_4_
  96.0 2.4 %assemble.4.refs_0_ = bf16[8,56,4096]{2,1,0:T(8,128)(2,1)} custom-call(bf16[448,448]{1,0:T(8,128)(2,1)S(1)} %fusion.12.order_ref, bf16[8,56,4096]{2,1,0:T(8,128)(2,1)} %assemble.3.refs_0_, bf16[14,8,1536]{2,1,0:T(8,128)(2,1)S(1)} %bitcast.17, bf16[14,8,1536]{2,1,0:T(8,128)(2,1)S(1)} %collective-permute-done.19.refs_2_, ...), custom_call_target="tpu_custom_call", output_to_operand_aliasing={{}: (1, {})} | custom-call | flops 290000000 | bytes 10730000 | tf_op jit(solution)/shard_map/assemble/pallas_call | solution.py:381
  98.5 1.7 %assemble.5 = bf16[8,56,4096]{2,1,0:T(8,128)(2,1)} custom-call(bf16[448,448]{1,0:T(8,128)(2,1)S(1)} %fusion.12.order_ref, bf16[8,56,4096]{2,1,0:T(8,128)(2,1)} %assemble.4.refs_0_, bf16[14,8,1024]{2,1,0:T(8,128)(2,1)S(1)} %bitcast.24, bf16[14,8,1024]{2,1,0:T(8,128)(2,1)S(1)} %collective-permute-done.21.refs_2_, ...), custom_call_target="tpu_custom_call", output_to_operand_aliasing={{}: (1, {})} | custom-call | flops 290000000 | bytes 10730000 | tf_op jit(solution)/shard_map/assemble/pallas_call | solution.py:381
  (37 shorter events, 0.2 us)
Async XLA Ops:
  0.0 1.4 %copy-start = (bf16[24,8,4096]{2,1,0:T(8,128)(2,1)S(1)}, bf16[24,8,4096]{2,1,0:T(8,128)(2,1)}, u32[]{:S(2)}) copy-start(bf16[24,8,4096]{2,1,0:T(8,128)(2,1)} %x_ref.4) | copy-start | bytes 4718596
  1.4 5.0 %copy-start.4 = (s32[192,4]{0,1:T(4,128)S(1)}, s32[192,4]{0,1:T(4,128)}, u32[]{:S(2)}) copy-start(s32[192,4]{0,1:T(4,128)} %param.9) | copy-start | bytes 9220
  1.4 8.2 %copy-start.6 = (s32[24,32]{1,0:T(8,128)S(1)}, s32[24,32]{1,0:T(8,128)}, u32[]{:S(2)}) copy-start(s32[24,32]{1,0:T(8,128)} %param.6) | copy-start | bytes 9220
  1.4 8.2 %copy-start.7 = (s32[24]{0:T(128)S(1)}, s32[24]{0:T(128)}, u32[]{:S(2)}) copy-start(s32[24]{0:T(128)} %param.7) | copy-start | bytes 292
  1.4 8.3 %copy-start.1 = (bf16[24,8,4096]{2,1,0:T(8,128)(2,1)S(1)}, bf16[24,8,4096]{2,1,0:T(8,128)(2,1)}, u32[]{:S(2)}) copy-start(bf16[24,8,4096]{2,1,0:T(8,128)(2,1)} %x_ref.4) | copy-start | bytes 4718596
  2.2 4.3 %collective-permute-start = (bf16[16,4,64,128]{3,2,1,0:T(8,128)(2,1)S(1)}, bf16[16,4,64,128]{3,2,1,0:T(8,128)(2,1)}, u32[]{:S(2)}, u32[]{:S(2)}) collective-permute-start(bf16[16,4,64,128]{3,2,1,0:T(8,128)(2,1)S(1)} %relayout.3.refs_0_), channel_id=1, source_target_pairs={{0,1},{1,0},{2,3},{3,2},{4,5},{5,4},{6,7},{7,6},{8,9},{9,8},{10,11... | collective-permute-start | bytes 3145736 | tf_op jit(solution)/shard_map/ppermute | solution.py:429
  3.0 24.8 %collective-permute-start.2 = (bf16[16,4,64,128]{3,2,1,0:T(8,128)(2,1)S(1)}, bf16[16,4,64,128]{3,2,1,0:T(8,128)(2,1)}, u32[]{:S(2)}, u32[]{:S(2)}) collective-permute-start(bf16[16,4,64,128]{3,2,1,0:T(8,128)(2,1)S(1)} %relayout.3.refs_0_), channel_id=1, source_target_pairs={{0,2},{1,3},{2,0},{3,1},{4,6},{5,7},{6,4},{7,5},{8,10},{9,11},{10,... | collective-permute-start | bytes 3145736 | tf_op jit(solution)/shard_map/ppermute | solution.py:426
  4.2 1.1 %copy-start.2 = (bf16[24,4,4096]{2,1,0:T(4,128)(2,1)S(1)}, bf16[24,4,4096]{2,1,0:T(4,128)(2,1)}, u32[]{:S(2)}) copy-start(bf16[24,4,4096]{2,1,0:T(4,128)(2,1)} %x_ref.5) | copy-start | bytes 2359300
  6.6 21.6 %collective-permute-start.1 = (bf16[24,2,64,128]{3,2,1,0:T(8,128)(2,1)S(1)}, bf16[24,2,64,128]{3,2,1,0:T(8,128)(2,1)S(1)}, u32[]{:S(2)}, u32[]{:S(2)}) collective-permute-start(bf16[24,2,64,128]{3,2,1,0:T(8,128)(2,1)S(1)} %relayout_rows.1.refs_0_), channel_id=1, source_target_pairs={{0,4},{2,6},{4,8},{5,1},{6,10},{7,3},{8,12},{9,5},{10,14},{11,7},{... | collective-permute-start | bytes 2359304 | tf_op jit(solution)/shard_map/ppermute | solution.py:423
  10.1 4.9 %collective-permute-start.3 = (bf16[8,4,64,128]{3,2,1,0:T(8,128)(2,1)S(1)}, bf16[8,4,64,128]{3,2,1,0:T(8,128)(2,1)S(1)}, u32[]{:S(2)}, u32[]{:S(2)}) collective-permute-start(bf16[8,4,64,128]{3,2,1,0:T(8,128)(2,1)S(1)} %relayout.4.refs_0_), channel_id=1, source_target_pairs={{0,1},{1,0},{2,3},{3,2},{4,5},{5,4},{6,7},{7,6},{8,9},{9,8},{10,11... | collective-permute-start | bytes 1572872 | tf_op jit(solution)/shard_map/ppermute | solution.py:429
  11.1 4.0 %copy-start.3 = (bf16[24,4,4096]{2,1,0:T(4,128)(2,1)S(1)}, bf16[24,4,4096]{2,1,0:T(4,128)(2,1)}, u32[]{:S(2)}) copy-start(bf16[24,4,4096]{2,1,0:T(4,128)(2,1)} %x_ref.5) | copy-start | bytes 2359300
  28.2 6.1 %collective-permute-start.6 = (bf16[16,4,64,128]{3,2,1,0:T(8,128)(2,1)}, bf16[16,4,64,128]{3,2,1,0:T(8,128)(2,1)S(1)}, u32[]{:S(2)}, u32[]{:S(2)}) collective-permute-start(bf16[16,4,64,128]{3,2,1,0:T(8,128)(2,1)} %collective-permute-done.2.refs_0_), channel_id=1, source_target_pairs={{0,1},{1,0},{2,3},{3,2},{4,5},{5,4},{6,7},{7,6},{8,9},{9,8},{10,11... | collective-permute-start | bytes 3145736 | tf_op jit(solution)/shard_map/ppermute | solution.py:429
  28.7 3.3 %collective-permute-start.5 = (bf16[24,2,64,128]{3,2,1,0:T(8,128)(2,1)S(1)}, bf16[24,2,64,128]{3,2,1,0:T(8,128)(2,1)S(1)}, u32[]{:S(2)}, u32[]{:S(2)}) collective-permute-start(bf16[24,2,64,128]{3,2,1,0:T(8,128)(2,1)S(1)} %collective-permute-done.1.refs_0_), channel_id=1, source_target_pairs={{0,1},{1,0},{2,3},{3,2},{4,5},{5,4},{6,7},{7,6},{8,9},{9,8},{10,11... | collective-permute-start | bytes 2359304 | tf_op jit(solution)/shard_map/ppermute | solution.py:429
  28.7 13.0 %collective-permute-start.4 = (bf16[8,4,64,128]{3,2,1,0:T(8,128)(2,1)S(1)}, bf16[8,4,64,128]{3,2,1,0:T(8,128)(2,1)S(1)}, u32[]{:S(2)}, u32[]{:S(2)}) collective-permute-start(bf16[8,4,64,128]{3,2,1,0:T(8,128)(2,1)S(1)} %relayout.4.refs_0_), channel_id=1, source_target_pairs={{0,2},{1,3},{2,0},{3,1},{4,6},{5,7},{6,4},{7,5},{8,10},{9,11},{10,... | collective-permute-start | bytes 1572872 | tf_op jit(solution)/shard_map/ppermute | solution.py:426
  41.7 6.1 %collective-permute-start.8 = (bf16[8,4,64,128]{3,2,1,0:T(8,128)(2,1)S(1)}, bf16[8,4,64,128]{3,2,1,0:T(8,128)(2,1)S(1)}, u32[]{:S(2)}, u32[]{:S(2)}) collective-permute-start(bf16[8,4,64,128]{3,2,1,0:T(8,128)(2,1)S(1)} %collective-permute-done.4.refs_0_), channel_id=1, source_target_pairs={{0,1},{1,0},{2,3},{3,2},{4,5},{5,4},{6,7},{7,6},{8,9},{9,8},{10,11... | collective-permute-start | bytes 1572872 | tf_op jit(solution)/shard_map/ppermute | solution.py:429
  44.0 11.8 %collective-permute-start.7 = (bf16[10,4,4096]{2,1,0:T(4,128)(2,1)S(1)}, bf16[10,4,4096]{2,1,0:T(4,128)(2,1)S(1)}, u32[]{:S(2)}, u32[]{:S(2)}) collective-permute-start(bf16[10,4,4096]{2,1,0:T(4,128)(2,1)S(1)} %coarse.9), channel_id=1, source_target_pairs={{4,0},{8,4},{12,8},{16,12},{20,16},{24,20},{28,24},{5,1},{9,5},{13... | collective-permute-start | bytes 983048 | tf_op jit(solution)/shard_map/ppermute | solution.py:435
  52.1 11.9 %collective-permute-start.11 = (bf16[10,4,1536]{2,1,0:T(4,128)(2,1)S(1)}, bf16[10,4,1536]{2,1,0:T(4,128)(2,1)S(1)}, u32[]{:S(2)}, u32[]{:S(2)}) collective-permute-start(bf16[10,4,1536]{2,1,0:T(4,128)(2,1)S(1)} %coarse.13), channel_id=1, source_target_pairs={{4,0},{8,4},{12,8},{16,12},{20,16},{24,20},{28,24},{5,1},{9,5},{13... | collective-permute-start | bytes 368648 | tf_op jit(solution)/shard_map/ppermute | solution.py:435
  55.7 7.5 %copy-start.5 = (bf16[10,4,4096]{2,1,0:T(4,128)(2,1)}, bf16[10,4,4096]{2,1,0:T(4,128)(2,1)S(1)}, u32[]{:S(2)}) copy-start(bf16[10,4,4096]{2,1,0:T(4,128)(2,1)S(1)} %collective-permute-done.7) | copy-start | bytes 983044
  55.7 10.5 %collective-permute-start.9 = (bf16[10,8,1536]{2,1,0:T(8,128)(2,1)S(1)}, bf16[10,8,1536]{2,1,0:T(8,128)(2,1)S(1)}, u32[]{:S(2)}, u32[]{:S(2)}) collective-permute-start(bf16[10,8,1536]{2,1,0:T(8,128)(2,1)S(1)} %coarse.10), channel_id=1, source_target_pairs={{0,4},{4,8},{8,12},{12,16},{16,20},{20,24},{24,28},{1,5},{5,9},{9,... | collective-permute-start | bytes 737288 | tf_op jit(solution)/shard_map/ppermute | solution.py:432
  63.4 2.7 %slice-start = ((bf16[10,4,4096]{2,1,0:T(4,128)(2,1)}), bf16[10,4,1536]{2,1,0:T(4,128)(2,1)S(1)}, s32[]{:S(2)}) async-start(bf16[10,4,4096]{2,1,0:T(4,128)(2,1)} %copy-done.5), calls=%async_computation | async-start | bytes 245760 | tf_op jit(solution)/shard_map/slice | solution.py:485
  64.0 8.4 %collective-permute-start.12 = (bf16[10,4,2560]{2,1,0:T(4,128)(2,1)S(1)}, bf16[10,4,2560]{2,1,0:T(4,128)(2,1)S(1)}, u32[]{:S(2)}, u32[]{:S(2)}) collective-permute-start(bf16[10,4,2560]{2,1,0:T(4,128)(2,1)S(1)} %coarse.14), channel_id=1, source_target_pairs={{4,0},{8,4},{12,8},{16,12},{20,16},{24,20},{28,24},{5,1},{9,5},{13... | collective-permute-start | bytes 614408 | tf_op jit(solution)/shard_map/ppermute | solution.py:435
  66.3 10.9 %collective-permute-start.10 = (bf16[10,8,1536]{2,1,0:T(8,128)(2,1)S(1)}, bf16[10,8,1536]{2,1,0:T(8,128)(2,1)S(1)}, u32[]{:S(2)}, u32[]{:S(2)}) collective-permute-start(bf16[10,8,1536]{2,1,0:T(8,128)(2,1)S(1)} %coarse.11), channel_id=1, source_target_pairs={{0,4},{4,8},{8,12},{12,16},{16,20},{20,24},{24,28},{1,5},{5,9},{9,... | collective-permute-start | bytes 737288 | tf_op jit(solution)/shard_map/ppermute | solution.py:432
  69.5 8.5 %collective-permute-start.17 = (bf16[14,8,1536]{2,1,0:T(8,128)(2,1)S(1)}, bf16[14,8,1536]{2,1,0:T(8,128)(2,1)S(1)}, u32[]{:S(2)}, u32[]{:S(2)}) collective-permute-start(bf16[14,8,1536]{2,1,0:T(8,128)(2,1)S(1)} %bitcast.18), channel_id=1, source_target_pairs={{0,2},{1,3},{2,0},{3,1},{4,6},{5,7},{6,4},{7,5},{8,10},{9,11},{10,... | collective-permute-start | bytes 1032200 | tf_op jit(solution)/shard_map/ppermute | solution.py:426
  70.2 18.4 %collective-permute-start.16 = (bf16[14,8,1536]{2,1,0:T(8,128)(2,1)S(1)}, bf16[14,8,1536]{2,1,0:T(8,128)(2,1)S(1)}, u32[]{:S(2)}, u32[]{:S(2)}) collective-permute-start(bf16[14,8,1536]{2,1,0:T(8,128)(2,1)S(1)} %bitcast.19), channel_id=1, source_target_pairs={{0,1},{1,0},{2,3},{3,2},{4,5},{5,4},{6,7},{7,6},{8,9},{9,8},{10,11... | collective-permute-start | bytes 1032200 | tf_op jit(solution)/shard_map/ppermute | solution.py:429
  72.4 10.3 %collective-permute-start.14 = (bf16[10,8,1024]{2,1,0:T(8,128)(2,1)S(1)}, bf16[10,8,1024]{2,1,0:T(8,128)(2,1)S(1)}, u32[]{:S(2)}, u32[]{:S(2)}) collective-permute-start(bf16[10,8,1024]{2,1,0:T(8,128)(2,1)S(1)} %coarse.15), channel_id=1, source_target_pairs={{0,4},{4,8},{8,12},{12,16},{16,20},{20,24},{24,28},{1,5},{5,9},{9,... | collective-permute-start | bytes 491528 | tf_op jit(solution)/shard_map/ppermute | solution.py:432
  77.2 11.4 %collective-permute-start.13 = (bf16[14,8,1536]{2,1,0:T(8,128)(2,1)S(1)}, bf16[14,8,1536]{2,1,0:T(8,128)(2,1)S(1)}, u32[]{:S(2)}, u32[]{:S(2)}) collective-permute-start(bf16[14,8,1536]{2,1,0:T(8,128)(2,1)S(1)} %bitcast.15), channel_id=1, source_target_pairs={{0,2},{1,3},{2,0},{3,1},{4,6},{5,7},{6,4},{7,5},{8,10},{9,11},{10,... | collective-permute-start | bytes 1032200 | tf_op jit(solution)/shard_map/ppermute | solution.py:426
  78.0 10.7 %collective-permute-start.18 = (bf16[14,8,1536]{2,1,0:T(8,128)(2,1)S(1)}, bf16[14,8,1536]{2,1,0:T(8,128)(2,1)S(1)}, u32[]{:S(2)}, u32[]{:S(2)}) collective-permute-start(bf16[14,8,1536]{2,1,0:T(8,128)(2,1)S(1)} %collective-permute-done.17.refs_2_), channel_id=1, source_target_pairs={{0,1},{1,0},{2,3},{3,2},{4,5},{5,4},{6,7},{7,6},{8,9},{9,8},{10,11... | collective-permute-start | bytes 1032200 | tf_op jit(solution)/shard_map/ppermute | solution.py:429
  82.8 8.3 %collective-permute-start.15 = (bf16[14,8,1024]{2,1,0:T(8,128)(2,1)S(1)}, bf16[14,8,1024]{2,1,0:T(8,128)(2,1)S(1)}, u32[]{:S(2)}, u32[]{:S(2)}) collective-permute-start(bf16[14,8,1024]{2,1,0:T(8,128)(2,1)S(1)} %bitcast.22), channel_id=1, source_target_pairs={{0,2},{1,3},{2,0},{3,1},{4,6},{5,7},{6,4},{7,5},{8,10},{9,11},{10,... | collective-permute-start | bytes 688136 | tf_op jit(solution)/shard_map/ppermute | solution.py:426
  84.5 10.7 %collective-permute-start.19 = (bf16[14,8,1536]{2,1,0:T(8,128)(2,1)S(1)}, bf16[14,8,1536]{2,1,0:T(8,128)(2,1)S(1)}, u32[]{:S(2)}, u32[]{:S(2)}) collective-permute-start(bf16[14,8,1536]{2,1,0:T(8,128)(2,1)S(1)} %bitcast.16), channel_id=1, source_target_pairs={{0,1},{1,0},{2,3},{3,2},{4,5},{5,4},{6,7},{7,6},{8,9},{9,8},{10,11... | collective-permute-start | bytes 1032200 | tf_op jit(solution)/shard_map/ppermute | solution.py:429
  91.1 4.9 %collective-permute-start.20 = (bf16[14,8,1536]{2,1,0:T(8,128)(2,1)S(1)}, bf16[14,8,1536]{2,1,0:T(8,128)(2,1)S(1)}, u32[]{:S(2)}, u32[]{:S(2)}) collective-permute-start(bf16[14,8,1536]{2,1,0:T(8,128)(2,1)S(1)} %collective-permute-done.13.refs_3_), channel_id=1, source_target_pairs={{0,1},{1,0},{2,3},{3,2},{4,5},{5,4},{6,7},{7,6},{8,9},{9,8},{10,11... | collective-permute-start | bytes 1032200 | tf_op jit(solution)/shard_map/ppermute | solution.py:429
  94.7 3.7 %collective-permute-start.21 = (bf16[14,8,1024]{2,1,0:T(8,128)(2,1)S(1)}, bf16[14,8,1024]{2,1,0:T(8,128)(2,1)S(1)}, u32[]{:S(2)}, u32[]{:S(2)}) collective-permute-start(bf16[14,8,1024]{2,1,0:T(8,128)(2,1)S(1)} %bitcast.23), channel_id=1, source_target_pairs={{0,1},{1,0},{2,3},{3,2},{4,5},{5,4},{6,7},{7,6},{8,9},{9,8},{10,11... | collective-permute-start | bytes 688136 | tf_op jit(solution)/shard_map/ppermute | solution.py:429
  94.7 3.7 %collective-permute-start.22 = (bf16[14,8,1024]{2,1,0:T(8,128)(2,1)S(1)}, bf16[14,8,1024]{2,1,0:T(8,128)(2,1)S(1)}, u32[]{:S(2)}, u32[]{:S(2)}) collective-permute-start(bf16[14,8,1024]{2,1,0:T(8,128)(2,1)S(1)} %collective-permute-done.15.refs_3_), channel_id=1, source_target_pairs={{0,1},{1,0},{2,3},{3,2},{4,5},{5,4},{6,7},{7,6},{8,9},{9,8},{10,11... | collective-permute-start | bytes 688136 | tf_op jit(solution)/shard_map/ppermute | solution.py:429

commit v12 on v11

--- a/solution.py
+++ b/solution.py
@@ -35,62 +35,55 @@
     return lax.dot_general(a, b, (((1,), (0,)), ((), ())), preferred_element_type=F32)
 
 
-def relayout_kernel(x_ref, o_ref, scr):
-    rows, nb, _ = x_ref.shape
+def relayout_kernel(first, natural, x_ref, o_ref, buf, sems, scr, mix):
+    parts, step, nb, _ = buf.shape
     low = low_lanes(32)
-    for r in range(rows):
-        for q in range(32):
-            scr[r, pl.ds(q * 8, nb), :] = x_ref[r, :, q * LANES : (q + 1) * LANES].astype(F32)
-        for k in range(0, nb, 2):
-            x0 = scr[r, pl.ds(k, 32, stride=8), :]
-            x1 = scr[r, pl.ds(k + 1, 32, stride=8), :]
-            o_ref[r, k // 2, 0:32] = jnp.where(low, x0, pltpu.roll(x1, BS, 1)).astype(BF)
-            o_ref[r, k // 2, 32:64] = jnp.where(low, pltpu.roll(x0, BS, 1), x1).astype(BF)
-
-
-def relayout(x, first, rows):
+
+    def fetch(g):
+        return pltpu.make_async_copy(x_ref.at[pl.ds(first + g * step, step)], buf.at[g], sems.at[g])
+
+    for g in range(parts):
+        fetch(g).start()
+
+    def part(g, carry):
+        fetch(g).wait()
+        for r in range(step):
+            for q in range(32):
+                scr[r, pl.ds(q * 8, nb), :] = buf[g, r, :, q * LANES : (q + 1) * LANES].astype(F32)
+            for k in range(0, nb, 2):
+                x0 = scr[r, pl.ds(k, 32, stride=8), :]
+                x1 = scr[r, pl.ds(k + 1, 32, stride=8), :]
+                even = jnp.where(low, x0, pltpu.roll(x1, BS, 1))
+                odd = jnp.where(low, pltpu.roll(x0, BS, 1), x1)
+                if natural:
+                    mix[r, k // 2, pl.ds(0, 32, stride=2), :] = even
+                    mix[r, k // 2, pl.ds(1, 32, stride=2), :] = odd
+                    o_ref[g * step + r, k // 2] = mix[r, k // 2].astype(BF)
+                else:
+                    o_ref[g * step + r, k // 2, 0:32] = even.astype(BF)
+                    o_ref[g * step + r, k // 2, 32:64] = odd.astype(BF)
+        return carry
+
+    lax.fori_loop(0, parts, part, 0)
+
+
+def relayout(x, first, rows, natural=False):
     nb = x.shape[1]
     step = 4
     return pl.pallas_call(
-        relayout_kernel,
-        grid=(rows // step,),
+        functools.partial(relayout_kernel, first, natural),
         out_shape=jax.ShapeDtypeStruct((rows, nb // 2, BS, LANES), BF),
-        in_specs=[pl.BlockSpec((step, nb, BS * BS), lambda i: (i + first // step, 0, 0))],
-        out_specs=pl.BlockSpec((step, nb // 2, BS, LANES), lambda i: (i, 0, 0, 0)),
-        scratch_shapes=[pltpu.VMEM((step, 256, LANES), F32)],
-        compiler_params=params(4),
-        cost_estimate=cost(0.6),
+        in_specs=[pl.BlockSpec(memory_space=pltpu.HBM)],
+        out_specs=VM,
+        scratch_shapes=[
+            pltpu.VMEM((rows // step, step, nb, BS * BS), BF),
+            pltpu.SemaphoreType.DMA((rows // step,)),
+            pltpu.VMEM((step, 256, LANES), F32),
+            pltpu.VMEM((step, nb // 2, BS, LANES), F32),
+        ],
+        compiler_params=params(8),
+        cost_estimate=cost(1.0),
         name="relayout",
-    )(x)
-
-
-def relayout_rows_kernel(x_ref, o_ref, scr, mix):
-    rows, nb, _ = x_ref.shape
-    low = low_lanes(32)
-    for r in range(rows):
-        for q in range(32):
-            scr[r, pl.ds(q * 8, nb), :] = x_ref[r, :, q * LANES : (q + 1) * LANES].astype(F32)
-        for k in range(0, nb, 2):
-            x0 = scr[r, pl.ds(k, 32, stride=8), :]
-            x1 = scr[r, pl.ds(k + 1, 32, stride=8), :]
-            mix[r, k // 2, pl.ds(0, 32, stride=2), :] = jnp.where(low, x0, pltpu.roll(x1, BS, 1))
-            mix[r, k // 2, pl.ds(1, 32, stride=2), :] = jnp.where(low, pltpu.roll(x0, BS, 1), x1)
-            o_ref[r, k // 2] = mix[r, k // 2].astype(BF)
-
-
-def relayout_rows(x):
-    rows, nb, _ = x.shape
-    step = 4
-    return pl.pallas_call(
-        relayout_rows_kernel,
-        grid=(rows // step,),
-        out_shape=jax.ShapeDtypeStruct((rows, nb // 2, BS, LANES), BF),
-        in_specs=[pl.BlockSpec((step, nb, BS * BS), lambda i: (i, 0, 0))],
-        out_specs=pl.BlockSpec((step, nb // 2, BS, LANES), lambda i: (i, 0, 0, 0)),
-        scratch_shapes=[pltpu.VMEM((step, 256, LANES), F32), pltpu.VMEM((step, nb // 2, BS, LANES), F32)],
-        compiler_params=params(4),
-        cost_estimate=cost(1.0),
-        name="relayout_rows",
     )(x)
 
 
@@ -139,7 +132,7 @@
     return (side, side + 3) if tiles == GROUPS else (0, tiles)
 
 
-def right_kernel(rb, tiles, table_ref, *refs):
+def right_kernel(kind, rb, tiles, table_ref, *refs):
     o_ref = refs[-1]
     core = lax.rem(lax.axis_index("col"), 2)
     low = lax.broadcasted_iota(jnp.int32, (1, LANES), 1) < BS
@@ -164,28 +157,45 @@
 
         lax.fori_loop(0, rb // 4, four, 0)
 
-    if len(refs) == 2:
+    quads = rb // 4
+    if kind == 0:
         fill(refs[0], 1, 0)
-    else:
-        first = refs[0]
-        second = refs[1]
+    elif kind == 1:
 
         @pl.when(core == 0)
         def _():
-            fill(first, 0, 0)
-            fill(second, 2, rb // 4)
+            fill(refs[0], 0, 0)
 
         @pl.when(core == 1)
         def _():
-            fill(second, 0, 0)
-            fill(first, 2, rb // 4)
-
-
-def right_factor(table, srcs, tiles, us):
+            fill(refs[0], 2, 0)
+    else:
+
+        def keep(side, out_first):
+            def one(jq, carry):
+                for p in range(*touched(side, tiles)):
+                    o_ref[out_first + jq, p] = refs[0][jq, p]
+                return carry
+
+            lax.fori_loop(0, quads, one, 0)
+
+        @pl.when(core == 0)
+        def _():
+            keep(0, 0)
+            fill(refs[1], 2, quads)
+
+        @pl.when(core == 1)
+        def _():
+            fill(refs[1], 0, 0)
+            keep(2, quads)
+
+
+def right_factor(kind, table, srcs, tiles, us):
     rb = table.shape[1] // 3
-    return pl.pallas_call(
-        functools.partial(right_kernel, rb, tiles),
-        out_shape=jax.ShapeDtypeStruct((len(srcs) * rb // 4, tiles, 4 * BS, LANES), BF),
+    quads = rb // 4 * (2 if kind == 2 else 1)
+    return pl.pallas_call(
+        functools.partial(right_kernel, kind, rb, tiles),
+        out_shape=jax.ShapeDtypeStruct((quads, tiles, 4 * BS, LANES), BF),
         in_specs=[SM] + [VM] * len(srcs),
         out_specs=VM,
         compiler_params=params(8),
@@ -367,7 +377,7 @@
 
 def assemble(order, srcs, a0, total, before):
     n, _, lanes = srcs[0].shape
-    step = 512
+    step = lanes
     per = lanes // step
     wide = n * len(srcs)
     specs = [pl.BlockSpec(order.shape, lambda i: (0, 0))]
@@ -444,18 +454,19 @@
         far_a.append([over_y(x, s) for s in range(1, ny)])
         side_a.append(over_core(x))
         if h == 0:
-            p_own = relayout_rows(p_blocks)
+            p_own = relayout(p_blocks, 0, rb, True)
             a_blocks, p_own, side_a[0] = lax.optimization_barrier((a_blocks, p_own, side_a[0]))
     beside = outward(p_own)
     p_blocks, p_own, side_a[1] = lax.optimization_barrier((p_blocks, p_own, side_a[1]))
     table = column_table(pct, rb, share)
     left = left_factor(pct, relayout(p_blocks, 0, rb))
-    own = right_factor(table, [p_own], tiles, 2.0)
+    own = right_factor(0, table, [p_own], tiles, 1.4)
     order = assembly_order(shifts, ncol, share)
     place = slot_places(a_cols, counts)
     bands = [near_band(place, [own_a[h], side_a[h]], shifts[:2], parts[h][0]) for h in range(2)]
     beside, far_a[0], left, own, order, bands = lax.optimization_barrier((beside, far_a[0], left, own, order, bands))
-    near = right_factor(table, [beside, over_core(beside)], tiles, 3.0)
+    near = right_factor(1, table, [beside], tiles, 1.2)
+    near = right_factor(2, table, [near, over_core(beside)], tiles, 1.4)
     aps = []
     for h in range(2):
         srcs = [z for g in far_a[h] for z in (g, over_core(g))]

time: 102 us -> 103 us (level)
  Pallas kernels: 39.4 us -> 41.1 us
    pallas_call x6 -> x7, Pallas kernels: 6.84 us -> 9.63 us  [the longest x4 5.26 us: relayout(): pl.pallas_call(functools.partial(relayout_kernel, first, natural), out_sh...]
    ppermute x5, starting transfers between devices: 5.73 us -> 4.19 us  [over_y(): lax.ppermute(x, 'col', [(y * 2 + c, (y + s) % ny * 2 + c) for y in range(...]
    ppermute x5, waiting for transfers between devices: 5.77 us -> 4.55 us  [over_y(): lax.ppermute(x, 'col', [(y * 2 + c, (y + s) % ny * 2 + c) for y in range(...]
    pallas_call x3, Pallas kernels: 6.56 us -> 5.48 us  [assemble(): pl.pallas_call(assemble_kernel, grid=(per,), out_shape=jax.ShapeDtypeStru...]
  transfers between devices with their start and end apart: 23 -> 23, of which waited for: 7 -> 8; matrix products, arithmetic and copies ran while one was open for 1% -> 1% of each run, Pallas kernels for 37% -> 38%
where the time goes in v12:
time: 103 us; the launch traced here: 101 us
  starting transfers between devices  44.8 us (43%)
  Pallas kernels  41.1 us (40%)
  waiting for transfers between devices  10.8 us (10%)
  local copies, waits for them, and re-layouts  2.64 us (3%)
    ppermute x11, starting transfers between devices, over_core(): return lax.ppermute(x, 'col', [(c, c ^ 1) for c in range(ncol)])  19.5 us
    pallas_call x2, Pallas kernels, product(): pl.pallas_call(functools.partial(product_kernel, first, rb, shifts), out_...  10.9 us
    ppermute x3, starting transfers between devices, upward(): return lax.ppermute(x, 'row', [(i, i + 1) for i in range(nrow - 1)])  9.82 us
    ppermute x3, starting transfers between devices, downward(): return lax.ppermute(x, 'row', [(i + 1, i) for i in range(nrow - 1)])  8.25 us
    pallas_call x9, Pallas kernels, coarse_rows(): pl.pallas_call(functools.partial(coarse_kernel, sets, a0, a1), out_shape=...  6.26 us
    pallas_call x2, Pallas kernels, near_band(): pl.pallas_call(functools.partial(band_kernel, first, shifts), out_shape=j...  5.98 us
    pallas_call x3, Pallas kernels, assemble(): pl.pallas_call(assemble_kernel, grid=(per,), out_shape=jax.ShapeDtypeStru...  5.48 us
    pallas_call x4, Pallas kernels, relayout(): pl.pallas_call(functools.partial(relayout_kernel, first, natural), out_sh...  5.26 us
  transfers between devices with their start and end apart: 23, of which 8 were waited for; matrix products, arithmetic and copies ran while one was open for 1% of the time, Pallas kernels for 38%

profile of v12, /device:TPU:9, one launch (start us, length us, event | category | flops | bytes accessed | tf_op | source)
XLA Modules:
  0.0 100.7 jit_solution(7382340382457947781)
XLA Ops:
  0.0 1.4 %copy-done = bf16[24,8,4096]{2,1,0:T(8,128)(2,1)S(1)} copy-done((bf16[24,8,4096]{2,1,0:T(8,128)(2,1)S(1)}, bf16[24,8,4096]{2,1,0:T(8,128)(2,1)}, u32[]{:S(2)}) %copy-start) | copy-done | bytes 1572888
  1.4 0.9 relayout.5.refs_0_
  2.3 0.7 collective-permute-start
  3.0 1.3 %collective-permute-start.2 = (bf16[16,4,64,128]{3,2,1,0:T(8,128)(2,1)S(1)}, bf16[16,4,64,128]{3,2,1,0:T(8,128)(2,1)}, u32[]{:S(2)}, u32[]{:S(2)}) collective-permute-start(bf16[16,4,64,128]{3,2,1,0:T(8,128)(2,1)S(1)} %relayout.5.refs_0_), channel_id=1, source_target_pairs={{0,2},{1,3},{2,0},{3,1},{4,6},{5,7},{6,4},{7,5},{8,10},{9,11},{10,... | collective-permute-start | bytes 3145736 | tf_op jit(solution)/shard_map/ppermute | solution.py:436
  4.3 1.1 %copy-done.2 = bf16[24,4,4096]{2,1,0:T(4,128)(2,1)S(1)} copy-done((bf16[24,4,4096]{2,1,0:T(4,128)(2,1)S(1)}, bf16[24,4,4096]{2,1,0:T(4,128)(2,1)}, u32[]{:S(2)}) %copy-start.2) | copy-done | bytes 786456
  5.4 2.1 %relayout.4.refs_0_ = bf16[24,2,64,128]{3,2,1,0:T(8,128)(2,1)S(1)} custom-call(bf16[24,4,4096]{2,1,0:T(4,128)(2,1)S(1)} %copy-done.2), custom_call_target="tpu_custom_call" | custom-call | flops 100000000 | bytes 3700000 | tf_op jit(solution)/shard_map/relayout/pallas_call | solution.py:73
  7.5 0.1 add_select_fusion.4.table_ref
  7.6 0.1 subtract_select_fusion.place_ref
  7.7 3.0 %collective-permute-start.1 = (bf16[24,2,64,128]{3,2,1,0:T(8,128)(2,1)S(1)}, bf16[24,2,64,128]{3,2,1,0:T(8,128)(2,1)S(1)}, u32[]{:S(2)}, u32[]{:S(2)}) collective-permute-start(bf16[24,2,64,128]{3,2,1,0:T(8,128)(2,1)S(1)} %relayout.4.refs_0_), channel_id=1, source_target_pairs={{0,4},{2,6},{4,8},{5,1},{6,10},{7,3},{8,12},{9,5},{10,14},{11,7},{... | collective-permute-start | bytes 2359304 | tf_op jit(solution)/shard_map/ppermute | solution.py:433
  10.8 0.4 relayout.6.refs_0_
  11.2 0.8 collective-permute-start.3
  12.0 0.2 fusion.12.order_ref
  12.2 3.9 %near_band.2.start_ref = bf16[4,27,256,128]{3,2,1,0:T(8,128)(2,1)S(1)} custom-call(s32[24,32]{1,0:T(8,128)S(1)} %subtract_select_fusion.place_ref, bf16[16,4,64,128]{3,2,1,0:T(8,128)(2,1)S(1)} %relayout.5.refs_0_, bf16[16,4,64,128]{3,2,1,0:T(8,128)(2,1)} %collective-permute-done.refs_1_), custom_call_target="tpu_custom_call" | custom-call | flops 256000000 | bytes 9472000 | tf_op jit(solution)/shard_map/near_band/pallas_call | solution.py:265
  16.2 1.9 %relayout.7.pl_ref = bf16[24,2,64,128]{3,2,1,0:T(8,128)(2,1)S(1)} custom-call(bf16[24,4,4096]{2,1,0:T(4,128)(2,1)S(1)} %copy-done.3), custom_call_target="tpu_custom_call" | custom-call | flops 100000000 | bytes 3700000 | tf_op jit(solution)/shard_map/relayout/pallas_call | solution.py:73
  18.1 2.1 %near_band.3.start_ref = bf16[2,27,256,128]{3,2,1,0:T(8,128)(2,1)S(1)} custom-call(s32[24,32]{1,0:T(8,128)S(1)} %subtract_select_fusion.place_ref, bf16[8,4,64,128]{3,2,1,0:T(8,128)(2,1)S(1)} %relayout.6.refs_0_, bf16[8,4,64,128]{3,2,1,0:T(8,128)(2,1)S(1)} %collective-permute-done.3.refs_1_), custom_call_target="tpu_custom_call" | custom-call | flops 128000000 | bytes 4736000 | tf_op jit(solution)/shard_map/near_band/pallas_call | solution.py:265
  20.1 1.4 %right_factor.3.own_ref = bf16[6,5,256,128]{3,2,1,0:T(8,128)(2,1)S(1)} custom-call(s32[4,72]{1,0:T(4,128)S(1)} %add_select_fusion.4.table_ref, bf16[24,2,64,128]{3,2,1,0:T(8,128)(2,1)S(1)} %relayout.4.refs_0_), custom_call_target="tpu_custom_call" | custom-call | flops 140000000 | bytes 5180000 | tf_op jit(solution)/shard_map/right_factor/pallas_call | solution.py:196
  21.6 2.9 %left_factor.1.left_ref = bf16[12,24,64,128]{3,2,1,0:T(8,128)(2,1)S(1)} custom-call(s32[4,192]{1,0:T(4,128)S(1)} %bitcast.26, bf16[24,2,64,128]{3,2,1,0:T(8,128)(2,1)S(1)} %relayout.7.pl_ref), custom_call_target="tpu_custom_call" | custom-call | flops 290000000 | bytes 10730000 | tf_op jit(solution)/shard_map/left_factor/pallas_call | solution.py:111
  24.5 3.4 %collective-permute-done.2.refs_0_ = bf16[16,4,64,128]{3,2,1,0:T(8,128)(2,1)} collective-permute-done((bf16[16,4,64,128]{3,2,1,0:T(8,128)(2,1)S(1)}, bf16[16,4,64,128]{3,2,1,0:T(8,128)(2,1)}, u32[]{:S(2)}, u32[]{:S(2)}) %collective-permute-start.2) | collective-permute-done | bytes 1048608 | tf_op jit(solution)/shard_map/ppermute | solution.py:436
  27.9 1.0 collective-permute-done.1.refs_0_
  28.9 0.5 collective-permute-start.6
  29.4 0.6 collective-permute-start.4
  30.0 1.4 %right_factor.4.refs_0_ = bf16[6,5,256,128]{3,2,1,0:T(8,128)(2,1)S(1)} custom-call(s32[4,72]{1,0:T(4,128)S(1)} %add_select_fusion.4.table_ref, bf16[24,2,64,128]{3,2,1,0:T(8,128)(2,1)S(1)} %collective-permute-done.1.refs_0_), custom_call_target="tpu_custom_call" | custom-call | flops 120000000 | bytes 4440000 | tf_op jit(solution)/shard_map/right_factor/pallas_call | solution.py:196
  31.4 1.2 %collective-permute-done.5.refs_1_ = bf16[24,2,64,128]{3,2,1,0:T(8,128)(2,1)S(1)} collective-permute-done((bf16[24,2,64,128]{3,2,1,0:T(8,128)(2,1)S(1)}, bf16[24,2,64,128]{3,2,1,0:T(8,128)(2,1)S(1)}, u32[]{:S(2)}, u32[]{:S(2)}) %collective-permute-start.5) | collective-permute-done | bytes 786464 | tf_op jit(solution)/shard_map/ppermute | solution.py:439
  32.7 1.5 %right_factor.5.near_ref = bf16[12,5,256,128]{3,2,1,0:T(8,128)(2,1)S(1)} custom-call(s32[4,72]{1,0:T(4,128)S(1)} %add_select_fusion.4.table_ref, bf16[6,5,256,128]{3,2,1,0:T(8,128)(2,1)S(1)} %right_factor.4.refs_0_, bf16[24,2,64,128]{3,2,1,0:T(8,128)(2,1)S(1)} %collective-permute-done.5.refs_1_), custom_call_target="tpu_custom_call" | custom-call | flops 140000000 | bytes 5180000 | tf_op jit(solution)/shard_map/right_factor/pallas_call | solution.py:196
  34.2 7.1 %product.2.refs_0_ = bf16[16,64,640]{2,1,0:T(8,128)(2,1)S(1)} custom-call(s32[24,32]{1,0:T(8,128)S(1)} %subtract_select_fusion.place_ref, bf16[6,5,256,128]{3,2,1,0:T(8,128)(2,1)S(1)} %right_factor.3.own_ref, bf16[12,5,256,128]{3,2,1,0:T(8,128)(2,1)S(1)} %right_factor.5.near_ref, bf16[4,27,256,128]{3,2,1,0:T(8,128)(2,1)S(1)} %near_band.2.start_ref, ...), custom_call_target="tpu_custom_call" | custom-call | flops 480000000 | bytes 17760000 | tf_op jit(solution)/shard_map/product/pallas_call | solution.py:309
  41.3 1.1 %collective-permute-done.4.refs_0_ = bf16[8,4,64,128]{3,2,1,0:T(8,128)(2,1)S(1)} collective-permute-done((bf16[8,4,64,128]{3,2,1,0:T(8,128)(2,1)S(1)}, bf16[8,4,64,128]{3,2,1,0:T(8,128)(2,1)S(1)}, u32[]{:S(2)}, u32[]{:S(2)}) %collective-permute-start.4) | collective-permute-done | bytes 524320 | tf_op jit(solution)/shard_map/ppermute | solution.py:436
  42.4 1.4 %collective-permute-start.8 = (bf16[8,4,64,128]{3,2,1,0:T(8,128)(2,1)S(1)}, bf16[8,4,64,128]{3,2,1,0:T(8,128)(2,1)S(1)}, u32[]{:S(2)}, u32[]{:S(2)}) collective-permute-start(bf16[8,4,64,128]{3,2,1,0:T(8,128)(2,1)S(1)} %collective-permute-done.4.refs_0_), channel_id=1, source_target_pairs={{0,1},{1,0},{2,3},{3,2},{4,5},{5,4},{6,7},{7,6},{8,9},{9,8},{10,11... | collective-permute-start | bytes 1572872 | tf_op jit(solution)/shard_map/ppermute | solution.py:439
  43.7 0.9 coarse.9
  44.7 4.2 %collective-permute-start.7 = (bf16[10,4,4096]{2,1,0:T(4,128)(2,1)S(1)}, bf16[10,4,4096]{2,1,0:T(4,128)(2,1)S(1)}, u32[]{:S(2)}, u32[]{:S(2)}) collective-permute-start(bf16[10,4,4096]{2,1,0:T(4,128)(2,1)S(1)} %coarse.9), channel_id=1, source_target_pairs={{4,0},{8,4},{12,8},{16,12},{20,16},{24,20},{28,24},{5,1},{9,5},{13... | collective-permute-start | bytes 983048 | tf_op jit(solution)/shard_map/ppermute | solution.py:445
  48.9 3.7 %product.3.refs_1_ = bf16[8,64,640]{2,1,0:T(8,128)(2,1)S(1)} custom-call(s32[24,32]{1,0:T(8,128)S(1)} %subtract_select_fusion.place_ref, bf16[6,5,256,128]{3,2,1,0:T(8,128)(2,1)S(1)} %right_factor.3.own_ref, bf16[12,5,256,128]{3,2,1,0:T(8,128)(2,1)S(1)} %right_factor.5.near_ref, bf16[2,27,256,128]{3,2,1,0:T(8,128)(2,1)S(1)} %near_band.3.start_ref, ...), custom_call_target="tpu_custom_call" | custom-call | flops 240000000 | bytes 8880000 | tf_op jit(solution)/shard_map/product/pallas_call | solution.py:309
  52.6 0.6 coarse.13
  53.2 1.9 %collective-permute-start.11 = (bf16[10,4,1536]{2,1,0:T(4,128)(2,1)S(1)}, bf16[10,4,1536]{2,1,0:T(4,128)(2,1)S(1)}, u32[]{:S(2)}, u32[]{:S(2)}) collective-permute-start(bf16[10,4,1536]{2,1,0:T(4,128)(2,1)S(1)} %coarse.13), channel_id=1, source_target_pairs={{4,0},{8,4},{12,8},{16,12},{20,16},{24,20},{28,24},{5,1},{9,5},{13... | collective-permute-start | bytes 368648 | tf_op jit(solution)/shard_map/ppermute | solution.py:445
  55.1 0.7 coarse.10
  55.9 1.0 collective-permute-done.7
  56.9 4.0 %collective-permute-start.9 = (bf16[10,8,1536]{2,1,0:T(8,128)(2,1)S(1)}, bf16[10,8,1536]{2,1,0:T(8,128)(2,1)S(1)}, u32[]{:S(2)}, u32[]{:S(2)}) collective-permute-start(bf16[10,8,1536]{2,1,0:T(8,128)(2,1)S(1)} %coarse.10), channel_id=1, source_target_pairs={{0,4},{4,8},{8,12},{12,16},{16,20},{20,24},{24,28},{1,5},{5,9},{9,... | collective-permute-start | bytes 737288 | tf_op jit(solution)/shard_map/ppermute | solution.py:442
  60.9 0.7 coarse.14
  61.6 0.7 coarse.17
  62.3 0.7 coarse.11
  63.1 0.6 coarse.15
  63.7 0.7 coarse.12
  64.4 0.1 slice.12
  64.5 0.6 coarse.16
  65.1 2.1 %collective-permute-start.12 = (bf16[10,4,2560]{2,1,0:T(4,128)(2,1)S(1)}, bf16[10,4,2560]{2,1,0:T(4,128)(2,1)S(1)}, u32[]{:S(2)}, u32[]{:S(2)}) collective-permute-start(bf16[10,4,2560]{2,1,0:T(4,128)(2,1)S(1)} %coarse.14), channel_id=1, source_target_pairs={{4,0},{8,4},{12,8},{16,12},{20,16},{24,20},{28,24},{5,1},{9,5},{13... | collective-permute-start | bytes 614408 | tf_op jit(solution)/shard_map/ppermute | solution.py:445
  67.2 0.1 pad_maximum_fusion
  67.4 3.1 %collective-permute-start.10 = (bf16[10,8,1536]{2,1,0:T(8,128)(2,1)S(1)}, bf16[10,8,1536]{2,1,0:T(8,128)(2,1)S(1)}, u32[]{:S(2)}, u32[]{:S(2)}) collective-permute-start(bf16[10,8,1536]{2,1,0:T(8,128)(2,1)S(1)} %coarse.11), channel_id=1, source_target_pairs={{0,4},{4,8},{8,12},{12,16},{16,20},{20,24},{24,28},{1,5},{5,9},{9,... | collective-permute-start | bytes 737288 | tf_op jit(solution)/shard_map/ppermute | solution.py:442
  70.5 0.1 add_convert_fusion
  70.6 0.3 collective-permute-start.17
  70.9 2.3 %collective-permute-start.16 = (bf16[14,8,1536]{2,1,0:T(8,128)(2,1)S(1)}, bf16[14,8,1536]{2,1,0:T(8,128)(2,1)S(1)}, u32[]{:S(2)}, u32[]{:S(2)}) collective-permute-start(bf16[14,8,1536]{2,1,0:T(8,128)(2,1)S(1)} %bitcast.19), channel_id=1, source_target_pairs={{0,1},{1,0},{2,3},{3,2},{4,5},{5,4},{6,7},{7,6},{8,9},{9,8},{10,11... | collective-permute-start | bytes 1032200 | tf_op jit(solution)/shard_map/ppermute | solution.py:439
  73.2 2.6 %collective-permute-start.14 = (bf16[10,8,1024]{2,1,0:T(8,128)(2,1)S(1)}, bf16[10,8,1024]{2,1,0:T(8,128)(2,1)S(1)}, u32[]{:S(2)}, u32[]{:S(2)}) collective-permute-start(bf16[10,8,1024]{2,1,0:T(8,128)(2,1)S(1)} %coarse.15), channel_id=1, source_target_pairs={{0,4},{4,8},{8,12},{12,16},{16,20},{20,24},{24,28},{1,5},{5,9},{9,... | collective-permute-start | bytes 491528 | tf_op jit(solution)/shard_map/ppermute | solution.py:442
  75.9 0.1 fusion.13
  76.0 2.3 %collective-permute-done.10 = bf16[10,8,1536]{2,1,0:T(8,128)(2,1)S(1)} collective-permute-done((bf16[10,8,1536]{2,1,0:T(8,128)(2,1)S(1)}, bf16[10,8,1536]{2,1,0:T(8,128)(2,1)S(1)}, u32[]{:S(2)}, u32[]{:S(2)}) %collective-permute-start.10) | collective-permute-done | bytes 245792 | tf_op jit(solution)/shard_map/ppermute | solution.py:442
  78.3 0.1 add_convert_fusion.1
  78.4 0.3 collective-permute-start.13
  78.6 5.2 %collective-permute-start.18 = (bf16[14,8,1536]{2,1,0:T(8,128)(2,1)S(1)}, bf16[14,8,1536]{2,1,0:T(8,128)(2,1)S(1)}, u32[]{:S(2)}, u32[]{:S(2)}) collective-permute-start(bf16[14,8,1536]{2,1,0:T(8,128)(2,1)S(1)} %collective-permute-done.17.refs_2_), channel_id=1, source_target_pairs={{0,1},{1,0},{2,3},{3,2},{4,5},{5,4},{6,7},{7,6},{8,9},{9,8},{10,11... | collective-permute-start | bytes 1032200 | tf_op jit(solution)/shard_map/ppermute | solution.py:439
  83.8 0.1 pad_maximum_fusion.1
  84.0 1.7 %collective-permute-start.15 = (bf16[14,8,1024]{2,1,0:T(8,128)(2,1)S(1)}, bf16[14,8,1024]{2,1,0:T(8,128)(2,1)S(1)}, u32[]{:S(2)}, u32[]{:S(2)}) collective-permute-start(bf16[14,8,1024]{2,1,0:T(8,128)(2,1)S(1)} %bitcast.22), channel_id=1, source_target_pairs={{0,2},{1,3},{2,0},{3,1},{4,6},{5,7},{6,4},{7,5},{8,10},{9,11},{10,... | collective-permute-start | bytes 688136 | tf_op jit(solution)/shard_map/ppermute | solution.py:436
  85.7 4.1 %collective-permute-start.19 = (bf16[14,8,1536]{2,1,0:T(8,128)(2,1)S(1)}, bf16[14,8,1536]{2,1,0:T(8,128)(2,1)S(1)}, u32[]{:S(2)}, u32[]{:S(2)}) collective-permute-start(bf16[14,8,1536]{2,1,0:T(8,128)(2,1)S(1)} %bitcast.16), channel_id=1, source_target_pairs={{0,1},{1,0},{2,3},{3,2},{4,5},{5,4},{6,7},{7,6},{8,9},{9,8},{10,11... | collective-permute-start | bytes 1032200 | tf_op jit(solution)/shard_map/ppermute | solution.py:439
  89.8 2.0 %assemble.3.refs_0_ = bf16[8,56,4096]{2,1,0:T(8,128)(2,1)} custom-call(bf16[448,448]{1,0:T(8,128)(2,1)S(1)} %fusion.12.order_ref, bf16[14,8,1536]{2,1,0:T(8,128)(2,1)S(1)} %bitcast.20, bf16[14,8,1536]{2,1,0:T(8,128)(2,1)S(1)} %collective-permute-done.16.refs_1_, bf16[14,8,1536]{2,1,0:T(8,128)(2,1)S(1)} %collective-permute-done.17.refs_2_, ...), custom_call_target="tpu_custom_call" | custom-call | flops 290000000 | bytes 10730000 | tf_op jit(solution)/shard_map/assemble/pallas_call | solution.py:391
  91.8 0.1 collective-permute-done.15.refs_3_
  91.8 4.0 %collective-permute-start.20 = (bf16[14,8,1536]{2,1,0:T(8,128)(2,1)S(1)}, bf16[14,8,1536]{2,1,0:T(8,128)(2,1)S(1)}, u32[]{:S(2)}, u32[]{:S(2)}) collective-permute-start(bf16[14,8,1536]{2,1,0:T(8,128)(2,1)S(1)} %collective-permute-done.13.refs_3_), channel_id=1, source_target_pairs={{0,1},{1,0},{2,3},{3,2},{4,5},{5,4},{6,7},{7,6},{8,9},{9,8},{10,11... | collective-permute-start | bytes 1032200 | tf_op jit(solution)/shard_map/ppermute | solution.py:439
  95.9 0.5 collective-permute-start.22
  96.4 0.8 collective-permute-done.20.refs_4_
  97.2 2.0 %assemble.4.refs_0_ = bf16[8,56,4096]{2,1,0:T(8,128)(2,1)} custom-call(bf16[448,448]{1,0:T(8,128)(2,1)S(1)} %fusion.12.order_ref, bf16[8,56,4096]{2,1,0:T(8,128)(2,1)} %assemble.3.refs_0_, bf16[14,8,1536]{2,1,0:T(8,128)(2,1)S(1)} %bitcast.17, bf16[14,8,1536]{2,1,0:T(8,128)(2,1)S(1)} %collective-permute-done.19.refs_2_, ...), custom_call_target="tpu_custom_call", output_to_operand_aliasing={{}: (1, {})} | custom-call | flops 290000000 | bytes 10730000 | tf_op jit(solution)/shard_map/assemble/pallas_call | solution.py:391
  99.1 1.6 %assemble.5 = bf16[8,56,4096]{2,1,0:T(8,128)(2,1)} custom-call(bf16[448,448]{1,0:T(8,128)(2,1)S(1)} %fusion.12.order_ref, bf16[8,56,4096]{2,1,0:T(8,128)(2,1)} %assemble.4.refs_0_, bf16[14,8,1024]{2,1,0:T(8,128)(2,1)S(1)} %bitcast.24, bf16[14,8,1024]{2,1,0:T(8,128)(2,1)S(1)} %collective-permute-done.21.refs_2_, ...), custom_call_target="tpu_custom_call", output_to_operand_aliasing={{}: (1, {})} | custom-call | flops 290000000 | bytes 10730000 | tf_op jit(solution)/shard_map/assemble/pallas_call | solution.py:391
  (38 shorter events, 0.2 us)
Async XLA Ops:
  0.0 1.4 %copy-start = (bf16[24,8,4096]{2,1,0:T(8,128)(2,1)S(1)}, bf16[24,8,4096]{2,1,0:T(8,128)(2,1)}, u32[]{:S(2)}) copy-start(bf16[24,8,4096]{2,1,0:T(8,128)(2,1)} %x_ref.4) | copy-start | bytes 4718596
  1.4 6.1 %copy-start.4 = (s32[192,4]{0,1:T(4,128)S(1)}, s32[192,4]{0,1:T(4,128)}, u32[]{:S(2)}) copy-start(s32[192,4]{0,1:T(4,128)} %param.9) | copy-start | bytes 9220
  1.4 6.2 %copy-start.6 = (s32[24,32]{1,0:T(8,128)S(1)}, s32[24,32]{1,0:T(8,128)}, u32[]{:S(2)}) copy-start(s32[24,32]{1,0:T(8,128)} %param.6) | copy-start | bytes 9220
  1.4 6.2 %copy-start.7 = (s32[24]{0:T(128)S(1)}, s32[24]{0:T(128)}, u32[]{:S(2)}) copy-start(s32[24]{0:T(128)} %param.7) | copy-start | bytes 292
  1.4 9.3 %copy-start.1 = (bf16[24,8,4096]{2,1,0:T(8,128)(2,1)S(1)}, bf16[24,8,4096]{2,1,0:T(8,128)(2,1)}, u32[]{:S(2)}) copy-start(bf16[24,8,4096]{2,1,0:T(8,128)(2,1)} %x_ref.4) | copy-start | bytes 4718596
  2.3 5.4 %collective-permute-start = (bf16[16,4,64,128]{3,2,1,0:T(8,128)(2,1)S(1)}, bf16[16,4,64,128]{3,2,1,0:T(8,128)(2,1)}, u32[]{:S(2)}, u32[]{:S(2)}) collective-permute-start(bf16[16,4,64,128]{3,2,1,0:T(8,128)(2,1)S(1)} %relayout.5.refs_0_), channel_id=1, source_target_pairs={{0,1},{1,0},{2,3},{3,2},{4,5},{5,4},{6,7},{7,6},{8,9},{9,8},{10,11... | collective-permute-start | bytes 3145736 | tf_op jit(solution)/shard_map/ppermute | solution.py:439
  3.0 24.8 %collective-permute-start.2 = (bf16[16,4,64,128]{3,2,1,0:T(8,128)(2,1)S(1)}, bf16[16,4,64,128]{3,2,1,0:T(8,128)(2,1)}, u32[]{:S(2)}, u32[]{:S(2)}) collective-permute-start(bf16[16,4,64,128]{3,2,1,0:T(8,128)(2,1)S(1)} %relayout.5.refs_0_), channel_id=1, source_target_pairs={{0,2},{1,3},{2,0},{3,1},{4,6},{5,7},{6,4},{7,5},{8,10},{9,11},{10,... | collective-permute-start | bytes 3145736 | tf_op jit(solution)/shard_map/ppermute | solution.py:436
  4.3 1.1 %copy-start.2 = (bf16[24,4,4096]{2,1,0:T(4,128)(2,1)S(1)}, bf16[24,4,4096]{2,1,0:T(4,128)(2,1)}, u32[]{:S(2)}) copy-start(bf16[24,4,4096]{2,1,0:T(4,128)(2,1)} %x_ref.5) | copy-start | bytes 2359300
  7.7 21.2 %collective-permute-start.1 = (bf16[24,2,64,128]{3,2,1,0:T(8,128)(2,1)S(1)}, bf16[24,2,64,128]{3,2,1,0:T(8,128)(2,1)S(1)}, u32[]{:S(2)}, u32[]{:S(2)}) collective-permute-start(bf16[24,2,64,128]{3,2,1,0:T(8,128)(2,1)S(1)} %relayout.4.refs_0_), channel_id=1, source_target_pairs={{0,4},{2,6},{4,8},{5,1},{6,10},{7,3},{8,12},{9,5},{10,14},{11,7},{... | collective-permute-start | bytes 2359304 | tf_op jit(solution)/shard_map/ppermute | solution.py:433
  11.2 4.9 %collective-permute-start.3 = (bf16[8,4,64,128]{3,2,1,0:T(8,128)(2,1)S(1)}, bf16[8,4,64,128]{3,2,1,0:T(8,128)(2,1)S(1)}, u32[]{:S(2)}, u32[]{:S(2)}) collective-permute-start(bf16[8,4,64,128]{3,2,1,0:T(8,128)(2,1)S(1)} %relayout.6.refs_0_), channel_id=1, source_target_pairs={{0,1},{1,0},{2,3},{3,2},{4,5},{5,4},{6,7},{7,6},{8,9},{9,8},{10,11... | collective-permute-start | bytes 1572872 | tf_op jit(solution)/shard_map/ppermute | solution.py:439
  12.2 4.0 %copy-start.3 = (bf16[24,4,4096]{2,1,0:T(4,128)(2,1)S(1)}, bf16[24,4,4096]{2,1,0:T(4,128)(2,1)}, u32[]{:S(2)}) copy-start(bf16[24,4,4096]{2,1,0:T(4,128)(2,1)} %x_ref.5) | copy-start | bytes 2359300
  28.9 5.3 %collective-permute-start.6 = (bf16[16,4,64,128]{3,2,1,0:T(8,128)(2,1)}, bf16[16,4,64,128]{3,2,1,0:T(8,128)(2,1)S(1)}, u32[]{:S(2)}, u32[]{:S(2)}) collective-permute-start(bf16[16,4,64,128]{3,2,1,0:T(8,128)(2,1)} %collective-permute-done.2.refs_0_), channel_id=1, source_target_pairs={{0,1},{1,0},{2,3},{3,2},{4,5},{5,4},{6,7},{7,6},{8,9},{9,8},{10,11... | collective-permute-start | bytes 3145736 | tf_op jit(solution)/shard_map/ppermute | solution.py:439
  29.4 3.3 %collective-permute-start.5 = (bf16[24,2,64,128]{3,2,1,0:T(8,128)(2,1)S(1)}, bf16[24,2,64,128]{3,2,1,0:T(8,128)(2,1)S(1)}, u32[]{:S(2)}, u32[]{:S(2)}) collective-permute-start(bf16[24,2,64,128]{3,2,1,0:T(8,128)(2,1)S(1)} %collective-permute-done.1.refs_0_), channel_id=1, source_target_pairs={{0,1},{1,0},{2,3},{3,2},{4,5},{5,4},{6,7},{7,6},{8,9},{9,8},{10,11... | collective-permute-start | bytes 2359304 | tf_op jit(solution)/shard_map/ppermute | solution.py:439
  29.4 13.0 %collective-permute-start.4 = (bf16[8,4,64,128]{3,2,1,0:T(8,128)(2,1)S(1)}, bf16[8,4,64,128]{3,2,1,0:T(8,128)(2,1)S(1)}, u32[]{:S(2)}, u32[]{:S(2)}) collective-permute-start(bf16[8,4,64,128]{3,2,1,0:T(8,128)(2,1)S(1)} %relayout.6.refs_0_), channel_id=1, source_target_pairs={{0,2},{1,3},{2,0},{3,1},{4,6},{5,7},{6,4},{7,5},{8,10},{9,11},{10,... | collective-permute-start | bytes 1572872 | tf_op jit(solution)/shard_map/ppermute | solution.py:436
  42.4 6.5 %collective-permute-start.8 = (bf16[8,4,64,128]{3,2,1,0:T(8,128)(2,1)S(1)}, bf16[8,4,64,128]{3,2,1,0:T(8,128)(2,1)S(1)}, u32[]{:S(2)}, u32[]{:S(2)}) collective-permute-start(bf16[8,4,64,128]{3,2,1,0:T(8,128)(2,1)S(1)} %collective-permute-done.4.refs_0_), channel_id=1, source_target_pairs={{0,1},{1,0},{2,3},{3,2},{4,5},{5,4},{6,7},{7,6},{8,9},{9,8},{10,11... | collective-permute-start | bytes 1572872 | tf_op jit(solution)/shard_map/ppermute | solution.py:439
  44.7 12.2 %collective-permute-start.7 = (bf16[10,4,4096]{2,1,0:T(4,128)(2,1)S(1)}, bf16[10,4,4096]{2,1,0:T(4,128)(2,1)S(1)}, u32[]{:S(2)}, u32[]{:S(2)}) collective-permute-start(bf16[10,4,4096]{2,1,0:T(4,128)(2,1)S(1)} %coarse.9), channel_id=1, source_target_pairs={{4,0},{8,4},{12,8},{16,12},{20,16},{24,20},{28,24},{5,1},{9,5},{13... | collective-permute-start | bytes 983048 | tf_op jit(solution)/shard_map/ppermute | solution.py:445
  53.2 11.9 %collective-permute-start.11 = (bf16[10,4,1536]{2,1,0:T(4,128)(2,1)S(1)}, bf16[10,4,1536]{2,1,0:T(4,128)(2,1)S(1)}, u32[]{:S(2)}, u32[]{:S(2)}) collective-permute-start(bf16[10,4,1536]{2,1,0:T(4,128)(2,1)S(1)} %coarse.13), channel_id=1, source_target_pairs={{4,0},{8,4},{12,8},{16,12},{20,16},{24,20},{28,24},{5,1},{9,5},{13... | collective-permute-start | bytes 368648 | tf_op jit(solution)/shard_map/ppermute | solution.py:445
  56.9 7.5 %copy-start.5 = (bf16[10,4,4096]{2,1,0:T(4,128)(2,1)}, bf16[10,4,4096]{2,1,0:T(4,128)(2,1)S(1)}, u32[]{:S(2)}) copy-start(bf16[10,4,4096]{2,1,0:T(4,128)(2,1)S(1)} %collective-permute-done.7) | copy-start | bytes 983044
  56.9 10.5 %collective-permute-start.9 = (bf16[10,8,1536]{2,1,0:T(8,128)(2,1)S(1)}, bf16[10,8,1536]{2,1,0:T(8,128)(2,1)S(1)}, u32[]{:S(2)}, u32[]{:S(2)}) collective-permute-start(bf16[10,8,1536]{2,1,0:T(8,128)(2,1)S(1)} %coarse.10), channel_id=1, source_target_pairs={{0,4},{4,8},{8,12},{12,16},{16,20},{20,24},{24,28},{1,5},{5,9},{9,... | collective-permute-start | bytes 737288 | tf_op jit(solution)/shard_map/ppermute | solution.py:442
  64.5 2.8 %slice-start = ((bf16[10,4,4096]{2,1,0:T(4,128)(2,1)}), bf16[10,4,1536]{2,1,0:T(4,128)(2,1)S(1)}, s32[]{:S(2)}) async-start(bf16[10,4,4096]{2,1,0:T(4,128)(2,1)} %copy-done.5), calls=%async_computation | async-start | bytes 245760 | tf_op jit(solution)/shard_map/slice | solution.py:496
  65.1 8.1 %collective-permute-start.12 = (bf16[10,4,2560]{2,1,0:T(4,128)(2,1)S(1)}, bf16[10,4,2560]{2,1,0:T(4,128)(2,1)S(1)}, u32[]{:S(2)}, u32[]{:S(2)}) collective-permute-start(bf16[10,4,2560]{2,1,0:T(4,128)(2,1)S(1)} %coarse.14), channel_id=1, source_target_pairs={{4,0},{8,4},{12,8},{16,12},{20,16},{24,20},{28,24},{5,1},{9,5},{13... | collective-permute-start | bytes 614408 | tf_op jit(solution)/shard_map/ppermute | solution.py:445
  67.4 10.9 %collective-permute-start.10 = (bf16[10,8,1536]{2,1,0:T(8,128)(2,1)S(1)}, bf16[10,8,1536]{2,1,0:T(8,128)(2,1)S(1)}, u32[]{:S(2)}, u32[]{:S(2)}) collective-permute-start(bf16[10,8,1536]{2,1,0:T(8,128)(2,1)S(1)} %coarse.11), channel_id=1, source_target_pairs={{0,4},{4,8},{8,12},{12,16},{16,20},{20,24},{24,28},{1,5},{5,9},{9,... | collective-permute-start | bytes 737288 | tf_op jit(solution)/shard_map/ppermute | solution.py:442
  70.6 8.0 %collective-permute-start.17 = (bf16[14,8,1536]{2,1,0:T(8,128)(2,1)S(1)}, bf16[14,8,1536]{2,1,0:T(8,128)(2,1)S(1)}, u32[]{:S(2)}, u32[]{:S(2)}) collective-permute-start(bf16[14,8,1536]{2,1,0:T(8,128)(2,1)S(1)} %bitcast.18), channel_id=1, source_target_pairs={{0,2},{1,3},{2,0},{3,1},{4,6},{5,7},{6,4},{7,5},{8,10},{9,11},{10,... | collective-permute-start | bytes 1032200 | tf_op jit(solution)/shard_map/ppermute | solution.py:436
  70.9 18.9 %collective-permute-start.16 = (bf16[14,8,1536]{2,1,0:T(8,128)(2,1)S(1)}, bf16[14,8,1536]{2,1,0:T(8,128)(2,1)S(1)}, u32[]{:S(2)}, u32[]{:S(2)}) collective-permute-start(bf16[14,8,1536]{2,1,0:T(8,128)(2,1)S(1)} %bitcast.19), channel_id=1, source_target_pairs={{0,1},{1,0},{2,3},{3,2},{4,5},{5,4},{6,7},{7,6},{8,9},{9,8},{10,11... | collective-permute-start | bytes 1032200 | tf_op jit(solution)/shard_map/ppermute | solution.py:439
  73.2 10.7 %collective-permute-start.14 = (bf16[10,8,1024]{2,1,0:T(8,128)(2,1)S(1)}, bf16[10,8,1024]{2,1,0:T(8,128)(2,1)S(1)}, u32[]{:S(2)}, u32[]{:S(2)}) collective-permute-start(bf16[10,8,1024]{2,1,0:T(8,128)(2,1)S(1)} %coarse.15), channel_id=1, source_target_pairs={{0,4},{4,8},{8,12},{12,16},{16,20},{20,24},{24,28},{1,5},{5,9},{9,... | collective-permute-start | bytes 491528 | tf_op jit(solution)/shard_map/ppermute | solution.py:442
  78.4 11.4 %collective-permute-start.13 = (bf16[14,8,1536]{2,1,0:T(8,128)(2,1)S(1)}, bf16[14,8,1536]{2,1,0:T(8,128)(2,1)S(1)}, u32[]{:S(2)}, u32[]{:S(2)}) collective-permute-start(bf16[14,8,1536]{2,1,0:T(8,128)(2,1)S(1)} %bitcast.15), channel_id=1, source_target_pairs={{0,2},{1,3},{2,0},{3,1},{4,6},{5,7},{6,4},{7,5},{8,10},{9,11},{10,... | collective-permute-start | bytes 1032200 | tf_op jit(solution)/shard_map/ppermute | solution.py:436
  78.6 11.2 %collective-permute-start.18 = (bf16[14,8,1536]{2,1,0:T(8,128)(2,1)S(1)}, bf16[14,8,1536]{2,1,0:T(8,128)(2,1)S(1)}, u32[]{:S(2)}, u32[]{:S(2)}) collective-permute-start(bf16[14,8,1536]{2,1,0:T(8,128)(2,1)S(1)} %collective-permute-done.17.refs_2_), channel_id=1, source_target_pairs={{0,1},{1,0},{2,3},{3,2},{4,5},{5,4},{6,7},{7,6},{8,9},{9,8},{10,11... | collective-permute-start | bytes 1032200 | tf_op jit(solution)/shard_map/ppermute | solution.py:439
  84.0 7.9 %collective-permute-start.15 = (bf16[14,8,1024]{2,1,0:T(8,128)(2,1)S(1)}, bf16[14,8,1024]{2,1,0:T(8,128)(2,1)S(1)}, u32[]{:S(2)}, u32[]{:S(2)}) collective-permute-start(bf16[14,8,1024]{2,1,0:T(8,128)(2,1)S(1)} %bitcast.22), channel_id=1, source_target_pairs={{0,2},{1,3},{2,0},{3,1},{4,6},{5,7},{6,4},{7,5},{8,10},{9,11},{10,... | collective-permute-start | bytes 688136 | tf_op jit(solution)/shard_map/ppermute | solution.py:436
  85.7 10.7 %collective-permute-start.19 = (bf16[14,8,1536]{2,1,0:T(8,128)(2,1)S(1)}, bf16[14,8,1536]{2,1,0:T(8,128)(2,1)S(1)}, u32[]{:S(2)}, u32[]{:S(2)}) collective-permute-start(bf16[14,8,1536]{2,1,0:T(8,128)(2,1)S(1)} %bitcast.16), channel_id=1, source_target_pairs={{0,1},{1,0},{2,3},{3,2},{4,5},{5,4},{6,7},{7,6},{8,9},{9,8},{10,11... | collective-permute-start | bytes 1032200 | tf_op jit(solution)/shard_map/ppermute | solution.py:439
  91.8 5.3 %collective-permute-start.20 = (bf16[14,8,1536]{2,1,0:T(8,128)(2,1)S(1)}, bf16[14,8,1536]{2,1,0:T(8,128)(2,1)S(1)}, u32[]{:S(2)}, u32[]{:S(2)}) collective-permute-start(bf16[14,8,1536]{2,1,0:T(8,128)(2,1)S(1)} %collective-permute-done.13.refs_3_), channel_id=1, source_target_pairs={{0,1},{1,0},{2,3},{3,2},{4,5},{5,4},{6,7},{7,6},{8,9},{9,8},{10,11... | collective-permute-start | bytes 1032200 | tf_op jit(solution)/shard_map/ppermute | solution.py:439
  95.9 3.2 %collective-permute-start.21 = (bf16[14,8,1024]{2,1,0:T(8,128)(2,1)S(1)}, bf16[14,8,1024]{2,1,0:T(8,128)(2,1)S(1)}, u32[]{:S(2)}, u32[]{:S(2)}) collective-permute-start(bf16[14,8,1024]{2,1,0:T(8,128)(2,1)S(1)} %bitcast.23), channel_id=1, source_target_pairs={{0,1},{1,0},{2,3},{3,2},{4,5},{5,4},{6,7},{7,6},{8,9},{9,8},{10,11... | collective-permute-start | bytes 688136 | tf_op jit(solution)/shard_map/ppermute | solution.py:439
  95.9 3.2 %collective-permute-start.22 = (bf16[14,8,1024]{2,1,0:T(8,128)(2,1)S(1)}, bf16[14,8,1024]{2,1,0:T(8,128)(2,1)S(1)}, u32[]{:S(2)}, u32[]{:S(2)}) collective-permute-start(bf16[14,8,1024]{2,1,0:T(8,128)(2,1)S(1)} %collective-permute-done.15.refs_3_), channel_id=1, source_target_pairs={{0,1},{1,0},{2,3},{3,2},{4,5},{5,4},{6,7},{7,6},{8,9},{9,8},{10,11... | collective-permute-start | bytes 688136 | tf_op jit(solution)/shard_map/ppermute | solution.py:439

commit v13 on v11

--- a/solution.py
+++ b/solution.py
@@ -139,7 +139,7 @@
     return (side, side + 3) if tiles == GROUPS else (0, tiles)
 
 
-def right_kernel(rb, tiles, table_ref, *refs):
+def right_kernel(kind, rb, tiles, table_ref, *refs):
     o_ref = refs[-1]
     core = lax.rem(lax.axis_index("col"), 2)
     low = lax.broadcasted_iota(jnp.int32, (1, LANES), 1) < BS
@@ -164,28 +164,45 @@
 
         lax.fori_loop(0, rb // 4, four, 0)
 
-    if len(refs) == 2:
+    quads = rb // 4
+    if kind == 0:
         fill(refs[0], 1, 0)
-    else:
-        first = refs[0]
-        second = refs[1]
+    elif kind == 1:
 
         @pl.when(core == 0)
         def _():
-            fill(first, 0, 0)
-            fill(second, 2, rb // 4)
+            fill(refs[0], 0, 0)
 
         @pl.when(core == 1)
         def _():
-            fill(second, 0, 0)
-            fill(first, 2, rb // 4)
-
-
-def right_factor(table, srcs, tiles, us):
+            fill(refs[0], 2, 0)
+    else:
+
+        def keep(side, out_first):
+            def one(jq, carry):
+                for p in range(*touched(side, tiles)):
+                    o_ref[out_first + jq, p] = refs[0][jq, p]
+                return carry
+
+            lax.fori_loop(0, quads, one, 0)
+
+        @pl.when(core == 0)
+        def _():
+            keep(0, 0)
+            fill(refs[1], 2, quads)
+
+        @pl.when(core == 1)
+        def _():
+            fill(refs[1], 0, 0)
+            keep(2, quads)
+
+
+def right_factor(kind, table, srcs, tiles, us):
     rb = table.shape[1] // 3
-    return pl.pallas_call(
-        functools.partial(right_kernel, rb, tiles),
-        out_shape=jax.ShapeDtypeStruct((len(srcs) * rb // 4, tiles, 4 * BS, LANES), BF),
+    quads = rb // 4 * (2 if kind == 2 else 1)
+    return pl.pallas_call(
+        functools.partial(right_kernel, kind, rb, tiles),
+        out_shape=jax.ShapeDtypeStruct((quads, tiles, 4 * BS, LANES), BF),
         in_specs=[SM] + [VM] * len(srcs),
         out_specs=VM,
         compiler_params=params(8),
@@ -367,7 +384,7 @@
 
 def assemble(order, srcs, a0, total, before):
     n, _, lanes = srcs[0].shape
-    step = 512
+    step = lanes
     per = lanes // step
     wide = n * len(srcs)
     specs = [pl.BlockSpec(order.shape, lambda i: (0, 0))]
@@ -416,7 +433,7 @@
     share = CB // ncol
     tiles = (GROUPS * share + 1) // 2
     parts = ((0, rb * 2 // 3), (rb * 2 // 3, rb // 3))
-    chunks = ((0, 24), (24, 48), (48, 64))
+    chunks = ((0, 32), (32, 64))
 
     def outward(x):
         pairs = [(r * ncol + c, (r + 1 - 2 * (c % 2)) * ncol + c) for r in range(nrow) for c in range(ncol)]
@@ -450,12 +467,13 @@
     p_blocks, p_own, side_a[1] = lax.optimization_barrier((p_blocks, p_own, side_a[1]))
     table = column_table(pct, rb, share)
     left = left_factor(pct, relayout(p_blocks, 0, rb))
-    own = right_factor(table, [p_own], tiles, 2.0)
+    own = right_factor(0, table, [p_own], tiles, 1.4)
     order = assembly_order(shifts, ncol, share)
     place = slot_places(a_cols, counts)
     bands = [near_band(place, [own_a[h], side_a[h]], shifts[:2], parts[h][0]) for h in range(2)]
     beside, far_a[0], left, own, order, bands = lax.optimization_barrier((beside, far_a[0], left, own, order, bands))
-    near = right_factor(table, [beside, over_core(beside)], tiles, 3.0)
+    near = right_factor(1, table, [beside], tiles, 1.2)
+    near = right_factor(2, table, [near, over_core(beside)], tiles, 1.4)
     aps = []
     for h in range(2):
         srcs = [z for g in far_a[h] for z in (g, over_core(g))]
@@ -478,27 +496,24 @@
     late.append(downward(lows[1]))
     highs[0], raw[1] = lax.optimization_barrier((highs[0], raw[1]))
     highs.append(upward(raw[1]))
-    late[1], raw[2] = lax.optimization_barrier((late[1], raw[2]))
-    highs.append(upward(raw[2]))
     mids = [coarse_rows(left, aps, ((CB, 2 * CB),), a0, a1, F32, 1.0)[0] for a0, a1 in chunks]
     lower = [
         jnp.concatenate([early[:, :, : cut * BS], late[0]], axis=1),
         jnp.concatenate([early[:, :, cut * BS :], late[1]], axis=1),
     ]
-    totals, sides, fars = [], [], []
+    totals, fars = [], []
     for z, (a0, a1) in enumerate(chunks):
         low = lower[0] if z == 0 else lower[1][:, :, (a0 - cut) * BS : (a1 - cut) * BS]
         total = columns(highs[z], 0) + columns(mids[z], 1) + columns(low, 2)
         total = total.astype(BF).reshape((share * (GROUPS + 2),) + total.shape[2:])
         totals.append(total)
-        sides.append(over_core(total))
         fars.append([over_y(total, s) for s in range(1, ny)])
-    for z in range(len(chunks) - 1):
-        fars[z], _ = lax.optimization_barrier((fars[z], totals[z + 1]))
+    totals, fars[:-1] = lax.optimization_barrier((totals, fars[:-1]))
+    sides = [over_core(x) for x in totals]
     out = None
     for z, (a0, a1) in enumerate(chunks):
         if z == 1:
-            fars[1:], out = lax.optimization_barrier((fars[1:], out))
+            fars[1], sides[0] = lax.optimization_barrier((fars[1], sides[0]))
         srcs = [totals[z], sides[z]] + [q for x in fars[z] for q in (x, over_core(x))]
         out = assemble(order, srcs, a0, BS * BS, out)
     return out

time: 102 us -> 108 us (1.059)
  waiting for transfers between devices: 11.6 us -> 27.3 us
  starting transfers between devices: 45.2 us -> 37 us
    ppermute x5 -> x4, waiting for transfers between devices: 5.77 us -> 16 us  [over_y(): lax.ppermute(x, 'col', [(y * 2 + c, (y + s) % ny * 2 + c) for y in range(...]
    ppermute x11 -> x9, starting transfers between devices: 18.5 us -> 8.53 us  [over_core(): return lax.ppermute(x, 'col', [(c, c ^ 1) for c in range(ncol)])]
    ppermute x3 -> x2, waiting for transfers between devices: 1.7 us -> 7.95 us  [upward(): return lax.ppermute(x, 'row', [(i, i + 1) for i in range(nrow - 1)])]
    ppermute x3, starting transfers between devices: 7.8 us -> 11.8 us  [downward(): return lax.ppermute(x, 'row', [(i + 1, i) for i in range(nrow - 1)])]
    ppermute x11 -> x9, waiting for transfers between devices: 2.82 us -> 0.62 us  [over_core(): return lax.ppermute(x, 'col', [(c, c ^ 1) for c in range(ncol)])]
    pallas_call x3 -> x2, Pallas kernels: 6.56 us -> 4.7 us  [assemble(): pl.pallas_call(assemble_kernel, grid=(per,), out_shape=jax.ShapeDtypeStru...]
    ppermute x5 -> x4, starting transfers between devices: 5.73 us -> 3.96 us  [over_y(): lax.ppermute(x, 'col', [(y * 2 + c, (y + s) % ny * 2 + c) for y in range(...]
    ppermute x3, waiting for transfers between devices: 0.97 us -> 2.41 us  [downward(): return lax.ppermute(x, 'row', [(i + 1, i) for i in range(nrow - 1)])]
  transfers between devices with their start and end apart: 23 -> 19, of which waited for: 7 -> 9; matrix products, arithmetic and copies ran while one was open for 1% -> 1% of each run, Pallas kernels for 37% -> 33%
where the time goes in v13:
time: 108 us; the launch traced here: 107 us
  Pallas kernels  38.7 us (36%)
  starting transfers between devices  37 us (34%)
  waiting for transfers between devices  27.3 us (25%)
  local copies, waits for them, and re-layouts  2.69 us (2%)
    ppermute x4, waiting for transfers between devices, over_y(): lax.ppermute(x, 'col', [(y * 2 + c, (y + s) % ny * 2 + c) for y in range(...  16 us
    ppermute x3, starting transfers between devices, downward(): return lax.ppermute(x, 'row', [(i + 1, i) for i in range(nrow - 1)])  11.8 us
    pallas_call x2, Pallas kernels, product(): pl.pallas_call(functools.partial(product_kernel, first, rb, shifts), out_...  10.9 us
    ppermute x2, starting transfers between devices, upward(): return lax.ppermute(x, 'row', [(i, i + 1) for i in range(nrow - 1)])  9.64 us
    ppermute x9, starting transfers between devices, over_core(): return lax.ppermute(x, 'col', [(c, c ^ 1) for c in range(ncol)])  8.53 us
    ppermute x2, waiting for transfers between devices, upward(): return lax.ppermute(x, 'row', [(i, i + 1) for i in range(nrow - 1)])  7.95 us
    pallas_call x7, Pallas kernels, coarse_rows(): pl.pallas_call(functools.partial(coarse_kernel, sets, a0, a1), out_shape=...  6.72 us
    pallas_call x2, Pallas kernels, near_band(): pl.pallas_call(functools.partial(band_kernel, first, shifts), out_shape=j...  5.98 us
  transfers between devices with their start and end apart: 19, of which 9 were waited for; matrix products, arithmetic and copies ran while one was open for 1% of the time, Pallas kernels for 33%

profile of v13, /device:TPU:9, one launch (start us, length us, event | category | flops | bytes accessed | tf_op | source)
XLA Modules:
  0.0 106.9 jit_solution(4324127448645497288)
XLA Ops:
  0.0 1.4 %copy-done = bf16[24,8,4096]{2,1,0:T(8,128)(2,1)S(1)} copy-done((bf16[24,8,4096]{2,1,0:T(8,128)(2,1)S(1)}, bf16[24,8,4096]{2,1,0:T(8,128)(2,1)}, u32[]{:S(2)}) %copy-start) | copy-done | bytes 1572888
  1.4 0.8 relayout.3.refs_0_
  2.2 0.7 collective-permute-start
  3.0 1.3 %collective-permute-start.2 = (bf16[16,4,64,128]{3,2,1,0:T(8,128)(2,1)S(1)}, bf16[16,4,64,128]{3,2,1,0:T(8,128)(2,1)}, u32[]{:S(2)}, u32[]{:S(2)}) collective-permute-start(bf16[16,4,64,128]{3,2,1,0:T(8,128)(2,1)S(1)} %relayout.3.refs_0_), channel_id=1, source_target_pairs={{0,2},{1,3},{2,0},{3,1},{4,6},{5,7},{6,4},{7,5},{8,10},{9,11},{10,... | collective-permute-start | bytes 3145736 | tf_op jit(solution)/shard_map/ppermute | solution.py:443
  4.2 1.1 %copy-done.2 = bf16[24,4,4096]{2,1,0:T(4,128)(2,1)S(1)} copy-done((bf16[24,4,4096]{2,1,0:T(4,128)(2,1)S(1)}, bf16[24,4,4096]{2,1,0:T(4,128)(2,1)}, u32[]{:S(2)}) %copy-start.2) | copy-done | bytes 786456
  5.4 1.1 relayout_rows.1.refs_0_
  6.5 0.1 add_select_fusion.4.table_ref
  6.6 0.0 collective-permute-done.refs_1_
  6.6 3.0 %collective-permute-start.1 = (bf16[24,2,64,128]{3,2,1,0:T(8,128)(2,1)S(1)}, bf16[24,2,64,128]{3,2,1,0:T(8,128)(2,1)S(1)}, u32[]{:S(2)}, u32[]{:S(2)}) collective-permute-start(bf16[24,2,64,128]{3,2,1,0:T(8,128)(2,1)S(1)} %relayout_rows.1.refs_0_), channel_id=1, source_target_pairs={{0,4},{2,6},{4,8},{5,1},{6,10},{7,3},{8,12},{9,5},{10,14},{11,7},{... | collective-permute-start | bytes 2359304 | tf_op jit(solution)/shard_map/ppermute | solution.py:440
  9.6 0.1 subtract_select_fusion.place_ref
  9.7 0.4 relayout.4.refs_0_
  10.1 0.8 collective-permute-start.3
  10.9 0.2 fusion.12.order_ref
  11.1 0.0 copy-start.3
  11.1 3.9 %near_band.2.start_ref = bf16[4,27,256,128]{3,2,1,0:T(8,128)(2,1)S(1)} custom-call(s32[24,32]{1,0:T(8,128)S(1)} %subtract_select_fusion.place_ref, bf16[16,4,64,128]{3,2,1,0:T(8,128)(2,1)S(1)} %relayout.3.refs_0_, bf16[16,4,64,128]{3,2,1,0:T(8,128)(2,1)} %collective-permute-done.refs_1_), custom_call_target="tpu_custom_call" | custom-call | flops 256000000 | bytes 9472000 | tf_op jit(solution)/shard_map/near_band/pallas_call | solution.py:272
  15.1 0.0 collective-permute-done.3.refs_1_
  15.1 0.9 relayout.5.pl_ref
  16.0 2.1 %near_band.3.start_ref = bf16[2,27,256,128]{3,2,1,0:T(8,128)(2,1)S(1)} custom-call(s32[24,32]{1,0:T(8,128)S(1)} %subtract_select_fusion.place_ref, bf16[8,4,64,128]{3,2,1,0:T(8,128)(2,1)S(1)} %relayout.4.refs_0_, bf16[8,4,64,128]{3,2,1,0:T(8,128)(2,1)S(1)} %collective-permute-done.3.refs_1_), custom_call_target="tpu_custom_call" | custom-call | flops 128000000 | bytes 4736000 | tf_op jit(solution)/shard_map/near_band/pallas_call | solution.py:272
  18.0 1.4 %right_factor.3.own_ref = bf16[6,5,256,128]{3,2,1,0:T(8,128)(2,1)S(1)} custom-call(s32[4,72]{1,0:T(4,128)S(1)} %add_select_fusion.4.table_ref, bf16[24,2,64,128]{3,2,1,0:T(8,128)(2,1)S(1)} %relayout_rows.1.refs_0_), custom_call_target="tpu_custom_call" | custom-call | flops 140000000 | bytes 5180000 | tf_op jit(solution)/shard_map/right_factor/pallas_call | solution.py:203
  19.4 2.9 %left_factor.1.left_ref = bf16[12,24,64,128]{3,2,1,0:T(8,128)(2,1)S(1)} custom-call(s32[4,192]{1,0:T(4,128)S(1)} %bitcast.18, bf16[24,2,64,128]{3,2,1,0:T(8,128)(2,1)S(1)} %relayout.5.pl_ref), custom_call_target="tpu_custom_call" | custom-call | flops 290000000 | bytes 10730000 | tf_op jit(solution)/shard_map/left_factor/pallas_call | solution.py:118
  22.3 5.5 %collective-permute-done.2.refs_0_ = bf16[16,4,64,128]{3,2,1,0:T(8,128)(2,1)} collective-permute-done((bf16[16,4,64,128]{3,2,1,0:T(8,128)(2,1)S(1)}, bf16[16,4,64,128]{3,2,1,0:T(8,128)(2,1)}, u32[]{:S(2)}, u32[]{:S(2)}) %collective-permute-start.2) | collective-permute-done | bytes 1048608 | tf_op jit(solution)/shard_map/ppermute | solution.py:443
  27.8 0.3 collective-permute-done.1.refs_0_
  28.2 0.5 collective-permute-start.6
  28.7 0.0 collective-permute-start.5
  28.7 1.2 %collective-permute-start.4 = (bf16[8,4,64,128]{3,2,1,0:T(8,128)(2,1)S(1)}, bf16[8,4,64,128]{3,2,1,0:T(8,128)(2,1)S(1)}, u32[]{:S(2)}, u32[]{:S(2)}) collective-permute-start(bf16[8,4,64,128]{3,2,1,0:T(8,128)(2,1)S(1)} %relayout.4.refs_0_), channel_id=1, source_target_pairs={{0,2},{1,3},{2,0},{3,1},{4,6},{5,7},{6,4},{7,5},{8,10},{9,11},{10,... | collective-permute-start | bytes 1572872 | tf_op jit(solution)/shard_map/ppermute | solution.py:443
  29.9 1.4 %right_factor.4.refs_0_ = bf16[6,5,256,128]{3,2,1,0:T(8,128)(2,1)S(1)} custom-call(s32[4,72]{1,0:T(4,128)S(1)} %add_select_fusion.4.table_ref, bf16[24,2,64,128]{3,2,1,0:T(8,128)(2,1)S(1)} %collective-permute-done.1.refs_0_), custom_call_target="tpu_custom_call" | custom-call | flops 120000000 | bytes 4440000 | tf_op jit(solution)/shard_map/right_factor/pallas_call | solution.py:203
  31.4 0.6 collective-permute-done.5.refs_1_
  32.0 1.5 %right_factor.5.near_ref = bf16[12,5,256,128]{3,2,1,0:T(8,128)(2,1)S(1)} custom-call(s32[4,72]{1,0:T(4,128)S(1)} %add_select_fusion.4.table_ref, bf16[6,5,256,128]{3,2,1,0:T(8,128)(2,1)S(1)} %right_factor.4.refs_0_, bf16[24,2,64,128]{3,2,1,0:T(8,128)(2,1)S(1)} %collective-permute-done.5.refs_1_), custom_call_target="tpu_custom_call" | custom-call | flops 140000000 | bytes 5180000 | tf_op jit(solution)/shard_map/right_factor/pallas_call | solution.py:203
  33.5 0.0 collective-permute-done.6.refs_1_
  33.5 7.1 %product.2.refs_0_ = bf16[16,64,640]{2,1,0:T(8,128)(2,1)S(1)} custom-call(s32[24,32]{1,0:T(8,128)S(1)} %subtract_select_fusion.place_ref, bf16[6,5,256,128]{3,2,1,0:T(8,128)(2,1)S(1)} %right_factor.3.own_ref, bf16[12,5,256,128]{3,2,1,0:T(8,128)(2,1)S(1)} %right_factor.5.near_ref, bf16[4,27,256,128]{3,2,1,0:T(8,128)(2,1)S(1)} %near_band.2.start_ref, ...), custom_call_target="tpu_custom_call" | custom-call | flops 480000000 | bytes 17760000 | tf_op jit(solution)/shard_map/product/pallas_call | solution.py:316
  40.6 1.0 collective-permute-done.4.refs_0_
  41.7 1.4 %collective-permute-start.8 = (bf16[8,4,64,128]{3,2,1,0:T(8,128)(2,1)S(1)}, bf16[8,4,64,128]{3,2,1,0:T(8,128)(2,1)S(1)}, u32[]{:S(2)}, u32[]{:S(2)}) collective-permute-start(bf16[8,4,64,128]{3,2,1,0:T(8,128)(2,1)S(1)} %collective-permute-done.4.refs_0_), channel_id=1, source_target_pairs={{0,1},{1,0},{2,3},{3,2},{4,5},{5,4},{6,7},{7,6},{8,9},{9,8},{10,11... | collective-permute-start | bytes 1572872 | tf_op jit(solution)/shard_map/ppermute | solution.py:446
  43.0 0.9 coarse.7
  44.0 3.8 %collective-permute-start.7 = (bf16[10,4,4096]{2,1,0:T(4,128)(2,1)S(1)}, bf16[10,4,4096]{2,1,0:T(4,128)(2,1)S(1)}, u32[]{:S(2)}, u32[]{:S(2)}) collective-permute-start(bf16[10,4,4096]{2,1,0:T(4,128)(2,1)S(1)} %coarse.7), channel_id=1, source_target_pairs={{4,0},{8,4},{12,8},{16,12},{20,16},{24,20},{28,24},{5,1},{9,5},{13... | collective-permute-start | bytes 983048 | tf_op jit(solution)/shard_map/ppermute | solution.py:452
  47.7 3.8 %product.3.refs_1_ = bf16[8,64,640]{2,1,0:T(8,128)(2,1)S(1)} custom-call(s32[24,32]{1,0:T(8,128)S(1)} %subtract_select_fusion.place_ref, bf16[6,5,256,128]{3,2,1,0:T(8,128)(2,1)S(1)} %right_factor.3.own_ref, bf16[12,5,256,128]{3,2,1,0:T(8,128)(2,1)S(1)} %right_factor.5.near_ref, bf16[2,27,256,128]{3,2,1,0:T(8,128)(2,1)S(1)} %near_band.3.start_ref, ...), custom_call_target="tpu_custom_call" | custom-call | flops 240000000 | bytes 8880000 | tf_op jit(solution)/shard_map/product/pallas_call | solution.py:316
  51.5 1.1 %coarse.8 = bf16[10,8,2048]{2,1,0:T(8,128)(2,1)S(1)} custom-call(bf16[12,24,64,128]{3,2,1,0:T(8,128)(2,1)S(1)} %left_factor.1.left_ref, bf16[16,64,640]{2,1,0:T(8,128)(2,1)S(1)} %product.2.refs_0_, bf16[8,64,640]{2,1,0:T(8,128)(2,1)S(1)} %product.3.refs_1_), custom_call_target="tpu_custom_call" | custom-call | flops 100000000 | bytes 3700000 | tf_op jit(solution)/shard_map/coarse/pallas_call | solution.py:363
  52.6 0.7 coarse.11
  53.3 2.4 %collective-permute-done.7 = bf16[10,4,4096]{2,1,0:T(4,128)(2,1)S(1)} collective-permute-done((bf16[10,4,4096]{2,1,0:T(4,128)(2,1)S(1)}, bf16[10,4,4096]{2,1,0:T(4,128)(2,1)S(1)}, u32[]{:S(2)}, u32[]{:S(2)}) %collective-permute-start.7) | collective-permute-done | bytes 327712 | tf_op jit(solution)/shard_map/ppermute | solution.py:452
  55.7 3.9 %collective-permute-start.10 = (bf16[10,4,2048]{2,1,0:T(4,128)(2,1)S(1)}, bf16[10,4,2048]{2,1,0:T(4,128)(2,1)S(1)}, u32[]{:S(2)}, u32[]{:S(2)}) collective-permute-start(bf16[10,4,2048]{2,1,0:T(4,128)(2,1)S(1)} %coarse.11), channel_id=1, source_target_pairs={{4,0},{8,4},{12,8},{16,12},{20,16},{24,20},{28,24},{5,1},{9,5},{13... | collective-permute-start | bytes 491528 | tf_op jit(solution)/shard_map/ppermute | solution.py:452
  59.7 2.0 %collective-permute-start.9 = (bf16[10,8,2048]{2,1,0:T(8,128)(2,1)S(1)}, bf16[10,8,2048]{2,1,0:T(8,128)(2,1)S(1)}, u32[]{:S(2)}, u32[]{:S(2)}) collective-permute-start(bf16[10,8,2048]{2,1,0:T(8,128)(2,1)S(1)} %coarse.8), channel_id=1, source_target_pairs={{0,4},{4,8},{8,12},{12,16},{16,20},{20,24},{24,28},{1,5},{5,9},{9,... | collective-permute-start | bytes 983048 | tf_op jit(solution)/shard_map/ppermute | solution.py:449
  61.7 0.1 fusion.25
  61.9 0.7 coarse.12
  62.6 1.1 %coarse.13 = f32[10,8,2048]{2,1,0:T(8,128)S(1)} custom-call(bf16[12,24,64,128]{3,2,1,0:T(8,128)(2,1)S(1)} %left_factor.1.left_ref, bf16[16,64,640]{2,1,0:T(8,128)(2,1)S(1)} %product.2.refs_0_, bf16[8,64,640]{2,1,0:T(8,128)(2,1)S(1)} %product.3.refs_1_), custom_call_target="tpu_custom_call" | custom-call | flops 100000000 | bytes 3700000 | tf_op jit(solution)/shard_map/coarse/pallas_call | solution.py:363
  63.6 1.1 %coarse.9 = bf16[10,8,2048]{2,1,0:T(8,128)(2,1)S(1)} custom-call(bf16[12,24,64,128]{3,2,1,0:T(8,128)(2,1)S(1)} %left_factor.1.left_ref, bf16[16,64,640]{2,1,0:T(8,128)(2,1)S(1)} %product.2.refs_0_, bf16[8,64,640]{2,1,0:T(8,128)(2,1)S(1)} %product.3.refs_1_), custom_call_target="tpu_custom_call" | custom-call | flops 100000000 | bytes 3700000 | tf_op jit(solution)/shard_map/coarse/pallas_call | solution.py:363
  64.8 1.1 %coarse.10 = f32[10,8,2048]{2,1,0:T(8,128)S(1)} custom-call(bf16[12,24,64,128]{3,2,1,0:T(8,128)(2,1)S(1)} %left_factor.1.left_ref, bf16[16,64,640]{2,1,0:T(8,128)(2,1)S(1)} %product.2.refs_0_, bf16[8,64,640]{2,1,0:T(8,128)(2,1)S(1)} %product.3.refs_1_), custom_call_target="tpu_custom_call" | custom-call | flops 100000000 | bytes 3700000 | tf_op jit(solution)/shard_map/coarse/pallas_call | solution.py:363
  65.9 4.1 %collective-permute-start.12 = (bf16[10,4,2048]{2,1,0:T(4,128)(2,1)S(1)}, bf16[10,4,2048]{2,1,0:T(4,128)(2,1)S(1)}, u32[]{:S(2)}, u32[]{:S(2)}) collective-permute-start(bf16[10,4,2048]{2,1,0:T(4,128)(2,1)S(1)} %coarse.12), channel_id=1, source_target_pairs={{4,0},{8,4},{12,8},{16,12},{20,16},{24,20},{28,24},{5,1},{9,5},{13... | collective-permute-start | bytes 491528 | tf_op jit(solution)/shard_map/ppermute | solution.py:452
  70.0 0.2 pad_maximum_fusion
  70.2 1.4 %collective-permute-done.9 = bf16[10,8,2048]{2,1,0:T(8,128)(2,1)S(1)} collective-permute-done((bf16[10,8,2048]{2,1,0:T(8,128)(2,1)S(1)}, bf16[10,8,2048]{2,1,0:T(8,128)(2,1)S(1)}, u32[]{:S(2)}, u32[]{:S(2)}) %collective-permute-start.9) | collective-permute-done | bytes 327712 | tf_op jit(solution)/shard_map/ppermute | solution.py:449
  71.6 7.6 %collective-permute-start.11 = (bf16[10,8,2048]{2,1,0:T(8,128)(2,1)S(1)}, bf16[10,8,2048]{2,1,0:T(8,128)(2,1)S(1)}, u32[]{:S(2)}, u32[]{:S(2)}) collective-permute-start(bf16[10,8,2048]{2,1,0:T(8,128)(2,1)S(1)} %coarse.9), channel_id=1, source_target_pairs={{0,4},{4,8},{8,12},{12,16},{16,20},{20,24},{24,28},{1,5},{5,9},{9,... | collective-permute-start | bytes 983048 | tf_op jit(solution)/shard_map/ppermute | solution.py:449
  79.2 0.1 add_convert_fusion.1
  79.3 0.7 collective-permute-start.13
  80.1 0.0 collective-permute-done.12
  80.1 0.2 pad_maximum_fusion.1
  80.2 6.5 %collective-permute-done.11 = bf16[10,8,2048]{2,1,0:T(8,128)(2,1)S(1)} collective-permute-done((bf16[10,8,2048]{2,1,0:T(8,128)(2,1)S(1)}, bf16[10,8,2048]{2,1,0:T(8,128)(2,1)S(1)}, u32[]{:S(2)}, u32[]{:S(2)}) %collective-permute-start.11) | collective-permute-done | bytes 327712 | tf_op jit(solution)/shard_map/ppermute | solution.py:449
  86.7 0.1 add_convert_fusion
  86.8 0.7 collective-permute-start.17
  87.6 3.1 %collective-permute-done.13.refs_2_ = bf16[14,8,2048]{2,1,0:T(8,128)(2,1)S(1)} collective-permute-done((bf16[14,8,2048]{2,1,0:T(8,128)(2,1)S(1)}, bf16[14,8,2048]{2,1,0:T(8,128)(2,1)S(1)}, u32[]{:S(2)}, u32[]{:S(2)}) %collective-permute-start.13) | collective-permute-done | bytes 458784 | tf_op jit(solution)/shard_map/ppermute | solution.py:443
  90.7 2.9 %collective-permute-start.14 = (bf16[14,8,2048]{2,1,0:T(8,128)(2,1)S(1)}, bf16[14,8,2048]{2,1,0:T(8,128)(2,1)S(1)}, u32[]{:S(2)}, u32[]{:S(2)}) collective-permute-start(bf16[14,8,2048]{2,1,0:T(8,128)(2,1)S(1)} %bitcast.12), channel_id=1, source_target_pairs={{0,1},{1,0},{2,3},{3,2},{4,5},{5,4},{6,7},{7,6},{8,9},{9,8},{10,11... | collective-permute-start | bytes 1376264 | tf_op jit(solution)/shard_map/ppermute | solution.py:446
  93.6 0.0 collective-permute-start.15
  93.6 0.5 collective-permute-start.16
  94.1 6.4 %collective-permute-done.17.refs_3_ = bf16[14,8,2048]{2,1,0:T(8,128)(2,1)S(1)} collective-permute-done((bf16[14,8,2048]{2,1,0:T(8,128)(2,1)S(1)}, bf16[14,8,2048]{2,1,0:T(8,128)(2,1)S(1)}, u32[]{:S(2)}, u32[]{:S(2)}) %collective-permute-start.17) | collective-permute-done | bytes 458784 | tf_op jit(solution)/shard_map/ppermute | solution.py:443
  100.5 1.7 %collective-permute-start.18 = (bf16[14,8,2048]{2,1,0:T(8,128)(2,1)S(1)}, bf16[14,8,2048]{2,1,0:T(8,128)(2,1)S(1)}, u32[]{:S(2)}, u32[]{:S(2)}) collective-permute-start(bf16[14,8,2048]{2,1,0:T(8,128)(2,1)S(1)} %collective-permute-done.17.refs_3_), channel_id=1, source_target_pairs={{0,1},{1,0},{2,3},{3,2},{4,5},{5,4},{6,7},{7,6},{8,9},{9,8},{10,11... | collective-permute-start | bytes 1376264 | tf_op jit(solution)/shard_map/ppermute | solution.py:446
  102.2 2.3 %assemble.2.refs_0_ = bf16[8,56,4096]{2,1,0:T(8,128)(2,1)} custom-call(bf16[448,448]{1,0:T(8,128)(2,1)S(1)} %fusion.12.order_ref, bf16[14,8,2048]{2,1,0:T(8,128)(2,1)S(1)} %bitcast.13, bf16[14,8,2048]{2,1,0:T(8,128)(2,1)S(1)} %collective-permute-done.14.refs_1_, bf16[14,8,2048]{2,1,0:T(8,128)(2,1)S(1)} %collective-permute-done.13.refs_2_, ...), custom_call_target="tpu_custom_call" | custom-call | flops 290000000 | bytes 10730000 | tf_op jit(solution)/shard_map/assemble/pallas_call | solution.py:398
  104.5 2.4 %assemble.3 = bf16[8,56,4096]{2,1,0:T(8,128)(2,1)} custom-call(bf16[448,448]{1,0:T(8,128)(2,1)S(1)} %fusion.12.order_ref, bf16[8,56,4096]{2,1,0:T(8,128)(2,1)} %assemble.2.refs_0_, bf16[14,8,2048]{2,1,0:T(8,128)(2,1)S(1)} %bitcast.16, bf16[14,8,2048]{2,1,0:T(8,128)(2,1)S(1)} %collective-permute-done.16.refs_2_, ...), custom_call_target="tpu_custom_call", output_to_operand_aliasing={{}: (1, {})} | custom-call | flops 290000000 | bytes 10730000 | tf_op jit(solution)/shard_map/assemble/pallas_call | solution.py:398
  (21 shorter events, 0.1 us)
Async XLA Ops:
  0.0 1.4 %copy-start = (bf16[24,8,4096]{2,1,0:T(8,128)(2,1)S(1)}, bf16[24,8,4096]{2,1,0:T(8,128)(2,1)}, u32[]{:S(2)}) copy-start(bf16[24,8,4096]{2,1,0:T(8,128)(2,1)} %x_ref.4) | copy-start | bytes 4718596
  1.4 5.0 %copy-start.4 = (s32[192,4]{0,1:T(4,128)S(1)}, s32[192,4]{0,1:T(4,128)}, u32[]{:S(2)}) copy-start(s32[192,4]{0,1:T(4,128)} %param.9) | copy-start | bytes 9220
  1.4 8.2 %copy-start.5 = (s32[24,32]{1,0:T(8,128)S(1)}, s32[24,32]{1,0:T(8,128)}, u32[]{:S(2)}) copy-start(s32[24,32]{1,0:T(8,128)} %param.6) | copy-start | bytes 9220
  1.4 8.2 %copy-start.6 = (s32[24]{0:T(128)S(1)}, s32[24]{0:T(128)}, u32[]{:S(2)}) copy-start(s32[24]{0:T(128)} %param.7) | copy-start | bytes 292
  1.4 8.3 %copy-start.1 = (bf16[24,8,4096]{2,1,0:T(8,128)(2,1)S(1)}, bf16[24,8,4096]{2,1,0:T(8,128)(2,1)}, u32[]{:S(2)}) copy-start(bf16[24,8,4096]{2,1,0:T(8,128)(2,1)} %x_ref.4) | copy-start | bytes 4718596
  2.2 4.3 %collective-permute-start = (bf16[16,4,64,128]{3,2,1,0:T(8,128)(2,1)S(1)}, bf16[16,4,64,128]{3,2,1,0:T(8,128)(2,1)}, u32[]{:S(2)}, u32[]{:S(2)}) collective-permute-start(bf16[16,4,64,128]{3,2,1,0:T(8,128)(2,1)S(1)} %relayout.3.refs_0_), channel_id=1, source_target_pairs={{0,1},{1,0},{2,3},{3,2},{4,5},{5,4},{6,7},{7,6},{8,9},{9,8},{10,11... | collective-permute-start | bytes 3145736 | tf_op jit(solution)/shard_map/ppermute | solution.py:446
  3.0 24.8 %collective-permute-start.2 = (bf16[16,4,64,128]{3,2,1,0:T(8,128)(2,1)S(1)}, bf16[16,4,64,128]{3,2,1,0:T(8,128)(2,1)}, u32[]{:S(2)}, u32[]{:S(2)}) collective-permute-start(bf16[16,4,64,128]{3,2,1,0:T(8,128)(2,1)S(1)} %relayout.3.refs_0_), channel_id=1, source_target_pairs={{0,2},{1,3},{2,0},{3,1},{4,6},{5,7},{6,4},{7,5},{8,10},{9,11},{10,... | collective-permute-start | bytes 3145736 | tf_op jit(solution)/shard_map/ppermute | solution.py:443
  4.2 1.1 %copy-start.2 = (bf16[24,4,4096]{2,1,0:T(4,128)(2,1)S(1)}, bf16[24,4,4096]{2,1,0:T(4,128)(2,1)}, u32[]{:S(2)}) copy-start(bf16[24,4,4096]{2,1,0:T(4,128)(2,1)} %x_ref.5) | copy-start | bytes 2359300
  6.6 21.6 %collective-permute-start.1 = (bf16[24,2,64,128]{3,2,1,0:T(8,128)(2,1)S(1)}, bf16[24,2,64,128]{3,2,1,0:T(8,128)(2,1)S(1)}, u32[]{:S(2)}, u32[]{:S(2)}) collective-permute-start(bf16[24,2,64,128]{3,2,1,0:T(8,128)(2,1)S(1)} %relayout_rows.1.refs_0_), channel_id=1, source_target_pairs={{0,4},{2,6},{4,8},{5,1},{6,10},{7,3},{8,12},{9,5},{10,14},{11,7},{... | collective-permute-start | bytes 2359304 | tf_op jit(solution)/shard_map/ppermute | solution.py:440
  10.1 4.9 %collective-permute-start.3 = (bf16[8,4,64,128]{3,2,1,0:T(8,128)(2,1)S(1)}, bf16[8,4,64,128]{3,2,1,0:T(8,128)(2,1)S(1)}, u32[]{:S(2)}, u32[]{:S(2)}) collective-permute-start(bf16[8,4,64,128]{3,2,1,0:T(8,128)(2,1)S(1)} %relayout.4.refs_0_), channel_id=1, source_target_pairs={{0,1},{1,0},{2,3},{3,2},{4,5},{5,4},{6,7},{7,6},{8,9},{9,8},{10,11... | collective-permute-start | bytes 1572872 | tf_op jit(solution)/shard_map/ppermute | solution.py:446
  11.1 4.0 %copy-start.3 = (bf16[24,4,4096]{2,1,0:T(4,128)(2,1)S(1)}, bf16[24,4,4096]{2,1,0:T(4,128)(2,1)}, u32[]{:S(2)}) copy-start(bf16[24,4,4096]{2,1,0:T(4,128)(2,1)} %x_ref.5) | copy-start | bytes 2359300
  28.2 5.3 %collective-permute-start.6 = (bf16[16,4,64,128]{3,2,1,0:T(8,128)(2,1)}, bf16[16,4,64,128]{3,2,1,0:T(8,128)(2,1)S(1)}, u32[]{:S(2)}, u32[]{:S(2)}) collective-permute-start(bf16[16,4,64,128]{3,2,1,0:T(8,128)(2,1)} %collective-permute-done.2.refs_0_), channel_id=1, source_target_pairs={{0,1},{1,0},{2,3},{3,2},{4,5},{5,4},{6,7},{7,6},{8,9},{9,8},{10,11... | collective-permute-start | bytes 3145736 | tf_op jit(solution)/shard_map/ppermute | solution.py:446
  28.7 3.3 %collective-permute-start.5 = (bf16[24,2,64,128]{3,2,1,0:T(8,128)(2,1)S(1)}, bf16[24,2,64,128]{3,2,1,0:T(8,128)(2,1)S(1)}, u32[]{:S(2)}, u32[]{:S(2)}) collective-permute-start(bf16[24,2,64,128]{3,2,1,0:T(8,128)(2,1)S(1)} %collective-permute-done.1.refs_0_), channel_id=1, source_target_pairs={{0,1},{1,0},{2,3},{3,2},{4,5},{5,4},{6,7},{7,6},{8,9},{9,8},{10,11... | collective-permute-start | bytes 2359304 | tf_op jit(solution)/shard_map/ppermute | solution.py:446
  28.7 13.0 %collective-permute-start.4 = (bf16[8,4,64,128]{3,2,1,0:T(8,128)(2,1)S(1)}, bf16[8,4,64,128]{3,2,1,0:T(8,128)(2,1)S(1)}, u32[]{:S(2)}, u32[]{:S(2)}) collective-permute-start(bf16[8,4,64,128]{3,2,1,0:T(8,128)(2,1)S(1)} %relayout.4.refs_0_), channel_id=1, source_target_pairs={{0,2},{1,3},{2,0},{3,1},{4,6},{5,7},{6,4},{7,5},{8,10},{9,11},{10,... | collective-permute-start | bytes 1572872 | tf_op jit(solution)/shard_map/ppermute | solution.py:443
  41.7 6.1 %collective-permute-start.8 = (bf16[8,4,64,128]{3,2,1,0:T(8,128)(2,1)S(1)}, bf16[8,4,64,128]{3,2,1,0:T(8,128)(2,1)S(1)}, u32[]{:S(2)}, u32[]{:S(2)}) collective-permute-start(bf16[8,4,64,128]{3,2,1,0:T(8,128)(2,1)S(1)} %collective-permute-done.4.refs_0_), channel_id=1, source_target_pairs={{0,1},{1,0},{2,3},{3,2},{4,5},{5,4},{6,7},{7,6},{8,9},{9,8},{10,11... | collective-permute-start | bytes 1572872 | tf_op jit(solution)/shard_map/ppermute | solution.py:446
  44.0 11.8 %collective-permute-start.7 = (bf16[10,4,4096]{2,1,0:T(4,128)(2,1)S(1)}, bf16[10,4,4096]{2,1,0:T(4,128)(2,1)S(1)}, u32[]{:S(2)}, u32[]{:S(2)}) collective-permute-start(bf16[10,4,4096]{2,1,0:T(4,128)(2,1)S(1)} %coarse.7), channel_id=1, source_target_pairs={{4,0},{8,4},{12,8},{16,12},{20,16},{24,20},{28,24},{5,1},{9,5},{13... | collective-permute-start | bytes 983048 | tf_op jit(solution)/shard_map/ppermute | solution.py:452
  55.7 10.1 %collective-permute-start.10 = (bf16[10,4,2048]{2,1,0:T(4,128)(2,1)S(1)}, bf16[10,4,2048]{2,1,0:T(4,128)(2,1)S(1)}, u32[]{:S(2)}, u32[]{:S(2)}) collective-permute-start(bf16[10,4,2048]{2,1,0:T(4,128)(2,1)S(1)} %coarse.11), channel_id=1, source_target_pairs={{4,0},{8,4},{12,8},{16,12},{20,16},{24,20},{28,24},{5,1},{9,5},{13... | collective-permute-start | bytes 491528 | tf_op jit(solution)/shard_map/ppermute | solution.py:452
  59.7 11.9 %collective-permute-start.9 = (bf16[10,8,2048]{2,1,0:T(8,128)(2,1)S(1)}, bf16[10,8,2048]{2,1,0:T(8,128)(2,1)S(1)}, u32[]{:S(2)}, u32[]{:S(2)}) collective-permute-start(bf16[10,8,2048]{2,1,0:T(8,128)(2,1)S(1)} %coarse.8), channel_id=1, source_target_pairs={{0,4},{4,8},{8,12},{12,16},{16,20},{20,24},{24,28},{1,5},{5,9},{9,... | collective-permute-start | bytes 983048 | tf_op jit(solution)/shard_map/ppermute | solution.py:449
  65.9 14.2 %collective-permute-start.12 = (bf16[10,4,2048]{2,1,0:T(4,128)(2,1)S(1)}, bf16[10,4,2048]{2,1,0:T(4,128)(2,1)S(1)}, u32[]{:S(2)}, u32[]{:S(2)}) collective-permute-start(bf16[10,4,2048]{2,1,0:T(4,128)(2,1)S(1)} %coarse.12), channel_id=1, source_target_pairs={{4,0},{8,4},{12,8},{16,12},{20,16},{24,20},{28,24},{5,1},{9,5},{13... | collective-permute-start | bytes 491528 | tf_op jit(solution)/shard_map/ppermute | solution.py:452
  71.6 15.1 %collective-permute-start.11 = (bf16[10,8,2048]{2,1,0:T(8,128)(2,1)S(1)}, bf16[10,8,2048]{2,1,0:T(8,128)(2,1)S(1)}, u32[]{:S(2)}, u32[]{:S(2)}) collective-permute-start(bf16[10,8,2048]{2,1,0:T(8,128)(2,1)S(1)} %coarse.9), channel_id=1, source_target_pairs={{0,4},{4,8},{8,12},{12,16},{16,20},{20,24},{24,28},{1,5},{5,9},{9,... | collective-permute-start | bytes 983048 | tf_op jit(solution)/shard_map/ppermute | solution.py:449
  79.3 11.3 %collective-permute-start.13 = (bf16[14,8,2048]{2,1,0:T(8,128)(2,1)S(1)}, bf16[14,8,2048]{2,1,0:T(8,128)(2,1)S(1)}, u32[]{:S(2)}, u32[]{:S(2)}) collective-permute-start(bf16[14,8,2048]{2,1,0:T(8,128)(2,1)S(1)} %bitcast.11), channel_id=1, source_target_pairs={{0,2},{1,3},{2,0},{3,1},{4,6},{5,7},{6,4},{7,5},{8,10},{9,11},{10,... | collective-permute-start | bytes 1376264 | tf_op jit(solution)/shard_map/ppermute | solution.py:443
  86.8 13.7 %collective-permute-start.17 = (bf16[14,8,2048]{2,1,0:T(8,128)(2,1)S(1)}, bf16[14,8,2048]{2,1,0:T(8,128)(2,1)S(1)}, u32[]{:S(2)}, u32[]{:S(2)}) collective-permute-start(bf16[14,8,2048]{2,1,0:T(8,128)(2,1)S(1)} %bitcast.14), channel_id=1, source_target_pairs={{0,2},{1,3},{2,0},{3,1},{4,6},{5,7},{6,4},{7,5},{8,10},{9,11},{10,... | collective-permute-start | bytes 1376264 | tf_op jit(solution)/shard_map/ppermute | solution.py:443
  90.7 9.8 %collective-permute-start.14 = (bf16[14,8,2048]{2,1,0:T(8,128)(2,1)S(1)}, bf16[14,8,2048]{2,1,0:T(8,128)(2,1)S(1)}, u32[]{:S(2)}, u32[]{:S(2)}) collective-permute-start(bf16[14,8,2048]{2,1,0:T(8,128)(2,1)S(1)} %bitcast.12), channel_id=1, source_target_pairs={{0,1},{1,0},{2,3},{3,2},{4,5},{5,4},{6,7},{7,6},{8,9},{9,8},{10,11... | collective-permute-start | bytes 1376264 | tf_op jit(solution)/shard_map/ppermute | solution.py:446
  93.6 8.6 %collective-permute-start.15 = (bf16[14,8,2048]{2,1,0:T(8,128)(2,1)S(1)}, bf16[14,8,2048]{2,1,0:T(8,128)(2,1)S(1)}, u32[]{:S(2)}, u32[]{:S(2)}) collective-permute-start(bf16[14,8,2048]{2,1,0:T(8,128)(2,1)S(1)} %collective-permute-done.13.refs_2_), channel_id=1, source_target_pairs={{0,1},{1,0},{2,3},{3,2},{4,5},{5,4},{6,7},{7,6},{8,9},{9,8},{10,11... | collective-permute-start | bytes 1376264 | tf_op jit(solution)/shard_map/ppermute | solution.py:446
  93.6 10.9 %collective-permute-start.16 = (bf16[14,8,2048]{2,1,0:T(8,128)(2,1)S(1)}, bf16[14,8,2048]{2,1,0:T(8,128)(2,1)S(1)}, u32[]{:S(2)}, u32[]{:S(2)}) collective-permute-start(bf16[14,8,2048]{2,1,0:T(8,128)(2,1)S(1)} %bitcast.15), channel_id=1, source_target_pairs={{0,1},{1,0},{2,3},{3,2},{4,5},{5,4},{6,7},{7,6},{8,9},{9,8},{10,11... | collective-permute-start | bytes 1376264 | tf_op jit(solution)/shard_map/ppermute | solution.py:446
  100.5 4.0 %collective-permute-start.18 = (bf16[14,8,2048]{2,1,0:T(8,128)(2,1)S(1)}, bf16[14,8,2048]{2,1,0:T(8,128)(2,1)S(1)}, u32[]{:S(2)}, u32[]{:S(2)}) collective-permute-start(bf16[14,8,2048]{2,1,0:T(8,128)(2,1)S(1)} %collective-permute-done.17.refs_3_), channel_id=1, source_target_pairs={{0,1},{1,0},{2,3},{3,2},{4,5},{5,4},{6,7},{7,6},{8,9},{9,8},{10,11... | collective-permute-start | bytes 1376264 | tf_op jit(solution)/shard_map/ppermute | solution.py:446

commit v14 on v13

--- a/solution.py
+++ b/solution.py
@@ -433,7 +433,7 @@
     share = CB // ncol
     tiles = (GROUPS * share + 1) // 2
     parts = ((0, rb * 2 // 3), (rb * 2 // 3, rb // 3))
-    chunks = ((0, 32), (32, 64))
+    chunks = ((0, 24), (24, 48), (48, 64))
 
     def outward(x):
         pairs = [(r * ncol + c, (r + 1 - 2 * (c % 2)) * ncol + c) for r in range(nrow) for c in range(ncol)]
@@ -496,24 +496,27 @@
     late.append(downward(lows[1]))
     highs[0], raw[1] = lax.optimization_barrier((highs[0], raw[1]))
     highs.append(upward(raw[1]))
+    late[1], raw[2] = lax.optimization_barrier((late[1], raw[2]))
+    highs.append(upward(raw[2]))
     mids = [coarse_rows(left, aps, ((CB, 2 * CB),), a0, a1, F32, 1.0)[0] for a0, a1 in chunks]
     lower = [
         jnp.concatenate([early[:, :, : cut * BS], late[0]], axis=1),
         jnp.concatenate([early[:, :, cut * BS :], late[1]], axis=1),
     ]
-    totals, fars = [], []
+    totals, sides, fars = [], [], []
     for z, (a0, a1) in enumerate(chunks):
         low = lower[0] if z == 0 else lower[1][:, :, (a0 - cut) * BS : (a1 - cut) * BS]
         total = columns(highs[z], 0) + columns(mids[z], 1) + columns(low, 2)
         total = total.astype(BF).reshape((share * (GROUPS + 2),) + total.shape[2:])
         totals.append(total)
+        sides.append(over_core(total))
         fars.append([over_y(total, s) for s in range(1, ny)])
-    totals, fars[:-1] = lax.optimization_barrier((totals, fars[:-1]))
-    sides = [over_core(x) for x in totals]
+    for z in range(len(chunks) - 1):
+        fars[z], _ = lax.optimization_barrier((fars[z], totals[z + 1]))
     out = None
     for z, (a0, a1) in enumerate(chunks):
         if z == 1:
-            fars[1], sides[0] = lax.optimization_barrier((fars[1], sides[0]))
+            fars[1:], out = lax.optimization_barrier((fars[1:], out))
         srcs = [totals[z], sides[z]] + [q for x in fars[z] for q in (x, over_core(x))]
         out = assemble(order, srcs, a0, BS * BS, out)
     return out

time: 108 us -> 101 us (0.935)
  waiting for transfers between devices: 27.3 us -> 11 us
  starting transfers between devices: 37 us -> 45.6 us
    ppermute x9 -> x11, starting transfers between devices: 8.53 us -> 18.9 us  [over_core(): return lax.ppermute(x, 'col', [(c, c ^ 1) for c in range(ncol)])]
    ppermute x4 -> x5, waiting for transfers between devices: 16 us -> 6.61 us  [over_y(): lax.ppermute(x, 'col', [(y * 2 + c, (y + s) % ny * 2 + c) for y in range(...]
    ppermute x2 -> x3, waiting for transfers between devices: 7.95 us -> 1.71 us  [upward(): return lax.ppermute(x, 'row', [(i, i + 1) for i in range(nrow - 1)])]
    ppermute x3, starting transfers between devices: 11.8 us -> 7.8 us  [downward(): return lax.ppermute(x, 'row', [(i + 1, i) for i in range(nrow - 1)])]
    ppermute x4 -> x5, starting transfers between devices: 3.96 us -> 5.73 us  [over_y(): lax.ppermute(x, 'col', [(y * 2 + c, (y + s) % ny * 2 + c) for y in range(...]
    ppermute x3, waiting for transfers between devices: 2.41 us -> 1.01 us  [downward(): return lax.ppermute(x, 'row', [(i + 1, i) for i in range(nrow - 1)])]
    pallas_call x2 -> x3, Pallas kernels: 4.7 us -> 5.47 us  [assemble(): pl.pallas_call(assemble_kernel, grid=(per,), out_shape=jax.ShapeDtypeStru...]
    ppermute x2 -> x3, starting transfers between devices: 9.64 us -> 10.1 us  [upward(): return lax.ppermute(x, 'row', [(i, i + 1) for i in range(nrow - 1)])]
  transfers between devices with their start and end apart: 19 -> 23, of which waited for: 9 -> 8; matrix products, arithmetic and copies ran while one was open for 1% -> 1% of each run, Pallas kernels for 33% -> 37%
where the time goes in v14:
time: 101 us; the launch traced here: 99.6 us
  starting transfers between devices  45.6 us (45%)
  Pallas kernels  39 us (39%)
  waiting for transfers between devices  11 us (11%)
  local copies, waits for them, and re-layouts  2.64 us (3%)
    ppermute x11, starting transfers between devices, over_core(): return lax.ppermute(x, 'col', [(c, c ^ 1) for c in range(ncol)])  18.9 us
    pallas_call x2, Pallas kernels, product(): pl.pallas_call(functools.partial(product_kernel, first, rb, shifts), out_...  10.9 us
    ppermute x3, starting transfers between devices, upward(): return lax.ppermute(x, 'row', [(i, i + 1) for i in range(nrow - 1)])  10.1 us
    ppermute x3, starting transfers between devices, downward(): return lax.ppermute(x, 'row', [(i + 1, i) for i in range(nrow - 1)])  7.8 us
    ppermute x5, waiting for transfers between devices, over_y(): lax.ppermute(x, 'col', [(y * 2 + c, (y + s) % ny * 2 + c) for y in range(...  6.61 us
    pallas_call x9, Pallas kernels, coarse_rows(): pl.pallas_call(functools.partial(coarse_kernel, sets, a0, a1), out_shape=...  6.26 us
    pallas_call x2, Pallas kernels, near_band(): pl.pallas_call(functools.partial(band_kernel, first, shifts), out_shape=j...  5.98 us
    ppermute x5, starting transfers between devices, over_y(): lax.ppermute(x, 'col', [(y * 2 + c, (y + s) % ny * 2 + c) for y in range(...  5.73 us
  transfers between devices with their start and end apart: 23, of which 8 were waited for; matrix products, arithmetic and copies ran while one was open for 1% of the time, Pallas kernels for 37%

profile of v14, /device:TPU:9, one launch (start us, length us, event | category | flops | bytes accessed | tf_op | source)
XLA Modules:
  0.0 99.6 jit_solution(4183119583009046836)
XLA Ops:
  0.0 1.4 %copy-done = bf16[24,8,4096]{2,1,0:T(8,128)(2,1)S(1)} copy-done((bf16[24,8,4096]{2,1,0:T(8,128)(2,1)S(1)}, bf16[24,8,4096]{2,1,0:T(8,128)(2,1)}, u32[]{:S(2)}) %copy-start) | copy-done | bytes 1572888
  1.4 0.8 relayout.3.refs_0_
  2.2 0.7 collective-permute-start
  3.0 1.3 %collective-permute-start.2 = (bf16[16,4,64,128]{3,2,1,0:T(8,128)(2,1)S(1)}, bf16[16,4,64,128]{3,2,1,0:T(8,128)(2,1)}, u32[]{:S(2)}, u32[]{:S(2)}) collective-permute-start(bf16[16,4,64,128]{3,2,1,0:T(8,128)(2,1)S(1)} %relayout.3.refs_0_), channel_id=1, source_target_pairs={{0,2},{1,3},{2,0},{3,1},{4,6},{5,7},{6,4},{7,5},{8,10},{9,11},{10,... | collective-permute-start | bytes 3145736 | tf_op jit(solution)/shard_map/ppermute | solution.py:443
  4.2 1.1 %copy-done.2 = bf16[24,4,4096]{2,1,0:T(4,128)(2,1)S(1)} copy-done((bf16[24,4,4096]{2,1,0:T(4,128)(2,1)S(1)}, bf16[24,4,4096]{2,1,0:T(4,128)(2,1)}, u32[]{:S(2)}) %copy-start.2) | copy-done | bytes 786456
  5.4 1.1 %relayout_rows.1.refs_0_ = bf16[24,2,64,128]{3,2,1,0:T(8,128)(2,1)S(1)} custom-call(bf16[24,4,4096]{2,1,0:T(4,128)(2,1)S(1)} %copy-done.2), custom_call_target="tpu_custom_call" | custom-call | flops 100000000 | bytes 3700000 | tf_op jit(solution)/shard_map/relayout_rows/pallas_call | solution.py:84
  6.5 0.1 add_select_fusion.4.table_ref
  6.6 3.0 %collective-permute-start.1 = (bf16[24,2,64,128]{3,2,1,0:T(8,128)(2,1)S(1)}, bf16[24,2,64,128]{3,2,1,0:T(8,128)(2,1)S(1)}, u32[]{:S(2)}, u32[]{:S(2)}) collective-permute-start(bf16[24,2,64,128]{3,2,1,0:T(8,128)(2,1)S(1)} %relayout_rows.1.refs_0_), channel_id=1, source_target_pairs={{0,4},{2,6},{4,8},{5,1},{6,10},{7,3},{8,12},{9,5},{10,14},{11,7},{... | collective-permute-start | bytes 2359304 | tf_op jit(solution)/shard_map/ppermute | solution.py:440
  9.6 0.1 subtract_select_fusion.place_ref
  9.7 0.4 relayout.4.refs_0_
  10.1 0.8 collective-permute-start.3
  10.9 0.2 fusion.12.order_ref
  11.1 3.9 %near_band.2.start_ref = bf16[4,27,256,128]{3,2,1,0:T(8,128)(2,1)S(1)} custom-call(s32[24,32]{1,0:T(8,128)S(1)} %subtract_select_fusion.place_ref, bf16[16,4,64,128]{3,2,1,0:T(8,128)(2,1)S(1)} %relayout.3.refs_0_, bf16[16,4,64,128]{3,2,1,0:T(8,128)(2,1)} %collective-permute-done.refs_1_), custom_call_target="tpu_custom_call" | custom-call | flops 256000000 | bytes 9472000 | tf_op jit(solution)/shard_map/near_band/pallas_call | solution.py:272
  15.1 0.9 relayout.5.pl_ref
  16.0 2.1 %near_band.3.start_ref = bf16[2,27,256,128]{3,2,1,0:T(8,128)(2,1)S(1)} custom-call(s32[24,32]{1,0:T(8,128)S(1)} %subtract_select_fusion.place_ref, bf16[8,4,64,128]{3,2,1,0:T(8,128)(2,1)S(1)} %relayout.4.refs_0_, bf16[8,4,64,128]{3,2,1,0:T(8,128)(2,1)S(1)} %collective-permute-done.3.refs_1_), custom_call_target="tpu_custom_call" | custom-call | flops 128000000 | bytes 4736000 | tf_op jit(solution)/shard_map/near_band/pallas_call | solution.py:272
  18.0 1.4 %right_factor.3.own_ref = bf16[6,5,256,128]{3,2,1,0:T(8,128)(2,1)S(1)} custom-call(s32[4,72]{1,0:T(4,128)S(1)} %add_select_fusion.4.table_ref, bf16[24,2,64,128]{3,2,1,0:T(8,128)(2,1)S(1)} %relayout_rows.1.refs_0_), custom_call_target="tpu_custom_call" | custom-call | flops 140000000 | bytes 5180000 | tf_op jit(solution)/shard_map/right_factor/pallas_call | solution.py:203
  19.4 2.9 %left_factor.1.left_ref = bf16[12,24,64,128]{3,2,1,0:T(8,128)(2,1)S(1)} custom-call(s32[4,192]{1,0:T(4,128)S(1)} %bitcast.26, bf16[24,2,64,128]{3,2,1,0:T(8,128)(2,1)S(1)} %relayout.5.pl_ref), custom_call_target="tpu_custom_call" | custom-call | flops 290000000 | bytes 10730000 | tf_op jit(solution)/shard_map/left_factor/pallas_call | solution.py:118
  22.3 5.5 %collective-permute-done.2.refs_0_ = bf16[16,4,64,128]{3,2,1,0:T(8,128)(2,1)} collective-permute-done((bf16[16,4,64,128]{3,2,1,0:T(8,128)(2,1)S(1)}, bf16[16,4,64,128]{3,2,1,0:T(8,128)(2,1)}, u32[]{:S(2)}, u32[]{:S(2)}) %collective-permute-start.2) | collective-permute-done | bytes 1048608 | tf_op jit(solution)/shard_map/ppermute | solution.py:443
  27.8 0.3 collective-permute-done.1.refs_0_
  28.2 0.5 collective-permute-start.6
  28.7 1.2 %collective-permute-start.4 = (bf16[8,4,64,128]{3,2,1,0:T(8,128)(2,1)S(1)}, bf16[8,4,64,128]{3,2,1,0:T(8,128)(2,1)S(1)}, u32[]{:S(2)}, u32[]{:S(2)}) collective-permute-start(bf16[8,4,64,128]{3,2,1,0:T(8,128)(2,1)S(1)} %relayout.4.refs_0_), channel_id=1, source_target_pairs={{0,2},{1,3},{2,0},{3,1},{4,6},{5,7},{6,4},{7,5},{8,10},{9,11},{10,... | collective-permute-start | bytes 1572872 | tf_op jit(solution)/shard_map/ppermute | solution.py:443
  29.9 1.4 %right_factor.4.refs_0_ = bf16[6,5,256,128]{3,2,1,0:T(8,128)(2,1)S(1)} custom-call(s32[4,72]{1,0:T(4,128)S(1)} %add_select_fusion.4.table_ref, bf16[24,2,64,128]{3,2,1,0:T(8,128)(2,1)S(1)} %collective-permute-done.1.refs_0_), custom_call_target="tpu_custom_call" | custom-call | flops 120000000 | bytes 4440000 | tf_op jit(solution)/shard_map/right_factor/pallas_call | solution.py:203
  31.4 0.6 collective-permute-done.5.refs_1_
  32.0 1.5 %right_factor.5.near_ref = bf16[12,5,256,128]{3,2,1,0:T(8,128)(2,1)S(1)} custom-call(s32[4,72]{1,0:T(4,128)S(1)} %add_select_fusion.4.table_ref, bf16[6,5,256,128]{3,2,1,0:T(8,128)(2,1)S(1)} %right_factor.4.refs_0_, bf16[24,2,64,128]{3,2,1,0:T(8,128)(2,1)S(1)} %collective-permute-done.5.refs_1_), custom_call_target="tpu_custom_call" | custom-call | flops 140000000 | bytes 5180000 | tf_op jit(solution)/shard_map/right_factor/pallas_call | solution.py:203
  33.5 7.1 %product.2.refs_0_ = bf16[16,64,640]{2,1,0:T(8,128)(2,1)S(1)} custom-call(s32[24,32]{1,0:T(8,128)S(1)} %subtract_select_fusion.place_ref, bf16[6,5,256,128]{3,2,1,0:T(8,128)(2,1)S(1)} %right_factor.3.own_ref, bf16[12,5,256,128]{3,2,1,0:T(8,128)(2,1)S(1)} %right_factor.5.near_ref, bf16[4,27,256,128]{3,2,1,0:T(8,128)(2,1)S(1)} %near_band.2.start_ref, ...), custom_call_target="tpu_custom_call" | custom-call | flops 480000000 | bytes 17760000 | tf_op jit(solution)/shard_map/product/pallas_call | solution.py:316
  40.6 1.0 %collective-permute-done.4.refs_0_ = bf16[8,4,64,128]{3,2,1,0:T(8,128)(2,1)S(1)} collective-permute-done((bf16[8,4,64,128]{3,2,1,0:T(8,128)(2,1)S(1)}, bf16[8,4,64,128]{3,2,1,0:T(8,128)(2,1)S(1)}, u32[]{:S(2)}, u32[]{:S(2)}) %collective-permute-start.4) | collective-permute-done | bytes 524320 | tf_op jit(solution)/shard_map/ppermute | solution.py:443
  41.7 1.4 %collective-permute-start.8 = (bf16[8,4,64,128]{3,2,1,0:T(8,128)(2,1)S(1)}, bf16[8,4,64,128]{3,2,1,0:T(8,128)(2,1)S(1)}, u32[]{:S(2)}, u32[]{:S(2)}) collective-permute-start(bf16[8,4,64,128]{3,2,1,0:T(8,128)(2,1)S(1)} %collective-permute-done.4.refs_0_), channel_id=1, source_target_pairs={{0,1},{1,0},{2,3},{3,2},{4,5},{5,4},{6,7},{7,6},{8,9},{9,8},{10,11... | collective-permute-start | bytes 1572872 | tf_op jit(solution)/shard_map/ppermute | solution.py:446
  43.0 0.9 coarse.9
  44.0 3.8 %collective-permute-start.7 = (bf16[10,4,4096]{2,1,0:T(4,128)(2,1)S(1)}, bf16[10,4,4096]{2,1,0:T(4,128)(2,1)S(1)}, u32[]{:S(2)}, u32[]{:S(2)}) collective-permute-start(bf16[10,4,4096]{2,1,0:T(4,128)(2,1)S(1)} %coarse.9), channel_id=1, source_target_pairs={{4,0},{8,4},{12,8},{16,12},{20,16},{24,20},{28,24},{5,1},{9,5},{13... | collective-permute-start | bytes 983048 | tf_op jit(solution)/shard_map/ppermute | solution.py:452
  47.7 3.7 %product.3.refs_1_ = bf16[8,64,640]{2,1,0:T(8,128)(2,1)S(1)} custom-call(s32[24,32]{1,0:T(8,128)S(1)} %subtract_select_fusion.place_ref, bf16[6,5,256,128]{3,2,1,0:T(8,128)(2,1)S(1)} %right_factor.3.own_ref, bf16[12,5,256,128]{3,2,1,0:T(8,128)(2,1)S(1)} %right_factor.5.near_ref, bf16[2,27,256,128]{3,2,1,0:T(8,128)(2,1)S(1)} %near_band.3.start_ref, ...), custom_call_target="tpu_custom_call" | custom-call | flops 240000000 | bytes 8880000 | tf_op jit(solution)/shard_map/product/pallas_call | solution.py:316
  51.5 0.6 coarse.13
  52.1 1.9 %collective-permute-start.11 = (bf16[10,4,1536]{2,1,0:T(4,128)(2,1)S(1)}, bf16[10,4,1536]{2,1,0:T(4,128)(2,1)S(1)}, u32[]{:S(2)}, u32[]{:S(2)}) collective-permute-start(bf16[10,4,1536]{2,1,0:T(4,128)(2,1)S(1)} %coarse.13), channel_id=1, source_target_pairs={{4,0},{8,4},{12,8},{16,12},{20,16},{24,20},{28,24},{5,1},{9,5},{13... | collective-permute-start | bytes 368648 | tf_op jit(solution)/shard_map/ppermute | solution.py:452
  54.0 0.7 coarse.10
  54.7 1.0 %collective-permute-done.7 = bf16[10,4,4096]{2,1,0:T(4,128)(2,1)S(1)} collective-permute-done((bf16[10,4,4096]{2,1,0:T(4,128)(2,1)S(1)}, bf16[10,4,4096]{2,1,0:T(4,128)(2,1)S(1)}, u32[]{:S(2)}, u32[]{:S(2)}) %collective-permute-start.7) | collective-permute-done | bytes 327712 | tf_op jit(solution)/shard_map/ppermute | solution.py:452
  55.7 4.0 %collective-permute-start.9 = (bf16[10,8,1536]{2,1,0:T(8,128)(2,1)S(1)}, bf16[10,8,1536]{2,1,0:T(8,128)(2,1)S(1)}, u32[]{:S(2)}, u32[]{:S(2)}) collective-permute-start(bf16[10,8,1536]{2,1,0:T(8,128)(2,1)S(1)} %coarse.10), channel_id=1, source_target_pairs={{0,4},{4,8},{8,12},{12,16},{16,20},{20,24},{24,28},{1,5},{5,9},{9,... | collective-permute-start | bytes 737288 | tf_op jit(solution)/shard_map/ppermute | solution.py:449
  59.8 0.7 coarse.14
  60.5 0.7 coarse.17
  61.2 0.7 coarse.11
  61.9 0.6 coarse.15
  62.5 0.7 coarse.12
  63.3 0.1 slice.12
  63.4 0.6 coarse.16
  64.0 2.1 %collective-permute-start.12 = (bf16[10,4,2560]{2,1,0:T(4,128)(2,1)S(1)}, bf16[10,4,2560]{2,1,0:T(4,128)(2,1)S(1)}, u32[]{:S(2)}, u32[]{:S(2)}) collective-permute-start(bf16[10,4,2560]{2,1,0:T(4,128)(2,1)S(1)} %coarse.14), channel_id=1, source_target_pairs={{4,0},{8,4},{12,8},{16,12},{20,16},{24,20},{28,24},{5,1},{9,5},{13... | collective-permute-start | bytes 614408 | tf_op jit(solution)/shard_map/ppermute | solution.py:452
  66.1 0.1 pad_maximum_fusion
  66.3 3.2 %collective-permute-start.10 = (bf16[10,8,1536]{2,1,0:T(8,128)(2,1)S(1)}, bf16[10,8,1536]{2,1,0:T(8,128)(2,1)S(1)}, u32[]{:S(2)}, u32[]{:S(2)}) collective-permute-start(bf16[10,8,1536]{2,1,0:T(8,128)(2,1)S(1)} %coarse.11), channel_id=1, source_target_pairs={{0,4},{4,8},{8,12},{12,16},{16,20},{20,24},{24,28},{1,5},{5,9},{9,... | collective-permute-start | bytes 737288 | tf_op jit(solution)/shard_map/ppermute | solution.py:449
  69.4 0.1 add_convert_fusion
  69.5 0.7 collective-permute-start.17
  70.2 2.2 %collective-permute-start.16 = (bf16[14,8,1536]{2,1,0:T(8,128)(2,1)S(1)}, bf16[14,8,1536]{2,1,0:T(8,128)(2,1)S(1)}, u32[]{:S(2)}, u32[]{:S(2)}) collective-permute-start(bf16[14,8,1536]{2,1,0:T(8,128)(2,1)S(1)} %bitcast.19), channel_id=1, source_target_pairs={{0,1},{1,0},{2,3},{3,2},{4,5},{5,4},{6,7},{7,6},{8,9},{9,8},{10,11... | collective-permute-start | bytes 1032200 | tf_op jit(solution)/shard_map/ppermute | solution.py:446
  72.4 2.9 %collective-permute-start.14 = (bf16[10,8,1024]{2,1,0:T(8,128)(2,1)S(1)}, bf16[10,8,1024]{2,1,0:T(8,128)(2,1)S(1)}, u32[]{:S(2)}, u32[]{:S(2)}) collective-permute-start(bf16[10,8,1024]{2,1,0:T(8,128)(2,1)S(1)} %coarse.15), channel_id=1, source_target_pairs={{0,4},{4,8},{8,12},{12,16},{16,20},{20,24},{24,28},{1,5},{5,9},{9,... | collective-permute-start | bytes 491528 | tf_op jit(solution)/shard_map/ppermute | solution.py:449
  75.3 0.1 fusion.13
  75.5 1.7 %collective-permute-done.10 = bf16[10,8,1536]{2,1,0:T(8,128)(2,1)S(1)} collective-permute-done((bf16[10,8,1536]{2,1,0:T(8,128)(2,1)S(1)}, bf16[10,8,1536]{2,1,0:T(8,128)(2,1)S(1)}, u32[]{:S(2)}, u32[]{:S(2)}) %collective-permute-start.10) | collective-permute-done | bytes 245792 | tf_op jit(solution)/shard_map/ppermute | solution.py:449
  77.2 0.1 add_convert_fusion.1
  77.2 0.8 collective-permute-start.13
  78.0 4.7 %collective-permute-start.18 = (bf16[14,8,1536]{2,1,0:T(8,128)(2,1)S(1)}, bf16[14,8,1536]{2,1,0:T(8,128)(2,1)S(1)}, u32[]{:S(2)}, u32[]{:S(2)}) collective-permute-start(bf16[14,8,1536]{2,1,0:T(8,128)(2,1)S(1)} %collective-permute-done.17.refs_2_), channel_id=1, source_target_pairs={{0,1},{1,0},{2,3},{3,2},{4,5},{5,4},{6,7},{7,6},{8,9},{9,8},{10,11... | collective-permute-start | bytes 1032200 | tf_op jit(solution)/shard_map/ppermute | solution.py:446
  82.7 0.1 pad_maximum_fusion.1
  82.8 1.7 %collective-permute-start.15 = (bf16[14,8,1024]{2,1,0:T(8,128)(2,1)S(1)}, bf16[14,8,1024]{2,1,0:T(8,128)(2,1)S(1)}, u32[]{:S(2)}, u32[]{:S(2)}) collective-permute-start(bf16[14,8,1024]{2,1,0:T(8,128)(2,1)S(1)} %bitcast.22), channel_id=1, source_target_pairs={{0,2},{1,3},{2,0},{3,1},{4,6},{5,7},{6,4},{7,5},{8,10},{9,11},{10,... | collective-permute-start | bytes 688136 | tf_op jit(solution)/shard_map/ppermute | solution.py:443
  84.6 4.1 %collective-permute-start.19 = (bf16[14,8,1536]{2,1,0:T(8,128)(2,1)S(1)}, bf16[14,8,1536]{2,1,0:T(8,128)(2,1)S(1)}, u32[]{:S(2)}, u32[]{:S(2)}) collective-permute-start(bf16[14,8,1536]{2,1,0:T(8,128)(2,1)S(1)} %bitcast.16), channel_id=1, source_target_pairs={{0,1},{1,0},{2,3},{3,2},{4,5},{5,4},{6,7},{7,6},{8,9},{9,8},{10,11... | collective-permute-start | bytes 1032200 | tf_op jit(solution)/shard_map/ppermute | solution.py:446
  88.7 2.0 %assemble.3.refs_0_ = bf16[8,56,4096]{2,1,0:T(8,128)(2,1)} custom-call(bf16[448,448]{1,0:T(8,128)(2,1)S(1)} %fusion.12.order_ref, bf16[14,8,1536]{2,1,0:T(8,128)(2,1)S(1)} %bitcast.20, bf16[14,8,1536]{2,1,0:T(8,128)(2,1)S(1)} %collective-permute-done.16.refs_1_, bf16[14,8,1536]{2,1,0:T(8,128)(2,1)S(1)} %collective-permute-done.17.refs_2_, ...), custom_call_target="tpu_custom_call" | custom-call | flops 290000000 | bytes 10730000 | tf_op jit(solution)/shard_map/assemble/pallas_call | solution.py:398
  90.6 0.1 collective-permute-done.15.refs_3_
  90.7 4.0 %collective-permute-start.20 = (bf16[14,8,1536]{2,1,0:T(8,128)(2,1)S(1)}, bf16[14,8,1536]{2,1,0:T(8,128)(2,1)S(1)}, u32[]{:S(2)}, u32[]{:S(2)}) collective-permute-start(bf16[14,8,1536]{2,1,0:T(8,128)(2,1)S(1)} %collective-permute-done.13.refs_3_), channel_id=1, source_target_pairs={{0,1},{1,0},{2,3},{3,2},{4,5},{5,4},{6,7},{7,6},{8,9},{9,8},{10,11... | collective-permute-start | bytes 1032200 | tf_op jit(solution)/shard_map/ppermute | solution.py:446
  94.8 0.5 collective-permute-start.22
  95.3 0.8 collective-permute-done.20.refs_4_
  96.0 2.0 %assemble.4.refs_0_ = bf16[8,56,4096]{2,1,0:T(8,128)(2,1)} custom-call(bf16[448,448]{1,0:T(8,128)(2,1)S(1)} %fusion.12.order_ref, bf16[8,56,4096]{2,1,0:T(8,128)(2,1)} %assemble.3.refs_0_, bf16[14,8,1536]{2,1,0:T(8,128)(2,1)S(1)} %bitcast.17, bf16[14,8,1536]{2,1,0:T(8,128)(2,1)S(1)} %collective-permute-done.19.refs_2_, ...), custom_call_target="tpu_custom_call", output_to_operand_aliasing={{}: (1, {})} | custom-call | flops 290000000 | bytes 10730000 | tf_op jit(solution)/shard_map/assemble/pallas_call | solution.py:398
  98.0 1.6 %assemble.5 = bf16[8,56,4096]{2,1,0:T(8,128)(2,1)} custom-call(bf16[448,448]{1,0:T(8,128)(2,1)S(1)} %fusion.12.order_ref, bf16[8,56,4096]{2,1,0:T(8,128)(2,1)} %assemble.4.refs_0_, bf16[14,8,1024]{2,1,0:T(8,128)(2,1)S(1)} %bitcast.24, bf16[14,8,1024]{2,1,0:T(8,128)(2,1)S(1)} %collective-permute-done.21.refs_2_, ...), custom_call_target="tpu_custom_call", output_to_operand_aliasing={{}: (1, {})} | custom-call | flops 290000000 | bytes 10730000 | tf_op jit(solution)/shard_map/assemble/pallas_call | solution.py:398
  (38 shorter events, 0.2 us)
Async XLA Ops:
  0.0 1.4 %copy-start = (bf16[24,8,4096]{2,1,0:T(8,128)(2,1)S(1)}, bf16[24,8,4096]{2,1,0:T(8,128)(2,1)}, u32[]{:S(2)}) copy-start(bf16[24,8,4096]{2,1,0:T(8,128)(2,1)} %x_ref.4) | copy-start | bytes 4718596
  1.4 5.0 %copy-start.4 = (s32[192,4]{0,1:T(4,128)S(1)}, s32[192,4]{0,1:T(4,128)}, u32[]{:S(2)}) copy-start(s32[192,4]{0,1:T(4,128)} %param.9) | copy-start | bytes 9220
  1.4 8.2 %copy-start.6 = (s32[24,32]{1,0:T(8,128)S(1)}, s32[24,32]{1,0:T(8,128)}, u32[]{:S(2)}) copy-start(s32[24,32]{1,0:T(8,128)} %param.6) | copy-start | bytes 9220
  1.4 8.2 %copy-start.7 = (s32[24]{0:T(128)S(1)}, s32[24]{0:T(128)}, u32[]{:S(2)}) copy-start(s32[24]{0:T(128)} %param.7) | copy-start | bytes 292
  1.4 8.3 %copy-start.1 = (bf16[24,8,4096]{2,1,0:T(8,128)(2,1)S(1)}, bf16[24,8,4096]{2,1,0:T(8,128)(2,1)}, u32[]{:S(2)}) copy-start(bf16[24,8,4096]{2,1,0:T(8,128)(2,1)} %x_ref.4) | copy-start | bytes 4718596
  2.2 4.3 %collective-permute-start = (bf16[16,4,64,128]{3,2,1,0:T(8,128)(2,1)S(1)}, bf16[16,4,64,128]{3,2,1,0:T(8,128)(2,1)}, u32[]{:S(2)}, u32[]{:S(2)}) collective-permute-start(bf16[16,4,64,128]{3,2,1,0:T(8,128)(2,1)S(1)} %relayout.3.refs_0_), channel_id=1, source_target_pairs={{0,1},{1,0},{2,3},{3,2},{4,5},{5,4},{6,7},{7,6},{8,9},{9,8},{10,11... | collective-permute-start | bytes 3145736 | tf_op jit(solution)/shard_map/ppermute | solution.py:446
  3.0 24.8 %collective-permute-start.2 = (bf16[16,4,64,128]{3,2,1,0:T(8,128)(2,1)S(1)}, bf16[16,4,64,128]{3,2,1,0:T(8,128)(2,1)}, u32[]{:S(2)}, u32[]{:S(2)}) collective-permute-start(bf16[16,4,64,128]{3,2,1,0:T(8,128)(2,1)S(1)} %relayout.3.refs_0_), channel_id=1, source_target_pairs={{0,2},{1,3},{2,0},{3,1},{4,6},{5,7},{6,4},{7,5},{8,10},{9,11},{10,... | collective-permute-start | bytes 3145736 | tf_op jit(solution)/shard_map/ppermute | solution.py:443
  4.2 1.1 %copy-start.2 = (bf16[24,4,4096]{2,1,0:T(4,128)(2,1)S(1)}, bf16[24,4,4096]{2,1,0:T(4,128)(2,1)}, u32[]{:S(2)}) copy-start(bf16[24,4,4096]{2,1,0:T(4,128)(2,1)} %x_ref.5) | copy-start | bytes 2359300
  6.6 21.6 %collective-permute-start.1 = (bf16[24,2,64,128]{3,2,1,0:T(8,128)(2,1)S(1)}, bf16[24,2,64,128]{3,2,1,0:T(8,128)(2,1)S(1)}, u32[]{:S(2)}, u32[]{:S(2)}) collective-permute-start(bf16[24,2,64,128]{3,2,1,0:T(8,128)(2,1)S(1)} %relayout_rows.1.refs_0_), channel_id=1, source_target_pairs={{0,4},{2,6},{4,8},{5,1},{6,10},{7,3},{8,12},{9,5},{10,14},{11,7},{... | collective-permute-start | bytes 2359304 | tf_op jit(solution)/shard_map/ppermute | solution.py:440
  10.1 4.9 %collective-permute-start.3 = (bf16[8,4,64,128]{3,2,1,0:T(8,128)(2,1)S(1)}, bf16[8,4,64,128]{3,2,1,0:T(8,128)(2,1)S(1)}, u32[]{:S(2)}, u32[]{:S(2)}) collective-permute-start(bf16[8,4,64,128]{3,2,1,0:T(8,128)(2,1)S(1)} %relayout.4.refs_0_), channel_id=1, source_target_pairs={{0,1},{1,0},{2,3},{3,2},{4,5},{5,4},{6,7},{7,6},{8,9},{9,8},{10,11... | collective-permute-start | bytes 1572872 | tf_op jit(solution)/shard_map/ppermute | solution.py:446
  11.1 4.0 %copy-start.3 = (bf16[24,4,4096]{2,1,0:T(4,128)(2,1)S(1)}, bf16[24,4,4096]{2,1,0:T(4,128)(2,1)}, u32[]{:S(2)}) copy-start(bf16[24,4,4096]{2,1,0:T(4,128)(2,1)} %x_ref.5) | copy-start | bytes 2359300
  28.2 5.3 %collective-permute-start.6 = (bf16[16,4,64,128]{3,2,1,0:T(8,128)(2,1)}, bf16[16,4,64,128]{3,2,1,0:T(8,128)(2,1)S(1)}, u32[]{:S(2)}, u32[]{:S(2)}) collective-permute-start(bf16[16,4,64,128]{3,2,1,0:T(8,128)(2,1)} %collective-permute-done.2.refs_0_), channel_id=1, source_target_pairs={{0,1},{1,0},{2,3},{3,2},{4,5},{5,4},{6,7},{7,6},{8,9},{9,8},{10,11... | collective-permute-start | bytes 3145736 | tf_op jit(solution)/shard_map/ppermute | solution.py:446
  28.7 3.3 %collective-permute-start.5 = (bf16[24,2,64,128]{3,2,1,0:T(8,128)(2,1)S(1)}, bf16[24,2,64,128]{3,2,1,0:T(8,128)(2,1)S(1)}, u32[]{:S(2)}, u32[]{:S(2)}) collective-permute-start(bf16[24,2,64,128]{3,2,1,0:T(8,128)(2,1)S(1)} %collective-permute-done.1.refs_0_), channel_id=1, source_target_pairs={{0,1},{1,0},{2,3},{3,2},{4,5},{5,4},{6,7},{7,6},{8,9},{9,8},{10,11... | collective-permute-start | bytes 2359304 | tf_op jit(solution)/shard_map/ppermute | solution.py:446
  28.7 13.0 %collective-permute-start.4 = (bf16[8,4,64,128]{3,2,1,0:T(8,128)(2,1)S(1)}, bf16[8,4,64,128]{3,2,1,0:T(8,128)(2,1)S(1)}, u32[]{:S(2)}, u32[]{:S(2)}) collective-permute-start(bf16[8,4,64,128]{3,2,1,0:T(8,128)(2,1)S(1)} %relayout.4.refs_0_), channel_id=1, source_target_pairs={{0,2},{1,3},{2,0},{3,1},{4,6},{5,7},{6,4},{7,5},{8,10},{9,11},{10,... | collective-permute-start | bytes 1572872 | tf_op jit(solution)/shard_map/ppermute | solution.py:443
  41.7 6.1 %collective-permute-start.8 = (bf16[8,4,64,128]{3,2,1,0:T(8,128)(2,1)S(1)}, bf16[8,4,64,128]{3,2,1,0:T(8,128)(2,1)S(1)}, u32[]{:S(2)}, u32[]{:S(2)}) collective-permute-start(bf16[8,4,64,128]{3,2,1,0:T(8,128)(2,1)S(1)} %collective-permute-done.4.refs_0_), channel_id=1, source_target_pairs={{0,1},{1,0},{2,3},{3,2},{4,5},{5,4},{6,7},{7,6},{8,9},{9,8},{10,11... | collective-permute-start | bytes 1572872 | tf_op jit(solution)/shard_map/ppermute | solution.py:446
  44.0 11.8 %collective-permute-start.7 = (bf16[10,4,4096]{2,1,0:T(4,128)(2,1)S(1)}, bf16[10,4,4096]{2,1,0:T(4,128)(2,1)S(1)}, u32[]{:S(2)}, u32[]{:S(2)}) collective-permute-start(bf16[10,4,4096]{2,1,0:T(4,128)(2,1)S(1)} %coarse.9), channel_id=1, source_target_pairs={{4,0},{8,4},{12,8},{16,12},{20,16},{24,20},{28,24},{5,1},{9,5},{13... | collective-permute-start | bytes 983048 | tf_op jit(solution)/shard_map/ppermute | solution.py:452
  52.1 11.9 %collective-permute-start.11 = (bf16[10,4,1536]{2,1,0:T(4,128)(2,1)S(1)}, bf16[10,4,1536]{2,1,0:T(4,128)(2,1)S(1)}, u32[]{:S(2)}, u32[]{:S(2)}) collective-permute-start(bf16[10,4,1536]{2,1,0:T(4,128)(2,1)S(1)} %coarse.13), channel_id=1, source_target_pairs={{4,0},{8,4},{12,8},{16,12},{20,16},{24,20},{28,24},{5,1},{9,5},{13... | collective-permute-start | bytes 368648 | tf_op jit(solution)/shard_map/ppermute | solution.py:452
  55.7 7.5 %copy-start.5 = (bf16[10,4,4096]{2,1,0:T(4,128)(2,1)}, bf16[10,4,4096]{2,1,0:T(4,128)(2,1)S(1)}, u32[]{:S(2)}) copy-start(bf16[10,4,4096]{2,1,0:T(4,128)(2,1)S(1)} %collective-permute-done.7) | copy-start | bytes 983044
  55.7 10.5 %collective-permute-start.9 = (bf16[10,8,1536]{2,1,0:T(8,128)(2,1)S(1)}, bf16[10,8,1536]{2,1,0:T(8,128)(2,1)S(1)}, u32[]{:S(2)}, u32[]{:S(2)}) collective-permute-start(bf16[10,8,1536]{2,1,0:T(8,128)(2,1)S(1)} %coarse.10), channel_id=1, source_target_pairs={{0,4},{4,8},{8,12},{12,16},{16,20},{20,24},{24,28},{1,5},{5,9},{9,... | collective-permute-start | bytes 737288 | tf_op jit(solution)/shard_map/ppermute | solution.py:449
  63.4 2.7 %slice-start = ((bf16[10,4,4096]{2,1,0:T(4,128)(2,1)}), bf16[10,4,1536]{2,1,0:T(4,128)(2,1)S(1)}, s32[]{:S(2)}) async-start(bf16[10,4,4096]{2,1,0:T(4,128)(2,1)} %copy-done.5), calls=%async_computation | async-start | bytes 245760 | tf_op jit(solution)/shard_map/slice | solution.py:503
  64.0 8.4 %collective-permute-start.12 = (bf16[10,4,2560]{2,1,0:T(4,128)(2,1)S(1)}, bf16[10,4,2560]{2,1,0:T(4,128)(2,1)S(1)}, u32[]{:S(2)}, u32[]{:S(2)}) collective-permute-start(bf16[10,4,2560]{2,1,0:T(4,128)(2,1)S(1)} %coarse.14), channel_id=1, source_target_pairs={{4,0},{8,4},{12,8},{16,12},{20,16},{24,20},{28,24},{5,1},{9,5},{13... | collective-permute-start | bytes 614408 | tf_op jit(solution)/shard_map/ppermute | solution.py:452
  66.3 10.9 %collective-permute-start.10 = (bf16[10,8,1536]{2,1,0:T(8,128)(2,1)S(1)}, bf16[10,8,1536]{2,1,0:T(8,128)(2,1)S(1)}, u32[]{:S(2)}, u32[]{:S(2)}) collective-permute-start(bf16[10,8,1536]{2,1,0:T(8,128)(2,1)S(1)} %coarse.11), channel_id=1, source_target_pairs={{0,4},{4,8},{8,12},{12,16},{16,20},{20,24},{24,28},{1,5},{5,9},{9,... | collective-permute-start | bytes 737288 | tf_op jit(solution)/shard_map/ppermute | solution.py:449
  69.5 8.5 %collective-permute-start.17 = (bf16[14,8,1536]{2,1,0:T(8,128)(2,1)S(1)}, bf16[14,8,1536]{2,1,0:T(8,128)(2,1)S(1)}, u32[]{:S(2)}, u32[]{:S(2)}) collective-permute-start(bf16[14,8,1536]{2,1,0:T(8,128)(2,1)S(1)} %bitcast.18), channel_id=1, source_target_pairs={{0,2},{1,3},{2,0},{3,1},{4,6},{5,7},{6,4},{7,5},{8,10},{9,11},{10,... | collective-permute-start | bytes 1032200 | tf_op jit(solution)/shard_map/ppermute | solution.py:443
  70.2 18.4 %collective-permute-start.16 = (bf16[14,8,1536]{2,1,0:T(8,128)(2,1)S(1)}, bf16[14,8,1536]{2,1,0:T(8,128)(2,1)S(1)}, u32[]{:S(2)}, u32[]{:S(2)}) collective-permute-start(bf16[14,8,1536]{2,1,0:T(8,128)(2,1)S(1)} %bitcast.19), channel_id=1, source_target_pairs={{0,1},{1,0},{2,3},{3,2},{4,5},{5,4},{6,7},{7,6},{8,9},{9,8},{10,11... | collective-permute-start | bytes 1032200 | tf_op jit(solution)/shard_map/ppermute | solution.py:446
  72.4 10.4 %collective-permute-start.14 = (bf16[10,8,1024]{2,1,0:T(8,128)(2,1)S(1)}, bf16[10,8,1024]{2,1,0:T(8,128)(2,1)S(1)}, u32[]{:S(2)}, u32[]{:S(2)}) collective-permute-start(bf16[10,8,1024]{2,1,0:T(8,128)(2,1)S(1)} %coarse.15), channel_id=1, source_target_pairs={{0,4},{4,8},{8,12},{12,16},{16,20},{20,24},{24,28},{1,5},{5,9},{9,... | collective-permute-start | bytes 491528 | tf_op jit(solution)/shard_map/ppermute | solution.py:449
  77.2 11.4 %collective-permute-start.13 = (bf16[14,8,1536]{2,1,0:T(8,128)(2,1)S(1)}, bf16[14,8,1536]{2,1,0:T(8,128)(2,1)S(1)}, u32[]{:S(2)}, u32[]{:S(2)}) collective-permute-start(bf16[14,8,1536]{2,1,0:T(8,128)(2,1)S(1)} %bitcast.15), channel_id=1, source_target_pairs={{0,2},{1,3},{2,0},{3,1},{4,6},{5,7},{6,4},{7,5},{8,10},{9,11},{10,... | collective-permute-start | bytes 1032200 | tf_op jit(solution)/shard_map/ppermute | solution.py:443
  78.0 10.7 %collective-permute-start.18 = (bf16[14,8,1536]{2,1,0:T(8,128)(2,1)S(1)}, bf16[14,8,1536]{2,1,0:T(8,128)(2,1)S(1)}, u32[]{:S(2)}, u32[]{:S(2)}) collective-permute-start(bf16[14,8,1536]{2,1,0:T(8,128)(2,1)S(1)} %collective-permute-done.17.refs_2_), channel_id=1, source_target_pairs={{0,1},{1,0},{2,3},{3,2},{4,5},{5,4},{6,7},{7,6},{8,9},{9,8},{10,11... | collective-permute-start | bytes 1032200 | tf_op jit(solution)/shard_map/ppermute | solution.py:446
  82.8 7.9 %collective-permute-start.15 = (bf16[14,8,1024]{2,1,0:T(8,128)(2,1)S(1)}, bf16[14,8,1024]{2,1,0:T(8,128)(2,1)S(1)}, u32[]{:S(2)}, u32[]{:S(2)}) collective-permute-start(bf16[14,8,1024]{2,1,0:T(8,128)(2,1)S(1)} %bitcast.22), channel_id=1, source_target_pairs={{0,2},{1,3},{2,0},{3,1},{4,6},{5,7},{6,4},{7,5},{8,10},{9,11},{10,... | collective-permute-start | bytes 688136 | tf_op jit(solution)/shard_map/ppermute | solution.py:443
  84.6 10.7 %collective-permute-start.19 = (bf16[14,8,1536]{2,1,0:T(8,128)(2,1)S(1)}, bf16[14,8,1536]{2,1,0:T(8,128)(2,1)S(1)}, u32[]{:S(2)}, u32[]{:S(2)}) collective-permute-start(bf16[14,8,1536]{2,1,0:T(8,128)(2,1)S(1)} %bitcast.16), channel_id=1, source_target_pairs={{0,1},{1,0},{2,3},{3,2},{4,5},{5,4},{6,7},{7,6},{8,9},{9,8},{10,11... | collective-permute-start | bytes 1032200 | tf_op jit(solution)/shard_map/ppermute | solution.py:446
  90.7 5.3 %collective-permute-start.20 = (bf16[14,8,1536]{2,1,0:T(8,128)(2,1)S(1)}, bf16[14,8,1536]{2,1,0:T(8,128)(2,1)S(1)}, u32[]{:S(2)}, u32[]{:S(2)}) collective-permute-start(bf16[14,8,1536]{2,1,0:T(8,128)(2,1)S(1)} %collective-permute-done.13.refs_3_), channel_id=1, source_target_pairs={{0,1},{1,0},{2,3},{3,2},{4,5},{5,4},{6,7},{7,6},{8,9},{9,8},{10,11... | collective-permute-start | bytes 1032200 | tf_op jit(solution)/shard_map/ppermute | solution.py:446
  94.8 3.2 %collective-permute-start.21 = (bf16[14,8,1024]{2,1,0:T(8,128)(2,1)S(1)}, bf16[14,8,1024]{2,1,0:T(8,128)(2,1)S(1)}, u32[]{:S(2)}, u32[]{:S(2)}) collective-permute-start(bf16[14,8,1024]{2,1,0:T(8,128)(2,1)S(1)} %bitcast.23), channel_id=1, source_target_pairs={{0,1},{1,0},{2,3},{3,2},{4,5},{5,4},{6,7},{7,6},{8,9},{9,8},{10,11... | collective-permute-start | bytes 688136 | tf_op jit(solution)/shard_map/ppermute | solution.py:446
  94.8 3.2 %collective-permute-start.22 = (bf16[14,8,1024]{2,1,0:T(8,128)(2,1)S(1)}, bf16[14,8,1024]{2,1,0:T(8,128)(2,1)S(1)}, u32[]{:S(2)}, u32[]{:S(2)}) collective-permute-start(bf16[14,8,1024]{2,1,0:T(8,128)(2,1)S(1)} %collective-permute-done.15.refs_3_), channel_id=1, source_target_pairs={{0,1},{1,0},{2,3},{3,2},{4,5},{5,4},{6,7},{7,6},{8,9},{9,8},{10,11... | collective-permute-start | bytes 688136 | tf_op jit(solution)/shard_map/ppermute | solution.py:446

commit v15 on v14

--- a/solution.py
+++ b/solution.py
@@ -468,7 +468,7 @@
     table = column_table(pct, rb, share)
     left = left_factor(pct, relayout(p_blocks, 0, rb))
     own = right_factor(0, table, [p_own], tiles, 1.4)
-    order = assembly_order(shifts, ncol, share)
+    order = assembly_order([(s, f) for f in range(2) for s in range(ny)], ncol, share)
     place = slot_places(a_cols, counts)
     bands = [near_band(place, [own_a[h], side_a[h]], shifts[:2], parts[h][0]) for h in range(2)]
     beside, far_a[0], left, own, order, bands = lax.optimization_barrier((beside, far_a[0], left, own, order, bands))
@@ -503,22 +503,21 @@
         jnp.concatenate([early[:, :, : cut * BS], late[0]], axis=1),
         jnp.concatenate([early[:, :, cut * BS :], late[1]], axis=1),
     ]
-    totals, sides, fars = [], [], []
+    totals, fars = [], []
     for z, (a0, a1) in enumerate(chunks):
         low = lower[0] if z == 0 else lower[1][:, :, (a0 - cut) * BS : (a1 - cut) * BS]
         total = columns(highs[z], 0) + columns(mids[z], 1) + columns(low, 2)
         total = total.astype(BF).reshape((share * (GROUPS + 2),) + total.shape[2:])
         totals.append(total)
-        sides.append(over_core(total))
         fars.append([over_y(total, s) for s in range(1, ny)])
     for z in range(len(chunks) - 1):
         fars[z], _ = lax.optimization_barrier((fars[z], totals[z + 1]))
     out = None
     for z, (a0, a1) in enumerate(chunks):
-        if z == 1:
-            fars[1:], out = lax.optimization_barrier((fars[1:], out))
-        srcs = [totals[z], sides[z]] + [q for x in fars[z] for q in (x, over_core(x))]
-        out = assemble(order, srcs, a0, BS * BS, out)
+        if z == 2:
+            fars[2], out = lax.optimization_barrier((fars[2], out))
+        mine = jnp.concatenate([totals[z]] + fars[z], axis=0)
+        out = assemble(order, [mine, over_core(mine)], a0, BS * BS, out)
     return out
 
 

time: 101 us -> 103 us (1.020)
  waiting for transfers between devices: 11 us -> 16.5 us
  starting transfers between devices: 45.6 us -> 41.5 us
    ppermute x11 -> x8, starting transfers between devices: 18.9 us -> 15.2 us  [over_core(): return lax.ppermute(x, 'col', [(c, c ^ 1) for c in range(ncol)])]
    ppermute x5, waiting for transfers between devices: 6.61 us -> 9.1 us  [over_y(): lax.ppermute(x, 'col', [(y * 2 + c, (y + s) % ny * 2 + c) for y in range(...]
    ppermute x3, waiting for transfers between devices: 1.71 us -> 3.29 us  [upward(): return lax.ppermute(x, 'row', [(i, i + 1) for i in range(nrow - 1)])]
  transfers between devices with their start and end apart: 23 -> 20, of which waited for: 8 -> 10; matrix products, arithmetic and copies ran while one was open for 1% -> 1% of each run, Pallas kernels for 37% -> 36%
where the time goes in v15:
time: 103 us; the launch traced here: 101 us
  starting transfers between devices  41.5 us (40%)
  Pallas kernels  39 us (38%)
  waiting for transfers between devices  16.5 us (16%)
  local copies, waits for them, and re-layouts  2.64 us (3%)
  other arithmetic  1.1 us (1%)
    ppermute x8, starting transfers between devices, over_core(): return lax.ppermute(x, 'col', [(c, c ^ 1) for c in range(ncol)])  15.2 us
    pallas_call x2, Pallas kernels, product(): pl.pallas_call(functools.partial(product_kernel, first, rb, shifts), out_...  10.9 us
    ppermute x3, starting transfers between devices, upward(): return lax.ppermute(x, 'row', [(i, i + 1) for i in range(nrow - 1)])  10.8 us
    ppermute x5, waiting for transfers between devices, over_y(): lax.ppermute(x, 'col', [(y * 2 + c, (y + s) % ny * 2 + c) for y in range(...  9.1 us
    ppermute x3, starting transfers between devices, downward(): return lax.ppermute(x, 'row', [(i + 1, i) for i in range(nrow - 1)])  7.79 us
    pallas_call x9, Pallas kernels, coarse_rows(): pl.pallas_call(functools.partial(coarse_kernel, sets, a0, a1), out_shape=...  6.29 us
    pallas_call x2, Pallas kernels, near_band(): pl.pallas_call(functools.partial(band_kernel, first, shifts), out_shape=j...  5.98 us
    pallas_call x3, Pallas kernels, assemble(): pl.pallas_call(assemble_kernel, grid=(per,), out_shape=jax.ShapeDtypeStru...  5.48 us
  transfers between devices with their start and end apart: 20, of which 10 were waited for; matrix products, arithmetic and copies ran while one was open for 1% of the time, Pallas kernels for 36%

profile of v15, /device:TPU:9, one launch (start us, length us, event | category | flops | bytes accessed | tf_op | source)
XLA Modules:
  0.0 101.2 jit_solution(7561014675154893351)
XLA Ops:
  0.0 1.4 %copy-done = bf16[24,8,4096]{2,1,0:T(8,128)(2,1)S(1)} copy-done((bf16[24,8,4096]{2,1,0:T(8,128)(2,1)S(1)}, bf16[24,8,4096]{2,1,0:T(8,128)(2,1)}, u32[]{:S(2)}) %copy-start) | copy-done | bytes 1572888
  1.4 0.8 relayout.3.refs_0_
  2.2 0.7 collective-permute-start
  3.0 1.3 %collective-permute-start.2 = (bf16[16,4,64,128]{3,2,1,0:T(8,128)(2,1)S(1)}, bf16[16,4,64,128]{3,2,1,0:T(8,128)(2,1)}, u32[]{:S(2)}, u32[]{:S(2)}) collective-permute-start(bf16[16,4,64,128]{3,2,1,0:T(8,128)(2,1)S(1)} %relayout.3.refs_0_), channel_id=1, source_target_pairs={{0,2},{1,3},{2,0},{3,1},{4,6},{5,7},{6,4},{7,5},{8,10},{9,11},{10,... | collective-permute-start | bytes 3145736 | tf_op jit(solution)/shard_map/ppermute | solution.py:443
  4.2 1.1 %copy-done.2 = bf16[24,4,4096]{2,1,0:T(4,128)(2,1)S(1)} copy-done((bf16[24,4,4096]{2,1,0:T(4,128)(2,1)S(1)}, bf16[24,4,4096]{2,1,0:T(4,128)(2,1)}, u32[]{:S(2)}) %copy-start.2) | copy-done | bytes 786456
  5.4 1.1 %relayout_rows.1.refs_0_ = bf16[24,2,64,128]{3,2,1,0:T(8,128)(2,1)S(1)} custom-call(bf16[24,4,4096]{2,1,0:T(4,128)(2,1)S(1)} %copy-done.2), custom_call_target="tpu_custom_call" | custom-call | flops 100000000 | bytes 3700000 | tf_op jit(solution)/shard_map/relayout_rows/pallas_call | solution.py:84
  6.5 0.1 add_select_fusion.4.table_ref
  6.6 3.0 %collective-permute-start.1 = (bf16[24,2,64,128]{3,2,1,0:T(8,128)(2,1)S(1)}, bf16[24,2,64,128]{3,2,1,0:T(8,128)(2,1)S(1)}, u32[]{:S(2)}, u32[]{:S(2)}) collective-permute-start(bf16[24,2,64,128]{3,2,1,0:T(8,128)(2,1)S(1)} %relayout_rows.1.refs_0_), channel_id=1, source_target_pairs={{0,4},{2,6},{4,8},{5,1},{6,10},{7,3},{8,12},{9,5},{10,14},{11,7},{... | collective-permute-start | bytes 2359304 | tf_op jit(solution)/shard_map/ppermute | solution.py:440
  9.6 0.1 subtract_select_fusion.place_ref
  9.7 0.4 relayout.4.refs_0_
  10.1 0.8 collective-permute-start.3
  10.9 0.2 fusion.12.order_ref
  11.1 3.9 %near_band.2.start_ref = bf16[4,27,256,128]{3,2,1,0:T(8,128)(2,1)S(1)} custom-call(s32[24,32]{1,0:T(8,128)S(1)} %subtract_select_fusion.place_ref, bf16[16,4,64,128]{3,2,1,0:T(8,128)(2,1)S(1)} %relayout.3.refs_0_, bf16[16,4,64,128]{3,2,1,0:T(8,128)(2,1)} %collective-permute-done.refs_1_), custom_call_target="tpu_custom_call" | custom-call | flops 256000000 | bytes 9472000 | tf_op jit(solution)/shard_map/near_band/pallas_call | solution.py:272
  15.1 0.9 relayout.5.pl_ref
  16.0 2.1 %near_band.3.start_ref = bf16[2,27,256,128]{3,2,1,0:T(8,128)(2,1)S(1)} custom-call(s32[24,32]{1,0:T(8,128)S(1)} %subtract_select_fusion.place_ref, bf16[8,4,64,128]{3,2,1,0:T(8,128)(2,1)S(1)} %relayout.4.refs_0_, bf16[8,4,64,128]{3,2,1,0:T(8,128)(2,1)S(1)} %collective-permute-done.3.refs_1_), custom_call_target="tpu_custom_call" | custom-call | flops 128000000 | bytes 4736000 | tf_op jit(solution)/shard_map/near_band/pallas_call | solution.py:272
  18.0 1.4 %right_factor.3.own_ref = bf16[6,5,256,128]{3,2,1,0:T(8,128)(2,1)S(1)} custom-call(s32[4,72]{1,0:T(4,128)S(1)} %add_select_fusion.4.table_ref, bf16[24,2,64,128]{3,2,1,0:T(8,128)(2,1)S(1)} %relayout_rows.1.refs_0_), custom_call_target="tpu_custom_call" | custom-call | flops 140000000 | bytes 5180000 | tf_op jit(solution)/shard_map/right_factor/pallas_call | solution.py:203
  19.4 2.9 %left_factor.1.left_ref = bf16[12,24,64,128]{3,2,1,0:T(8,128)(2,1)S(1)} custom-call(s32[4,192]{1,0:T(4,128)S(1)} %bitcast.17, bf16[24,2,64,128]{3,2,1,0:T(8,128)(2,1)S(1)} %relayout.5.pl_ref), custom_call_target="tpu_custom_call" | custom-call | flops 290000000 | bytes 10730000 | tf_op jit(solution)/shard_map/left_factor/pallas_call | solution.py:118
  22.3 5.5 %collective-permute-done.2.refs_0_ = bf16[16,4,64,128]{3,2,1,0:T(8,128)(2,1)} collective-permute-done((bf16[16,4,64,128]{3,2,1,0:T(8,128)(2,1)S(1)}, bf16[16,4,64,128]{3,2,1,0:T(8,128)(2,1)}, u32[]{:S(2)}, u32[]{:S(2)}) %collective-permute-start.2) | collective-permute-done | bytes 1048608 | tf_op jit(solution)/shard_map/ppermute | solution.py:443
  27.8 0.3 collective-permute-done.1.refs_0_
  28.2 0.5 collective-permute-start.6
  28.7 1.2 %collective-permute-start.4 = (bf16[8,4,64,128]{3,2,1,0:T(8,128)(2,1)S(1)}, bf16[8,4,64,128]{3,2,1,0:T(8,128)(2,1)S(1)}, u32[]{:S(2)}, u32[]{:S(2)}) collective-permute-start(bf16[8,4,64,128]{3,2,1,0:T(8,128)(2,1)S(1)} %relayout.4.refs_0_), channel_id=1, source_target_pairs={{0,2},{1,3},{2,0},{3,1},{4,6},{5,7},{6,4},{7,5},{8,10},{9,11},{10,... | collective-permute-start | bytes 1572872 | tf_op jit(solution)/shard_map/ppermute | solution.py:443
  29.9 1.4 %right_factor.4.refs_0_ = bf16[6,5,256,128]{3,2,1,0:T(8,128)(2,1)S(1)} custom-call(s32[4,72]{1,0:T(4,128)S(1)} %add_select_fusion.4.table_ref, bf16[24,2,64,128]{3,2,1,0:T(8,128)(2,1)S(1)} %collective-permute-done.1.refs_0_), custom_call_target="tpu_custom_call" | custom-call | flops 120000000 | bytes 4440000 | tf_op jit(solution)/shard_map/right_factor/pallas_call | solution.py:203
  31.4 0.6 collective-permute-done.5.refs_1_
  32.0 1.5 %right_factor.5.near_ref = bf16[12,5,256,128]{3,2,1,0:T(8,128)(2,1)S(1)} custom-call(s32[4,72]{1,0:T(4,128)S(1)} %add_select_fusion.4.table_ref, bf16[6,5,256,128]{3,2,1,0:T(8,128)(2,1)S(1)} %right_factor.4.refs_0_, bf16[24,2,64,128]{3,2,1,0:T(8,128)(2,1)S(1)} %collective-permute-done.5.refs_1_), custom_call_target="tpu_custom_call" | custom-call | flops 140000000 | bytes 5180000 | tf_op jit(solution)/shard_map/right_factor/pallas_call | solution.py:203
  33.5 7.1 %product.2.refs_0_ = bf16[16,64,640]{2,1,0:T(8,128)(2,1)S(1)} custom-call(s32[24,32]{1,0:T(8,128)S(1)} %subtract_select_fusion.place_ref, bf16[6,5,256,128]{3,2,1,0:T(8,128)(2,1)S(1)} %right_factor.3.own_ref, bf16[12,5,256,128]{3,2,1,0:T(8,128)(2,1)S(1)} %right_factor.5.near_ref, bf16[4,27,256,128]{3,2,1,0:T(8,128)(2,1)S(1)} %near_band.2.start_ref, ...), custom_call_target="tpu_custom_call" | custom-call | flops 480000000 | bytes 17760000 | tf_op jit(solution)/shard_map/product/pallas_call | solution.py:316
  40.6 1.0 %collective-permute-done.4.refs_0_ = bf16[8,4,64,128]{3,2,1,0:T(8,128)(2,1)S(1)} collective-permute-done((bf16[8,4,64,128]{3,2,1,0:T(8,128)(2,1)S(1)}, bf16[8,4,64,128]{3,2,1,0:T(8,128)(2,1)S(1)}, u32[]{:S(2)}, u32[]{:S(2)}) %collective-permute-start.4) | collective-permute-done | bytes 524320 | tf_op jit(solution)/shard_map/ppermute | solution.py:443
  41.7 1.4 %collective-permute-start.7 = (bf16[8,4,64,128]{3,2,1,0:T(8,128)(2,1)S(1)}, bf16[8,4,64,128]{3,2,1,0:T(8,128)(2,1)S(1)}, u32[]{:S(2)}, u32[]{:S(2)}) collective-permute-start(bf16[8,4,64,128]{3,2,1,0:T(8,128)(2,1)S(1)} %collective-permute-done.4.refs_0_), channel_id=1, source_target_pairs={{0,1},{1,0},{2,3},{3,2},{4,5},{5,4},{6,7},{7,6},{8,9},{9,8},{10,11... | collective-permute-start | bytes 1572872 | tf_op jit(solution)/shard_map/ppermute | solution.py:446
  43.0 0.9 coarse.13
  44.0 3.8 %collective-permute-start.11 = (bf16[10,4,4096]{2,1,0:T(4,128)(2,1)S(1)}, bf16[10,4,4096]{2,1,0:T(4,128)(2,1)S(1)}, u32[]{:S(2)}, u32[]{:S(2)}) collective-permute-start(bf16[10,4,4096]{2,1,0:T(4,128)(2,1)S(1)} %coarse.13), channel_id=1, source_target_pairs={{4,0},{8,4},{12,8},{16,12},{20,16},{24,20},{28,24},{5,1},{9,5},{13... | collective-permute-start | bytes 983048 | tf_op jit(solution)/shard_map/ppermute | solution.py:452
  47.7 3.7 %product.3.refs_1_ = bf16[8,64,640]{2,1,0:T(8,128)(2,1)S(1)} custom-call(s32[24,32]{1,0:T(8,128)S(1)} %subtract_select_fusion.place_ref, bf16[6,5,256,128]{3,2,1,0:T(8,128)(2,1)S(1)} %right_factor.3.own_ref, bf16[12,5,256,128]{3,2,1,0:T(8,128)(2,1)S(1)} %right_factor.5.near_ref, bf16[2,27,256,128]{3,2,1,0:T(8,128)(2,1)S(1)} %near_band.3.start_ref, ...), custom_call_target="tpu_custom_call" | custom-call | flops 240000000 | bytes 8880000 | tf_op jit(solution)/shard_map/product/pallas_call | solution.py:316
  51.5 0.6 coarse.9
  52.1 1.9 %collective-permute-start.8 = (bf16[10,4,1536]{2,1,0:T(4,128)(2,1)S(1)}, bf16[10,4,1536]{2,1,0:T(4,128)(2,1)S(1)}, u32[]{:S(2)}, u32[]{:S(2)}) collective-permute-start(bf16[10,4,1536]{2,1,0:T(4,128)(2,1)S(1)} %coarse.9), channel_id=1, source_target_pairs={{4,0},{8,4},{12,8},{16,12},{20,16},{24,20},{28,24},{5,1},{9,5},{13... | collective-permute-start | bytes 368648 | tf_op jit(solution)/shard_map/ppermute | solution.py:452
  54.0 0.7 coarse.14
  54.8 1.0 collective-permute-done.11
  55.7 4.0 %collective-permute-start.13 = (bf16[10,8,1536]{2,1,0:T(8,128)(2,1)S(1)}, bf16[10,8,1536]{2,1,0:T(8,128)(2,1)S(1)}, u32[]{:S(2)}, u32[]{:S(2)}) collective-permute-start(bf16[10,8,1536]{2,1,0:T(8,128)(2,1)S(1)} %coarse.14), channel_id=1, source_target_pairs={{0,4},{4,8},{8,12},{12,16},{16,20},{20,24},{24,28},{1,5},{5,9},{9,... | collective-permute-start | bytes 737288 | tf_op jit(solution)/shard_map/ppermute | solution.py:449
  59.8 0.6 coarse.11
  60.4 0.7 coarse.10
  61.1 0.7 coarse.17
  61.8 0.7 coarse.15
  62.5 0.6 coarse.12
  63.1 0.1 slice.12
  63.2 0.7 coarse.16
  64.0 2.1 %collective-permute-start.9 = (bf16[10,4,2560]{2,1,0:T(4,128)(2,1)S(1)}, bf16[10,4,2560]{2,1,0:T(4,128)(2,1)S(1)}, u32[]{:S(2)}, u32[]{:S(2)}) collective-permute-start(bf16[10,4,2560]{2,1,0:T(4,128)(2,1)S(1)} %coarse.10), channel_id=1, source_target_pairs={{4,0},{8,4},{12,8},{16,12},{20,16},{24,20},{28,24},{5,1},{9,5},{13... | collective-permute-start | bytes 614408 | tf_op jit(solution)/shard_map/ppermute | solution.py:452
  66.1 0.1 pad_maximum_fusion.4
  66.3 3.2 %collective-permute-start.15 = (bf16[10,8,1536]{2,1,0:T(8,128)(2,1)S(1)}, bf16[10,8,1536]{2,1,0:T(8,128)(2,1)S(1)}, u32[]{:S(2)}, u32[]{:S(2)}) collective-permute-start(bf16[10,8,1536]{2,1,0:T(8,128)(2,1)S(1)} %coarse.15), channel_id=1, source_target_pairs={{0,4},{4,8},{8,12},{12,16},{16,20},{20,24},{24,28},{1,5},{5,9},{9,... | collective-permute-start | bytes 737288 | tf_op jit(solution)/shard_map/ppermute | solution.py:449
  69.4 0.1 add_convert_fusion.1
  69.5 0.7 collective-permute-start.14
  70.3 0.7 collective-permute-done.9
  71.0 3.6 %collective-permute-start.10 = (bf16[10,8,1024]{2,1,0:T(8,128)(2,1)S(1)}, bf16[10,8,1024]{2,1,0:T(8,128)(2,1)S(1)}, u32[]{:S(2)}, u32[]{:S(2)}) collective-permute-start(bf16[10,8,1024]{2,1,0:T(8,128)(2,1)S(1)} %coarse.11), channel_id=1, source_target_pairs={{0,4},{4,8},{8,12},{12,16},{16,20},{20,24},{24,28},{1,5},{5,9},{9,... | collective-permute-start | bytes 491528 | tf_op jit(solution)/shard_map/ppermute | solution.py:449
  74.6 0.1 pad_maximum_fusion.5
  74.7 0.1 pad_maximum_fusion.3
  74.8 2.3 %collective-permute-done.15 = bf16[10,8,1536]{2,1,0:T(8,128)(2,1)S(1)} collective-permute-done((bf16[10,8,1536]{2,1,0:T(8,128)(2,1)S(1)}, bf16[10,8,1536]{2,1,0:T(8,128)(2,1)S(1)}, u32[]{:S(2)}, u32[]{:S(2)}) %collective-permute-start.15) | collective-permute-done | bytes 245792 | tf_op jit(solution)/shard_map/ppermute | solution.py:449
  77.1 0.1 add_convert_fusion
  77.2 0.8 collective-permute-start.17
  78.0 1.0 collective-permute-done.10
  79.2 9.5 %collective-permute-start.16 = (bf16[28,8,1536]{2,1,0:T(8,128)(2,1)S(1)}, bf16[28,8,1536]{2,1,0:T(8,128)(2,1)S(1)}, u32[]{:S(2)}, u32[]{:S(2)}) collective-permute-start(bf16[28,8,1536]{2,1,0:T(8,128)(2,1)S(1)} %pad_maximum_fusion.refs_0_), channel_id=1, source_target_pairs={{0,1},{1,0},{2,3},{3,2},{4,5},{5,4},{6,7},{7,6},{8,9},{9,8},{10,11... | collective-permute-start | bytes 2064392 | tf_op jit(solution)/shard_map/ppermute | solution.py:446
  88.8 1.3 %collective-permute-start.18 = (bf16[28,8,1536]{2,1,0:T(8,128)(2,1)S(1)}, bf16[28,8,1536]{2,1,0:T(8,128)(2,1)S(1)}, u32[]{:S(2)}, u32[]{:S(2)}) collective-permute-start(bf16[28,8,1536]{2,1,0:T(8,128)(2,1)S(1)} %pad_maximum_fusion.1.refs_1_), channel_id=1, source_target_pairs={{0,1},{1,0},{2,3},{3,2},{4,5},{5,4},{6,7},{7,6},{8,9},{9,8},{10,11... | collective-permute-start | bytes 2064392 | tf_op jit(solution)/shard_map/ppermute | solution.py:446
  90.1 0.7 collective-permute-start.12
  90.8 2.0 %assemble.3.refs_0_ = bf16[8,56,4096]{2,1,0:T(8,128)(2,1)} custom-call(bf16[448,448]{1,0:T(8,128)(2,1)S(1)} %fusion.12.order_ref, bf16[28,8,1536]{2,1,0:T(8,128)(2,1)S(1)} %pad_maximum_fusion.refs_0_, bf16[28,8,1536]{2,1,0:T(8,128)(2,1)S(1)} %collective-permute-done.16.refs_1_), custom_call_target="tpu_custom_call" | custom-call | flops 290000000 | bytes 10730000 | tf_op jit(solution)/shard_map/assemble/pallas_call | solution.py:398
  92.7 2.0 %assemble.4.refs_0_ = bf16[8,56,4096]{2,1,0:T(8,128)(2,1)} custom-call(bf16[448,448]{1,0:T(8,128)(2,1)S(1)} %fusion.12.order_ref, bf16[8,56,4096]{2,1,0:T(8,128)(2,1)} %assemble.3.refs_0_, bf16[28,8,1536]{2,1,0:T(8,128)(2,1)S(1)} %pad_maximum_fusion.1.refs_1_, bf16[28,8,1536]{2,1,0:T(8,128)(2,1)S(1)} %collective-permute-done.18.refs_2_), custom_call_target="tpu_custom_call", output_to_operand_aliasing={{}: (1, {})} | custom-call | flops 290000000 | bytes 10730000 | tf_op jit(solution)/shard_map/assemble/pallas_call | solution.py:398
  94.7 2.6 %collective-permute-done.12 = bf16[14,8,1024]{2,1,0:T(8,128)(2,1)S(1)} collective-permute-done((bf16[14,8,1024]{2,1,0:T(8,128)(2,1)S(1)}, bf16[14,8,1024]{2,1,0:T(8,128)(2,1)S(1)}, u32[]{:S(2)}, u32[]{:S(2)}) %collective-permute-start.12) | collective-permute-done | bytes 229408 | tf_op jit(solution)/shard_map/ppermute | solution.py:443
  97.3 0.9 collective-permute-start.19
  98.2 1.4 %collective-permute-done.19.refs_2_ = bf16[28,8,1024]{2,1,0:T(8,128)(2,1)S(1)} collective-permute-done((bf16[28,8,1024]{2,1,0:T(8,128)(2,1)S(1)}, bf16[28,8,1024]{2,1,0:T(8,128)(2,1)S(1)}, u32[]{:S(2)}, u32[]{:S(2)}) %collective-permute-start.19) | collective-permute-done | bytes 458784 | tf_op jit(solution)/shard_map/ppermute | solution.py:446
  99.7 1.6 %assemble.5 = bf16[8,56,4096]{2,1,0:T(8,128)(2,1)} custom-call(bf16[448,448]{1,0:T(8,128)(2,1)S(1)} %fusion.12.order_ref, bf16[8,56,4096]{2,1,0:T(8,128)(2,1)} %assemble.4.refs_0_, bf16[28,8,1024]{2,1,0:T(8,128)(2,1)S(1)} %pad_maximum_fusion.2.refs_1_, bf16[28,8,1024]{2,1,0:T(8,128)(2,1)S(1)} %collective-permute-done.19.refs_2_), custom_call_target="tpu_custom_call", output_to_operand_aliasing={{}: (1, {})} | custom-call | flops 290000000 | bytes 10730000 | tf_op jit(solution)/shard_map/assemble/pallas_call | solution.py:398
  (35 shorter events, 0.3 us)
Async XLA Ops:
  0.0 1.4 %copy-start = (bf16[24,8,4096]{2,1,0:T(8,128)(2,1)S(1)}, bf16[24,8,4096]{2,1,0:T(8,128)(2,1)}, u32[]{:S(2)}) copy-start(bf16[24,8,4096]{2,1,0:T(8,128)(2,1)} %x_ref.4) | copy-start | bytes 4718596
  1.4 5.0 %copy-start.4 = (s32[192,4]{0,1:T(4,128)S(1)}, s32[192,4]{0,1:T(4,128)}, u32[]{:S(2)}) copy-start(s32[192,4]{0,1:T(4,128)} %param.9) | copy-start | bytes 9220
  1.4 8.2 %copy-start.6 = (s32[24,32]{1,0:T(8,128)S(1)}, s32[24,32]{1,0:T(8,128)}, u32[]{:S(2)}) copy-start(s32[24,32]{1,0:T(8,128)} %param.6) | copy-start | bytes 9220
  1.4 8.2 %copy-start.7 = (s32[24]{0:T(128)S(1)}, s32[24]{0:T(128)}, u32[]{:S(2)}) copy-start(s32[24]{0:T(128)} %param.7) | copy-start | bytes 292
  1.4 8.3 %copy-start.1 = (bf16[24,8,4096]{2,1,0:T(8,128)(2,1)S(1)}, bf16[24,8,4096]{2,1,0:T(8,128)(2,1)}, u32[]{:S(2)}) copy-start(bf16[24,8,4096]{2,1,0:T(8,128)(2,1)} %x_ref.4) | copy-start | bytes 4718596
  2.2 4.3 %collective-permute-start = (bf16[16,4,64,128]{3,2,1,0:T(8,128)(2,1)S(1)}, bf16[16,4,64,128]{3,2,1,0:T(8,128)(2,1)}, u32[]{:S(2)}, u32[]{:S(2)}) collective-permute-start(bf16[16,4,64,128]{3,2,1,0:T(8,128)(2,1)S(1)} %relayout.3.refs_0_), channel_id=1, source_target_pairs={{0,1},{1,0},{2,3},{3,2},{4,5},{5,4},{6,7},{7,6},{8,9},{9,8},{10,11... | collective-permute-start | bytes 3145736 | tf_op jit(solution)/shard_map/ppermute | solution.py:446
  3.0 24.8 %collective-permute-start.2 = (bf16[16,4,64,128]{3,2,1,0:T(8,128)(2,1)S(1)}, bf16[16,4,64,128]{3,2,1,0:T(8,128)(2,1)}, u32[]{:S(2)}, u32[]{:S(2)}) collective-permute-start(bf16[16,4,64,128]{3,2,1,0:T(8,128)(2,1)S(1)} %relayout.3.refs_0_), channel_id=1, source_target_pairs={{0,2},{1,3},{2,0},{3,1},{4,6},{5,7},{6,4},{7,5},{8,10},{9,11},{10,... | collective-permute-start | bytes 3145736 | tf_op jit(solution)/shard_map/ppermute | solution.py:443
  4.2 1.1 %copy-start.2 = (bf16[24,4,4096]{2,1,0:T(4,128)(2,1)S(1)}, bf16[24,4,4096]{2,1,0:T(4,128)(2,1)}, u32[]{:S(2)}) copy-start(bf16[24,4,4096]{2,1,0:T(4,128)(2,1)} %x_ref.5) | copy-start | bytes 2359300
  6.6 21.6 %collective-permute-start.1 = (bf16[24,2,64,128]{3,2,1,0:T(8,128)(2,1)S(1)}, bf16[24,2,64,128]{3,2,1,0:T(8,128)(2,1)S(1)}, u32[]{:S(2)}, u32[]{:S(2)}) collective-permute-start(bf16[24,2,64,128]{3,2,1,0:T(8,128)(2,1)S(1)} %relayout_rows.1.refs_0_), channel_id=1, source_target_pairs={{0,4},{2,6},{4,8},{5,1},{6,10},{7,3},{8,12},{9,5},{10,14},{11,7},{... | collective-permute-start | bytes 2359304 | tf_op jit(solution)/shard_map/ppermute | solution.py:440
  10.1 4.9 %collective-permute-start.3 = (bf16[8,4,64,128]{3,2,1,0:T(8,128)(2,1)S(1)}, bf16[8,4,64,128]{3,2,1,0:T(8,128)(2,1)S(1)}, u32[]{:S(2)}, u32[]{:S(2)}) collective-permute-start(bf16[8,4,64,128]{3,2,1,0:T(8,128)(2,1)S(1)} %relayout.4.refs_0_), channel_id=1, source_target_pairs={{0,1},{1,0},{2,3},{3,2},{4,5},{5,4},{6,7},{7,6},{8,9},{9,8},{10,11... | collective-permute-start | bytes 1572872 | tf_op jit(solution)/shard_map/ppermute | solution.py:446
  11.1 4.0 %copy-start.3 = (bf16[24,4,4096]{2,1,0:T(4,128)(2,1)S(1)}, bf16[24,4,4096]{2,1,0:T(4,128)(2,1)}, u32[]{:S(2)}) copy-start(bf16[24,4,4096]{2,1,0:T(4,128)(2,1)} %x_ref.5) | copy-start | bytes 2359300
  28.2 5.3 %collective-permute-start.6 = (bf16[16,4,64,128]{3,2,1,0:T(8,128)(2,1)}, bf16[16,4,64,128]{3,2,1,0:T(8,128)(2,1)S(1)}, u32[]{:S(2)}, u32[]{:S(2)}) collective-permute-start(bf16[16,4,64,128]{3,2,1,0:T(8,128)(2,1)} %collective-permute-done.2.refs_0_), channel_id=1, source_target_pairs={{0,1},{1,0},{2,3},{3,2},{4,5},{5,4},{6,7},{7,6},{8,9},{9,8},{10,11... | collective-permute-start | bytes 3145736 | tf_op jit(solution)/shard_map/ppermute | solution.py:446
  28.7 3.3 %collective-permute-start.5 = (bf16[24,2,64,128]{3,2,1,0:T(8,128)(2,1)S(1)}, bf16[24,2,64,128]{3,2,1,0:T(8,128)(2,1)S(1)}, u32[]{:S(2)}, u32[]{:S(2)}) collective-permute-start(bf16[24,2,64,128]{3,2,1,0:T(8,128)(2,1)S(1)} %collective-permute-done.1.refs_0_), channel_id=1, source_target_pairs={{0,1},{1,0},{2,3},{3,2},{4,5},{5,4},{6,7},{7,6},{8,9},{9,8},{10,11... | collective-permute-start | bytes 2359304 | tf_op jit(solution)/shard_map/ppermute | solution.py:446
  28.7 13.0 %collective-permute-start.4 = (bf16[8,4,64,128]{3,2,1,0:T(8,128)(2,1)S(1)}, bf16[8,4,64,128]{3,2,1,0:T(8,128)(2,1)S(1)}, u32[]{:S(2)}, u32[]{:S(2)}) collective-permute-start(bf16[8,4,64,128]{3,2,1,0:T(8,128)(2,1)S(1)} %relayout.4.refs_0_), channel_id=1, source_target_pairs={{0,2},{1,3},{2,0},{3,1},{4,6},{5,7},{6,4},{7,5},{8,10},{9,11},{10,... | collective-permute-start | bytes 1572872 | tf_op jit(solution)/shard_map/ppermute | solution.py:443
  41.7 6.1 %collective-permute-start.7 = (bf16[8,4,64,128]{3,2,1,0:T(8,128)(2,1)S(1)}, bf16[8,4,64,128]{3,2,1,0:T(8,128)(2,1)S(1)}, u32[]{:S(2)}, u32[]{:S(2)}) collective-permute-start(bf16[8,4,64,128]{3,2,1,0:T(8,128)(2,1)S(1)} %collective-permute-done.4.refs_0_), channel_id=1, source_target_pairs={{0,1},{1,0},{2,3},{3,2},{4,5},{5,4},{6,7},{7,6},{8,9},{9,8},{10,11... | collective-permute-start | bytes 1572872 | tf_op jit(solution)/shard_map/ppermute | solution.py:446
  44.0 11.8 %collective-permute-start.11 = (bf16[10,4,4096]{2,1,0:T(4,128)(2,1)S(1)}, bf16[10,4,4096]{2,1,0:T(4,128)(2,1)S(1)}, u32[]{:S(2)}, u32[]{:S(2)}) collective-permute-start(bf16[10,4,4096]{2,1,0:T(4,128)(2,1)S(1)} %coarse.13), channel_id=1, source_target_pairs={{4,0},{8,4},{12,8},{16,12},{20,16},{24,20},{28,24},{5,1},{9,5},{13... | collective-permute-start | bytes 983048 | tf_op jit(solution)/shard_map/ppermute | solution.py:452
  52.1 11.9 %collective-permute-start.8 = (bf16[10,4,1536]{2,1,0:T(4,128)(2,1)S(1)}, bf16[10,4,1536]{2,1,0:T(4,128)(2,1)S(1)}, u32[]{:S(2)}, u32[]{:S(2)}) collective-permute-start(bf16[10,4,1536]{2,1,0:T(4,128)(2,1)S(1)} %coarse.9), channel_id=1, source_target_pairs={{4,0},{8,4},{12,8},{16,12},{20,16},{24,20},{28,24},{5,1},{9,5},{13... | collective-permute-start | bytes 368648 | tf_op jit(solution)/shard_map/ppermute | solution.py:452
  55.7 7.5 %copy-start.5 = (bf16[10,4,4096]{2,1,0:T(4,128)(2,1)}, bf16[10,4,4096]{2,1,0:T(4,128)(2,1)S(1)}, u32[]{:S(2)}) copy-start(bf16[10,4,4096]{2,1,0:T(4,128)(2,1)S(1)} %collective-permute-done.11) | copy-start | bytes 983044
  55.7 10.5 %collective-permute-start.13 = (bf16[10,8,1536]{2,1,0:T(8,128)(2,1)S(1)}, bf16[10,8,1536]{2,1,0:T(8,128)(2,1)S(1)}, u32[]{:S(2)}, u32[]{:S(2)}) collective-permute-start(bf16[10,8,1536]{2,1,0:T(8,128)(2,1)S(1)} %coarse.14), channel_id=1, source_target_pairs={{0,4},{4,8},{8,12},{12,16},{16,20},{20,24},{24,28},{1,5},{5,9},{9,... | collective-permute-start | bytes 737288 | tf_op jit(solution)/shard_map/ppermute | solution.py:449
  63.2 2.9 %slice-start = ((bf16[10,4,4096]{2,1,0:T(4,128)(2,1)}), bf16[10,4,1536]{2,1,0:T(4,128)(2,1)S(1)}, s32[]{:S(2)}) async-start(bf16[10,4,4096]{2,1,0:T(4,128)(2,1)} %copy-done.5), calls=%async_computation | async-start | bytes 245760 | tf_op jit(solution)/shard_map/slice | solution.py:503
  64.0 7.0 %collective-permute-start.9 = (bf16[10,4,2560]{2,1,0:T(4,128)(2,1)S(1)}, bf16[10,4,2560]{2,1,0:T(4,128)(2,1)S(1)}, u32[]{:S(2)}, u32[]{:S(2)}) collective-permute-start(bf16[10,4,2560]{2,1,0:T(4,128)(2,1)S(1)} %coarse.10), channel_id=1, source_target_pairs={{4,0},{8,4},{12,8},{16,12},{20,16},{24,20},{28,24},{5,1},{9,5},{13... | collective-permute-start | bytes 614408 | tf_op jit(solution)/shard_map/ppermute | solution.py:452
  66.3 10.9 %collective-permute-start.15 = (bf16[10,8,1536]{2,1,0:T(8,128)(2,1)S(1)}, bf16[10,8,1536]{2,1,0:T(8,128)(2,1)S(1)}, u32[]{:S(2)}, u32[]{:S(2)}) collective-permute-start(bf16[10,8,1536]{2,1,0:T(8,128)(2,1)S(1)} %coarse.15), channel_id=1, source_target_pairs={{0,4},{4,8},{8,12},{12,16},{16,20},{20,24},{24,28},{1,5},{5,9},{9,... | collective-permute-start | bytes 737288 | tf_op jit(solution)/shard_map/ppermute | solution.py:449
  69.5 9.6 %collective-permute-start.14 = (bf16[14,8,1536]{2,1,0:T(8,128)(2,1)S(1)}, bf16[14,8,1536]{2,1,0:T(8,128)(2,1)S(1)}, u32[]{:S(2)}, u32[]{:S(2)}) collective-permute-start(bf16[14,8,1536]{2,1,0:T(8,128)(2,1)S(1)} %bitcast.18), channel_id=1, source_target_pairs={{0,2},{1,3},{2,0},{3,1},{4,6},{5,7},{6,4},{7,5},{8,10},{9,11},{10,... | collective-permute-start | bytes 1032200 | tf_op jit(solution)/shard_map/ppermute | solution.py:443
  71.0 8.0 %collective-permute-start.10 = (bf16[10,8,1024]{2,1,0:T(8,128)(2,1)S(1)}, bf16[10,8,1024]{2,1,0:T(8,128)(2,1)S(1)}, u32[]{:S(2)}, u32[]{:S(2)}) collective-permute-start(bf16[10,8,1024]{2,1,0:T(8,128)(2,1)S(1)} %coarse.11), channel_id=1, source_target_pairs={{0,4},{4,8},{8,12},{12,16},{16,20},{20,24},{24,28},{1,5},{5,9},{9,... | collective-permute-start | bytes 491528 | tf_op jit(solution)/shard_map/ppermute | solution.py:449
  77.2 11.5 %collective-permute-start.17 = (bf16[14,8,1536]{2,1,0:T(8,128)(2,1)S(1)}, bf16[14,8,1536]{2,1,0:T(8,128)(2,1)S(1)}, u32[]{:S(2)}, u32[]{:S(2)}) collective-permute-start(bf16[14,8,1536]{2,1,0:T(8,128)(2,1)S(1)} %bitcast.20), channel_id=1, source_target_pairs={{0,2},{1,3},{2,0},{3,1},{4,6},{5,7},{6,4},{7,5},{8,10},{9,11},{10,... | collective-permute-start | bytes 1032200 | tf_op jit(solution)/shard_map/ppermute | solution.py:443
  79.2 11.6 %collective-permute-start.16 = (bf16[28,8,1536]{2,1,0:T(8,128)(2,1)S(1)}, bf16[28,8,1536]{2,1,0:T(8,128)(2,1)S(1)}, u32[]{:S(2)}, u32[]{:S(2)}) collective-permute-start(bf16[28,8,1536]{2,1,0:T(8,128)(2,1)S(1)} %pad_maximum_fusion.refs_0_), channel_id=1, source_target_pairs={{0,1},{1,0},{2,3},{3,2},{4,5},{5,4},{6,7},{7,6},{8,9},{9,8},{10,11... | collective-permute-start | bytes 2064392 | tf_op jit(solution)/shard_map/ppermute | solution.py:446
  88.8 4.0 %collective-permute-start.18 = (bf16[28,8,1536]{2,1,0:T(8,128)(2,1)S(1)}, bf16[28,8,1536]{2,1,0:T(8,128)(2,1)S(1)}, u32[]{:S(2)}, u32[]{:S(2)}) collective-permute-start(bf16[28,8,1536]{2,1,0:T(8,128)(2,1)S(1)} %pad_maximum_fusion.1.refs_1_), channel_id=1, source_target_pairs={{0,1},{1,0},{2,3},{3,2},{4,5},{5,4},{6,7},{7,6},{8,9},{9,8},{10,11... | collective-permute-start | bytes 2064392 | tf_op jit(solution)/shard_map/ppermute | solution.py:446
  90.1 7.2 %collective-permute-start.12 = (bf16[14,8,1024]{2,1,0:T(8,128)(2,1)S(1)}, bf16[14,8,1024]{2,1,0:T(8,128)(2,1)S(1)}, u32[]{:S(2)}, u32[]{:S(2)}) collective-permute-start(bf16[14,8,1024]{2,1,0:T(8,128)(2,1)S(1)} %bitcast.24), channel_id=1, source_target_pairs={{0,2},{1,3},{2,0},{3,1},{4,6},{5,7},{6,4},{7,5},{8,10},{9,11},{10,... | collective-permute-start | bytes 688136 | tf_op jit(solution)/shard_map/ppermute | solution.py:443
  97.3 2.4 %collective-permute-start.19 = (bf16[28,8,1024]{2,1,0:T(8,128)(2,1)S(1)}, bf16[28,8,1024]{2,1,0:T(8,128)(2,1)S(1)}, u32[]{:S(2)}, u32[]{:S(2)}) collective-permute-start(bf16[28,8,1024]{2,1,0:T(8,128)(2,1)S(1)} %pad_maximum_fusion.2.refs_1_), channel_id=1, source_target_pairs={{0,1},{1,0},{2,3},{3,2},{4,5},{5,4},{6,7},{7,6},{8,9},{9,8},{10,11... | collective-permute-start | bytes 1376264 | tf_op jit(solution)/shard_map/ppermute | solution.py:446
